TPU v7x, 256 devices: a whole 4x4x8 slice. The times are simulated.
256 devices in a mesh: leaf: 256 (over x, z, y, core).
Axes of the slice: x: 4, y: 4, z: 8, core: 2. Of those that a mesh axis runs over, the one named last changes fastest.
Arguments:
- cotangent: float32 [2, 64, 65536], P(None, None, 'leaf'), may hold values from -30 to 30
- nodal_mass: float32 [64, 65536], P(None, 'leaf'), may hold values from 0.5 to 2
- curvature: float32 [64, 65536], P(None, 'leaf'), may hold values from -1 to 2
- stiffness: float32 [64, 64], replicated, may hold values from -0.75 to 0.75
- levels: int32 [65536], P('leaf'), may hold values from 0 to 3
- neighbours: int32 [6, 65536], P(None, 'leaf'), may hold values from -1 to 65535, as said below
- mortars: int32 [6, 32768], P(None, 'leaf'), may hold values from -1 to 65535, as said below
Outputs:
- adjoint: float32 [2, 64, 65536], P(None, None, 'leaf')
Inputs may be any that keep to these rules, and one draw needn't show every extreme that they name: For each a of 0, 1, 2: neighbours[2 a + 1, i] = j >= 0 exactly when neighbours[2 a, j] = i. Every neighbour belongs to the same, the previous or the next device's block of 256 leaves. `mortars`: on each device's 128 slots the used ones come first; an unused slot holds -1 in all six rows. A used slot has a face of 0 to 5, a coarse leaf of the same device and fine leaves of the same, the previous or the next device. On some device all 128 slots are used.
All inputs are finite; a program needn't handle non-finite values.
Results may differ from a plain program's by a relative error of at most 0.002.
Values sent between devices are 32-bit elements; how exact they have to be, the bound alone decides.
No kernel may reach another device: no remote copies, remote signals or barrier semaphores. Data moves between devices by JAX's collectives and lax.ppermute only.
A program may use at most 128 MiB of HBM per device.

v0:
```python
import jax
import jax.numpy as jnp
import numpy as np
from jax import lax
from jax.sharding import PartitionSpec as P

TAU_WEIGHT = 0.15
EPS_WEIGHT = 0.1
FLIP_ORDER = [1, 0, 3, 2, 5, 4]


def with_halo(cells, sides, width):
    for axis, dim in sides:
        count = lax.axis_size(axis)
        ends = count - 1
        head = lax.slice_in_dim(cells, 0, width, axis=dim)
        tail = lax.slice_in_dim(cells, cells.shape[dim] - width, cells.shape[dim], axis=dim)
        cells = jnp.concatenate(
            [
                lax.ppermute(tail, axis, [(i, (i + 1) % count) for i in range(ends)]),
                cells,
                lax.ppermute(head, axis, [((i + 1) % count, i) for i in range(ends)]),
            ],
            axis=dim,
        )
    return cells


def face_tables():
    select = np.zeros((6, 16, 64))
    node_at = np.zeros((6, 16), dtype=np.int64)
    for face_id in range(6):
        axis_id = face_id // 2
        layer_at = 3 * (face_id % 2)
        for row_pos in range(4):
            for col_pos in range(4):
                coords = [row_pos, col_pos]
                coords.insert(axis_id, layer_at)
                node_id = 16 * coords[0] + 4 * coords[1] + coords[2]
                select[face_id, 4 * row_pos + col_pos, node_id] = 1.0
                node_at[face_id, 4 * row_pos + col_pos] = node_id
    across = np.zeros((6, 64, 64))
    for face_id in range(6):
        other_face = FLIP_ORDER[face_id]
        for place in range(16):
            across[face_id, node_at[face_id, place], node_at[other_face, place]] += 1.0
    counts = select.sum(axis=(0, 1))
    points = np.array([-1.0, -1.0 / np.sqrt(5.0), 1.0 / np.sqrt(5.0), 1.0])
    halves = np.zeros((2, 4, 4))
    for half_id in range(2):
        target = (points + 2.0 * half_id - 1.0) / 2.0
        for column in range(4):
            lagrange = np.ones(4)
            for other_id in range(4):
                if other_id != column:
                    lagrange = (
                        lagrange * (target - points[other_id]) / (points[column] - points[other_id])
                    )
            halves[half_id, :, column] = lagrange
    mortar = np.stack([np.kron(halves[quarter // 2], halves[quarter % 2]) for quarter in range(4)])
    return (
        jnp.asarray(select, jnp.float32),
        jnp.asarray(across, jnp.float32),
        jnp.asarray(counts, jnp.float32),
        jnp.asarray(mortar, jnp.float32),
    )


def least_squares(rhs_norm, first_diag, first_below, upper_right, second_diag, second_below):
    first_len = jnp.sqrt(first_diag * first_diag + first_below * first_below)
    cos_one = first_diag / first_len
    sin_one = first_below / first_len
    rotated_top = cos_one * upper_right + sin_one * second_diag
    rotated_low = cos_one * second_diag - sin_one * upper_right
    second_len = jnp.sqrt(rotated_low * rotated_low + second_below * second_below)
    cos_two = rotated_low / second_len
    y_two = cos_two * (-sin_one * rhs_norm) / second_len
    y_one = (cos_one * rhs_norm - rotated_top * y_two) / first_len
    return (y_one, y_two)


def one_hot_faces(face_row):
    return (face_row[None, :] == jnp.arange(6, dtype=jnp.int32)[:, None]).astype(jnp.float32)


def on_device(cotangent, nodal_mass, curvature, stiffness, levels, neighbours, mortars):
    select, across, counts, mortar = face_tables()
    highest = lax.Precision.HIGHEST
    flip_index = jnp.array(FLIP_ORDER, dtype=jnp.int32)
    leaves = cotangent.shape[2]
    offset = lax.axis_index("leaf") * leaves
    level_scale = jnp.left_shift(jnp.ones_like(levels), levels).astype(jnp.float32)
    near_index = jnp.clip(neighbours - offset + leaves, 0, 3 * leaves - 1)
    near_valid = neighbours >= 0
    coarse_local = jnp.clip(mortars[0] - offset, 0, leaves - 1)
    facing = one_hot_faces(mortars[1])
    flipped = facing[flip_index]
    fine_near = jnp.clip(mortars[2:6] - offset + leaves, 0, 3 * leaves - 1)

    def lap_t(nodal_in):
        weighted = nodal_in * level_scale
        extended = with_halo(weighted, (("leaf", 2),), leaves)
        result = (
            jnp.einsum("mn,xmL->xnL", stiffness, weighted, precision=highest)
            + counts[:, None] * weighted
        )
        for face_id in range(6):
            values = jnp.take(extended, near_index[face_id], axis=2)
            moved_in = jnp.einsum("nm,xmL->xnL", across[face_id], values, precision=highest)
            result = result - jnp.where(near_valid[face_id], moved_in, 0.0)
        coarse_trace = jnp.einsum(
            "fpn,xnS,fS->xpS",
            select,
            jnp.take(weighted, coarse_local, axis=2),
            facing,
            precision=highest,
        )
        coarse_sum = jnp.zeros_like(coarse_trace)
        mismatches = []
        for quarter in range(4):
            fine_vals = jnp.take(extended, fine_near[quarter], axis=2)
            fine_trace = jnp.einsum(
                "fpn,xnS,fS->xpS", select, fine_vals, flipped, precision=highest
            )
            mismatch = (
                jnp.einsum("pr,xrS->xpS", mortar[quarter], coarse_trace, precision=highest)
                - fine_trace
            )
            coarse_sum = coarse_sum + jnp.einsum(
                "rp,xrS->xpS", mortar[quarter], mismatch, precision=highest
            )
            mismatches.append(mismatch)
        spread = jnp.einsum("fpn,xpS,fS->xnS", select, coarse_sum, facing, precision=highest)
        result = result.at[:, :, coarse_local].add(spread)
        buffer = jnp.zeros((nodal_in.shape[0], nodal_in.shape[1], 3 * leaves), jnp.float32)
        for quarter in range(4):
            spread = jnp.einsum(
                "fpn,xpS,fS->xnS", select, mismatches[quarter], flipped, precision=highest
            )
            buffer = buffer.at[:, :, fine_near[quarter]].add(-spread)
        outgoing = jnp.concatenate([buffer[:, :, :leaves], buffer[:, :, 2 * leaves :]], axis=2)
        arrived = with_halo(outgoing, (("leaf", 2),), leaves)
        result = (
            result
            + buffer[:, :, leaves : 2 * leaves]
            + arrived[:, :, :leaves]
            + arrived[:, :, 3 * leaves :]
        )
        return result

    def apply_t(vector):
        lapped = lap_t(jnp.stack([vector[1], vector[0]]))
        return jnp.stack(
            [
                nodal_mass * vector[0] - curvature * vector[1] - EPS_WEIGHT * lapped[0],
                TAU_WEIGHT * lapped[1] + nodal_mass * vector[1],
            ]
        )

    rhs_norm = jnp.sqrt(lax.psum(jnp.sum(cotangent * cotangent), "leaf"))
    basis_one = cotangent / rhs_norm
    image = apply_t(basis_one)
    first_diag = lax.psum(jnp.sum(image * basis_one), "leaf")
    image = image - first_diag * basis_one
    first_below = jnp.sqrt(lax.psum(jnp.sum(image * image), "leaf"))
    basis_two = image / first_below
    image = apply_t(basis_two)
    upper_right, second_diag = lax.psum(
        (jnp.sum(image * basis_one), jnp.sum(image * basis_two)), "leaf"
    )
    image = image - upper_right * basis_one - second_diag * basis_two
    second_below = jnp.sqrt(lax.psum(jnp.sum(image * image), "leaf"))
    y_one, y_two = least_squares(
        rhs_norm, first_diag, first_below, upper_right, second_diag, second_below
    )
    return y_one * basis_one + y_two * basis_two


def solution(mesh):
    placed = (
        P(None, None, "leaf"),
        P(None, "leaf"),
        P(None, "leaf"),
        P(),
        P("leaf"),
        P(None, "leaf"),
        P(None, "leaf"),
    )
    return jax.shard_map(
        on_device, mesh=mesh, in_specs=placed, out_specs=P(None, None, "leaf"), check_vma=False
    )
```

profile of v0, /device:TPU:1, one launch (start us, length us, event | category | flops | bytes accessed | tf_op | source)
XLA Modules:
  0.0 600.6 jit_solution(1014361008719830291)
XLA Ops:
  0.0 1.6 multiply_reduce_fusion.5
  1.6 81.4 %psum.42 = f32[]{:T(128)} all-reduce(f32[]{:T(128)} %multiply_reduce_fusion.5), channel_id=1, replica_groups=mesh['leaf'=256] {'leaf'}, use_global_device_ids=true, to_apply=%region_1.2 | all-reduce | flops 1 | bytes 8 | tf_op jit(solution)/shard_map/psum | solution.py:160
  85.4 1.9 collective-permute-start
  87.3 2.4 collective-permute-start.1
  98.3 1.8 convolution_bitcast_fusion.2
  103.7 1.8 fusion.79
  106.9 1.8 fusion.77
  110.0 1.8 fusion.75
  113.8 2.5 fusion.73
  122.0 1.1 fusion.6
  123.1 1.5 fusion.5
  124.8 5.2 scatter_fusion
  130.0 5.2 scatter_fusion.1
  135.2 5.2 scatter_fusion.2
  140.4 5.2 scatter_fusion.3
  146.4 1.8 copy.186
  148.2 3.4 collective-permute-start.2
  151.5 1.7 copy.187
  153.2 2.0 collective-permute-start.3
  156.1 1.7 gather_fusion.6
  157.7 1.7 gather_fusion.5
  159.4 1.7 gather_fusion.4
  161.1 1.7 gather_fusion.3
  164.7 1.3 select_bitcast_fusion.6
  166.1 1.3 select_bitcast_fusion.7
  172.8 1.3 fusion.18
  174.4 5.2 scatter_fusion.4
  181.1 82.0 %psum.43 = f32[]{:T(128)} all-reduce(f32[]{:T(128)} %multiply_reduce_fusion.4), channel_id=1, replica_groups=mesh['leaf'=256] {'leaf'}, use_global_device_ids=true, to_apply=%region_8.12 | all-reduce | flops 1 | bytes 8 | tf_op jit(solution)/shard_map/psum | solution.py:163
  263.1 1.2 multiply_reduce_fusion.3
  265.4 73.4 %psum.44 = f32[]{:T(128)} all-reduce(f32[]{:T(128)} %multiply_reduce_fusion.3), channel_id=1, replica_groups=mesh['leaf'=256] {'leaf'}, use_global_device_ids=true, to_apply=%region_10.14 | all-reduce | flops 1 | bytes 8 | tf_op jit(solution)/shard_map/psum | solution.py:165
  340.7 2.8 collective-permute-start.4
  343.5 1.9 collective-permute-start.5
  347.2 1.8 convolution_bitcast_fusion
  350.5 1.5 gather_fusion.22
  354.6 2.7 fusion.62
  358.9 1.5 fusion.159
  361.2 2.4 fusion.64
  364.5 1.5 fusion.158
  366.8 2.4 fusion.66
  371.0 1.8 fusion.68
  374.6 1.8 gather_fusion.17
  376.4 1.8 gather_fusion.16
  378.2 1.8 gather_fusion.15
  380.0 1.8 gather_fusion.14
  381.8 1.1 gather_fusion.13
  382.9 1.1 gather_fusion.12
  384.0 1.5 copy.182
  385.5 1.5 copy.181
  387.7 1.5 copy.179
  389.2 2.2 fusion
  392.6 1.1 fusion.2
  395.0 5.2 scatter_fusion.5
  400.2 5.2 scatter_fusion.6
  405.4 5.2 scatter_fusion.7
  410.5 5.2 scatter_fusion.8
  416.6 3.1 collective-permute-start.6
  420.5 1.9 collective-permute-start.7
  428.7 1.3 fusion.27
  430.2 5.4 scatter_fusion.9
  436.6 1.2 multiply_reduce_fusion.2
  437.8 82.0 %all-reduce = (f32[]{:T(128)}, f32[]{:T(128)}) all-reduce(f32[]{:T(128)} %get-tuple-element.8, f32[]{:T(128)} %get-tuple-element.6), channel_id=1, replica_groups=mesh['leaf'=256] {'leaf'}, use_global_device_ids=true, to_apply=%region_19.23 | all-reduce | flops 2 | bytes 16 | tf_op jit(solution)/shard_map/psum | solution.py:168
  521.0 2.5 multiply_reduce_fusion
  524.8 73.4 %psum.47 = f32[]{:T(128)} all-reduce(f32[]{:T(128)} %multiply_reduce_fusion), channel_id=1, replica_groups=mesh['leaf'=256] {'leaf'}, use_global_device_ids=true, to_apply=%region_21.25 | all-reduce | flops 1 | bytes 8 | tf_op jit(solution)/shard_map/psum | solution.py:172
  599.1 1.3 multiply_add_fusion
  (380 shorter events, 59.7 us)
Async XLA Ops:
  0.0 172.8 %copy-start = (f32[64,64]{1,0:T(8,128)S(1)}, f32[64,64]{1,0:T(8,128)}, u32[]{:S(2)}) copy-start(f32[64,64]{1,0:T(8,128)} %param.21) | copy-start | bytes 49156
  0.0 94.9 %copy-start.112 = (s32[6]{0:T(128)S(1)}, s32[6]{0:T(128)}, u32[]{:S(2)}) copy-start(s32[6]{0:T(128)} %constant.101) | copy-start | bytes 76
  0.0 94.9 %copy-start.34 = (f32[6,16,64]{2,0,1:T(8,128)S(1)}, f32[6,16,64]{2,0,1:T(8,128)}, u32[]{:S(2)}) copy-start(f32[6,16,64]{2,0,1:T(8,128)} %constant.51.clone) | copy-start | bytes 73732
  0.0 89.9 %copy-start.111 = (s32[6,128]{1,0:T(8,128)S(1)}, s32[6,128]{1,0:T(8,128)}, u32[]{:S(2)}) copy-start(s32[6,128]{1,0:T(8,128)} %param.24) | copy-start | bytes 9220
  0.0 91.1 %copy-start.56 = (s32[6,256]{1,0:T(8,128)S(1)}, s32[6,256]{1,0:T(8,128)}, u32[]{:S(2)}) copy-start(s32[6,256]{1,0:T(8,128)} %param.23) | copy-start | bytes 18436
  84.6 12.2 %copy-start.11 = (f32[2,64,256]{2,1,0:T(8,128)}, f32[2,64,256]{2,1,0:T(8,128)S(1)}, u32[]{:S(2)}) copy-start(f32[2,64,256]{2,1,0:T(8,128)S(1)} %broadcast_divide_fusion.1) | copy-start | bytes 393220
  85.4 16.0 %copy-start.7 = (f32[2,64,256]{2,1,0:T(8,128)}, f32[2,64,256]{2,1,0:T(8,128)S(1)}, u32[]{:S(2)}) copy-start(f32[2,64,256]{2,1,0:T(8,128)S(1)} %maximum_multiply_fusion) | copy-start | bytes 393220
  85.4 15.9 %collective-permute-start = (f32[2,64,256]{2,1,0:T(8,128)S(1)}, f32[2,64,256]{2,1,0:T(8,128)S(1)}, u32[]{:S(2)}, u32[]{:S(2)}) collective-permute-start(f32[2,64,256]{2,1,0:T(8,128)S(1)} %maximum_multiply_fusion), channel_id=1, source_target_pairs={{0,1},{1,2},{2,3},{3,4},{4,5},{5,6},{6,7},{7,8},{8,9},{9,10},{10,1... | collective-permute-start | bytes 393224 | tf_op jit(solution)/shard_map/ppermute | solution.py:20
  87.3 14.0 %collective-permute-start.1 = (f32[2,64,256]{2,1,0:T(8,128)S(1)}, f32[2,64,256]{2,1,0:T(8,128)}, u32[]{:S(2)}, u32[]{:S(2)}) collective-permute-start(f32[2,64,256]{2,1,0:T(8,128)S(1)} %maximum_multiply_fusion), channel_id=1, source_target_pairs={{1,0},{2,1},{3,2},{4,3},{5,4},{6,5},{7,6},{8,7},{9,8},{10,9},{11,1... | collective-permute-start | bytes 393224 | tf_op jit(solution)/shard_map/ppermute | solution.py:22
  90.0 8.3 %copy-start.85 = (pred[128]{0:T(512)(128)(4,1)}, pred[128]{0:T(512)(128)(4,1)S(1)}, u32[]{:S(2)}) copy-start(pred[128]{0:T(512)(128)(4,1)S(1)} %get-tuple-element.26) | copy-start | bytes 388
  90.5 13.2 %copy-start.79 = (pred[128]{0:T(512)(128)(4,1)}, pred[128]{0:T(512)(128)(4,1)S(1)}, u32[]{:S(2)}) copy-start(pred[128]{0:T(512)(128)(4,1)S(1)} %get-tuple-element.52) | copy-start | bytes 388
  90.5 16.3 %copy-start.83 = (pred[128]{0:T(512)(128)(4,1)}, pred[128]{0:T(512)(128)(4,1)S(1)}, u32[]{:S(2)}) copy-start(pred[128]{0:T(512)(128)(4,1)S(1)} %get-tuple-element.54) | copy-start | bytes 388
  90.5 19.5 %copy-start.84 = (pred[128]{0:T(512)(128)(4,1)}, pred[128]{0:T(512)(128)(4,1)S(1)}, u32[]{:S(2)}) copy-start(pred[128]{0:T(512)(128)(4,1)S(1)} %get-tuple-element.56) | copy-start | bytes 388
  97.3 58.7 %copy-start.58 = (s32[1024]{0:T(1024)}, s32[1024]{0:T(1024)S(1)}, u32[]{:S(2)}) copy-start(s32[1024]{0:T(1024)S(1)} %pad_clamp_fusion.6) | copy-start | bytes 12292
  97.4 60.4 %copy-start.59 = (s32[1024]{0:T(1024)}, s32[1024]{0:T(1024)S(1)}, u32[]{:S(2)}) copy-start(s32[1024]{0:T(1024)S(1)} %pad_clamp_fusion.7) | copy-start | bytes 12292
  97.4 62.0 %copy-start.60 = (s32[1024]{0:T(1024)}, s32[1024]{0:T(1024)S(1)}, u32[]{:S(2)}) copy-start(s32[1024]{0:T(1024)S(1)} %pad_clamp_fusion.8) | copy-start | bytes 12292
  97.4 63.7 %copy-start.61 = (s32[1024]{0:T(1024)}, s32[1024]{0:T(1024)S(1)}, u32[]{:S(2)}) copy-start(s32[1024]{0:T(1024)S(1)} %pad_clamp_fusion.9) | copy-start | bytes 12292
  97.4 65.3 %copy-start.62 = (s32[1024]{0:T(1024)}, s32[1024]{0:T(1024)S(1)}, u32[]{:S(2)}) copy-start(s32[1024]{0:T(1024)S(1)} %pad_clamp_fusion.10) | copy-start | bytes 12292
  97.5 11.8 %copy-start.64 = (s32[1024]{0:T(1024)}, s32[1024]{0:T(1024)S(1)}, u32[]{:S(2)}) copy-start(s32[1024]{0:T(1024)S(1)} %get-tuple-element.63) | copy-start | bytes 12292
  97.5 15.6 %copy-start.65 = (s32[1024]{0:T(1024)}, s32[1024]{0:T(1024)S(1)}, u32[]{:S(2)}) copy-start(s32[1024]{0:T(1024)S(1)} %get-tuple-element.62) | copy-start | bytes 12292
  98.2 4.7 copy-start.66
  98.2 7.9 %copy-start.67 = (s32[1024]{0:T(1024)}, s32[1024]{0:T(1024)S(1)}, u32[]{:S(2)}) copy-start(s32[1024]{0:T(1024)S(1)} %get-tuple-element.64) | copy-start | bytes 12292
  100.1 63.6 %copy-start.63 = (s32[1024]{0:T(1024)}, s32[1024]{0:T(1024)S(1)}, u32[]{:S(2)}) copy-start(s32[1024]{0:T(1024)S(1)} %pad_clamp_fusion.11) | copy-start | bytes 12292
  101.3 67.6 %copy-start.81 = (pred[256]{0:T(512)(128)(4,1)}, pred[256]{0:T(512)(128)(4,1)S(1)}, u32[]{:S(2)}) copy-start(pred[256]{0:T(512)(128)(4,1)S(1)} %get-tuple-element.11) | copy-start | bytes 772
  101.3 68.1 %copy-start.77 = (pred[256]{0:T(512)(128)(4,1)}, pred[256]{0:T(512)(128)(4,1)S(1)}, u32[]{:S(2)}) copy-start(pred[256]{0:T(512)(128)(4,1)S(1)} %get-tuple-element.12) | copy-start | bytes 772
  101.3 68.5 %copy-start.75 = (pred[256]{0:T(512)(128)(4,1)}, pred[256]{0:T(512)(128)(4,1)S(1)}, u32[]{:S(2)}) copy-start(pred[256]{0:T(512)(128)(4,1)S(1)} %get-tuple-element.13) | copy-start | bytes 772
  101.3 69.0 %copy-start.73 = (pred[256]{0:T(512)(128)(4,1)}, pred[256]{0:T(512)(128)(4,1)S(1)}, u32[]{:S(2)}) copy-start(pred[256]{0:T(512)(128)(4,1)S(1)} %get-tuple-element.14) | copy-start | bytes 772
  102.9 10.1 %copy-start.3 = (f32[2,64,768]{1,0,2:T(2,128)}, f32[2,64,768]{1,0,2:T(2,128)S(1)}, u32[]{:S(2)}) copy-start(f32[2,64,768]{1,0,2:T(2,128)S(1)} %copy.82) | copy-start | bytes 1179652
  124.8 5.2 copy-start.91
  130.0 5.2 copy-start.89
  135.2 5.2 copy-start.87
  146.4 9.7 %copy-start.4 = (f32[2,64,768]{1,0,2:T(2,128)S(1)}, f32[2,64,768]{1,0,2:T(2,128)}, u32[]{:S(2)}) copy-start(f32[2,64,768]{1,0,2:T(2,128)} %copy-done.3) | copy-start | bytes 1179652
  148.2 24.6 %collective-permute-start.2 = (f32[2,64,256]{2,1,0:T(8,128)}, f32[2,64,256]{2,1,0:T(8,128)}, u32[]{:S(2)}, u32[]{:S(2)}) collective-permute-start(f32[2,64,256]{2,1,0:T(8,128)} %copy.186), channel_id=1, source_target_pairs={{0,1},{1,2},{2,3},{3,4},{4,5},{5,6},{6,7},{7,8},{8,9},{9,10},{10,1... | collective-permute-start | bytes 393224 | tf_op jit(solution)/shard_map/ppermute | solution.py:20
  153.2 11.4 %copy-start.109 = (pred[256]{0:T(512)(128)(4,1)S(1)}, pred[256]{0:T(512)(128)(4,1)}, u32[]{:S(2)}) copy-start(pred[256]{0:T(512)(128)(4,1)} %compare_and_fusion.5) | copy-start | bytes 772
  153.2 19.5 %collective-permute-start.3 = (f32[2,64,256]{2,1,0:T(8,128)}, f32[2,64,256]{2,1,0:T(8,128)}, u32[]{:S(2)}, u32[]{:S(2)}) collective-permute-start(f32[2,64,256]{2,1,0:T(8,128)} %copy.187), channel_id=1, source_target_pairs={{1,0},{2,1},{3,2},{4,3},{5,4},{6,5},{7,6},{8,7},{9,8},{10,9},{11,1... | collective-permute-start | bytes 393224 | tf_op jit(solution)/shard_map/ppermute | solution.py:22
  156.1 10.0 %copy-start.107 = (pred[256]{0:T(512)(128)(4,1)S(1)}, pred[256]{0:T(512)(128)(4,1)}, u32[]{:S(2)}) copy-start(pred[256]{0:T(512)(128)(4,1)} %compare_and_fusion.6) | copy-start | bytes 772
  159.4 8.0 %copy-start.105 = (pred[256]{0:T(512)(128)(4,1)S(1)}, pred[256]{0:T(512)(128)(4,1)}, u32[]{:S(2)}) copy-start(pred[256]{0:T(512)(128)(4,1)} %compare_and_fusion.7) | copy-start | bytes 772
  162.7 5.1 copy-start.103
  174.3 5.6 copy-start.12
  174.3 5.6 copy-start.35
  174.4 5.6 copy-start.37
  180.0 169.0 %copy-start.5 = (f32[1,64,256]{2,1,0:T(8,128)}, f32[1,64,256]{2,1,0:T(8,128)S(1)}, u32[]{:S(2)}) copy-start(f32[1,64,256]{2,1,0:T(8,128)S(1)} %get-tuple-element.41) | copy-start | bytes 196612
  180.0 167.1 %copy-start.86 = (pred[128]{0:T(512)(128)(4,1)S(1)}, pred[128]{0:T(512)(128)(4,1)}, u32[]{:S(2)}) copy-start(pred[128]{0:T(512)(128)(4,1)} %copy-done.85) | copy-start | bytes 388
  340.7 9.1 %copy-start.9 = (f32[2,64,256]{2,1,0:T(8,128)}, f32[2,64,256]{2,1,0:T(8,128)S(1)}, u32[]{:S(2)}) copy-start(f32[2,64,256]{2,1,0:T(8,128)S(1)} %maximum_multiply_fusion.1) | copy-start | bytes 393220
  340.7 8.3 %collective-permute-start.4 = (f32[2,64,256]{2,1,0:T(8,128)S(1)}, f32[2,64,256]{2,1,0:T(8,128)S(1)}, u32[]{:S(2)}, u32[]{:S(2)}) collective-permute-start(f32[2,64,256]{2,1,0:T(8,128)S(1)} %maximum_multiply_fusion.1), channel_id=1, source_target_pairs={{0,1},{1,2},{2,3},{3,4},{4,5},{5,6},{6,7},{7,8},{8,9},{9,10},{10,1... | collective-permute-start | bytes 393224 | tf_op jit(solution)/shard_map/ppermute | solution.py:20
  343.5 6.3 %collective-permute-start.5 = (f32[2,64,256]{2,1,0:T(8,128)S(1)}, f32[2,64,256]{2,1,0:T(8,128)S(1)}, u32[]{:S(2)}, u32[]{:S(2)}) collective-permute-start(f32[2,64,256]{2,1,0:T(8,128)S(1)} %maximum_multiply_fusion.1), channel_id=1, source_target_pairs={{1,0},{2,1},{3,2},{4,3},{5,4},{6,5},{7,6},{8,7},{9,8},{10,9},{11,1... | collective-permute-start | bytes 393224 | tf_op jit(solution)/shard_map/ppermute | solution.py:22
  363.6 5.7 copy-start.53
  363.6 7.4 %copy-start.80 = (pred[128]{0:T(512)(128)(4,1)S(1)}, pred[128]{0:T(512)(128)(4,1)}, u32[]{:S(2)}) copy-start(pred[128]{0:T(512)(128)(4,1)} %copy-done.79) | copy-start | bytes 388
  373.0 14.0 %copy-start.57 = (f32[2,128,16]{1,2,0:T(8,128)S(1)}, f32[2,128,16]{1,2,0:T(8,128)}, u32[]{:S(2)}) copy-start(f32[2,128,16]{1,2,0:T(8,128)} %fusion.157) | copy-start | bytes 49156
  384.0 7.4 %copy-start.21 = (f32[2,16,128]{1,0,2:T(2,128)S(1)}, f32[2,16,128]{1,0,2:T(2,128)}, u32[]{:S(2)}) copy-start(f32[2,16,128]{1,0,2:T(2,128)} %copy.159) | copy-start | bytes 49156
  395.0 5.2 copy-start.92
  400.2 5.2 copy-start.90
  405.4 5.2 copy-start.88
  415.7 6.8 %copy-start.18 = (f32[256,2,64]{2,1,0:T(2,128)S(1)}, f32[256,2,64]{2,1,0:T(2,128)}, u32[]{:S(2)}) copy-start(f32[256,2,64]{2,1,0:T(2,128)} %gather_fusion.17) | copy-start | bytes 393220
  415.7 6.8 %copy-start.110 = (pred[256]{0:T(512)(128)(4,1)S(1)}, pred[256]{0:T(512)(128)(4,1)}, u32[]{:S(2)}) copy-start(pred[256]{0:T(512)(128)(4,1)} %compare_and_fusion.5) | copy-start | bytes 772
  415.8 7.1 %copy-start.49 = (f32[64,64,1]{1,0,2:T(8,128)S(1)}, f32[64,64,1]{1,0,2:T(8,128)}, u32[]{:S(2)}) copy-start(f32[64,64,1]{1,0,2:T(8,128)} %constant.107) | copy-start | bytes 49156
  415.8 7.1 %copy-start.82 = (pred[256]{0:T(512)(128)(4,1)S(1)}, pred[256]{0:T(512)(128)(4,1)}, u32[]{:S(2)}) copy-start(pred[256]{0:T(512)(128)(4,1)} %copy-done.81) | copy-start | bytes 772
  415.8 7.6 %copy-start.17 = (f32[256,2,64]{2,1,0:T(2,128)S(1)}, f32[256,2,64]{2,1,0:T(2,128)}, u32[]{:S(2)}) copy-start(f32[256,2,64]{2,1,0:T(2,128)} %gather_fusion.16) | copy-start | bytes 393220
  415.8 7.6 %copy-start.108 = (pred[256]{0:T(512)(128)(4,1)S(1)}, pred[256]{0:T(512)(128)(4,1)}, u32[]{:S(2)}) copy-start(pred[256]{0:T(512)(128)(4,1)} %compare_and_fusion.6) | copy-start | bytes 772
  416.6 12.1 %collective-permute-start.6 = (f32[2,64,256]{2,1,0:T(8,128)}, f32[2,64,256]{2,1,0:T(8,128)}, u32[]{:S(2)}, u32[]{:S(2)}) collective-permute-start(f32[2,64,256]{2,1,0:T(8,128)} %copy.191), channel_id=1, source_target_pairs={{0,1},{1,2},{2,3},{3,4},{4,5},{5,6},{6,7},{7,8},{8,9},{9,10},{10,1... | collective-permute-start | bytes 393224 | tf_op jit(solution)/shard_map/ppermute | solution.py:20
  420.5 8.2 %collective-permute-start.7 = (f32[2,64,256]{2,1,0:T(8,128)}, f32[2,64,256]{2,1,0:T(8,128)}, u32[]{:S(2)}, u32[]{:S(2)}) collective-permute-start(f32[2,64,256]{2,1,0:T(8,128)} %copy.192), channel_id=1, source_target_pairs={{1,0},{2,1},{3,2},{4,3},{5,4},{6,5},{7,6},{8,7},{9,8},{10,9},{11,1... | collective-permute-start | bytes 393224 | tf_op jit(solution)/shard_map/ppermute | solution.py:22
  430.2 5.9 copy-start.14
  430.2 5.9 copy-start.36
  430.2 5.9 copy-start.38
  (57 other events, 116.0 us)
where the time goes:
time: 607 us; the launch traced here: 601 us
  blocking collectives  392 us (65%)
  other arithmetic  74.5 us (12%)
  local copies, waits for them, and re-layouts  54.3 us (9%)
  matrix products  50.2 us (8%)
  starting transfers between devices  19.4 us (3%)
  between operations  9.24 us (2%)
    psum x1, blocking collectives, on_device(): first_diag = lax.psum(jnp.sum(image * basis_one), 'leaf')  82 us
    psum x1, blocking collectives, on_device(): lax.psum((jnp.sum(image * basis_one), jnp.sum(image * basis_two)), 'leaf')  82 us
    psum x1, blocking collectives, on_device(): rhs_norm = jnp.sqrt(lax.psum(jnp.sum(cotangent * cotangent), 'leaf'))  81.4 us
    psum x1, blocking collectives, on_device(): second_below = jnp.sqrt(lax.psum(jnp.sum(image * image), 'leaf'))  73.4 us
    psum x1, blocking collectives, on_device(): first_below = jnp.sqrt(lax.psum(jnp.sum(image * image), 'leaf'))  73.4 us
    scatter-add x8, other arithmetic, lap_t(): buffer = buffer.at[:, :, fine_near[quarter]].add(-spread)  41.3 us
    gather x12, local copies, waits for them, and re-layouts, lap_t(): values = jnp.take(extended, near_index[face_id], axis=2)  18 us
    dot_general x9, matrix products, lap_t(): jnp.einsum('fpn,xnS,fS->xpS', select, fine_vals, flipped, precision=highest)  17.9 us
  transfers between devices with their start and end apart: 8, of which 1 were waited for; matrix products, arithmetic and copies ran while one was open for 7% of the time, Pallas kernels for 0%

commit v1 on v0

v1 whole, which is shorter than its diff:
```python
import jax
import jax.numpy as jnp
import ml_dtypes
import numpy as np
from jax import lax
from jax.experimental import pallas as pl
from jax.experimental.pallas import tpu as pltpu
from jax.sharding import PartitionSpec as P

TAU_WEIGHT = 0.15
EPS_WEIGHT = 0.1
FACES = 6
NODES = 64
LANES = 128
TRACE = 256
F32 = jnp.float32
BF16 = jnp.bfloat16


def face_tables():
    node_at = np.zeros((6, 16), dtype=np.int64)
    for face_id in range(6):
        for row_pos in range(4):
            for col_pos in range(4):
                coords = [row_pos, col_pos]
                coords.insert(face_id // 2, 3 * (face_id % 2))
                node_at[face_id, 4 * row_pos + col_pos] = (
                    16 * coords[0] + 4 * coords[1] + coords[2]
                )
    counts = np.zeros(64)
    for face_id in range(6):
        counts[node_at[face_id]] += 1.0
    points = np.array([-1.0, -1.0 / np.sqrt(5.0), 1.0 / np.sqrt(5.0), 1.0])
    halves = np.zeros((2, 4, 4))
    for half_id in range(2):
        target = (points + 2.0 * half_id - 1.0) / 2.0
        for column in range(4):
            lagrange = np.ones(4)
            for other_id in range(4):
                if other_id != column:
                    lagrange = (
                        lagrange * (target - points[other_id]) / (points[column] - points[other_id])
                    )
            halves[half_id, :, column] = lagrange
    mortar = np.stack([np.kron(halves[quarter // 2], halves[quarter % 2]) for quarter in range(4)])
    return node_at, counts, mortar


def matrices():
    node_at, counts, mortar = face_tables()
    traces = np.zeros((2 * LANES, TRACE))
    across = np.zeros((FACES * 2 * LANES, LANES))
    spread = np.zeros((TRACE, LANES))
    prolong = np.zeros((TRACE, 4 * TRACE))
    for face in range(FACES):
        other = face ^ 1
        for field in range(2):
            base = 32 * face + 16 * field
            lifted = 32 * other + 16 * field
            for place in range(16):
                node = 64 * field + node_at[face, place]
                facing = 64 * field + node_at[other, place]
                spread[base + place, node] = 1.0
                for part in range(2):
                    traces[part * LANES + node, base + place] = 1.0
                    across[(2 * face + part) * LANES + facing, node] = 1.0
            for quarter in range(4):
                start = quarter * TRACE + lifted
                prolong[base : base + 16, start : start + 16] = mortar[quarter].T
    count_row = np.tile(np.concatenate([counts, counts])[None, :], (8, 1))
    return traces, across, spread, prolong, count_row


def two_parts(table):
    high = table.astype(np.float32).astype(ml_dtypes.bfloat16)
    low = (table - high.astype(np.float64)).astype(np.float32).astype(ml_dtypes.bfloat16)
    return high, low


def split(values):
    high = values.astype(BF16)
    low = (values - high.astype(F32)).astype(BF16)
    return high, low


def dot(left, right):
    return jnp.dot(left, right, preferred_element_type=F32)


def dot3(values, high, low):
    v_high, v_low = split(values)
    return dot(v_high, high) + dot(v_low, high) + dot(v_high, low)


def pick(index, shape, dim):
    return jnp.where(index == lax.broadcasted_iota(jnp.int32, shape, dim), 1.0, 0.0).astype(BF16)


def prep_kernel(cot_ref, levels_ref, mortars_ref, pack_ref):
    leaves = cot_ref.shape[1]
    scale = jnp.left_shift(jnp.ones_like(levels_ref[...]), levels_ref[...]).astype(F32)
    pack_ref[0:leaves, :] = (cot_ref[...] * scale).T
    table = mortars_ref[...].astype(F32) + 1.0
    pack_ref[leaves : leaves + 8, :] = jnp.concatenate(
        [table, jnp.zeros((2, table.shape[1]), F32)], axis=0
    )


def laplace(blocks, tables, neighbours, stiffness, offset, consts):
    traces_ref, across_ref, spread_ref, pro_hi, pro_lo, res_hi, res_lo, count_ref = consts
    leaves = blocks[1].shape[0]
    slots = tables[1].shape[1]
    own = blocks[1]
    values = jnp.concatenate(blocks, axis=0)
    halves = jnp.concatenate(split(values), axis=1)
    near = jnp.where(neighbours >= 0, neighbours - offset + leaves, -1)
    near = jnp.concatenate([near, jnp.full((2, leaves), -1, jnp.int32)], axis=0)
    near = near.astype(F32).T.astype(jnp.int32)
    moved = jnp.zeros((leaves, LANES), F32)
    for face in range(FACES):
        chosen = dot(pick(near[:, face : face + 1], (leaves, 3 * leaves), 1), halves)
        moved = moved + dot(
            chosen.astype(BF16), across_ref[2 * LANES * face : 2 * LANES * (face + 1), :]
        )
    wide = jnp.concatenate([stiffness, stiffness], axis=1)
    wide = jnp.concatenate([wide, wide], axis=0)
    same = (lax.broadcasted_iota(jnp.int32, wide.shape, 0) < NODES) == (
        lax.broadcasted_iota(jnp.int32, wide.shape, 1) < NODES
    )
    result = count_ref[0:1, :] * own - moved + dot3(own, *split(jnp.where(same, wide, 0.0)))

    rows = [table.astype(jnp.int32) - 1 for table in tables]
    columns = [table.T.astype(jnp.int32) - 1 for table in tables]
    lane_face = lax.broadcasted_iota(jnp.int32, (slots, TRACE), 1) // 32
    coarse = []
    for place in range(3):
        local = columns[place][:, 0:1] - offset - (place - 1) * leaves
        block = halves[place * leaves : (place + 1) * leaves, :]
        chosen = dot(pick(local, (slots, leaves), 1), block).astype(BF16)
        trace = dot(chosen, traces_ref[...])
        coarse.append(jnp.where(lane_face == columns[place][:, 1:2], trace, 0.0))
    lifted = dot3(jnp.concatenate(coarse, axis=0), pro_hi[...], pro_lo[...])
    coarse_sum = jnp.zeros((slots, TRACE), F32)
    gathered = jnp.zeros((leaves, TRACE), F32)
    for quarter in range(4):
        fine = []
        for place in range(3):
            local = columns[place][:, 2 + quarter : 3 + quarter] - offset
            if place == 1:
                chosen = dot(pick(local + leaves, (slots, 3 * leaves), 1), halves)
            else:
                chosen = dot(
                    pick(local, (slots, leaves), 1), halves[leaves : 2 * leaves, :]
                )
            trace = dot(chosen.astype(BF16), traces_ref[...])
            face = columns[place][:, 1:2]
            other = jnp.where(face >= 0, face ^ 1, -1)
            fine.append(jnp.where(lane_face == other, trace, 0.0))
        jump = lifted[:, quarter * TRACE : (quarter + 1) * TRACE] - jnp.concatenate(fine, axis=0)
        high, low = split(jump)
        index = jnp.concatenate(
            [row[2 + quarter : 3 + quarter, :] - offset for row in rows], axis=1
        )
        back = pick(index, (leaves, 3 * slots), 0)
        gathered = gathered - (dot(back, high) + dot(back, low))
        part = slice(quarter * TRACE, (quarter + 1) * TRACE)
        coarse_sum = coarse_sum + dot3(
            jump[slots : 2 * slots, :], res_hi[part, :], res_lo[part, :]
        )
    high, low = split(coarse_sum)
    back = pick(rows[1][0:1, :] - offset, (leaves, slots), 0)
    gathered = gathered + (dot(back, high) + dot(back, low))
    high, low = split(gathered)
    return result + (dot(high, spread_ref[...]) + dot(low, spread_ref[...]))


def apply_t(vector, lapped, mass_ref, curve_ref):
    first = lax.broadcasted_iota(jnp.int32, vector.shape, 1) < NODES
    mass = jnp.concatenate([mass_ref[...], mass_ref[...]], axis=0).T
    curve = jnp.concatenate([curve_ref[...], curve_ref[...]], axis=0).T
    turned = pltpu.roll(lapped, NODES, 1)
    swapped = pltpu.roll(vector, NODES, 1)
    return mass * vector + jnp.where(
        first, -curve * swapped - EPS_WEIGHT * turned, TAU_WEIGHT * turned
    )


def columns_scale(levels):
    scale = jnp.left_shift(jnp.ones_like(levels), levels).astype(F32)
    return jnp.broadcast_to(scale, (LANES, levels.shape[1])).T


def first_kernel(
    offset_ref, own_ref, prev_ref, next_ref, levels_ref, neighbours_ref, mass_ref, curve_ref,
    stiffness_ref, *rest
):
    consts, (image_ref, send_ref) = rest[:-2], rest[-2:]
    leaves = levels_ref.shape[1]
    refs = (prev_ref, own_ref, next_ref)
    blocks = [ref[0:leaves, :] for ref in refs]
    tables = [ref[leaves : leaves + 8, :] for ref in refs]
    lapped = laplace(
        blocks, tables, neighbours_ref[...], stiffness_ref[...], offset_ref[0], consts
    )
    scale = columns_scale(levels_ref[...])
    image = apply_t(blocks[1] / scale, lapped, mass_ref, curve_ref)
    image_ref[...] = image
    send_ref[...] = image * scale


def over(top, bottom):
    return jnp.where(bottom > 0.0, top / jnp.where(bottom > 0.0, bottom, 1.0), 0.0)


def total(values):
    return jnp.sum(values, keepdims=True)


def second_kernel(
    offset_ref, own_ref, prev_ref, next_ref, levels_ref, neighbours_ref, mass_ref, curve_ref,
    stiffness_ref, pack_ref, pack_prev_ref, pack_next_ref, image_ref, *rest
):
    consts, stats_ref = rest[:-1], rest[-1]
    leaves = levels_ref.shape[1]
    blocks = [prev_ref[...], own_ref[...], next_ref[...]]
    tables = [ref[leaves : leaves + 8, :] for ref in (pack_prev_ref, pack_ref, pack_next_ref)]
    lapped = laplace(
        blocks, tables, neighbours_ref[...], stiffness_ref[...], offset_ref[0], consts
    )
    one = image_ref[...]
    two = apply_t(one, lapped, mass_ref, curve_ref)
    base = pack_ref[0:leaves, :] / columns_scale(levels_ref[...])
    r00 = jnp.sqrt(total(base * base))
    r01 = over(total(base * one), r00)
    r02 = over(total(base * two), r00)
    one = one - over(r01, r00) * base
    two = two - over(r02, r00) * base
    r11 = jnp.sqrt(total(one * one))
    r12 = over(total(one * two), r11)
    two = two - over(r12, r11) * one
    r22 = jnp.sqrt(total(two * two))
    lane = lax.broadcasted_iota(jnp.int32, stats_ref.shape, 1)
    row = jnp.zeros(stats_ref.shape, F32)
    for at, value in enumerate((r00, r01, r02, r11, r12, r22)):
        row = jnp.where(lane == at, value, row)
    stats_ref[...] = row


def final_kernel(stats_ref, cot_ref, image_ref, out_ref):
    table = stats_ref[...].T
    a0, a1, a2, b1, b2, c2 = [table[at : at + 1, :] for at in range(6)]
    r00_sq = total(a0 * a0)
    r00 = jnp.sqrt(r00_sq)
    f01 = total(a0 * a1) / r00_sq
    f02 = total(a0 * a2) / r00_sq
    a1 = a1 - f01 * a0
    a2 = a2 - f02 * a0
    r11_sq = total(a1 * a1) + total(b1 * b1)
    r11 = jnp.sqrt(r11_sq)
    f12 = (total(a1 * a2) + total(b1 * b2)) / r11_sq
    a2 = a2 - f12 * a1
    b2 = b2 - f12 * b1
    r22 = jnp.sqrt(total(a2 * a2) + total(b2 * b2) + total(c2 * c2))
    rhs_norm = r00
    first_diag = f01
    first_below = r11 / r00
    upper_right = (f02 - first_diag * f01) / first_below
    second_diag = f12 - first_diag
    second_below = r22 / r11
    first_len = jnp.sqrt(first_diag * first_diag + first_below * first_below)
    cos_one = first_diag / first_len
    sin_one = first_below / first_len
    rotated_top = cos_one * upper_right + sin_one * second_diag
    rotated_low = cos_one * second_diag - sin_one * upper_right
    second_len = jnp.sqrt(rotated_low * rotated_low + second_below * second_below)
    cos_two = rotated_low / second_len
    y_two = cos_two * (-sin_one * rhs_norm) / second_len
    y_one = (cos_one * rhs_norm - rotated_top * y_two) / first_len
    on_one = y_two / r11
    on_base = y_one / r00 - on_one * f01
    out_ref[...] = on_base * cot_ref[...] + on_one * image_ref[...].T


def on_device(cotangent, nodal_mass, curvature, stiffness, levels, neighbours, mortars):
    fields, nodes, leaves = cotangent.shape
    count = lax.axis_size("leaf")
    flat = cotangent.reshape(fields * nodes, leaves)
    levels = levels.reshape(1, leaves)
    offset = (lax.axis_index("leaf") * leaves).astype(jnp.int32).reshape(1)
    traces, across, spread, prolong, count_row = matrices()
    pro_hi, pro_lo = two_parts(prolong)
    res_hi, res_lo = two_parts(np.ascontiguousarray(prolong.T))
    small = ml_dtypes.bfloat16
    consts = [
        jnp.asarray(table)
        for table in (
            traces.astype(small), across.astype(small), spread.astype(small),
            pro_hi, pro_lo, res_hi, res_lo, count_row.astype(np.float32),
        )
    ]
    forward = [(i, i + 1) for i in range(count - 1)]
    backward = [(i + 1, i) for i in range(count - 1)]
    vmem = pl.BlockSpec(memory_space=pltpu.VMEM)
    smem = pl.BlockSpec(memory_space=pltpu.SMEM)
    params = pltpu.CompilerParams(vmem_limit_bytes=48 * 1024 * 1024)

    def call(kernel, outs, *operands, scalars=0):
        return pl.pallas_call(
            kernel,
            out_shape=outs,
            in_specs=[smem] * scalars + [vmem] * (len(operands) - scalars),
            out_specs=jax.tree.map(lambda _: vmem, outs),
            compiler_params=params,
        )(*operands)

    rows = jax.ShapeDtypeStruct((leaves, LANES), F32)
    pack = call(
        prep_kernel, jax.ShapeDtypeStruct((leaves + 8, LANES), F32), flat, levels, mortars
    )
    pack_prev = lax.ppermute(pack, "leaf", forward)
    pack_next = lax.ppermute(pack, "leaf", backward)
    local = (levels, neighbours, nodal_mass, curvature, stiffness)
    image, send = call(
        first_kernel, (rows, rows), offset, pack, pack_prev, pack_next, *local, *consts, scalars=1
    )
    send_prev = lax.ppermute(send, "leaf", forward)
    send_next = lax.ppermute(send, "leaf", backward)
    stats = call(
        second_kernel, jax.ShapeDtypeStruct((1, LANES), F32), offset, send, send_prev, send_next,
        *local, pack, pack_prev, pack_next, image, *consts, scalars=1
    )
    gathered = lax.all_to_all(
        jnp.broadcast_to(stats, (count, LANES)), "leaf", 0, 0, tiled=True
    )
    out = call(final_kernel, jax.ShapeDtypeStruct(flat.shape, F32), gathered, flat, image)
    return out.reshape(cotangent.shape)


def solution(mesh):
    placed = (
        P(None, None, "leaf"),
        P(None, "leaf"),
        P(None, "leaf"),
        P(),
        P("leaf"),
        P(None, "leaf"),
        P(None, "leaf"),
    )
    return jax.shard_map(
        on_device, mesh=mesh, in_specs=placed, out_specs=P(None, None, "leaf"), check_vma=False
    )
```

time: 607 us -> 75.3 us (0.12)
  blocking collectives: 392 us -> 34.4 us
  other arithmetic: 74.5 us -> 0 us
  matrix products: 50.2 us -> 0 us
  local copies, waits for them, and re-layouts: 54.3 us -> 9.12 us
  Pallas kernels: 0 us -> 13.6 us
  between operations: 9.24 us -> 0.12 us
    psum x5 -> x0, blocking collectives: 392 us -> none  [the longest x1 82 us: on_device(): first_diag = lax.psum(jnp.sum(image * basis_one), 'leaf')]
    scatter-add x10 -> x0, other arithmetic: 51.8 us -> none  [the longest x8 41.3 us: lap_t(): buffer = buffer.at[:, :, fine_near[quarter]].add(-spread)]
    dot_general x52 -> x0, matrix products: 50.2 us -> none  [the longest x9 17.9 us: lap_t(): jnp.einsum('fpn,xnS,fS->xpS', select, fine_vals, flipped, precision=highest)]
    all_to_all x0 -> x1, blocking collectives: none -> 34.4 us  [on_device(): lax.all_to_all(jnp.broadcast_to(stats, (count, LANES)), 'leaf', 0, 0, til...]
    gather x23 -> x0, local copies, waits for them, and re-layouts: 27.2 us -> none  [the longest x12 18 us: lap_t(): values = jnp.take(extended, near_index[face_id], axis=2)]
    pallas_call x0 -> x4, Pallas kernels: none -> 13.6 us  [call(): pl.pallas_call(kernel, out_shape=outs, in_specs=[smem] * scalars + [vmem]...]
    dot_general x18 -> x0, local copies, waits for them, and re-layouts: 10.3 us -> none  [the longest x8 8.21 us: lap_t(): jnp.einsum('rp,xrS->xpS', mortar[quarter], mismatch, precision=highest)]
    select_n x20 -> x0, other arithmetic: 7.2 us -> none  [the longest x18 6 us: lap_t(): values = jnp.take(extended, near_index[face_id], axis=2)]
  transfers between devices with their start and end apart: 8 -> 4, of which waited for: 1 -> 4; matrix products, arithmetic and copies ran while one was open for 7% -> 0% of each run, Pallas kernels for 0% -> 0%
where the time goes in v1:
time: 75.3 us; the launch traced here: 74.7 us
  blocking collectives  34.4 us (46%)
  Pallas kernels  13.6 us (18%)
  starting transfers between devices  13.5 us (18%)
  local copies, waits for them, and re-layouts  9.12 us (12%)
  waiting for transfers between devices  3.88 us (5%)
    all_to_all x1, blocking collectives, on_device(): lax.all_to_all(jnp.broadcast_to(stats, (count, LANES)), 'leaf', 0, 0, til...  34.4 us
    pallas_call x4, Pallas kernels, call(): pl.pallas_call(kernel, out_shape=outs, in_specs=[smem] * scalars + [vmem]...  13.6 us
    unnamed x32, local copies, waits for them, and re-layouts  9.05 us
    ppermute x1, starting transfers between devices, on_device(): pack_next = lax.ppermute(pack, 'leaf', backward)  5.28 us
    ppermute x1, starting transfers between devices, on_device(): send_prev = lax.ppermute(send, 'leaf', forward)  4.36 us
    ppermute x1, starting transfers between devices, on_device(): pack_prev = lax.ppermute(pack, 'leaf', forward)  1.92 us
    ppermute x1, starting transfers between devices, on_device(): send_next = lax.ppermute(send, 'leaf', backward)  1.92 us
    ppermute x1, waiting for transfers between devices, on_device(): pack_prev = lax.ppermute(pack, 'leaf', forward)  1.77 us
  transfers between devices with their start and end apart: 4, of which 4 were waited for; matrix products, arithmetic and copies ran while one was open for 0% of the time, Pallas kernels for 0%

profile of v1, /device:TPU:1, one launch (start us, length us, event | category | flops | bytes accessed | tf_op | source)
XLA Modules:
  0.0 74.7 jit_solution(95929290564633656)
XLA Ops:
  0.0 0.0 copy-start.14
  0.0 0.7 copy-done.14
  0.7 0.0 copy-start.6
  0.7 0.9 %copy-done.6 = f32[2,64,256]{2,1,0:T(8,128)S(1)} copy-done((f32[2,64,256]{2,1,0:T(8,128)S(1)}, f32[2,64,256]{2,1,0:T(8,128)}, u32[]{:S(2)}) %copy-start.6) | copy-done | bytes 131096
  1.6 0.0 copy-start.15
  1.6 0.7 copy-done.15
  2.3 0.0 copy-start.5
  2.3 0.0 copy-start.8
  2.3 0.0 copy-start.9
  2.3 0.0 copy-start.13
  2.3 0.1 shard_map.145.own_ref.pack_ref
  2.4 0.0 copy-start.12
  2.4 5.3 %collective-permute-start.1 = (f32[264,128]{1,0:T(8,128)S(1)}, f32[264,128]{1,0:T(8,128)S(1)}, u32[]{:S(2)}, u32[]{:S(2)}) collective-permute-start(f32[264,128]{1,0:T(8,128)S(1)} %shard_map.145.own_ref.pack_ref), channel_id=1, source_target_pairs={{1,0},{2,1},{3,2},{4,3},{5,4},{6,5},{7,6},{8,7},{9,8},{10,9},{11,1... | collective-permute-start | bytes 405512 | tf_op jit(solution)/shard_map/ppermute | solution.py:321
  7.7 1.9 %collective-permute-start = (f32[264,128]{1,0:T(8,128)S(1)}, f32[264,128]{1,0:T(8,128)S(1)}, u32[]{:S(2)}, u32[]{:S(2)}) collective-permute-start(f32[264,128]{1,0:T(8,128)S(1)} %shard_map.145.own_ref.pack_ref), channel_id=1, source_target_pairs={{0,1},{1,2},{2,3},{3,4},{4,5},{5,6},{6,7},{7,8},{8,9},{9,10},{10,1... | collective-permute-start | bytes 405512 | tf_op jit(solution)/shard_map/ppermute | solution.py:320
  9.6 0.2 collective-permute-done.1.next_ref.pack_next_ref
  9.8 1.8 %collective-permute-done.prev_ref.pack_prev_ref = f32[264,128]{1,0:T(8,128)S(1)} collective-permute-done((f32[264,128]{1,0:T(8,128)S(1)}, f32[264,128]{1,0:T(8,128)S(1)}, u32[]{:S(2)}, u32[]{:S(2)}) %collective-permute-start) | collective-permute-done | bytes 135200 | tf_op jit(solution)/shard_map/ppermute | solution.py:320
  11.6 0.0 copy-done.5
  11.6 0.0 copy-done.8
  11.6 0.0 copy-done.9
  11.6 0.0 copy-done.13
  11.6 0.0 copy-done.12
  11.6 0.0 copy-start
  11.6 1.0 %copy-done = bf16[1024,256]{1,0:T(8,128)(2,1)S(1)} copy-done((bf16[1024,256]{1,0:T(8,128)(2,1)S(1)}, bf16[1024,256]{1,0:T(8,128)(2,1)}, u32[]{:S(2)}) %copy-start) | copy-done | bytes 524312
  12.6 0.0 copy-start.1
  12.6 1.0 %copy-done.1 = bf16[1024,256]{1,0:T(8,128)(2,1)S(1)} copy-done((bf16[1024,256]{1,0:T(8,128)(2,1)S(1)}, bf16[1024,256]{1,0:T(8,128)(2,1)}, u32[]{:S(2)}) %copy-start.1) | copy-done | bytes 524312
  13.7 0.0 copy-start.2
  13.7 1.0 %copy-done.2 = bf16[256,1024]{1,0:T(8,128)(2,1)S(1)} copy-done((bf16[256,1024]{1,0:T(8,128)(2,1)S(1)}, bf16[256,1024]{1,0:T(8,128)(2,1)}, u32[]{:S(2)}) %copy-start.2) | copy-done | bytes 524312
  14.7 0.0 copy-start.3
  14.7 1.0 %copy-done.3 = bf16[256,1024]{1,0:T(8,128)(2,1)S(1)} copy-done((bf16[256,1024]{1,0:T(8,128)(2,1)S(1)}, bf16[256,1024]{1,0:T(8,128)(2,1)}, u32[]{:S(2)}) %copy-start.3) | copy-done | bytes 524312
  15.8 0.0 copy-start.4
  15.8 1.0 %copy-done.4 = bf16[1536,128]{1,0:T(8,128)(2,1)S(1)} copy-done((bf16[1536,128]{1,0:T(8,128)(2,1)S(1)}, bf16[1536,128]{1,0:T(8,128)(2,1)}, u32[]{:S(2)}) %copy-start.4) | copy-done | bytes 393240
  16.8 0.0 copy-start.10
  16.8 0.8 %copy-done.10 = bf16[256,128]{1,0:T(8,128)(2,1)S(1)} copy-done((bf16[256,128]{1,0:T(8,128)(2,1)S(1)}, bf16[256,128]{1,0:T(8,128)(2,1)}, u32[]{:S(2)}) %copy-start.10) | copy-done | bytes 65560
  17.6 0.0 copy-start.11
  17.6 0.8 %copy-done.11 = f32[64,64]{1,0:T(8,128)S(1)} copy-done((f32[64,64]{1,0:T(8,128)S(1)}, f32[64,64]{1,0:T(8,128)}, u32[]{:S(2)}) %copy-start.11) | copy-done | bytes 16408
  18.4 5.9 %shard_map.146 = (f32[256,128]{1,0:T(8,128)S(1)}, f32[256,128]{1,0:T(8,128)S(1)}) custom-call(s32[1]{0:T(128)} %bitcast.offset_ref, f32[264,128]{1,0:T(8,128)S(1)} %shard_map.145.own_ref.pack_ref, f32[264,128]{1,0:T(8,128)S(1)} %collective-permute-done.prev_ref.pack_prev_ref, f32[264,128]{1,0:T(8,128)S(1)} %collective-permute-done.1.next_ref.pack_next_ref, ...), custom_call_target="tpu_custom_call" | custom-call | tf_op jit(solution)/shard_map/pallas_call | solution.py:308
  24.3 1.9 %collective-permute-start.3 = (f32[256,128]{1,0:T(8,128)S(1)}, f32[256,128]{1,0:T(8,128)S(1)}, u32[]{:S(2)}, u32[]{:S(2)}) collective-permute-start(f32[256,128]{1,0:T(8,128)S(1)} %get-tuple-element.7.own_ref), channel_id=1, source_target_pairs={{1,0},{2,1},{3,2},{4,3},{5,4},{6,5},{7,6},{8,7},{9,8},{10,9},{11,1... | collective-permute-start | bytes 393224 | tf_op jit(solution)/shard_map/ppermute | solution.py:327
  26.2 4.4 %collective-permute-start.2 = (f32[256,128]{1,0:T(8,128)S(1)}, f32[256,128]{1,0:T(8,128)S(1)}, u32[]{:S(2)}, u32[]{:S(2)}) collective-permute-start(f32[256,128]{1,0:T(8,128)S(1)} %get-tuple-element.7.own_ref), channel_id=1, source_target_pairs={{0,1},{1,2},{2,3},{3,4},{4,5},{5,6},{6,7},{7,8},{8,9},{9,10},{10,1... | collective-permute-start | bytes 393224 | tf_op jit(solution)/shard_map/ppermute | solution.py:326
  30.6 0.7 collective-permute-done.3.next_ref
  31.3 1.2 %collective-permute-done.2.prev_ref = f32[256,128]{1,0:T(8,128)S(1)} collective-permute-done((f32[256,128]{1,0:T(8,128)S(1)}, f32[256,128]{1,0:T(8,128)S(1)}, u32[]{:S(2)}, u32[]{:S(2)}) %collective-permute-start.2) | collective-permute-done | bytes 131104 | tf_op jit(solution)/shard_map/ppermute | solution.py:326
  32.5 6.4 %shard_map.147 = f32[1,128]{1,0:T(1,128)S(1)} custom-call(s32[1]{0:T(128)} %bitcast.offset_ref, f32[256,128]{1,0:T(8,128)S(1)} %get-tuple-element.7.own_ref, f32[256,128]{1,0:T(8,128)S(1)} %collective-permute-done.2.prev_ref, f32[256,128]{1,0:T(8,128)S(1)} %collective-permute-done.3.next_ref, s32[1,256]{1,0:T(1,128)S(1)} %bitcast.11, ...), custom_call_target="tpu_custom_call" | custom-call | tf_op jit(solution)/shard_map/pallas_call | solution.py:308
  39.0 0.1 broadcast_in_dim.2
  39.0 0.0 copy-start.7
  39.1 34.4 %all_to_all.8 = f32[256,1,128]{2,1,0:T(1,128)S(1)} all-to-all(f32[256,1,128]{2,1,0:T(1,128)S(1)} %broadcast_in_dim.2), channel_id=1, replica_groups=mesh['leaf'=256] {'leaf'}, dimensions={0} | all-to-all | bytes 262144 | tf_op jit(solution)/shard_map/all_to_all | solution.py:332
  73.5 0.0 copy-done.7
  73.5 1.1 %shard_map.148 = f32[128,256]{1,0:T(8,128)} custom-call(f32[256,128]{1,0:T(8,128)S(1)} %bitcast.8, f32[128,256]{1,0:T(8,128)S(1)} %bitcast.7, f32[256,128]{1,0:T(8,128)S(1)} %get-tuple-element.8.image_ref), custom_call_target="tpu_custom_call" | custom-call | tf_op jit(solution)/shard_map/pallas_call | solution.py:308
Async XLA Ops:
  0.0 0.7 copy-start.14
  0.7 0.9 %copy-start.6 = (f32[2,64,256]{2,1,0:T(8,128)S(1)}, f32[2,64,256]{2,1,0:T(8,128)}, u32[]{:S(2)}) copy-start(f32[2,64,256]{2,1,0:T(8,128)} %param.15) | copy-start | bytes 393220
  1.6 0.7 copy-start.15
  2.3 9.3 %copy-start.5 = (bf16[256,256]{1,0:T(8,128)(2,1)S(1)}, bf16[256,256]{1,0:T(8,128)(2,1)}, u32[]{:S(2)}) copy-start(bf16[256,256]{1,0:T(8,128)(2,1)} %constant.22.clone.rest_0_) | copy-start | bytes 393220
  2.3 9.3 %copy-start.8 = (f32[64,256]{1,0:T(8,128)S(1)}, f32[64,256]{1,0:T(8,128)}, u32[]{:S(2)}) copy-start(f32[64,256]{1,0:T(8,128)} %mass_ref.3) | copy-start | bytes 196612
  2.3 9.3 %copy-start.9 = (f32[64,256]{1,0:T(8,128)S(1)}, f32[64,256]{1,0:T(8,128)}, u32[]{:S(2)}) copy-start(f32[64,256]{1,0:T(8,128)} %curve_ref.3) | copy-start | bytes 196612
  2.3 9.3 %copy-start.13 = (f32[8,128]{1,0:T(8,128)S(1)}, f32[8,128]{1,0:T(8,128)}, u32[]{:S(2)}) copy-start(f32[8,128]{1,0:T(8,128)} %constant.29.clone.rest_7_) | copy-start | bytes 12292
  2.4 9.2 %copy-start.12 = (s32[6,256]{1,0:T(8,128)S(1)}, s32[6,256]{1,0:T(8,128)}, u32[]{:S(2)}) copy-start(s32[6,256]{1,0:T(8,128)} %neighbours_ref.3) | copy-start | bytes 18436
  2.4 7.4 %collective-permute-start.1 = (f32[264,128]{1,0:T(8,128)S(1)}, f32[264,128]{1,0:T(8,128)S(1)}, u32[]{:S(2)}, u32[]{:S(2)}) collective-permute-start(f32[264,128]{1,0:T(8,128)S(1)} %shard_map.145.own_ref.pack_ref), channel_id=1, source_target_pairs={{1,0},{2,1},{3,2},{4,3},{5,4},{6,5},{7,6},{8,7},{9,8},{10,9},{11,1... | collective-permute-start | bytes 405512 | tf_op jit(solution)/shard_map/ppermute | solution.py:321
  7.7 3.9 %collective-permute-start = (f32[264,128]{1,0:T(8,128)S(1)}, f32[264,128]{1,0:T(8,128)S(1)}, u32[]{:S(2)}, u32[]{:S(2)}) collective-permute-start(f32[264,128]{1,0:T(8,128)S(1)} %shard_map.145.own_ref.pack_ref), channel_id=1, source_target_pairs={{0,1},{1,2},{2,3},{3,4},{4,5},{5,6},{6,7},{7,8},{8,9},{9,10},{10,1... | collective-permute-start | bytes 405512 | tf_op jit(solution)/shard_map/ppermute | solution.py:320
  11.6 1.0 %copy-start = (bf16[1024,256]{1,0:T(8,128)(2,1)S(1)}, bf16[1024,256]{1,0:T(8,128)(2,1)}, u32[]{:S(2)}) copy-start(bf16[1024,256]{1,0:T(8,128)(2,1)} %constant.28.clone.rest_6_) | copy-start | bytes 1572868
  12.6 1.0 %copy-start.1 = (bf16[1024,256]{1,0:T(8,128)(2,1)S(1)}, bf16[1024,256]{1,0:T(8,128)(2,1)}, u32[]{:S(2)}) copy-start(bf16[1024,256]{1,0:T(8,128)(2,1)} %constant.27.clone.rest_5_) | copy-start | bytes 1572868
  13.7 1.0 %copy-start.2 = (bf16[256,1024]{1,0:T(8,128)(2,1)S(1)}, bf16[256,1024]{1,0:T(8,128)(2,1)}, u32[]{:S(2)}) copy-start(bf16[256,1024]{1,0:T(8,128)(2,1)} %constant.26.clone.rest_4_) | copy-start | bytes 1572868
  14.7 1.0 %copy-start.3 = (bf16[256,1024]{1,0:T(8,128)(2,1)S(1)}, bf16[256,1024]{1,0:T(8,128)(2,1)}, u32[]{:S(2)}) copy-start(bf16[256,1024]{1,0:T(8,128)(2,1)} %constant.25.clone.rest_3_) | copy-start | bytes 1572868
  15.8 1.0 %copy-start.4 = (bf16[1536,128]{1,0:T(8,128)(2,1)S(1)}, bf16[1536,128]{1,0:T(8,128)(2,1)}, u32[]{:S(2)}) copy-start(bf16[1536,128]{1,0:T(8,128)(2,1)} %constant.23.clone.rest_1_) | copy-start | bytes 1179652
  16.8 0.8 %copy-start.10 = (bf16[256,128]{1,0:T(8,128)(2,1)S(1)}, bf16[256,128]{1,0:T(8,128)(2,1)}, u32[]{:S(2)}) copy-start(bf16[256,128]{1,0:T(8,128)(2,1)} %constant.24.clone.rest_2_) | copy-start | bytes 196612
  17.6 0.8 %copy-start.11 = (f32[64,64]{1,0:T(8,128)S(1)}, f32[64,64]{1,0:T(8,128)}, u32[]{:S(2)}) copy-start(f32[64,64]{1,0:T(8,128)} %stiffness_ref.3) | copy-start | bytes 49156
  24.3 7.0 %collective-permute-start.3 = (f32[256,128]{1,0:T(8,128)S(1)}, f32[256,128]{1,0:T(8,128)S(1)}, u32[]{:S(2)}, u32[]{:S(2)}) collective-permute-start(f32[256,128]{1,0:T(8,128)S(1)} %get-tuple-element.7.own_ref), channel_id=1, source_target_pairs={{1,0},{2,1},{3,2},{4,3},{5,4},{6,5},{7,6},{8,7},{9,8},{10,9},{11,1... | collective-permute-start | bytes 393224 | tf_op jit(solution)/shard_map/ppermute | solution.py:327
  26.2 6.3 %collective-permute-start.2 = (f32[256,128]{1,0:T(8,128)S(1)}, f32[256,128]{1,0:T(8,128)S(1)}, u32[]{:S(2)}, u32[]{:S(2)}) collective-permute-start(f32[256,128]{1,0:T(8,128)S(1)} %get-tuple-element.7.own_ref), channel_id=1, source_target_pairs={{0,1},{1,2},{2,3},{3,4},{4,5},{5,6},{6,7},{7,8},{8,9},{9,10},{10,1... | collective-permute-start | bytes 393224 | tf_op jit(solution)/shard_map/ppermute | solution.py:326
  39.0 34.5 %copy-start.7 = (f32[2,64,256]{2,1,0:T(8,128)S(1)}, f32[2,64,256]{2,1,0:T(8,128)}, u32[]{:S(2)}) copy-start(f32[2,64,256]{2,1,0:T(8,128)} %param.15) | copy-start | bytes 393220

commit v2 on v1

v2 whole, which is shorter than its diff:
```python
import jax
import jax.numpy as jnp
import ml_dtypes
import numpy as np
from jax import lax
from jax.experimental import pallas as pl
from jax.experimental.pallas import tpu as pltpu
from jax.sharding import PartitionSpec as P

TAU_WEIGHT = 0.15
EPS_WEIGHT = 0.1
FACES = 6
NODES = 64
LANES = 128
TRACE = 256
F32 = jnp.float32
BF16 = jnp.bfloat16


def face_tables():
    node_at = np.zeros((6, 16), dtype=np.int64)
    for face_id in range(6):
        for row_pos in range(4):
            for col_pos in range(4):
                coords = [row_pos, col_pos]
                coords.insert(face_id // 2, 3 * (face_id % 2))
                node_at[face_id, 4 * row_pos + col_pos] = (
                    16 * coords[0] + 4 * coords[1] + coords[2]
                )
    counts = np.zeros(64)
    for face_id in range(6):
        counts[node_at[face_id]] += 1.0
    points = np.array([-1.0, -1.0 / np.sqrt(5.0), 1.0 / np.sqrt(5.0), 1.0])
    halves = np.zeros((2, 4, 4))
    for half_id in range(2):
        target = (points + 2.0 * half_id - 1.0) / 2.0
        for column in range(4):
            lagrange = np.ones(4)
            for other_id in range(4):
                if other_id != column:
                    lagrange = (
                        lagrange * (target - points[other_id]) / (points[column] - points[other_id])
                    )
            halves[half_id, :, column] = lagrange
    mortar = np.stack([np.kron(halves[quarter // 2], halves[quarter % 2]) for quarter in range(4)])
    return node_at, counts, mortar


def two_parts(table):
    high = table.astype(np.float32).astype(ml_dtypes.bfloat16)
    low = (table - high.astype(np.float64)).astype(np.float32).astype(ml_dtypes.bfloat16)
    return np.concatenate([high, low], axis=-1)


def matrices():
    node_at, counts, mortar = face_tables()
    traces = np.zeros((2 * LANES, TRACE))
    across = np.zeros((FACES * 2 * LANES, LANES))
    spread = np.zeros((TRACE, LANES))
    to_fine = np.zeros((4, TRACE, LANES))
    to_coarse = np.zeros((4, TRACE, LANES))
    stay = np.zeros((TRACE, LANES))
    square = sum(mortar[quarter].T @ mortar[quarter] for quarter in range(4))
    for face in range(FACES):
        other = face ^ 1
        for field in range(2):
            base = 32 * face + 16 * field
            lifted = 32 * other + 16 * field
            nodes = 64 * field + node_at[face]
            facing = 64 * field + node_at[other]
            for place in range(16):
                spread[base + place, nodes[place]] = 1.0
                for part in range(2):
                    traces[part * LANES + nodes[place], base + place] = 1.0
                    across[(2 * face + part) * LANES + facing[place], nodes[place]] = 1.0
                stay[base + place, nodes] = square[:, place]
                for quarter in range(4):
                    to_fine[quarter, base + place, facing] = mortar[quarter][:, place]
                    to_coarse[quarter, lifted + place, nodes] = mortar[quarter][place, :]
    small = ml_dtypes.bfloat16
    counts = np.tile(np.concatenate([counts, counts])[None, :], (8, 1)).astype(np.float32)
    return (
        traces.astype(small),
        across.astype(small),
        spread.astype(small),
        np.concatenate(list(two_parts(to_fine)), axis=-1),
        np.concatenate(list(two_parts(to_coarse)), axis=0),
        two_parts(stay),
        counts,
    )


def split(values, axis=1):
    high = values.astype(BF16)
    return jnp.concatenate([high, (values - high.astype(F32)).astype(BF16)], axis=axis)


def dot(left, right):
    return jnp.dot(left, right, preferred_element_type=F32)


def fold(values):
    return values[:, :LANES] + values[:, LANES:]


def dot_parts(values, table):
    high = values.astype(BF16)
    low = (values - high.astype(F32)).astype(BF16)
    return dot(high, table) + dot(low, table)


def pick(index, shape, dim):
    return jnp.where(index == lax.broadcasted_iota(jnp.int32, shape, dim), 1.0, 0.0).astype(BF16)


def on_face(face, slots):
    return lax.broadcasted_iota(jnp.int32, (slots, TRACE), 1) // 32 == face


def opposite(face):
    return jnp.where(face >= 0, face ^ 1, -1)


def level_rows(levels):
    scale = jnp.left_shift(jnp.ones_like(levels), levels).astype(F32)
    return jnp.broadcast_to(scale, (LANES, levels.shape[1])).T


def fetch(pairs, sems):
    copies = [
        pltpu.make_async_copy(source, target, sems.at[at])
        for at, (source, target) in enumerate(pairs)
    ]
    for copy in copies:
        copy.start()
    return copies


def prep_kernel(cot_hbm, levels_hbm, mortars_hbm, pack_ref, cot_ref, levels_ref, mortars_ref, sems):
    for copy in fetch(
        ((cot_hbm, cot_ref), (levels_hbm, levels_ref), (mortars_hbm, mortars_ref)), sems
    ):
        copy.wait()
    leaves = cot_ref.shape[1]
    scale = jnp.left_shift(jnp.ones_like(levels_ref[...]), levels_ref[...]).astype(F32)
    pack_ref[0:leaves, :] = (cot_ref[...] * scale).T
    table = mortars_ref[...].astype(F32) + 1.0
    pack_ref[leaves : leaves + 8, :] = jnp.concatenate(
        [table, jnp.zeros((2, table.shape[1]), F32)], axis=0
    )


TABLES = ("traces", "across", "to_fine", "to_coarse", "stay")
KEPT = (
    "oh_own", "oh_near", "coarse_pick", "fine_own", "fine_near", "fine_back", "coarse_back",
    "coarse_count", "diagonal", "stiff", "mass", "curve", "scale",
) + TABLES


def own_part(rows, kept):
    slots = kept["coarse_pick"].shape[0]
    parts = split(rows)
    chosen = dot(kept["oh_own"][...], parts).astype(BF16)
    leaves = rows.shape[0]
    moved = jnp.zeros(rows.shape, F32)
    for face in range(FACES):
        moved = moved + dot(
            chosen[leaves * face : leaves * (face + 1), :],
            kept["across"][2 * LANES * face : 2 * LANES * (face + 1), :],
        )
    result = kept["diagonal"][...] * rows - moved + fold(dot(parts, kept["stiff"][...]))
    here = dot(parts, kept["traces"][...]) * kept["coarse_count"][...]
    result = result + fold(dot_parts(here, kept["stay"][...]))
    face = kept["face"][...]
    trace = dot(dot(kept["coarse_pick"][...], parts).astype(BF16), kept["traces"][...])
    trace = jnp.where(on_face(face, slots), trace, 0.0)
    lifted = dot_parts(trace, kept["to_fine"][...])
    lifted = jnp.concatenate(
        [split(fold(lifted[:, TRACE * q : TRACE * (q + 1)])) for q in range(4)], axis=0
    )
    result = result - fold(dot(kept["fine_back"][...], lifted))
    return result - from_fine(kept["fine_own"], parts, kept)


def from_fine(picks, parts, kept):
    slots = kept["coarse_back"].shape[1]
    trace = dot(dot(picks[...], parts).astype(BF16), kept["traces"][...])
    other = on_face(opposite(kept["face"][...]), slots)
    sent = jnp.zeros((slots, 2 * LANES), F32)
    for quarter in range(4):
        part = jnp.where(other, trace[slots * quarter : slots * (quarter + 1), :], 0.0)
        sent = sent + dot_parts(part, kept["to_coarse"][TRACE * quarter : TRACE * (quarter + 1), :])
    return fold(dot(kept["coarse_back"][...], split(fold(sent))))


def fine_count(back, other, spread):
    weights = jnp.where(other, 1.0, 0.0).astype(BF16)
    times = dot(back, jnp.concatenate([weights] * 4, axis=0))
    return dot_parts(times, spread)


def near_index(index, offset, first, leaves):
    local = index - offset
    here = jnp.where(local < 0, local + leaves, local - leaves)
    is_first = (local < 0) == (first < 0)
    outside = (local >= 0) & (local < leaves)
    return jnp.where(outside | (index < 0), -1, jnp.where(is_first, here, here + leaves))


def own_index(index, offset):
    return jnp.where(index < 0, -1, index - offset)


def to_columns(table):
    return table.astype(F32).T.astype(jnp.int32)


def near_kernel(place_ref, pack_ref, *refs):
    names = ("neighbours", "mass", "curve", "stiffness", "levels", "spread", "counts") + TABLES
    sources = dict(zip(names, refs))
    refs = refs[len(names) :]
    kept = dict(zip(KEPT + ("face", "partial"), refs))
    refs = refs[len(KEPT) + 2 :]
    local = dict(zip(names[: -len(TABLES)], refs))
    sems = refs[-1]
    targets = [local[name] if name in local else kept[name] for name in names]
    copies = fetch(tuple(zip((sources[name] for name in names), targets)), sems)
    leaves = pack_ref.shape[0] - 8
    offset, first = place_ref[0], place_ref[1]
    table = pack_ref[leaves : leaves + 8, :].astype(jnp.int32) - 1
    columns = to_columns(pack_ref[leaves : leaves + 8, :]) - 1
    slots = table.shape[1]
    face = columns[:, 1:2]
    kept["face"][...] = face
    copies[0].wait()
    neighbours = jnp.concatenate(
        [local["neighbours"][...], jnp.full((2, leaves), -1, jnp.int32)], axis=0
    )
    own = to_columns(own_index(neighbours, offset))
    near = to_columns(near_index(neighbours, offset, first, leaves))
    for f in range(FACES):
        rows = slice(leaves * f, leaves * (f + 1))
        kept["oh_own"][rows, :] = pick(own[:, f : f + 1], (leaves, leaves), 1)
        kept["oh_near"][rows, :] = pick(near[:, f : f + 1], (leaves, 2 * leaves), 1)
    kept["coarse_pick"][...] = pick(columns[:, 0:1] - offset, (slots, leaves), 1)
    coarse_back = pick(table[0:1, :] - offset, (leaves, slots), 0)
    kept["coarse_back"][...] = coarse_back
    fine_own = own_index(columns, offset)
    fine_near = near_index(columns, offset, first, leaves)
    fine_rows = own_index(table, offset)
    for q in range(4):
        rows = slice(slots * q, slots * (q + 1))
        kept["fine_own"][rows, :] = pick(fine_own[:, 2 + q : 3 + q], (slots, leaves), 1)
        kept["fine_near"][rows, :] = pick(fine_near[:, 2 + q : 3 + q], (slots, 2 * leaves), 1)
        kept["fine_back"][:, rows] = pick(fine_rows[2 + q : 3 + q, :], (leaves, slots), 0)
    for copy in copies[1:]:
        copy.wait()
    weights = jnp.where(on_face(face, slots), 1.0, 0.0).astype(BF16)
    kept["coarse_count"][...] = dot(coarse_back, weights)
    kept["diagonal"][...] = local["counts"][0:1, :] + fine_count(
        kept["fine_back"][...], on_face(opposite(face), slots), local["spread"][...]
    )
    wide = jnp.concatenate([local["stiffness"][...]] * 2, axis=1)
    wide = jnp.concatenate([wide, wide], axis=0)
    same = (lax.broadcasted_iota(jnp.int32, wide.shape, 0) < NODES) == (
        lax.broadcasted_iota(jnp.int32, wide.shape, 1) < NODES
    )
    wide = split(jnp.where(same, wide, 0.0))
    kept["stiff"][...] = jnp.concatenate([wide, wide], axis=0)
    kept["mass"][...] = jnp.concatenate([local["mass"][...]] * 2, axis=0).T
    curve = local["curve"][...]
    kept["curve"][...] = jnp.concatenate([-curve, jnp.zeros_like(curve)], axis=0).T
    kept["scale"][...] = level_rows(local["levels"][...])
    kept["partial"][...] = own_part(pack_ref[0:leaves, :], kept)


def near_part(rows, kept, picks, backs, faces):
    leaves = rows.shape[0] // 2
    slots = picks.shape[0] // 2
    parts = split(rows)
    chosen = dot(kept["oh_near"][...], parts).astype(BF16)
    moved = jnp.zeros((leaves, LANES), F32)
    for face in range(FACES):
        moved = moved + dot(
            chosen[leaves * face : leaves * (face + 1), :],
            kept["across"][2 * LANES * face : 2 * LANES * (face + 1), :],
        )
    trace = jnp.concatenate(
        [
            dot(picks[slots * k : slots * (k + 1), :], parts[leaves * k : leaves * (k + 1), :])
            for k in range(2)
        ],
        axis=0,
    )
    trace = dot(trace.astype(BF16), kept["traces"][...])
    trace = jnp.where(on_face(faces, 2 * slots), trace, 0.0)
    lifted = dot_parts(trace, kept["to_fine"][...])
    lifted = jnp.concatenate(
        [split(fold(lifted[:, TRACE * q : TRACE * (q + 1)])) for q in range(4)], axis=0
    )
    return -moved - fold(dot(backs, lifted)) - from_fine(kept["fine_near"], parts, kept)


def apply_t(vector, lapped, kept):
    first = lax.broadcasted_iota(jnp.int32, vector.shape, 1) < NODES
    turned = pltpu.roll(lapped, NODES, 1)
    swapped = pltpu.roll(vector, NODES, 1)
    weight = jnp.where(first, -EPS_WEIGHT, TAU_WEIGHT)
    return kept["mass"][...] * vector + kept["curve"][...] * swapped + weight * turned


KEPT_FIRST = ("oh_near", "fine_near", "coarse_back", "mass", "curve", "scale") + TABLES[:4] + ("face",)
KEPT_AGAIN = (
    "oh_own", "coarse_pick", "fine_own", "fine_back", "coarse_back", "coarse_count", "diagonal",
    "stiff", "face",
) + TABLES


def first_kernel(place_ref, pack_ref, one_ref, two_ref, spread_ref, partial_ref, *refs):
    kept = dict(zip(KEPT_FIRST, refs))
    image_ref, send_ref, picks_ref, backs_ref, faces_ref, extra_ref = refs[len(KEPT_FIRST) :]
    leaves = pack_ref.shape[0] - 8
    offset, first = place_ref[0], place_ref[1]
    tables, columns = [], []
    for ref in (one_ref, two_ref):
        table = ref[leaves : leaves + 8, :]
        tables.append(table.astype(jnp.int32) - 1)
        columns.append(to_columns(table) - 1)
    slots = tables[0].shape[1]
    starts = (offset + first, offset - first)
    picks_ref[...] = jnp.concatenate(
        [pick(columns[k][:, 0:1] - starts[k], (slots, leaves), 1) for k in range(2)], axis=0
    )
    faces = jnp.concatenate([column[:, 1:2] for column in columns], axis=0)
    faces_ref[...] = faces
    index = jnp.concatenate([own_index(table, offset) for table in tables], axis=1)
    for q in range(4):
        backs_ref[:, 2 * slots * q : 2 * slots * (q + 1)] = pick(
            index[2 + q : 3 + q, :], (leaves, 2 * slots), 0
        )
    extra = fine_count(backs_ref[...], on_face(opposite(faces), 2 * slots), spread_ref[...])
    extra_ref[...] = extra
    own = pack_ref[0:leaves, :]
    rows = jnp.concatenate([one_ref[0:leaves, :], two_ref[0:leaves, :]], axis=0)
    lapped = partial_ref[...] + extra * own + near_part(
        rows, kept, picks_ref[...], backs_ref[...], faces
    )
    scale = kept["scale"][...]
    image = apply_t(own / scale, lapped, kept)
    image_ref[...] = image
    send_ref[...] = image * scale


def again_kernel(send_ref, extra_ref, *refs):
    kept = dict(zip(KEPT_AGAIN, refs))
    partial_ref = refs[len(KEPT_AGAIN)]
    rows = send_ref[...]
    partial_ref[...] = own_part(rows, kept) + extra_ref[...] * rows


def over(top, bottom):
    return jnp.where(bottom > 0.0, top / jnp.where(bottom > 0.0, bottom, 1.0), 0.0)


def total(values):
    return jnp.sum(values, keepdims=True)


def second_kernel(
    pack_ref, one_ref, two_ref, partial_ref, image_ref, picks_ref, backs_ref, faces_ref, *refs
):
    kept = dict(zip(KEPT_FIRST, refs))
    stats_ref = refs[len(KEPT_FIRST)]
    leaves = pack_ref.shape[0] - 8
    rows = jnp.concatenate([one_ref[...], two_ref[...]], axis=0)
    lapped = partial_ref[...] + near_part(
        rows, kept, picks_ref[...], backs_ref[...], faces_ref[...]
    )
    one = image_ref[...]
    two = apply_t(one, lapped, kept)
    base = pack_ref[0:leaves, :] / kept["scale"][...]
    r00 = jnp.sqrt(total(base * base))
    r01 = over(total(base * one), r00)
    r02 = over(total(base * two), r00)
    one = one - over(r01, r00) * base
    two = two - over(r02, r00) * base
    r11 = jnp.sqrt(total(one * one))
    r12 = over(total(one * two), r11)
    two = two - over(r12, r11) * one
    r22 = jnp.sqrt(total(two * two))
    lane = lax.broadcasted_iota(jnp.int32, stats_ref.shape, 1)
    row = jnp.zeros(stats_ref.shape, F32)
    for at, value in enumerate((r00, r01, r02, r11, r12, r22)):
        row = jnp.where(lane == at, value, row)
    stats_ref[...] = row


def final_kernel(stats_ref, cot_ref, image_ref, out_ref):
    table = stats_ref[...].T
    a0, a1, a2, b1, b2, c2 = [table[at : at + 1, :] for at in range(6)]
    r00_sq = total(a0 * a0)
    r00 = jnp.sqrt(r00_sq)
    f01 = total(a0 * a1) / r00_sq
    f02 = total(a0 * a2) / r00_sq
    a1 = a1 - f01 * a0
    a2 = a2 - f02 * a0
    r11_sq = total(a1 * a1) + total(b1 * b1)
    r11 = jnp.sqrt(r11_sq)
    f12 = (total(a1 * a2) + total(b1 * b2)) / r11_sq
    a2 = a2 - f12 * a1
    b2 = b2 - f12 * b1
    r22 = jnp.sqrt(total(a2 * a2) + total(b2 * b2) + total(c2 * c2))
    rhs_norm = r00
    first_diag = f01
    first_below = r11 / r00
    upper_right = (f02 - first_diag * f01) / first_below
    second_diag = f12 - first_diag
    second_below = r22 / r11
    first_len = jnp.sqrt(first_diag * first_diag + first_below * first_below)
    cos_one = first_diag / first_len
    sin_one = first_below / first_len
    rotated_top = cos_one * upper_right + sin_one * second_diag
    rotated_low = cos_one * second_diag - sin_one * upper_right
    second_len = jnp.sqrt(rotated_low * rotated_low + second_below * second_below)
    cos_two = rotated_low / second_len
    y_two = cos_two * (-sin_one * rhs_norm) / second_len
    y_one = (cos_one * rhs_norm - rotated_top * y_two) / first_len
    on_one = y_two / r11
    on_base = y_one / r00 - on_one * f01
    out_ref[...] = on_base * cot_ref[...] + on_one * image_ref[...].T


def on_device(cotangent, nodal_mass, curvature, stiffness, levels, neighbours, mortars):
    fields, nodes, leaves = cotangent.shape
    slots = mortars.shape[1]
    count = lax.axis_size("leaf")
    flat = cotangent.reshape(fields * nodes, leaves)
    levels = levels.reshape(1, leaves)
    me = lax.axis_index("leaf").astype(jnp.int32)
    place = jnp.stack([me * leaves, leaves - 2 * leaves * (me % 2)])
    traces, across, spread, to_fine, to_coarse, stay, counts = [
        jnp.asarray(table) for table in matrices()
    ]
    vmem = pl.BlockSpec(memory_space=pltpu.VMEM)
    smem = pl.BlockSpec(memory_space=pltpu.SMEM)
    hbm = pl.BlockSpec(memory_space=pltpu.HBM)

    def call(kernel, outs, specs, operands, scratch=(), flops=0, moved=0, mib=40):
        return pl.pallas_call(
            kernel,
            out_shape=outs,
            in_specs=specs,
            out_specs=jax.tree.map(lambda _: vmem, outs),
            scratch_shapes=scratch,
            compiler_params=pltpu.CompilerParams(vmem_limit_bytes=mib * 1024 * 1024),
            cost_estimate=pl.CostEstimate(flops=flops, bytes_accessed=moved, transcendentals=0),
        )(*operands)

    def shape(*dims, dtype=F32):
        return jax.ShapeDtypeStruct(dims, dtype)

    def exchange(values):
        pairs = [(i, i ^ 1) for i in range(count) if i ^ 1 < count]
        across_pairs = [(i, i + 1) for i in range(1, count - 1, 2)]
        across_pairs = across_pairs + [(j, i) for i, j in across_pairs]
        second = lax.ppermute(values, "leaf", across_pairs)
        return lax.ppermute(values, "leaf", pairs), second

    wide = 2 * LANES
    kept_shapes = dict(
        oh_own=shape(FACES * leaves, leaves, dtype=BF16),
        oh_near=shape(FACES * leaves, 2 * leaves, dtype=BF16),
        coarse_pick=shape(slots, leaves, dtype=BF16),
        fine_own=shape(4 * slots, leaves, dtype=BF16),
        fine_near=shape(4 * slots, 2 * leaves, dtype=BF16),
        fine_back=shape(leaves, 4 * slots, dtype=BF16),
        coarse_back=shape(leaves, slots, dtype=BF16),
        coarse_count=shape(leaves, TRACE),
        diagonal=shape(leaves, LANES),
        stiff=shape(wide, wide, dtype=BF16),
        mass=shape(leaves, LANES),
        curve=shape(leaves, LANES),
        scale=shape(leaves, LANES),
        traces=shape(*traces.shape, dtype=BF16),
        across=shape(*across.shape, dtype=BF16),
        to_fine=shape(*to_fine.shape, dtype=BF16),
        to_coarse=shape(*to_coarse.shape, dtype=BF16),
        stay=shape(*stay.shape, dtype=BF16),
        face=shape(slots, 1, dtype=jnp.int32),
        partial=shape(leaves, LANES),
    )
    rows = shape(leaves, LANES)
    pack = call(
        prep_kernel,
        shape(leaves + 8, LANES),
        [hbm] * 3,
        (flat, levels, mortars),
        scratch=[
            pltpu.VMEM(flat.shape, F32),
            pltpu.VMEM(levels.shape, jnp.int32),
            pltpu.VMEM(mortars.shape, jnp.int32),
            pltpu.SemaphoreType.DMA((3,)),
        ],
    )
    one, two = exchange(pack)
    sources = (neighbours, nodal_mass, curvature, stiffness, levels, spread, counts)
    loaded = sources + (traces, across, to_fine, to_coarse, stay)
    names = KEPT + ("face", "partial")
    kept = call(
        near_kernel,
        [kept_shapes[name] for name in names],
        [smem, vmem] + [hbm] * len(loaded),
        (place, pack) + loaded,
        scratch=[pltpu.VMEM(source.shape, source.dtype) for source in sources]
        + [pltpu.SemaphoreType.DMA((len(loaded),))],
        flops=2_000_000_000,
        moved=4_000_000,
    )
    kept = dict(zip(names, kept))
    first_kept = [kept[name] for name in KEPT_FIRST]
    image, send, picks, backs, faces, extra = call(
        first_kernel,
        [
            rows, rows, shape(2 * slots, leaves, dtype=BF16),
            shape(leaves, 8 * slots, dtype=BF16), shape(2 * slots, 1, dtype=jnp.int32), rows,
        ],
        [smem] + [vmem] * (5 + len(first_kept)),
        [place, pack, one, two, spread, kept["partial"]] + first_kept,
    )
    one, two = exchange(send)
    partial = call(
        again_kernel,
        rows,
        [vmem] * (2 + len(KEPT_AGAIN)),
        [send, extra] + [kept[name] for name in KEPT_AGAIN],
        flops=2_000_000_000,
        moved=4_000_000,
    )
    stats = call(
        second_kernel,
        shape(1, LANES),
        [vmem] * (8 + len(first_kept)),
        [pack, one, two, partial, image, picks, backs, faces] + first_kept,
    )
    gathered = lax.all_to_all(
        jnp.broadcast_to(stats, (count, LANES)), "leaf", 0, 0, tiled=True
    )
    out = call(final_kernel, shape(*flat.shape), [vmem] * 3, (gathered, flat, image))
    return out.reshape(cotangent.shape)


def solution(mesh):
    placed = (
        P(None, None, "leaf"),
        P(None, "leaf"),
        P(None, "leaf"),
        P(),
        P("leaf"),
        P(None, "leaf"),
        P(None, "leaf"),
    )
    return jax.shard_map(
        on_device, mesh=mesh, in_specs=placed, out_specs=P(None, None, "leaf"), check_vma=False
    )
```

time: 75.3 us -> 67 us (0.89)
  blocking collectives: 34.4 us -> 28.7 us
  starting transfers between devices: 13.5 us -> 8.34 us
  local copies, waits for them, and re-layouts: 9.12 us -> 12.6 us
  waiting for transfers between devices: 3.88 us -> 0.61 us
  Pallas kernels: 13.6 us -> 15.9 us
    all_to_all x1, blocking collectives: 34.4 us -> 28.7 us  [on_device(): lax.all_to_all(jnp.broadcast_to(stats, (count, LANES)), 'leaf', 0, 0, til...]
    ppermute x4, starting transfers between devices: 13.5 us -> 8.34 us  [the longest x2 8.16 us: exchange(): second = lax.ppermute(values, 'leaf', across_pairs)]
    unnamed x32, local copies, waits for them, and re-layouts: 9.05 us -> 12.5 us
    ppermute x4, waiting for transfers between devices: 3.88 us -> 0.61 us  [the longest x2 0.6 us: exchange(): second = lax.ppermute(values, 'leaf', across_pairs)]
    pallas_call x4 -> x6, Pallas kernels: 13.6 us -> 15.9 us  [call(): pl.pallas_call(kernel, out_shape=outs, in_specs=specs, out_specs=jax.tree...]
  transfers between devices with their start and end apart: 4 -> 4, of which waited for: 4 -> 1; matrix products, arithmetic and copies ran while one was open for 0% -> 0% of each run, Pallas kernels for 0% -> 11%
where the time goes in v2:
time: 67 us; the launch traced here: 66.3 us
  blocking collectives  28.7 us (43%)
  Pallas kernels  15.9 us (24%)
  local copies, waits for them, and re-layouts  12.6 us (19%)
  starting transfers between devices  8.34 us (12%)
    all_to_all x1, blocking collectives, on_device(): lax.all_to_all(jnp.broadcast_to(stats, (count, LANES)), 'leaf', 0, 0, til...  28.7 us
    pallas_call x6, Pallas kernels, call(): pl.pallas_call(kernel, out_shape=outs, in_specs=specs, out_specs=jax.tree...  15.9 us
    unnamed x32, local copies, waits for them, and re-layouts  12.5 us
    ppermute x2, starting transfers between devices, exchange(): second = lax.ppermute(values, 'leaf', across_pairs)  8.16 us
  transfers between devices with their start and end apart: 4, of which 1 were waited for; matrix products, arithmetic and copies ran while one was open for 0% of the time, Pallas kernels for 11%

profile of v2, /device:TPU:1, one launch (start us, length us, event | category | flops | bytes accessed | tf_op | source)
XLA Modules:
  0.0 66.3 jit_solution(5640255793839033318)
XLA Ops:
  0.0 0.0 copy-start
  0.0 0.9 %copy-done = f32[2,64,256]{2,1,0:T(8,128)S(1)} copy-done((f32[2,64,256]{2,1,0:T(8,128)S(1)}, f32[2,64,256]{2,1,0:T(8,128)}, u32[]{:S(2)}) %copy-start) | copy-done | bytes 131096
  0.9 0.0 copy-start.3
  0.9 0.7 %copy-done.3 = s32[6,128]{1,0:T(8,128)S(1)} copy-done((s32[6,128]{1,0:T(8,128)S(1)}, s32[6,128]{1,0:T(8,128)}, u32[]{:S(2)}) %copy-start.3) | copy-done | bytes 3096
  1.6 0.0 copy-start.4
  1.6 0.7 %copy-done.4 = s32[256]{0:T(256)S(1)} copy-done((s32[256]{0:T(256)S(1)}, s32[256]{0:T(256)}, u32[]{:S(2)}) %copy-start.4) | copy-done | bytes 1048
  2.3 0.3 shard_map.136.pack_ref
  2.6 4.6 %collective-permute-start.1 = (f32[264,128]{1,0:T(8,128)S(1)}, f32[264,128]{1,0:T(8,128)S(1)}, u32[]{:S(2)}, u32[]{:S(2)}) collective-permute-start(f32[264,128]{1,0:T(8,128)S(1)} %shard_map.136.pack_ref), channel_id=1, source_target_pairs={{1,2},{3,4},{5,6},{7,8},{9,10},{11,12},{13,14},{15,16},{17,18},{19... | collective-permute-start | bytes 405512 | tf_op jit(solution)/shard_map/ppermute | solution.py:466
  7.2 0.1 collective-permute-start
  7.3 0.1 pad_add_fusion.place_ref
  7.3 0.0 copy-start.2
  7.3 0.8 %copy-done.2 = bf16[256,128]{1,0:T(8,128)(2,1)S(1)} copy-done((bf16[256,128]{1,0:T(8,128)(2,1)S(1)}, bf16[256,128]{1,0:T(8,128)(2,1)}, u32[]{:S(2)}) %copy-start.2) | copy-done | bytes 65560
  8.2 0.0 copy-start.5
  8.2 0.7 %copy-done.5 = s32[256]{0:T(256)S(1)} copy-done((s32[256]{0:T(256)S(1)}, s32[256]{0:T(256)}, u32[]{:S(2)}) %copy-start.5) | copy-done | bytes 1048
  8.9 0.0 copy-start.6
  8.9 0.8 %copy-done.6 = f32[64,256]{1,0:T(8,128)S(1)} copy-done((f32[64,256]{1,0:T(8,128)S(1)}, f32[64,256]{1,0:T(8,128)}, u32[]{:S(2)}) %copy-start.6) | copy-done | bytes 65560
  9.7 0.0 copy-start.7
  9.7 0.8 %copy-done.7 = f32[64,256]{1,0:T(8,128)S(1)} copy-done((f32[64,256]{1,0:T(8,128)S(1)}, f32[64,256]{1,0:T(8,128)}, u32[]{:S(2)}) %copy-start.7) | copy-done | bytes 65560
  10.5 0.0 copy-start.8
  10.5 0.8 %copy-done.8 = f32[64,64]{1,0:T(8,128)S(1)} copy-done((f32[64,64]{1,0:T(8,128)S(1)}, f32[64,64]{1,0:T(8,128)}, u32[]{:S(2)}) %copy-start.8) | copy-done | bytes 16408
  11.3 0.0 copy-start.9
  11.3 0.7 %copy-done.9 = s32[6,256]{1,0:T(8,128)S(1)} copy-done((s32[6,256]{1,0:T(8,128)S(1)}, s32[6,256]{1,0:T(8,128)}, u32[]{:S(2)}) %copy-start.9) | copy-done | bytes 6168
  12.0 0.0 copy-start.10
  12.0 1.0 %copy-done.10 = bf16[1024,256]{1,0:T(8,128)(2,1)S(1)} copy-done((bf16[1024,256]{1,0:T(8,128)(2,1)S(1)}, bf16[1024,256]{1,0:T(8,128)(2,1)}, u32[]{:S(2)}) %copy-start.10) | copy-done | bytes 524312
  13.0 0.0 copy-start.11
  13.0 1.0 %copy-done.11 = bf16[256,1024]{1,0:T(8,128)(2,1)S(1)} copy-done((bf16[256,1024]{1,0:T(8,128)(2,1)S(1)}, bf16[256,1024]{1,0:T(8,128)(2,1)}, u32[]{:S(2)}) %copy-start.11) | copy-done | bytes 524312
  14.1 0.0 copy-start.12
  14.1 1.0 %copy-done.12 = bf16[1536,128]{1,0:T(8,128)(2,1)S(1)} copy-done((bf16[1536,128]{1,0:T(8,128)(2,1)S(1)}, bf16[1536,128]{1,0:T(8,128)(2,1)}, u32[]{:S(2)}) %copy-start.12) | copy-done | bytes 393240
  15.1 0.0 copy-start.13
  15.1 0.9 %copy-done.13 = bf16[256,256]{1,0:T(8,128)(2,1)S(1)} copy-done((bf16[256,256]{1,0:T(8,128)(2,1)S(1)}, bf16[256,256]{1,0:T(8,128)(2,1)}, u32[]{:S(2)}) %copy-start.13) | copy-done | bytes 131096
  16.0 0.0 copy-start.14
  16.0 0.9 %copy-done.14 = bf16[256,256]{1,0:T(8,128)(2,1)S(1)} copy-done((bf16[256,256]{1,0:T(8,128)(2,1)S(1)}, bf16[256,256]{1,0:T(8,128)(2,1)}, u32[]{:S(2)}) %copy-start.14) | copy-done | bytes 131096
  16.9 0.0 copy-start.15
  16.9 0.7 %copy-done.15 = f32[8,128]{1,0:T(8,128)S(1)} copy-done((f32[8,128]{1,0:T(8,128)S(1)}, f32[8,128]{1,0:T(8,128)}, u32[]{:S(2)}) %copy-start.15) | copy-done | bytes 4120
  17.6 5.2 %shard_map.137 = (bf16[1536,256]{1,0:T(8,128)(2,1)S(1)}, bf16[1536,512]{1,0:T(8,128)(2,1)S(1)}, bf16[128,256]{1,0:T(8,128)(2,1)S(1)}, bf16[512,256]{1,0:T(8,128)...) custom-call(s32[2]{0:T(128)S(1)} %pad_add_fusion.place_ref, ...), custom_call_target="tpu_custom_call" | custom-call | flops 2000000000 | bytes 4000000 | tf_op jit(solution)/shard_map/pallas_call | solution.py:449
  22.8 0.0 collective-permute-done.1.two_ref
  22.8 0.0 collective-permute-done.one_ref
  22.8 4.0 %shard_map.138 = (f32[256,128]{1,0:T(8,128)S(1)}, f32[256,128]{1,0:T(8,128)S(1)}, bf16[256,256]{1,0:T(8,128)(2,1)S(1)}, bf16[256,1024]{1,0:T(8,128)(2,1)S(1)}, s...) custom-call(s32[2]{0:T(128)S(1)} %pad_add_fusion.place_ref, f32[264,128]{1,0:T(8,128)S(1)} %shard_map.136.pack_ref, ...), custom_call_target="tpu_custom_call" | custom-call | tf_op jit(solution)/shard_map/pallas_call | solution.py:449
  26.8 3.6 %collective-permute-start.3 = (f32[256,128]{1,0:T(8,128)S(1)}, f32[256,128]{1,0:T(8,128)S(1)}, u32[]{:S(2)}, u32[]{:S(2)}) collective-permute-start(f32[256,128]{1,0:T(8,128)S(1)} %get-tuple-element.43.send_ref), channel_id=1, source_target_pairs={{1,2},{3,4},{5,6},{7,8},{9,10},{11,12},{13,14},{15,16},{17,18},{19... | collective-permute-start | bytes 393224 | tf_op jit(solution)/shard_map/ppermute | solution.py:466
  30.3 0.1 collective-permute-start.2
  30.4 2.0 %shard_map.139.partial_ref = f32[256,128]{1,0:T(8,128)S(1)} custom-call(f32[256,128]{1,0:T(8,128)S(1)} %get-tuple-element.43.send_ref, f32[256,128]{1,0:T(8,128)S(1)} %get-tuple-element.44.extra_ref, bf16[1536,256]{1,0:T(8,128)(2,1)S(1)} %get-tuple-element.45.refs_0_, bf16[128,256]{1,0:T(8,128)(2,1)S(1)} %get-tuple-element.46.refs_1_, ...), custom_call_target="tpu_custom_call" | custom-call | flops 2000000000 | bytes 4000000 | tf_op jit(solution)/shard_map/pallas_call | solution.py:449
  32.5 0.6 collective-permute-done.3.two_ref
  33.1 0.0 collective-permute-done.2.one_ref
  33.1 0.0 copy-start.1
  33.1 3.3 %shard_map.140 = f32[1,128]{1,0:T(1,128)S(1)} custom-call(f32[264,128]{1,0:T(8,128)S(1)} %shard_map.136.pack_ref, f32[256,128]{1,0:T(8,128)S(1)} %collective-permute-done.2.one_ref, f32[256,128]{1,0:T(8,128)S(1)} %collective-permute-done.3.two_ref, f32[256,128]{1,0:T(8,128)S(1)} %shard_map.139.partial_ref, f32[256,128]{1,0:T(8,128)S(1)} %get-tuple-element.53.image_ref, ...), custom_call_target="tpu_custom_call" | custom-call | tf_op jit(solution)/shard_map/pallas_call | solution.py:449
  36.4 0.1 broadcast_in_dim.2
  36.5 28.7 %all_to_all.8 = f32[256,1,128]{2,1,0:T(1,128)S(1)} all-to-all(f32[256,1,128]{2,1,0:T(1,128)S(1)} %broadcast_in_dim.2), channel_id=1, replica_groups=mesh['leaf'=256] {'leaf'}, dimensions={0} | all-to-all | bytes 262144 | tf_op jit(solution)/shard_map/all_to_all | solution.py:545
  65.2 0.0 copy-done.1
  65.2 1.1 %shard_map.141 = f32[128,256]{1,0:T(8,128)} custom-call(f32[256,128]{1,0:T(8,128)S(1)} %bitcast.9, f32[128,256]{1,0:T(8,128)S(1)} %bitcast.8, f32[256,128]{1,0:T(8,128)S(1)} %get-tuple-element.53.image_ref), custom_call_target="tpu_custom_call" | custom-call | tf_op jit(solution)/shard_map/pallas_call | solution.py:449
Async XLA Ops:
  0.0 0.9 %copy-start = (f32[2,64,256]{2,1,0:T(8,128)S(1)}, f32[2,64,256]{2,1,0:T(8,128)}, u32[]{:S(2)}) copy-start(f32[2,64,256]{2,1,0:T(8,128)} %param.14) | copy-start | bytes 393220
  0.9 0.7 %copy-start.3 = (s32[6,128]{1,0:T(8,128)S(1)}, s32[6,128]{1,0:T(8,128)}, u32[]{:S(2)}) copy-start(s32[6,128]{1,0:T(8,128)} %mortars_hbm.1) | copy-start | bytes 9220
  1.6 0.7 %copy-start.4 = (s32[256]{0:T(256)S(1)}, s32[256]{0:T(256)}, u32[]{:S(2)}) copy-start(s32[256]{0:T(256)} %param.18) | copy-start | bytes 3076
  2.6 20.2 %collective-permute-start.1 = (f32[264,128]{1,0:T(8,128)S(1)}, f32[264,128]{1,0:T(8,128)S(1)}, u32[]{:S(2)}, u32[]{:S(2)}) collective-permute-start(f32[264,128]{1,0:T(8,128)S(1)} %shard_map.136.pack_ref), channel_id=1, source_target_pairs={{1,2},{3,4},{5,6},{7,8},{9,10},{11,12},{13,14},{15,16},{17,18},{19... | collective-permute-start | bytes 405512 | tf_op jit(solution)/shard_map/ppermute | solution.py:466
  7.2 15.6 %collective-permute-start = (f32[264,128]{1,0:T(8,128)S(1)}, f32[264,128]{1,0:T(8,128)S(1)}, u32[]{:S(2)}, u32[]{:S(2)}) collective-permute-start(f32[264,128]{1,0:T(8,128)S(1)} %shard_map.136.pack_ref), channel_id=1, source_target_pairs={{0,1},{1,0},{2,3},{3,2},{4,5},{5,4},{6,7},{7,6},{8,9},{9,8},{10,11... | collective-permute-start | bytes 405512 | tf_op jit(solution)/shard_map/ppermute | solution.py:467
  7.3 0.8 %copy-start.2 = (bf16[256,128]{1,0:T(8,128)(2,1)S(1)}, bf16[256,128]{1,0:T(8,128)(2,1)}, u32[]{:S(2)}) copy-start(bf16[256,128]{1,0:T(8,128)(2,1)} %constant.37.clone.refs_5_.spread_ref) | copy-start | bytes 196612
  8.2 0.7 %copy-start.5 = (s32[256]{0:T(256)S(1)}, s32[256]{0:T(256)}, u32[]{:S(2)}) copy-start(s32[256]{0:T(256)} %param.18) | copy-start | bytes 3076
  8.9 0.8 %copy-start.6 = (f32[64,256]{1,0:T(8,128)S(1)}, f32[64,256]{1,0:T(8,128)}, u32[]{:S(2)}) copy-start(f32[64,256]{1,0:T(8,128)} %refs_1_.1) | copy-start | bytes 196612
  9.7 0.8 %copy-start.7 = (f32[64,256]{1,0:T(8,128)S(1)}, f32[64,256]{1,0:T(8,128)}, u32[]{:S(2)}) copy-start(f32[64,256]{1,0:T(8,128)} %refs_2_.1) | copy-start | bytes 196612
  10.5 0.8 %copy-start.8 = (f32[64,64]{1,0:T(8,128)S(1)}, f32[64,64]{1,0:T(8,128)}, u32[]{:S(2)}) copy-start(f32[64,64]{1,0:T(8,128)} %refs_3_.1) | copy-start | bytes 49156
  11.3 0.7 %copy-start.9 = (s32[6,256]{1,0:T(8,128)S(1)}, s32[6,256]{1,0:T(8,128)}, u32[]{:S(2)}) copy-start(s32[6,256]{1,0:T(8,128)} %refs_0_.1) | copy-start | bytes 18436
  12.0 1.0 %copy-start.10 = (bf16[1024,256]{1,0:T(8,128)(2,1)S(1)}, bf16[1024,256]{1,0:T(8,128)(2,1)}, u32[]{:S(2)}) copy-start(bf16[1024,256]{1,0:T(8,128)(2,1)} %constant.39.clone.refs_10_) | copy-start | bytes 1572868
  13.0 1.0 %copy-start.11 = (bf16[256,1024]{1,0:T(8,128)(2,1)S(1)}, bf16[256,1024]{1,0:T(8,128)(2,1)}, u32[]{:S(2)}) copy-start(bf16[256,1024]{1,0:T(8,128)(2,1)} %constant.38.clone.refs_9_) | copy-start | bytes 1572868
  14.1 1.0 %copy-start.12 = (bf16[1536,128]{1,0:T(8,128)(2,1)S(1)}, bf16[1536,128]{1,0:T(8,128)(2,1)}, u32[]{:S(2)}) copy-start(bf16[1536,128]{1,0:T(8,128)(2,1)} %constant.36.clone.refs_8_) | copy-start | bytes 1179652
  15.1 0.9 %copy-start.13 = (bf16[256,256]{1,0:T(8,128)(2,1)S(1)}, bf16[256,256]{1,0:T(8,128)(2,1)}, u32[]{:S(2)}) copy-start(bf16[256,256]{1,0:T(8,128)(2,1)} %constant.40.clone.refs_11_) | copy-start | bytes 393220
  16.0 0.9 %copy-start.14 = (bf16[256,256]{1,0:T(8,128)(2,1)S(1)}, bf16[256,256]{1,0:T(8,128)(2,1)}, u32[]{:S(2)}) copy-start(bf16[256,256]{1,0:T(8,128)(2,1)} %constant.35.clone.refs_7_) | copy-start | bytes 393220
  16.9 0.7 %copy-start.15 = (f32[8,128]{1,0:T(8,128)S(1)}, f32[8,128]{1,0:T(8,128)}, u32[]{:S(2)}) copy-start(f32[8,128]{1,0:T(8,128)} %constant.41.clone.refs_6_) | copy-start | bytes 12292
  26.8 6.3 %collective-permute-start.3 = (f32[256,128]{1,0:T(8,128)S(1)}, f32[256,128]{1,0:T(8,128)S(1)}, u32[]{:S(2)}, u32[]{:S(2)}) collective-permute-start(f32[256,128]{1,0:T(8,128)S(1)} %get-tuple-element.43.send_ref), channel_id=1, source_target_pairs={{1,2},{3,4},{5,6},{7,8},{9,10},{11,12},{13,14},{15,16},{17,18},{19... | collective-permute-start | bytes 393224 | tf_op jit(solution)/shard_map/ppermute | solution.py:466
  30.3 2.7 %collective-permute-start.2 = (f32[256,128]{1,0:T(8,128)S(1)}, f32[256,128]{1,0:T(8,128)S(1)}, u32[]{:S(2)}, u32[]{:S(2)}) collective-permute-start(f32[256,128]{1,0:T(8,128)S(1)} %get-tuple-element.43.send_ref), channel_id=1, source_target_pairs={{0,1},{1,0},{2,3},{3,2},{4,5},{5,4},{6,7},{7,6},{8,9},{9,8},{10,11... | collective-permute-start | bytes 393224 | tf_op jit(solution)/shard_map/ppermute | solution.py:467
  33.1 32.1 %copy-start.1 = (f32[2,64,256]{2,1,0:T(8,128)S(1)}, f32[2,64,256]{2,1,0:T(8,128)}, u32[]{:S(2)}) copy-start(f32[2,64,256]{2,1,0:T(8,128)} %param.14) | copy-start | bytes 393220

commit v3 on v2

--- a/solution.py
+++ b/solution.py
@@ -110,7 +110,9 @@
 
 
 def pick(index, shape, dim):
-    return jnp.where(index == lax.broadcasted_iota(jnp.int32, shape, dim), 1.0, 0.0).astype(BF16)
+    places = lax.broadcasted_iota(jnp.int32, shape, dim).astype(F32).astype(BF16)
+    index = jnp.broadcast_to(index.astype(F32), shape).astype(BF16)
+    return jnp.where(index == places, jnp.ones(shape, BF16), jnp.zeros(shape, BF16))
 
 
 def on_face(face, slots):
@@ -199,16 +201,12 @@
     return dot_parts(times, spread)
 
 
-def near_index(index, offset, first, leaves):
-    local = index - offset
-    here = jnp.where(local < 0, local + leaves, local - leaves)
-    is_first = (local < 0) == (first < 0)
-    outside = (local >= 0) & (local < leaves)
-    return jnp.where(outside | (index < 0), -1, jnp.where(is_first, here, here + leaves))
-
-
 def own_index(index, offset):
     return jnp.where(index < 0, -1, index - offset)
+
+
+def pick_near(first_index, second_index, shape):
+    return jnp.concatenate([pick(first_index, shape, 1), pick(second_index, shape, 1)], axis=1)
 
 
 def to_columns(table):
@@ -237,21 +235,27 @@
         [local["neighbours"][...], jnp.full((2, leaves), -1, jnp.int32)], axis=0
     )
     own = to_columns(own_index(neighbours, offset))
-    near = to_columns(near_index(neighbours, offset, first, leaves))
+    near_one = to_columns(own_index(neighbours, offset + first))
+    near_two = to_columns(own_index(neighbours, offset - first))
     for f in range(FACES):
         rows = slice(leaves * f, leaves * (f + 1))
         kept["oh_own"][rows, :] = pick(own[:, f : f + 1], (leaves, leaves), 1)
-        kept["oh_near"][rows, :] = pick(near[:, f : f + 1], (leaves, 2 * leaves), 1)
+        kept["oh_near"][rows, :] = pick_near(
+            near_one[:, f : f + 1], near_two[:, f : f + 1], (leaves, leaves)
+        )
     kept["coarse_pick"][...] = pick(columns[:, 0:1] - offset, (slots, leaves), 1)
     coarse_back = pick(table[0:1, :] - offset, (leaves, slots), 0)
     kept["coarse_back"][...] = coarse_back
     fine_own = own_index(columns, offset)
-    fine_near = near_index(columns, offset, first, leaves)
+    fine_one = own_index(columns, offset + first)
+    fine_two = own_index(columns, offset - first)
     fine_rows = own_index(table, offset)
     for q in range(4):
         rows = slice(slots * q, slots * (q + 1))
         kept["fine_own"][rows, :] = pick(fine_own[:, 2 + q : 3 + q], (slots, leaves), 1)
-        kept["fine_near"][rows, :] = pick(fine_near[:, 2 + q : 3 + q], (slots, 2 * leaves), 1)
+        kept["fine_near"][rows, :] = pick_near(
+            fine_one[:, 2 + q : 3 + q], fine_two[:, 2 + q : 3 + q], (slots, leaves)
+        )
         kept["fine_back"][:, rows] = pick(fine_rows[2 + q : 3 + q, :], (leaves, slots), 0)
     for copy in copies[1:]:
         copy.wait()
@@ -490,11 +494,14 @@
         partial=shape(leaves, LANES),
     )
     rows = shape(leaves, LANES)
+    def stay_out(*arrays):
+        return tuple(pltpu.with_memory_space_constraint(array, pltpu.HBM) for array in arrays)
+
     pack = call(
         prep_kernel,
         shape(leaves + 8, LANES),
         [hbm] * 3,
-        (flat, levels, mortars),
+        stay_out(flat, levels, mortars),
         scratch=[
             pltpu.VMEM(flat.shape, F32),
             pltpu.VMEM(levels.shape, jnp.int32),
@@ -510,7 +517,7 @@
         near_kernel,
         [kept_shapes[name] for name in names],
         [smem, vmem] + [hbm] * len(loaded),
-        (place, pack) + loaded,
+        (place, pack) + stay_out(*loaded),
         scratch=[pltpu.VMEM(source.shape, source.dtype) for source in sources]
         + [pltpu.SemaphoreType.DMA((len(loaded),))],
         flops=2_000_000_000,

time: 67 us -> 57 us (0.85)
  local copies, waits for them, and re-layouts: 12.6 us -> 0.08 us
  blocking collectives: 28.7 us -> 31.5 us
    unnamed x32 -> x4, local copies, waits for them, and re-layouts: 12.5 us -> 0.01 us
    all_to_all x1, blocking collectives: 28.7 us -> 31.5 us  [on_device(): lax.all_to_all(jnp.broadcast_to(stats, (count, LANES)), 'leaf', 0, 0, til...]
  transfers between devices with their start and end apart: 4 -> 4, of which waited for: 1 -> 1; matrix products, arithmetic and copies ran while one was open for 0% -> 0% of each run, Pallas kernels for 11% -> 12%
where the time goes in v3:
time: 57 us; the launch traced here: 56.8 us
  blocking collectives  31.5 us (55%)
  Pallas kernels  16.1 us (28%)
  starting transfers between devices  8.34 us (15%)
  waiting for transfers between devices  0.61 us (1%)
    all_to_all x1, blocking collectives, on_device(): lax.all_to_all(jnp.broadcast_to(stats, (count, LANES)), 'leaf', 0, 0, til...  31.5 us
    pallas_call x6, Pallas kernels, call(): pl.pallas_call(kernel, out_shape=outs, in_specs=specs, out_specs=jax.tree...  16.1 us
    ppermute x2, starting transfers between devices, exchange(): second = lax.ppermute(values, 'leaf', across_pairs)  8.16 us
  transfers between devices with their start and end apart: 4, of which 1 were waited for; matrix products, arithmetic and copies ran while one was open for 0% of the time, Pallas kernels for 12%

profile of v3, /device:TPU:1, one launch (start us, length us, event | category | flops | bytes accessed | tf_op | source)
XLA Modules:
  0.0 56.8 jit_solution(16722571227207936728)
XLA Ops:
  0.0 1.0 %shard_map.136.pack_ref = f32[264,128]{1,0:T(8,128)S(1)} custom-call(f32[128,256]{1,0:T(8,128)} %bitcast.7, s32[1,256]{1,0:T(1,128)} %bitcast.11, s32[6,128]{1,0:T(8,128)} %mortars_hbm.1), custom_call_target="tpu_custom_call" | custom-call | tf_op jit(solution)/shard_map/pallas_call | solution.py:453
  1.0 4.6 %collective-permute-start.1 = (f32[264,128]{1,0:T(8,128)S(1)}, f32[264,128]{1,0:T(8,128)S(1)}, u32[]{:S(2)}, u32[]{:S(2)}) collective-permute-start(f32[264,128]{1,0:T(8,128)S(1)} %shard_map.136.pack_ref), channel_id=1, source_target_pairs={{1,2},{3,4},{5,6},{7,8},{9,10},{11,12},{13,14},{15,16},{17,18},{19... | collective-permute-start | bytes 405512 | tf_op jit(solution)/shard_map/ppermute | solution.py:470
  5.6 0.1 collective-permute-start
  5.8 0.1 pad_add_fusion.place_ref
  5.8 0.0 copy-start.1
  5.8 4.6 %shard_map.137 = (bf16[1536,256]{1,0:T(8,128)(2,1)S(1)}, bf16[1536,512]{1,0:T(8,128)(2,1)S(1)}, bf16[128,256]{1,0:T(8,128)(2,1)S(1)}, bf16[512,256]{1,0:T(8,128)...) custom-call(s32[2]{0:T(128)S(1)} %pad_add_fusion.place_ref, ...), custom_call_target="tpu_custom_call" | custom-call | flops 2000000000 | bytes 4000000 | tf_op jit(solution)/shard_map/pallas_call | solution.py:453
  10.5 0.0 collective-permute-done.1.two_ref
  10.5 0.0 collective-permute-done.one_ref
  10.5 0.0 copy-done.1
  10.5 3.9 %shard_map.138 = (f32[256,128]{1,0:T(8,128)S(1)}, f32[256,128]{1,0:T(8,128)S(1)}, bf16[256,256]{1,0:T(8,128)(2,1)S(1)}, bf16[256,1024]{1,0:T(8,128)(2,1)S(1)}, s...) custom-call(s32[2]{0:T(128)S(1)} %pad_add_fusion.place_ref, f32[264,128]{1,0:T(8,128)S(1)} %shard_map.136.pack_ref, ...), custom_call_target="tpu_custom_call" | custom-call | tf_op jit(solution)/shard_map/pallas_call | solution.py:453
  14.4 3.6 %collective-permute-start.3 = (f32[256,128]{1,0:T(8,128)S(1)}, f32[256,128]{1,0:T(8,128)S(1)}, u32[]{:S(2)}, u32[]{:S(2)}) collective-permute-start(f32[256,128]{1,0:T(8,128)S(1)} %get-tuple-element.43.send_ref), channel_id=1, source_target_pairs={{1,2},{3,4},{5,6},{7,8},{9,10},{11,12},{13,14},{15,16},{17,18},{19... | collective-permute-start | bytes 393224 | tf_op jit(solution)/shard_map/ppermute | solution.py:470
  18.0 0.1 collective-permute-start.2
  18.1 2.0 %shard_map.139.partial_ref = f32[256,128]{1,0:T(8,128)S(1)} custom-call(f32[256,128]{1,0:T(8,128)S(1)} %get-tuple-element.43.send_ref, f32[256,128]{1,0:T(8,128)S(1)} %get-tuple-element.44.extra_ref, bf16[1536,256]{1,0:T(8,128)(2,1)S(1)} %get-tuple-element.45.refs_0_, bf16[128,256]{1,0:T(8,128)(2,1)S(1)} %get-tuple-element.46.refs_1_, ...), custom_call_target="tpu_custom_call" | custom-call | flops 2000000000 | bytes 4000000 | tf_op jit(solution)/shard_map/pallas_call | solution.py:453
  20.1 0.6 %collective-permute-done.3.two_ref = f32[256,128]{1,0:T(8,128)S(1)} collective-permute-done((f32[256,128]{1,0:T(8,128)S(1)}, f32[256,128]{1,0:T(8,128)S(1)}, u32[]{:S(2)}, u32[]{:S(2)}) %collective-permute-start.3) | collective-permute-done | bytes 131104 | tf_op jit(solution)/shard_map/ppermute | solution.py:470
  20.7 0.0 collective-permute-done.2.one_ref
  20.7 0.0 copy-start
  20.7 3.3 %shard_map.140 = f32[1,128]{1,0:T(1,128)S(1)} custom-call(f32[264,128]{1,0:T(8,128)S(1)} %shard_map.136.pack_ref, f32[256,128]{1,0:T(8,128)S(1)} %collective-permute-done.2.one_ref, f32[256,128]{1,0:T(8,128)S(1)} %collective-permute-done.3.two_ref, f32[256,128]{1,0:T(8,128)S(1)} %shard_map.139.partial_ref, f32[256,128]{1,0:T(8,128)S(1)} %get-tuple-element.53.image_ref, ...), custom_call_target="tpu_custom_call" | custom-call | tf_op jit(solution)/shard_map/pallas_call | solution.py:453
  24.1 0.1 broadcast_in_dim.2
  24.1 31.5 %all_to_all.8 = f32[256,1,128]{2,1,0:T(1,128)S(1)} all-to-all(f32[256,1,128]{2,1,0:T(1,128)S(1)} %broadcast_in_dim.2), channel_id=1, replica_groups=mesh['leaf'=256] {'leaf'}, dimensions={0} | all-to-all | bytes 262144 | tf_op jit(solution)/shard_map/all_to_all | solution.py:552
  55.7 0.0 copy-done
  55.7 1.1 %shard_map.141 = f32[128,256]{1,0:T(8,128)} custom-call(f32[256,128]{1,0:T(8,128)S(1)} %bitcast.9, f32[128,256]{1,0:T(8,128)S(1)} %bitcast.8, f32[256,128]{1,0:T(8,128)S(1)} %get-tuple-element.53.image_ref), custom_call_target="tpu_custom_call" | custom-call | tf_op jit(solution)/shard_map/pallas_call | solution.py:453
Async XLA Ops:
  1.0 9.4 %collective-permute-start.1 = (f32[264,128]{1,0:T(8,128)S(1)}, f32[264,128]{1,0:T(8,128)S(1)}, u32[]{:S(2)}, u32[]{:S(2)}) collective-permute-start(f32[264,128]{1,0:T(8,128)S(1)} %shard_map.136.pack_ref), channel_id=1, source_target_pairs={{1,2},{3,4},{5,6},{7,8},{9,10},{11,12},{13,14},{15,16},{17,18},{19... | collective-permute-start | bytes 405512 | tf_op jit(solution)/shard_map/ppermute | solution.py:470
  5.6 4.8 %collective-permute-start = (f32[264,128]{1,0:T(8,128)S(1)}, f32[264,128]{1,0:T(8,128)S(1)}, u32[]{:S(2)}, u32[]{:S(2)}) collective-permute-start(f32[264,128]{1,0:T(8,128)S(1)} %shard_map.136.pack_ref), channel_id=1, source_target_pairs={{0,1},{1,0},{2,3},{3,2},{4,5},{5,4},{6,7},{7,6},{8,9},{9,8},{10,11... | collective-permute-start | bytes 405512 | tf_op jit(solution)/shard_map/ppermute | solution.py:471
  5.8 4.7 %copy-start.1 = (bf16[256,128]{1,0:T(8,128)(2,1)S(1)}, bf16[256,128]{1,0:T(8,128)(2,1)}, u32[]{:S(2)}) copy-start(bf16[256,128]{1,0:T(8,128)(2,1)} %constant.37.clone.refs_5_.spread_ref) | copy-start | bytes 196612
  14.4 6.3 %collective-permute-start.3 = (f32[256,128]{1,0:T(8,128)S(1)}, f32[256,128]{1,0:T(8,128)S(1)}, u32[]{:S(2)}, u32[]{:S(2)}) collective-permute-start(f32[256,128]{1,0:T(8,128)S(1)} %get-tuple-element.43.send_ref), channel_id=1, source_target_pairs={{1,2},{3,4},{5,6},{7,8},{9,10},{11,12},{13,14},{15,16},{17,18},{19... | collective-permute-start | bytes 393224 | tf_op jit(solution)/shard_map/ppermute | solution.py:470
  18.0 2.7 %collective-permute-start.2 = (f32[256,128]{1,0:T(8,128)S(1)}, f32[256,128]{1,0:T(8,128)S(1)}, u32[]{:S(2)}, u32[]{:S(2)}) collective-permute-start(f32[256,128]{1,0:T(8,128)S(1)} %get-tuple-element.43.send_ref), channel_id=1, source_target_pairs={{0,1},{1,0},{2,3},{3,2},{4,5},{5,4},{6,7},{7,6},{8,9},{9,8},{10,11... | collective-permute-start | bytes 393224 | tf_op jit(solution)/shard_map/ppermute | solution.py:471
  20.7 35.0 %copy-start = (f32[2,64,256]{2,1,0:T(8,128)S(1)}, f32[2,64,256]{2,1,0:T(8,128)}, u32[]{:S(2)}) copy-start(f32[2,64,256]{2,1,0:T(8,128)} %param.14) | copy-start | bytes 393220

commit v4 on v3

v4 whole, which is shorter than its diff:
```python
import jax
import jax.numpy as jnp
import ml_dtypes
import numpy as np
from jax import lax
from jax.experimental import pallas as pl
from jax.experimental.pallas import tpu as pltpu
from jax.sharding import PartitionSpec as P

TAU_WEIGHT = 0.15
EPS_WEIGHT = 0.1
FACES = 6
NODES = 64
LANES = 128
TRACE = 256
F32 = jnp.float32
BF16 = jnp.bfloat16


def face_tables():
    node_at = np.zeros((6, 16), dtype=np.int64)
    for face_id in range(6):
        for row_pos in range(4):
            for col_pos in range(4):
                coords = [row_pos, col_pos]
                coords.insert(face_id // 2, 3 * (face_id % 2))
                node_at[face_id, 4 * row_pos + col_pos] = (
                    16 * coords[0] + 4 * coords[1] + coords[2]
                )
    counts = np.zeros(64)
    for face_id in range(6):
        counts[node_at[face_id]] += 1.0
    points = np.array([-1.0, -1.0 / np.sqrt(5.0), 1.0 / np.sqrt(5.0), 1.0])
    halves = np.zeros((2, 4, 4))
    for half_id in range(2):
        target = (points + 2.0 * half_id - 1.0) / 2.0
        for column in range(4):
            lagrange = np.ones(4)
            for other_id in range(4):
                if other_id != column:
                    lagrange = (
                        lagrange * (target - points[other_id]) / (points[column] - points[other_id])
                    )
            halves[half_id, :, column] = lagrange
    mortar = np.stack([np.kron(halves[quarter // 2], halves[quarter % 2]) for quarter in range(4)])
    return node_at, counts, mortar


def two_parts(table):
    high = table.astype(np.float32).astype(ml_dtypes.bfloat16)
    low = (table - high.astype(np.float64)).astype(np.float32).astype(ml_dtypes.bfloat16)
    return np.concatenate([high, low], axis=-1)


def matrices():
    node_at, counts, mortar = face_tables()
    traces = np.zeros((2 * LANES, TRACE))
    across = np.zeros((FACES * 2 * LANES, LANES))
    spread = np.zeros((TRACE, LANES))
    to_fine = np.zeros((4, TRACE, LANES))
    to_coarse = np.zeros((4, TRACE, LANES))
    stay = np.zeros((TRACE, LANES))
    square = sum(mortar[quarter].T @ mortar[quarter] for quarter in range(4))
    for face in range(FACES):
        other = face ^ 1
        for field in range(2):
            base = 32 * face + 16 * field
            lifted = 32 * other + 16 * field
            nodes = 64 * field + node_at[face]
            facing = 64 * field + node_at[other]
            for place in range(16):
                spread[base + place, nodes[place]] = 1.0
                for part in range(2):
                    traces[part * LANES + nodes[place], base + place] = 1.0
                    across[(2 * face + part) * LANES + facing[place], nodes[place]] = 1.0
                stay[base + place, nodes] = square[:, place]
                for quarter in range(4):
                    to_fine[quarter, base + place, facing] = mortar[quarter][:, place]
                    to_coarse[quarter, lifted + place, nodes] = mortar[quarter][place, :]
    small = ml_dtypes.bfloat16
    counts = np.tile(np.concatenate([counts, counts])[None, :], (8, 1)).astype(np.float32)
    return (
        traces.astype(small),
        across.astype(small),
        spread.astype(small),
        np.concatenate(list(two_parts(to_fine)), axis=-1),
        np.concatenate(list(two_parts(to_coarse)), axis=0),
        two_parts(stay),
        counts,
    )


def split(values, axis=1):
    high = values.astype(BF16)
    return jnp.concatenate([high, (values - high.astype(F32)).astype(BF16)], axis=axis)


def dot(left, right):
    return jnp.dot(left, right, preferred_element_type=F32)


def fold(values):
    return values[:, :LANES] + values[:, LANES:]


def dot_parts(values, table):
    high = values.astype(BF16)
    low = (values - high.astype(F32)).astype(BF16)
    return dot(high, table) + dot(low, table)


def pick(index, shape, dim):
    places = lax.broadcasted_iota(jnp.int32, shape, dim).astype(F32).astype(BF16)
    index = jnp.broadcast_to(index.astype(F32), shape).astype(BF16)
    return jnp.where(index == places, jnp.ones(shape, BF16), jnp.zeros(shape, BF16))


def on_face(face, slots):
    return lax.broadcasted_iota(jnp.int32, (slots, TRACE), 1) // 32 == face


def opposite(face):
    return jnp.where(face >= 0, face ^ 1, -1)


def level_rows(levels):
    scale = jnp.left_shift(jnp.ones_like(levels), levels).astype(F32)
    return jnp.broadcast_to(scale, (LANES, levels.shape[1])).T


def fetch(pairs, sems):
    copies = [
        pltpu.make_async_copy(source, target, sems.at[at])
        for at, (source, target) in enumerate(pairs)
    ]
    for copy in copies:
        copy.start()
    return copies


def prep_kernel(cot_hbm, levels_hbm, mortars_hbm, pack_ref, cot_ref, levels_ref, mortars_ref, sems):
    for copy in fetch(
        ((cot_hbm, cot_ref), (levels_hbm, levels_ref), (mortars_hbm, mortars_ref)), sems
    ):
        copy.wait()
    leaves = cot_ref.shape[1]
    scale = jnp.left_shift(jnp.ones_like(levels_ref[...]), levels_ref[...]).astype(F32)
    pack_ref[0:leaves, :] = (cot_ref[...] * scale).T
    table = mortars_ref[...].astype(F32) + 1.0
    pack_ref[leaves : leaves + 8, :] = jnp.concatenate(
        [table, jnp.zeros((2, table.shape[1]), F32)], axis=0
    )


TABLES = ("traces", "across", "to_fine", "to_coarse", "stay")
LOCAL = ("neighbours", "mass", "curve", "stiffness", "levels", "spread", "counts")
KEPT = (
    "oh_own", "oh_one", "oh_two", "coarse_pick", "fine_own", "fine_one", "fine_two", "fine_back",
    "coarse_back", "coarse_count", "diagonal", "stiff", "mass", "curve", "scale", "face",
) + TABLES
KEPT_SIDE = ("coarse_back", "face") + TABLES[:4]
KEPT_OWN = (
    "oh_own", "coarse_pick", "fine_own", "fine_back", "coarse_count", "stiff", "mass", "curve",
    "stay",
) + KEPT_SIDE


def from_faces(chosen, across):
    leaves = chosen.shape[0] // FACES
    moved = jnp.zeros((leaves, LANES), F32)
    for face in range(FACES):
        moved = moved + dot(
            chosen[leaves * face : leaves * (face + 1), :],
            across[2 * LANES * face : 2 * LANES * (face + 1), :],
        )
    return moved


def to_fine(picks, backs, face, parts, kept):
    trace = dot(dot(picks, parts).astype(BF16), kept["traces"][...])
    trace = jnp.where(on_face(face, picks.shape[0]), trace, 0.0)
    lifted = dot_parts(trace, kept["to_fine"][...])
    lifted = jnp.concatenate(
        [split(fold(lifted[:, TRACE * q : TRACE * (q + 1)])) for q in range(4)], axis=0
    )
    return fold(dot(backs, lifted))


def to_coarse(picks, parts, kept):
    slots = kept["coarse_back"].shape[1]
    trace = dot(dot(picks, parts).astype(BF16), kept["traces"][...])
    other = on_face(opposite(kept["face"][...]), slots)
    sent = jnp.zeros((slots, 2 * LANES), F32)
    for quarter in range(4):
        part = jnp.where(other, trace[slots * quarter : slots * (quarter + 1), :], 0.0)
        sent = sent + dot_parts(part, kept["to_coarse"][TRACE * quarter : TRACE * (quarter + 1), :])
    return fold(dot(kept["coarse_back"][...], split(fold(sent))))


def placed(lapped):
    first = lax.broadcasted_iota(jnp.int32, lapped.shape, 1) < NODES
    return jnp.where(first, -EPS_WEIGHT, TAU_WEIGHT) * pltpu.roll(lapped, NODES, 1)


def own_part(rows, vector, diagonal, kept):
    parts = split(rows)
    lapped = diagonal * rows + fold(dot(parts, kept["stiff"][...]))
    lapped = lapped - from_faces(dot(kept["oh_own"][...], parts).astype(BF16), kept["across"])
    here = dot(parts, kept["traces"][...]) * kept["coarse_count"][...]
    lapped = lapped + fold(dot_parts(here, kept["stay"][...]))
    lapped = lapped - to_fine(
        kept["coarse_pick"][...], kept["fine_back"][...], kept["face"][...], parts, kept
    )
    lapped = lapped - to_coarse(kept["fine_own"][...], parts, kept)
    swapped = pltpu.roll(vector, NODES, 1)
    return kept["mass"][...] * vector + kept["curve"][...] * swapped + placed(lapped)


def side_part(rows, chooser, fine, picks, backs, face, kept):
    parts = split(rows)
    moved = from_faces(dot(chooser, parts).astype(BF16), kept["across"])
    return -moved - to_fine(picks, backs, face, parts, kept) - to_coarse(fine, parts, kept)


def fine_count(back, other, spread):
    weights = jnp.where(other, 1.0, 0.0).astype(BF16)
    times = dot(back, jnp.concatenate([weights] * 4, axis=0))
    return dot_parts(times, spread)


def own_index(index, offset):
    return jnp.where(index < 0, -1, index - offset)


def to_columns(table):
    return table.astype(F32).T.astype(jnp.int32)


def near_kernel(place_ref, pack_ref, *refs):
    names = LOCAL + TABLES
    sources = dict(zip(names, refs))
    refs = refs[len(names) :]
    kept = dict(zip(KEPT + ("partial",), refs))
    refs = refs[len(KEPT) + 1 :]
    local = dict(zip(LOCAL, refs))
    sems = refs[-1]
    targets = [local[name] if name in local else kept[name] for name in names]
    copies = fetch(tuple(zip((sources[name] for name in names), targets)), sems)
    leaves = pack_ref.shape[0] - 8
    offset, first = place_ref[0], place_ref[1]
    table = pack_ref[leaves : leaves + 8, :].astype(jnp.int32) - 1
    columns = to_columns(pack_ref[leaves : leaves + 8, :]) - 1
    slots = table.shape[1]
    face = columns[:, 1:2]
    kept["face"][...] = face
    copies[0].wait()
    neighbours = jnp.concatenate(
        [local["neighbours"][...], jnp.full((2, leaves), -1, jnp.int32)], axis=0
    )
    for name, start in (("own", offset), ("one", offset + first), ("two", offset - first)):
        places = to_columns(own_index(neighbours, start))
        for f in range(FACES):
            kept["oh_" + name][leaves * f : leaves * (f + 1), :] = pick(
                places[:, f : f + 1], (leaves, leaves), 1
            )
        fine = own_index(columns, start)
        for q in range(4):
            kept["fine_" + name][slots * q : slots * (q + 1), :] = pick(
                fine[:, 2 + q : 3 + q], (slots, leaves), 1
            )
    kept["coarse_pick"][...] = pick(columns[:, 0:1] - offset, (slots, leaves), 1)
    coarse_back = pick(table[0:1, :] - offset, (leaves, slots), 0)
    kept["coarse_back"][...] = coarse_back
    fine_rows = own_index(table, offset)
    for q in range(4):
        kept["fine_back"][:, slots * q : slots * (q + 1)] = pick(
            fine_rows[2 + q : 3 + q, :], (leaves, slots), 0
        )
    for copy in copies[1:]:
        copy.wait()
    weights = jnp.where(on_face(face, slots), 1.0, 0.0).astype(BF16)
    kept["coarse_count"][...] = dot(coarse_back, weights)
    diagonal = local["counts"][0:1, :] + fine_count(
        kept["fine_back"][...], on_face(opposite(face), slots), local["spread"][...]
    )
    kept["diagonal"][...] = diagonal
    wide = jnp.concatenate([local["stiffness"][...]] * 2, axis=1)
    wide = jnp.concatenate([wide, wide], axis=0)
    same = (lax.broadcasted_iota(jnp.int32, wide.shape, 0) < NODES) == (
        lax.broadcasted_iota(jnp.int32, wide.shape, 1) < NODES
    )
    wide = split(jnp.where(same, wide, 0.0))
    kept["stiff"][...] = jnp.concatenate([wide, wide], axis=0)
    kept["mass"][...] = jnp.concatenate([local["mass"][...]] * 2, axis=0).T
    curve = local["curve"][...]
    kept["curve"][...] = jnp.concatenate([-curve, jnp.zeros_like(curve)], axis=0).T
    scale = level_rows(local["levels"][...])
    kept["scale"][...] = scale
    rows = pack_ref[0:leaves, :]
    kept["partial"][...] = own_part(rows, rows / scale, diagonal, kept)


def first_side(place_ref, pack_ref, other_ref, partial_ref, diagonal_ref, spread_ref, oh_ref,
               fine_ref, kept, made, direction):
    picks_ref, backs_ref, face_ref, total_ref = made
    leaves = pack_ref.shape[0] - 8
    offset = place_ref[0]
    table = other_ref[leaves : leaves + 8, :]
    columns = to_columns(table) - 1
    table = table.astype(jnp.int32) - 1
    slots = table.shape[1]
    face = columns[:, 1:2]
    picks = pick(columns[:, 0:1] - (offset + direction * place_ref[1]), (slots, leaves), 1)
    index = own_index(table, offset)
    backs = jnp.concatenate(
        [pick(index[2 + q : 3 + q, :], (leaves, slots), 0) for q in range(4)], axis=1
    )
    extra = fine_count(backs, on_face(opposite(face), slots), spread_ref[...])
    picks_ref[...] = picks
    backs_ref[...] = backs
    face_ref[...] = face
    total_ref[...] = diagonal_ref[...] + extra
    lapped = extra * pack_ref[0:leaves, :] + side_part(
        other_ref[0:leaves, :], oh_ref[...], fine_ref[...], picks, backs, face, kept
    )
    return partial_ref[...] + placed(lapped)


def first_one_kernel(*refs):
    kept = dict(zip(KEPT_SIDE, refs[8:]))
    out_ref = refs[8 + len(KEPT_SIDE)]
    out_ref[...] = first_side(*refs[:8], kept, refs[9 + len(KEPT_SIDE) :], 1)


def first_two_kernel(scale_ref, *refs):
    kept = dict(zip(KEPT_SIDE, refs[8:]))
    image_ref, send_ref = refs[8 + len(KEPT_SIDE) : 10 + len(KEPT_SIDE)]
    image = first_side(*refs[:8], kept, refs[10 + len(KEPT_SIDE) :], -1)
    image_ref[...] = image
    send_ref[...] = image * scale_ref[...]


def total(values):
    return jnp.sum(values, keepdims=True)


def unit(values):
    length = jnp.sqrt(total(values * values))
    return length, values * jnp.where(length > 0.0, 1.0 / jnp.where(length > 0.0, length, 1.0), 0.0)


def in_lanes(shape, values):
    lane = lax.broadcasted_iota(jnp.int32, shape, 1)
    row = jnp.zeros(shape, F32)
    for at, value in enumerate(values):
        row = jnp.where(lane == at, value, row)
    return row


def again_kernel(pack_ref, send_ref, image_ref, scale_ref, total_ref, *refs):
    kept = dict(zip(KEPT_OWN, refs))
    partial_ref, zero_ref, one_ref, stats_ref, turned_ref = refs[len(KEPT_OWN) :]
    image = image_ref[...]
    partial_ref[...] = own_part(send_ref[...], image, total_ref[...], kept)
    turned_ref[...] = image.T
    r00, zero = unit(pack_ref[0 : image.shape[0], :] / scale_ref[...])
    r01 = total(zero * image)
    image = image - r01 * zero
    again = total(zero * image)
    r11, one = unit(image - again * zero)
    zero_ref[...] = zero
    one_ref[...] = one
    stats_ref[...] = in_lanes(stats_ref.shape, (r00, r01 + again, r11))


def second_one_kernel(other_ref, partial_ref, oh_ref, fine_ref, picks_ref, backs_ref, face_ref, *refs):
    kept = dict(zip(KEPT_SIDE, refs))
    refs[len(KEPT_SIDE)][...] = partial_ref[...] + placed(
        side_part(
            other_ref[...], oh_ref[...], fine_ref[...], picks_ref[...], backs_ref[...],
            face_ref[...], kept,
        )
    )


def second_two_kernel(
    zero_ref, one_ref, known_ref, other_ref, partial_ref, oh_ref, fine_ref, picks_ref, backs_ref,
    face_ref, *refs
):
    kept = dict(zip(KEPT_SIDE, refs))
    stats_ref = refs[len(KEPT_SIDE)]
    image = partial_ref[...] + placed(
        side_part(
            other_ref[...], oh_ref[...], fine_ref[...], picks_ref[...], backs_ref[...],
            face_ref[...], kept,
        )
    )
    zero, one = zero_ref[...], one_ref[...]
    r02 = total(zero * image)
    r12 = total(one * image)
    rest = image - r02 * zero - r12 * one
    r22 = jnp.sqrt(total(rest * rest))
    stats_ref[...] = known_ref[...] + in_lanes(stats_ref.shape, (0.0, 0.0, 0.0, r02, r12, r22))


def final_kernel(stats_ref, cot_ref, image_ref, out_ref):
    table = stats_ref[...].T
    a0, a1, b1, a2, b2, c2 = [table[at : at + 1, :] for at in range(6)]
    r00_sq = total(a0 * a0)
    r00 = jnp.sqrt(r00_sq)
    f01 = total(a0 * a1) / r00_sq
    f02 = total(a0 * a2) / r00_sq
    a1 = a1 - f01 * a0
    a2 = a2 - f02 * a0
    r11_sq = total(a1 * a1) + total(b1 * b1)
    r11 = jnp.sqrt(r11_sq)
    f12 = (total(a1 * a2) + total(b1 * b2)) / r11_sq
    a2 = a2 - f12 * a1
    b2 = b2 - f12 * b1
    r22 = jnp.sqrt(total(a2 * a2) + total(b2 * b2) + total(c2 * c2))
    rhs_norm = r00
    first_diag = f01
    first_below = r11 / r00
    upper_right = (f02 - first_diag * f01) / first_below
    second_diag = f12 - first_diag
    second_below = r22 / r11
    first_len = jnp.sqrt(first_diag * first_diag + first_below * first_below)
    cos_one = first_diag / first_len
    sin_one = first_below / first_len
    rotated_top = cos_one * upper_right + sin_one * second_diag
    rotated_low = cos_one * second_diag - sin_one * upper_right
    second_len = jnp.sqrt(rotated_low * rotated_low + second_below * second_below)
    cos_two = rotated_low / second_len
    y_two = cos_two * (-sin_one * rhs_norm) / second_len
    y_one = (cos_one * rhs_norm - rotated_top * y_two) / first_len
    on_one = y_two / r11
    on_base = y_one / r00 - on_one * f01
    out_ref[...] = on_base * cot_ref[...] + on_one * image_ref[...]


def on_device(cotangent, nodal_mass, curvature, stiffness, levels, neighbours, mortars):
    fields, nodes, leaves = cotangent.shape
    slots = mortars.shape[1]
    count = lax.axis_size("leaf")
    flat = cotangent.reshape(fields * nodes, leaves)
    levels = levels.reshape(1, leaves)
    me = lax.axis_index("leaf").astype(jnp.int32)
    place = jnp.stack([me * leaves, leaves - 2 * leaves * (me % 2)])
    traces, across, spread, to_fine_table, to_coarse_table, stay, counts = [
        jnp.asarray(table) for table in matrices()
    ]
    vmem = pl.BlockSpec(memory_space=pltpu.VMEM)
    smem = pl.BlockSpec(memory_space=pltpu.SMEM)
    hbm = pl.BlockSpec(memory_space=pltpu.HBM)

    def call(kernel, outs, specs, operands, scratch=(), flops=0, moved=0, mib=40):
        return pl.pallas_call(
            kernel,
            out_shape=outs,
            in_specs=specs,
            out_specs=jax.tree.map(lambda _: vmem, outs),
            scratch_shapes=scratch,
            compiler_params=pltpu.CompilerParams(vmem_limit_bytes=mib * 1024 * 1024),
            cost_estimate=pl.CostEstimate(flops=flops, bytes_accessed=moved, transcendentals=0),
        )(*operands)

    def shape(*dims, dtype=F32):
        return jax.ShapeDtypeStruct(dims, dtype)

    def exchange(values):
        pairs = [(i, i ^ 1) for i in range(count) if i ^ 1 < count]
        across_pairs = [(i, i + 1) for i in range(1, count - 1, 2)]
        across_pairs = across_pairs + [(j, i) for i, j in across_pairs]
        second = lax.ppermute(values, "leaf", across_pairs)
        return lax.ppermute(values, "leaf", pairs), second

    wide = 2 * LANES
    rows = shape(leaves, LANES)
    chooser = shape(FACES * leaves, leaves, dtype=BF16)
    fine = shape(4 * slots, leaves, dtype=BF16)
    kept_shapes = dict(
        oh_own=chooser,
        oh_one=chooser,
        oh_two=chooser,
        coarse_pick=shape(slots, leaves, dtype=BF16),
        fine_own=fine,
        fine_one=fine,
        fine_two=fine,
        fine_back=shape(leaves, 4 * slots, dtype=BF16),
        coarse_back=shape(leaves, slots, dtype=BF16),
        coarse_count=shape(leaves, TRACE),
        diagonal=rows,
        stiff=shape(wide, wide, dtype=BF16),
        mass=rows,
        curve=rows,
        scale=rows,
        face=shape(slots, 1, dtype=jnp.int32),
        traces=shape(*traces.shape, dtype=BF16),
        across=shape(*across.shape, dtype=BF16),
        to_fine=shape(*to_fine_table.shape, dtype=BF16),
        to_coarse=shape(*to_coarse_table.shape, dtype=BF16),
        stay=shape(*stay.shape, dtype=BF16),
        partial=rows,
    )

    def stay_out(*arrays):
        return tuple(pltpu.with_memory_space_constraint(array, pltpu.HBM) for array in arrays)

    pack = call(
        prep_kernel,
        shape(leaves + 8, LANES),
        [hbm] * 3,
        stay_out(flat, levels, mortars),
        scratch=[
            pltpu.VMEM(flat.shape, F32),
            pltpu.VMEM(levels.shape, jnp.int32),
            pltpu.VMEM(mortars.shape, jnp.int32),
            pltpu.SemaphoreType.DMA((3,)),
        ],
    )
    one, two = exchange(pack)
    sources = (neighbours, nodal_mass, curvature, stiffness, levels, spread, counts)
    loaded = sources + (traces, across, to_fine_table, to_coarse_table, stay)
    names = KEPT + ("partial",)
    kept = call(
        near_kernel,
        [kept_shapes[name] for name in names],
        [smem, vmem] + [hbm] * len(loaded),
        (place, pack) + stay_out(*loaded),
        scratch=[pltpu.VMEM(source.shape, source.dtype) for source in sources]
        + [pltpu.SemaphoreType.DMA((len(loaded),))],
        flops=2_000_000_000,
        moved=4_000_000,
    )
    kept = dict(zip(names, kept))
    side = [kept[name] for name in KEPT_SIDE]
    made = [
        shape(slots, leaves, dtype=BF16), shape(leaves, 4 * slots, dtype=BF16),
        shape(slots, 1, dtype=jnp.int32), rows,
    ]
    partial, *made_one = call(
        first_one_kernel,
        [rows] + made,
        [smem] + [vmem] * (7 + len(side)),
        [place, pack, one, kept["partial"], kept["diagonal"], spread, kept["oh_one"],
         kept["fine_one"]] + side,
        flops=1_000_000_000,
        moved=2_000_000,
    )
    image, send, *made_two = call(
        first_two_kernel,
        [rows, rows] + made,
        [vmem, smem] + [vmem] * (7 + len(side)),
        [kept["scale"], place, pack, two, partial, made_one[3], spread, kept["oh_two"],
         kept["fine_two"]] + side,
    )
    one, two = exchange(send)
    own = [kept[name] for name in KEPT_OWN]
    partial, zero, unit_one, known, turned = call(
        again_kernel,
        [rows, rows, rows, shape(1, LANES), shape(LANES, leaves)],
        [vmem] * (5 + len(own)),
        [pack, send, image, kept["scale"], made_two[3]] + own,
        flops=2_000_000_000,
        moved=4_000_000,
    )
    partial = call(
        second_one_kernel,
        rows,
        [vmem] * (7 + len(side)),
        [one, partial, kept["oh_one"], kept["fine_one"], *made_one[:3]] + side,
        flops=1_000_000_000,
        moved=2_000_000,
    )
    stats = call(
        second_two_kernel,
        shape(1, LANES),
        [vmem] * (10 + len(side)),
        [zero, unit_one, known, two, partial, kept["oh_two"], kept["fine_two"], *made_two[:3]]
        + side,
    )
    gathered = lax.all_to_all(
        jnp.broadcast_to(stats, (count, LANES)), "leaf", 0, 0, tiled=True
    )
    out = call(final_kernel, shape(*flat.shape), [vmem] * 3, (gathered, flat, turned))
    return out.reshape(cotangent.shape)


def solution(mesh):
    placed = (
        P(None, None, "leaf"),
        P(None, "leaf"),
        P(None, "leaf"),
        P(),
        P("leaf"),
        P(None, "leaf"),
        P(None, "leaf"),
    )
    return jax.shard_map(
        on_device, mesh=mesh, in_specs=placed, out_specs=P(None, None, "leaf"), check_vma=False
    )
```

time: 57 us -> 56.9 us (level)
  blocking collectives: 31.5 us -> 27.9 us
  Pallas kernels: 16.1 us -> 19.3 us
  starting transfers between devices: 8.34 us -> 9.15 us
  waiting for transfers between devices: 0.61 us -> 0.01 us
    all_to_all x1, blocking collectives: 31.5 us -> 27.9 us  [on_device(): lax.all_to_all(jnp.broadcast_to(stats, (count, LANES)), 'leaf', 0, 0, til...]
    pallas_call x6 -> x8, Pallas kernels: 16.1 us -> 19.3 us  [call(): pl.pallas_call(kernel, out_shape=outs, in_specs=specs, out_specs=jax.tree...]
    ppermute x2, starting transfers between devices: 0.19 us -> 3.42 us  [exchange(): return (lax.ppermute(values, 'leaf', pairs), second)]
    ppermute x2, starting transfers between devices: 8.16 us -> 5.73 us  [exchange(): second = lax.ppermute(values, 'leaf', across_pairs)]
    ppermute x2, waiting for transfers between devices: 0.6 us -> 0.01 us  [exchange(): second = lax.ppermute(values, 'leaf', across_pairs)]
  transfers between devices with their start and end apart: 4 -> 4, of which waited for: 1 -> 0; matrix products, arithmetic and copies ran while one was open for 0% -> 0% of each run, Pallas kernels for 12% -> 21%
where the time goes in v4:
time: 56.9 us; the launch traced here: 56.7 us
  blocking collectives  27.9 us (49%)
  Pallas kernels  19.3 us (34%)
  starting transfers between devices  9.15 us (16%)
    all_to_all x1, blocking collectives, on_device(): lax.all_to_all(jnp.broadcast_to(stats, (count, LANES)), 'leaf', 0, 0, til...  27.9 us
    pallas_call x8, Pallas kernels, call(): pl.pallas_call(kernel, out_shape=outs, in_specs=specs, out_specs=jax.tree...  19.3 us
    ppermute x2, starting transfers between devices, exchange(): second = lax.ppermute(values, 'leaf', across_pairs)  5.73 us
    ppermute x2, starting transfers between devices, exchange(): return (lax.ppermute(values, 'leaf', pairs), second)  3.42 us
  transfers between devices with their start and end apart: 4, of which 0 were waited for; matrix products, arithmetic and copies ran while one was open for 0% of the time, Pallas kernels for 21%

profile of v4, /device:TPU:1, one launch (start us, length us, event | category | flops | bytes accessed | tf_op | source)
XLA Modules:
  0.0 56.7 jit_solution(16800457969412941162)
XLA Ops:
  0.0 1.0 %shard_map.136.pack_ref.refs_1_ = f32[264,128]{1,0:T(8,128)S(1)} custom-call(f32[128,256]{1,0:T(8,128)} %bitcast.7, s32[1,256]{1,0:T(1,128)} %bitcast.11, s32[6,128]{1,0:T(8,128)} %mortars_hbm.1), custom_call_target="tpu_custom_call" | custom-call | tf_op jit(solution)/shard_map/pallas_call | solution.py:457
  1.0 3.3 %collective-permute-start.1 = (f32[264,128]{1,0:T(8,128)S(1)}, f32[264,128]{1,0:T(8,128)S(1)}, u32[]{:S(2)}, u32[]{:S(2)}) collective-permute-start(f32[264,128]{1,0:T(8,128)S(1)} %shard_map.136.pack_ref.refs_1_), channel_id=1, source_target_pairs={{0,1},{1,0},{2,3},{3,2},{4,5},{5,4},{6,7},{7,6},{8,9},{9,8},{10,11... | collective-permute-start | bytes 405512 | tf_op jit(solution)/shard_map/ppermute | solution.py:475
  4.4 1.9 %collective-permute-start = (f32[264,128]{1,0:T(8,128)S(1)}, f32[264,128]{1,0:T(8,128)S(1)}, u32[]{:S(2)}, u32[]{:S(2)}) collective-permute-start(f32[264,128]{1,0:T(8,128)S(1)} %shard_map.136.pack_ref.refs_1_), channel_id=1, source_target_pairs={{1,2},{3,4},{5,6},{7,8},{9,10},{11,12},{13,14},{15,16},{17,18},{19... | collective-permute-start | bytes 405512 | tf_op jit(solution)/shard_map/ppermute | solution.py:474
  6.3 0.1 pad_add_fusion.place_ref.refs_0_
  6.4 0.0 copy-start.1
  6.4 4.7 %shard_map.137 = (bf16[1536,256]{1,0:T(8,128)(2,1)S(1)}, bf16[1536,256]{1,0:T(8,128)(2,1)S(1)}, bf16[1536,256]{1,0:T(8,128)(2,1)S(1)}, bf16[128,256]{1,0:T(8,128...) custom-call(s32[2]{0:T(128)S(1)} %pad_add_fusion.place_ref.refs_0_, ...), custom_call_target="tpu_custom_call" | custom-call | flops 2000000000 | bytes 4000000 | tf_op jit(solution)/shard_map/pallas_call | solution.py:457
  11.0 0.0 collective-permute-done.1.refs_2_
  11.1 0.0 copy-done.1
  11.1 2.9 %shard_map.138 = (f32[256,128]{1,0:T(8,128)S(1)}, bf16[128,256]{1,0:T(8,128)(2,1)S(1)}, bf16[256,512]{1,0:T(8,128)(2,1)S(1)}, s32[128,1]{1,0:T(8,128)S(1)}, f32[256,128]{1,0:T(8,128)S(1)}) custom-call(s32[2]{0:T(128)S(1)} %pad_add_fusion.place_ref.refs_0_, f32[264,128]{1,0:T(8,128)S(1)} %shard_map.136.pack_ref.refs_1_, ...), custom_call_target="tpu_custom_call" | custom-call | flops 1000000000 | bytes 2000000 | tf_op jit(solution)/shard_map/pallas_call | solution.py:457
  14.0 0.0 collective-permute-done.refs_2_
  14.0 3.0 %shard_map.139 = (f32[256,128]{1,0:T(8,128)S(1)}, f32[256,128]{1,0:T(8,128)S(1)}, bf16[128,256]{1,0:T(8,128)(2,1)S(1)}, bf16[256,512]{1,0:T(8,128)(2,1)S(1)}, s3...) custom-call(f32[256,128]{1,0:T(8,128)S(1)} %get-tuple-element.43.scale_ref, s32[2]{0:T(128)S(1)} %pad_add_fusion.place_ref.refs_0_, ...), custom_call_target="tpu_custom_call" | custom-call | tf_op jit(solution)/shard_map/pallas_call | solution.py:457
  17.0 0.1 collective-permute-start.3
  17.1 3.8 %collective-permute-start.2 = (f32[256,128]{1,0:T(8,128)S(1)}, f32[256,128]{1,0:T(8,128)S(1)}, u32[]{:S(2)}, u32[]{:S(2)}) collective-permute-start(f32[256,128]{1,0:T(8,128)S(1)} %get-tuple-element.58.send_ref), channel_id=1, source_target_pairs={{1,2},{3,4},{5,6},{7,8},{9,10},{11,12},{13,14},{15,16},{17,18},{19... | collective-permute-start | bytes 393224 | tf_op jit(solution)/shard_map/ppermute | solution.py:474
  20.9 2.1 %shard_map.140 = (f32[256,128]{1,0:T(8,128)S(1)}, f32[256,128]{1,0:T(8,128)S(1)}, f32[256,128]{1,0:T(8,128)S(1)}, f32[1,128]{1,0:T(1,128)S(1)}, f32[128,256]{1,0:T(8,128)S(1)}) custom-call(f32[264,128]{1,0:T(8,128)S(1)} %shard_map.136.pack_ref.refs_1_, f32[256,128]{1,0:T(8,128)S(1)} %get-tuple-element.58.send_ref, ...), custom_call_target="tpu_custom_call" | custom-call | flops 2000000000 | bytes 4000000 | tf_op jit(solution)/shard_map/pallas_call | solution.py:457
  23.0 0.0 collective-permute-done.3.other_ref
  23.0 2.1 %shard_map.141.partial_ref = f32[256,128]{1,0:T(8,128)S(1)} custom-call(f32[256,128]{1,0:T(8,128)S(1)} %collective-permute-done.3.other_ref, f32[256,128]{1,0:T(8,128)S(1)} %get-tuple-element.73.partial_ref, bf16[1536,256]{1,0:T(8,128)(2,1)S(1)} %get-tuple-element.46.refs_6_.oh_ref, bf16[512,256]{1,0:T(8,128)(2,1)S(1)} %get-tuple-element.47.refs_7_.fine_ref, ...), custom_call_target="tpu_custom_call" | custom-call | flops 1000000000 | bytes 2000000 | tf_op jit(solution)/shard_map/pallas_call | solution.py:457
  25.1 0.0 collective-permute-done.2.other_ref
  25.1 2.4 %shard_map.142 = f32[1,128]{1,0:T(1,128)S(1)} custom-call(f32[256,128]{1,0:T(8,128)S(1)} %get-tuple-element.70.zero_ref, f32[256,128]{1,0:T(8,128)S(1)} %get-tuple-element.71.one_ref, f32[1,128]{1,0:T(1,128)S(1)} %get-tuple-element.72.known_ref, f32[256,128]{1,0:T(8,128)S(1)} %collective-permute-done.2.other_ref, f32[256,128]{1,0:T(8,128)S(1)} %shard_map.141.partial_ref, ...), custom_call_target="tpu_custom_call" | custom-call | tf_op jit(solution)/shard_map/pallas_call | solution.py:457
  27.6 0.1 broadcast_in_dim.2
  27.6 0.0 copy-start
  27.6 27.9 %all_to_all.8 = f32[256,1,128]{2,1,0:T(1,128)S(1)} all-to-all(f32[256,1,128]{2,1,0:T(1,128)S(1)} %broadcast_in_dim.2), channel_id=1, replica_groups=mesh['leaf'=256] {'leaf'}, dimensions={0} | all-to-all | bytes 262144 | tf_op jit(solution)/shard_map/all_to_all | solution.py:582
  55.6 0.0 copy-done
  55.6 1.2 %shard_map.143 = f32[128,256]{1,0:T(8,128)} custom-call(f32[256,128]{1,0:T(8,128)S(1)} %bitcast.9, f32[128,256]{1,0:T(8,128)S(1)} %bitcast.8, f32[128,256]{1,0:T(8,128)S(1)} %get-tuple-element.80.image_ref), custom_call_target="tpu_custom_call" | custom-call | tf_op jit(solution)/shard_map/pallas_call | solution.py:457
Async XLA Ops:
  1.0 10.0 %collective-permute-start.1 = (f32[264,128]{1,0:T(8,128)S(1)}, f32[264,128]{1,0:T(8,128)S(1)}, u32[]{:S(2)}, u32[]{:S(2)}) collective-permute-start(f32[264,128]{1,0:T(8,128)S(1)} %shard_map.136.pack_ref.refs_1_), channel_id=1, source_target_pairs={{0,1},{1,0},{2,3},{3,2},{4,5},{5,4},{6,7},{7,6},{8,9},{9,8},{10,11... | collective-permute-start | bytes 405512 | tf_op jit(solution)/shard_map/ppermute | solution.py:475
  4.4 9.6 %collective-permute-start = (f32[264,128]{1,0:T(8,128)S(1)}, f32[264,128]{1,0:T(8,128)S(1)}, u32[]{:S(2)}, u32[]{:S(2)}) collective-permute-start(f32[264,128]{1,0:T(8,128)S(1)} %shard_map.136.pack_ref.refs_1_), channel_id=1, source_target_pairs={{1,2},{3,4},{5,6},{7,8},{9,10},{11,12},{13,14},{15,16},{17,18},{19... | collective-permute-start | bytes 405512 | tf_op jit(solution)/shard_map/ppermute | solution.py:474
  6.4 4.7 %copy-start.1 = (bf16[256,128]{1,0:T(8,128)(2,1)S(1)}, bf16[256,128]{1,0:T(8,128)(2,1)}, u32[]{:S(2)}) copy-start(bf16[256,128]{1,0:T(8,128)(2,1)} %constant.37.clone.refs_5_) | copy-start | bytes 196612
  17.0 6.0 %collective-permute-start.3 = (f32[256,128]{1,0:T(8,128)S(1)}, f32[256,128]{1,0:T(8,128)S(1)}, u32[]{:S(2)}, u32[]{:S(2)}) collective-permute-start(f32[256,128]{1,0:T(8,128)S(1)} %get-tuple-element.58.send_ref), channel_id=1, source_target_pairs={{0,1},{1,0},{2,3},{3,2},{4,5},{5,4},{6,7},{7,6},{8,9},{9,8},{10,11... | collective-permute-start | bytes 393224 | tf_op jit(solution)/shard_map/ppermute | solution.py:475
  17.1 8.0 %collective-permute-start.2 = (f32[256,128]{1,0:T(8,128)S(1)}, f32[256,128]{1,0:T(8,128)S(1)}, u32[]{:S(2)}, u32[]{:S(2)}) collective-permute-start(f32[256,128]{1,0:T(8,128)S(1)} %get-tuple-element.58.send_ref), channel_id=1, source_target_pairs={{1,2},{3,4},{5,6},{7,8},{9,10},{11,12},{13,14},{15,16},{17,18},{19... | collective-permute-start | bytes 393224 | tf_op jit(solution)/shard_map/ppermute | solution.py:474
  27.6 27.9 %copy-start = (f32[2,64,256]{2,1,0:T(8,128)S(1)}, f32[2,64,256]{2,1,0:T(8,128)}, u32[]{:S(2)}) copy-start(f32[2,64,256]{2,1,0:T(8,128)} %param.14) | copy-start | bytes 393220

commit v5 on v4

v5 whole, which is shorter than its diff:
```python
import jax
import jax.numpy as jnp
import ml_dtypes
import numpy as np
from jax import lax
from jax.experimental import pallas as pl
from jax.experimental.pallas import tpu as pltpu
from jax.sharding import PartitionSpec as P

TAU_WEIGHT = 0.15
EPS_WEIGHT = 0.1
FACES = 6
NODES = 64
LANES = 128
TRACE = 256
F32 = jnp.float32
BF16 = jnp.bfloat16


def face_tables():
    node_at = np.zeros((6, 16), dtype=np.int64)
    for face_id in range(6):
        for row_pos in range(4):
            for col_pos in range(4):
                coords = [row_pos, col_pos]
                coords.insert(face_id // 2, 3 * (face_id % 2))
                node_at[face_id, 4 * row_pos + col_pos] = (
                    16 * coords[0] + 4 * coords[1] + coords[2]
                )
    points = np.array([-1.0, -1.0 / np.sqrt(5.0), 1.0 / np.sqrt(5.0), 1.0])
    halves = np.zeros((2, 4, 4))
    for half_id in range(2):
        target = (points + 2.0 * half_id - 1.0) / 2.0
        for column in range(4):
            lagrange = np.ones(4)
            for other_id in range(4):
                if other_id != column:
                    lagrange = (
                        lagrange * (target - points[other_id]) / (points[column] - points[other_id])
                    )
            halves[half_id, :, column] = lagrange
    mortar = np.stack([np.kron(halves[quarter // 2], halves[quarter % 2]) for quarter in range(4)])
    return node_at, mortar


def two_parts(table):
    high = table.astype(np.float32).astype(ml_dtypes.bfloat16)
    low = (table - high.astype(np.float64)).astype(np.float32).astype(ml_dtypes.bfloat16)
    return np.concatenate([high, low], axis=-1)


def matrices():
    node_at, mortar = face_tables()
    traces = np.zeros((2 * LANES, TRACE))
    across = np.zeros((FACES, 2 * LANES, LANES))
    to_fine = np.zeros((4, TRACE, LANES))
    to_coarse = np.zeros((4, TRACE, LANES))
    stay = np.zeros((TRACE, LANES))
    square = sum(mortar[quarter].T @ mortar[quarter] for quarter in range(4))
    for face in range(FACES):
        other = face ^ 1
        for field in range(2):
            base = 32 * face + 16 * field
            lifted = 32 * other + 16 * field
            nodes = 64 * field + node_at[face]
            facing = 64 * field + node_at[other]
            for place in range(16):
                for part in range(2):
                    traces[part * LANES + nodes[place], base + place] = 1.0
                    across[face, part * LANES + facing[place], nodes[place]] = 1.0
                stay[base + place, nodes] = square[:, place]
                for quarter in range(4):
                    to_fine[quarter, base + place, facing] = mortar[quarter][:, place]
                    to_coarse[quarter, lifted + place, nodes] = mortar[quarter][place, :]
    small = ml_dtypes.bfloat16
    pairs = [np.concatenate([across[f], across[f + 1]], axis=1) for f in (0, 2, 4)]
    return np.concatenate(
        [traces.astype(small)]
        + [pair.astype(small) for pair in pairs]
        + list(two_parts(to_fine))
        + list(two_parts(to_coarse))
        + [two_parts(stay)],
        axis=0,
    )


TRACES_AT, ACROSS_AT, FINE_AT, COARSE_AT, STAY_AT = 0, 256, 1024, 2048, 3072


def split(values, axis=1):
    high = values.astype(BF16)
    return jnp.concatenate([high, (values - high.astype(F32)).astype(BF16)], axis=axis)


def dot(left, right):
    return jnp.dot(left, right, preferred_element_type=F32)


def fold(values):
    return values[:, :LANES] + values[:, LANES:]


def dot_parts(values, table):
    products = dot(split(values, 0), table)
    return products[: values.shape[0], :] + products[values.shape[0] :, :]


def pick(index, shape, dim):
    places = lax.broadcasted_iota(jnp.int32, shape, dim).astype(F32).astype(BF16)
    index = jnp.broadcast_to(index.astype(F32), shape).astype(BF16)
    return jnp.where(index == places, jnp.ones(shape, BF16), jnp.zeros(shape, BF16))


def on_face(face, slots):
    return lax.broadcasted_iota(jnp.int32, (slots, TRACE), 1) // 32 == face


def face_nodes(face, shape):
    node = lax.broadcasted_iota(jnp.int32, shape, 1) % NODES
    place = jnp.right_shift(node, 4 - 2 * (face // 2)) & 3
    return (place == 3 * (face % 2)) & (face >= 0)


def opposite(face):
    return jnp.where(face >= 0, face ^ 1, -1)


def level_rows(levels):
    scale = jnp.left_shift(jnp.ones_like(levels), levels).astype(F32)
    return jnp.broadcast_to(scale, (LANES, levels.shape[1])).T


def fetch(pairs, sems):
    copies = [
        pltpu.make_async_copy(source, target, sems.at[at])
        for at, (source, target) in enumerate(pairs)
    ]
    for copy in copies:
        copy.start()
    return copies


def prep_kernel(cot_hbm, levels_hbm, mortars_hbm, pack_ref, cot_ref, levels_ref, mortars_ref, sems):
    for copy in fetch(
        ((cot_hbm, cot_ref), (levels_hbm, levels_ref), (mortars_hbm, mortars_ref)), sems
    ):
        copy.wait()
    leaves = cot_ref.shape[1]
    scale = jnp.left_shift(jnp.ones_like(levels_ref[...]), levels_ref[...]).astype(F32)
    pack_ref[0:leaves, :] = (cot_ref[...] * scale).T
    table = mortars_ref[...].astype(F32) + 1.0
    pack_ref[leaves : leaves + 8, :] = jnp.concatenate(
        [table, jnp.zeros((2, table.shape[1]), F32)], axis=0
    )


LOCAL = ("neighbours", "mass", "curve", "stiffness", "levels")
KEPT = (
    "own", "one", "two", "own_back", "coarse_count", "diagonal", "stiff", "mass", "curve", "scale",
    "face",
)
KEPT_SIDE = ("own_back", "face")
KEPT_OWN = KEPT_SIDE + ("own", "coarse_count", "stiff", "mass", "curve")


def from_rows(parts, chooser, picks, backs, coarse_face, kept, table):
    own_back, face = kept["own_back"], kept["face"]
    slots, leaves = own_back.shape[1], own_back.shape[0]
    chosen = dot(jnp.concatenate([chooser, picks], axis=0), parts).astype(BF16)
    moved = jnp.zeros((leaves, LANES), F32)
    for f in range(FACES):
        start = ACROSS_AT + 256 * (f // 2)
        moved = moved + dot(
            chosen[leaves * f : leaves * (f + 1), :],
            table[start : start + 256, LANES * (f % 2) : LANES * (f % 2 + 1)],
        )
    trace = dot(chosen[leaves * FACES :, :], table[TRACES_AT : TRACES_AT + 256, :])
    coarse = jnp.where(on_face(coarse_face, slots), trace[4 * slots :, :], 0.0)
    sent = [
        split(fold(dot_parts(coarse, table[FINE_AT + 256 * q : FINE_AT + 256 * (q + 1), :])))
        for q in range(4)
    ]
    other = on_face(opposite(face[...]), slots)
    fine = jnp.concatenate(
        [jnp.where(other, trace[slots * q : slots * (q + 1), :], 0.0) for q in range(4)], axis=1
    )
    sent.append(split(fold(dot_parts(fine, table[COARSE_AT : COARSE_AT + 1024, :]))))
    backs = jnp.concatenate([backs, own_back[...]], axis=1)
    return moved + fold(dot(backs, jnp.concatenate(sent, axis=0)))


def placed(lapped):
    first = lax.broadcasted_iota(jnp.int32, lapped.shape, 1) < NODES
    return jnp.where(first, -EPS_WEIGHT, TAU_WEIGHT) * pltpu.roll(lapped, NODES, 1)


def own_part(rows, vector, diagonal, backs, kept, table):
    parts = split(rows)
    slots = kept["own_back"].shape[1]
    above = kept["own"].shape[0] - slots
    here = dot(parts, table[TRACES_AT : TRACES_AT + 256, :]) * kept["coarse_count"][...]
    lapped = (
        diagonal * rows
        + fold(dot(parts, kept["stiff"][...]))
        + fold(dot_parts(here, table[STAY_AT : STAY_AT + 256, :]))
        - from_rows(
            parts, kept["own"][:above, :], kept["own"][above:, :], backs, kept["face"][...], kept,
            table,
        )
    )
    swapped = pltpu.roll(vector, NODES, 1)
    return kept["mass"][...] * vector + kept["curve"][...] * swapped + placed(lapped)


def fine_count(back, face):
    weights = jnp.where(
        face_nodes(opposite(face), (face.shape[0], LANES)), 1.0, 0.0
    ).astype(BF16)
    return dot(back, jnp.concatenate([weights] * 4, axis=0))


def own_index(index, offset):
    return jnp.where(index < 0, -1, index - offset)


def to_columns(table):
    return table.astype(F32).T.astype(jnp.int32)


def fine_backs(table, offset, leaves):
    index = own_index(table, offset)
    return jnp.concatenate(
        [pick(index[2 + q : 3 + q, :], (leaves, table.shape[1]), 0) for q in range(4)], axis=1
    )


def near_kernel(place_ref, pack_ref, table, *refs):
    sources = refs[: len(LOCAL)]
    refs = refs[len(LOCAL) :]
    kept = dict(zip(KEPT + ("fine_back", "partial"), refs))
    refs = refs[len(KEPT) + 2 :]
    local = dict(zip(LOCAL, refs))
    copies = fetch(tuple(zip(sources, refs)), refs[-1])
    leaves = pack_ref.shape[0] - 8
    offset, first = place_ref[0], place_ref[1]
    mortars = pack_ref[leaves : leaves + 8, :].astype(jnp.int32) - 1
    columns = to_columns(pack_ref[leaves : leaves + 8, :]) - 1
    slots = mortars.shape[1]
    face = columns[:, 1:2]
    kept["face"][...] = face
    backs = fine_backs(mortars, offset, leaves)
    kept["fine_back"][...] = backs
    own_back = pick(mortars[0:1, :] - offset, (leaves, slots), 0)
    kept["own_back"][...] = own_back
    copies[0].wait()
    neighbours = jnp.concatenate(
        [local["neighbours"][...], jnp.full((2, leaves), -1, jnp.int32)], axis=0
    )
    for name, start in (("own", offset), ("one", offset + first), ("two", offset - first)):
        places = to_columns(own_index(neighbours, start))
        for f in range(FACES):
            kept[name][leaves * f : leaves * (f + 1), :] = pick(
                places[:, f : f + 1], (leaves, leaves), 1
            )
        fine = own_index(columns, start)
        for q in range(4):
            at = leaves * FACES + slots * q
            kept[name][at : at + slots, :] = pick(fine[:, 2 + q : 3 + q], (slots, leaves), 1)
    at = leaves * FACES + slots * 4
    kept["own"][at : at + slots, :] = pick(columns[:, 0:1] - offset, (slots, leaves), 1)
    weights = jnp.where(on_face(face, slots), 1.0, 0.0).astype(BF16)
    kept["coarse_count"][...] = dot(own_back, weights)
    diagonal = fine_count(backs, face)
    for f in range(FACES):
        diagonal = diagonal + jnp.where(face_nodes(jnp.int32(f), diagonal.shape), 1.0, 0.0)
    kept["diagonal"][...] = diagonal
    for copy in copies[1:]:
        copy.wait()
    wide = jnp.concatenate([local["stiffness"][...]] * 2, axis=1)
    wide = jnp.concatenate([wide, wide], axis=0)
    same = (lax.broadcasted_iota(jnp.int32, wide.shape, 0) < NODES) == (
        lax.broadcasted_iota(jnp.int32, wide.shape, 1) < NODES
    )
    wide = split(jnp.where(same, wide, 0.0))
    kept["stiff"][...] = jnp.concatenate([wide, wide], axis=0)
    kept["mass"][...] = jnp.concatenate([local["mass"][...]] * 2, axis=0).T
    curve = local["curve"][...]
    kept["curve"][...] = jnp.concatenate([-curve, jnp.zeros_like(curve)], axis=0).T
    scale = level_rows(local["levels"][...])
    kept["scale"][...] = scale
    rows = pack_ref[0:leaves, :]
    kept["partial"][...] = own_part(rows, rows / scale, diagonal, backs, kept, table)


def first_side(
    place_ref, table, pack_ref, other_ref, partial_ref, diagonal_ref, chooser_ref, kept, made,
    direction,
):
    picks_ref, backs_ref, face_ref, total_ref = made
    leaves = pack_ref.shape[0] - 8
    mortars = other_ref[leaves : leaves + 8, :]
    columns = to_columns(mortars) - 1
    mortars = mortars.astype(jnp.int32) - 1
    slots = mortars.shape[1]
    face = columns[:, 1:2]
    start = place_ref[0] + direction * place_ref[1]
    picks = pick(columns[:, 0:1] - start, (slots, leaves), 1)
    backs = fine_backs(mortars, place_ref[0], leaves)
    extra = fine_count(backs, face)
    picks_ref[...] = picks
    backs_ref[...] = backs
    face_ref[...] = face
    total_ref[...] = diagonal_ref[...] + extra
    lapped = extra * pack_ref[0:leaves, :] - from_rows(
        split(other_ref[0:leaves, :]), chooser_ref[...], picks, backs, face, kept, table
    )
    return partial_ref[...] + placed(lapped)


def first_one_kernel(*refs):
    kept = dict(zip(KEPT_SIDE, refs[7:]))
    refs, rest = refs[:7], refs[7 + len(KEPT_SIDE) :]
    rest[0][...] = first_side(*refs, kept, rest[1:], 1)


def first_two_kernel(scale_ref, *refs):
    kept = dict(zip(KEPT_SIDE, refs[7:]))
    refs, rest = refs[:7], refs[7 + len(KEPT_SIDE) :]
    image = first_side(*refs, kept, rest[2:], -1)
    rest[0][...] = image
    rest[1][...] = image * scale_ref[...]


def total(values):
    return jnp.sum(values, keepdims=True)


def unit(values):
    length = jnp.sqrt(total(values * values))
    return length, values * jnp.where(length > 0.0, 1.0 / jnp.where(length > 0.0, length, 1.0), 0.0)


def in_lanes(shape, values):
    lane = lax.broadcasted_iota(jnp.int32, shape, 1)
    row = jnp.zeros(shape, F32)
    for at, value in enumerate(values):
        row = jnp.where(lane == at, value, row)
    return row


def again_kernel(
    table, pack_ref, send_ref, image_ref, scale_ref, total_ref, fine_back_ref, *refs
):
    kept = dict(zip(KEPT_OWN, refs))
    partial_ref, zero_ref, one_ref, stats_ref, turned_ref = refs[len(KEPT_OWN) :]
    image = image_ref[...]
    partial_ref[...] = own_part(
        send_ref[...], image, total_ref[...], fine_back_ref[...], kept, table
    )
    turned_ref[...] = image.T
    r00, zero = unit(pack_ref[0 : image.shape[0], :] / scale_ref[...])
    r01 = total(zero * image)
    image = image - r01 * zero
    again = total(zero * image)
    r11, one = unit(image - again * zero)
    zero_ref[...] = zero
    one_ref[...] = one
    stats_ref[...] = in_lanes(stats_ref.shape, (r00, r01 + again, r11))


def second_side(table, other_ref, partial_ref, chooser_ref, picks_ref, backs_ref, face_ref, kept):
    lapped = from_rows(
        split(other_ref[...]), chooser_ref[...], picks_ref[...], backs_ref[...], face_ref[...],
        kept, table,
    )
    return partial_ref[...] - placed(lapped)


def second_one_kernel(*refs):
    refs, rest = refs[:7], refs[7:]
    rest[len(KEPT_SIDE)][...] = second_side(*refs, dict(zip(KEPT_SIDE, rest)))


def second_two_kernel(zero_ref, one_ref, known_ref, *refs):
    refs, rest = refs[:7], refs[7:]
    stats_ref = rest[len(KEPT_SIDE)]
    image = second_side(*refs, dict(zip(KEPT_SIDE, rest)))
    zero, one = zero_ref[...], one_ref[...]
    r02 = total(zero * image)
    r12 = total(one * image)
    rest = image - r02 * zero - r12 * one
    r22 = jnp.sqrt(total(rest * rest))
    stats_ref[...] = known_ref[...] + in_lanes(stats_ref.shape, (0.0, 0.0, 0.0, r02, r12, r22))


def final_kernel(stats_ref, cot_ref, image_ref, out_ref):
    table = stats_ref[...].T
    a0, a1, b1, a2, b2, c2 = [table[at : at + 1, :] for at in range(6)]
    r00_sq = total(a0 * a0)
    r00 = jnp.sqrt(r00_sq)
    f01 = total(a0 * a1) / r00_sq
    f02 = total(a0 * a2) / r00_sq
    a1 = a1 - f01 * a0
    a2 = a2 - f02 * a0
    r11_sq = total(a1 * a1) + total(b1 * b1)
    r11 = jnp.sqrt(r11_sq)
    f12 = (total(a1 * a2) + total(b1 * b2)) / r11_sq
    a2 = a2 - f12 * a1
    b2 = b2 - f12 * b1
    r22 = jnp.sqrt(total(a2 * a2) + total(b2 * b2) + total(c2 * c2))
    rhs_norm = r00
    first_diag = f01
    first_below = r11 / r00
    upper_right = (f02 - first_diag * f01) / first_below
    second_diag = f12 - first_diag
    second_below = r22 / r11
    first_len = jnp.sqrt(first_diag * first_diag + first_below * first_below)
    cos_one = first_diag / first_len
    sin_one = first_below / first_len
    rotated_top = cos_one * upper_right + sin_one * second_diag
    rotated_low = cos_one * second_diag - sin_one * upper_right
    second_len = jnp.sqrt(rotated_low * rotated_low + second_below * second_below)
    cos_two = rotated_low / second_len
    y_two = cos_two * (-sin_one * rhs_norm) / second_len
    y_one = (cos_one * rhs_norm - rotated_top * y_two) / first_len
    on_one = y_two / r11
    on_base = y_one / r00 - on_one * f01
    out_ref[...] = on_base * cot_ref[...] + on_one * image_ref[...]


def on_device(cotangent, nodal_mass, curvature, stiffness, levels, neighbours, mortars):
    fields, nodes, leaves = cotangent.shape
    slots = mortars.shape[1]
    count = lax.axis_size("leaf")
    flat = cotangent.reshape(fields * nodes, leaves)
    levels = levels.reshape(1, leaves)
    me = lax.axis_index("leaf").astype(jnp.int32)
    place = jnp.stack([me * leaves, leaves - 2 * leaves * (me % 2)])
    table = jnp.asarray(matrices())
    vmem = pl.BlockSpec(memory_space=pltpu.VMEM)
    smem = pl.BlockSpec(memory_space=pltpu.SMEM)
    hbm = pl.BlockSpec(memory_space=pltpu.HBM)

    def call(kernel, outs, specs, operands, scratch=(), flops=0, moved=0, mib=40):
        return pl.pallas_call(
            kernel,
            out_shape=outs,
            in_specs=specs,
            out_specs=jax.tree.map(lambda _: vmem, outs),
            scratch_shapes=scratch,
            compiler_params=pltpu.CompilerParams(vmem_limit_bytes=mib * 1024 * 1024),
            cost_estimate=pl.CostEstimate(flops=flops, bytes_accessed=moved, transcendentals=0),
        )(*operands)

    def shape(*dims, dtype=F32):
        return jax.ShapeDtypeStruct(dims, dtype)

    def exchange(values):
        pairs = [(i, i ^ 1) for i in range(count) if i ^ 1 < count]
        across_pairs = [(i, i + 1) for i in range(1, count - 1, 2)]
        across_pairs = across_pairs + [(j, i) for i, j in across_pairs]
        second = lax.ppermute(values, "leaf", across_pairs)
        return lax.ppermute(values, "leaf", pairs), second

    wide = 2 * LANES
    rows = shape(leaves, LANES)
    chosen = FACES * leaves + 4 * slots
    picks = shape(slots, leaves, dtype=BF16)
    backs = shape(leaves, 4 * slots, dtype=BF16)
    face = shape(slots, 1, dtype=jnp.int32)
    kept_shapes = dict(
        own=shape(chosen + slots, leaves, dtype=BF16),
        one=shape(chosen, leaves, dtype=BF16),
        two=shape(chosen, leaves, dtype=BF16),
        own_back=shape(leaves, slots, dtype=BF16),
        coarse_count=shape(leaves, TRACE),
        diagonal=rows,
        stiff=shape(wide, wide, dtype=BF16),
        mass=rows,
        curve=rows,
        scale=rows,
        face=face,
        fine_back=backs,
        partial=rows,
    )

    def stay_out(*arrays):
        return tuple(pltpu.with_memory_space_constraint(array, pltpu.HBM) for array in arrays)

    pack = call(
        prep_kernel,
        shape(leaves + 8, LANES),
        [hbm] * 3,
        stay_out(flat, levels, mortars),
        scratch=[
            pltpu.VMEM(flat.shape, F32),
            pltpu.VMEM(levels.shape, jnp.int32),
            pltpu.VMEM(mortars.shape, jnp.int32),
            pltpu.SemaphoreType.DMA((3,)),
        ],
        flops=10_000_000_000,
        moved=4_000_000,
    )
    one, two = exchange(pack)
    sources = (neighbours, nodal_mass, curvature, stiffness, levels)
    names = KEPT + ("fine_back", "partial")
    kept = call(
        near_kernel,
        [kept_shapes[name] for name in names],
        [smem, vmem, vmem] + [hbm] * len(sources),
        (place, pack, table) + stay_out(*sources),
        scratch=[pltpu.VMEM(source.shape, source.dtype) for source in sources]
        + [pltpu.SemaphoreType.DMA((len(sources),))],
        flops=2_000_000_000,
        moved=4_000_000,
    )
    kept = dict(zip(names, kept))
    side = [kept[name] for name in KEPT_SIDE]
    made = [picks, backs, face, rows]
    partial, *made_one = call(
        first_one_kernel,
        [rows] + made,
        [smem] + [vmem] * (6 + len(side)),
        [place, table, pack, one, kept["partial"], kept["diagonal"], kept["one"]] + side,
        flops=1_000_000_000,
        moved=2_000_000,
    )
    image, send, *made_two = call(
        first_two_kernel,
        [rows, rows] + made,
        [vmem, smem] + [vmem] * (6 + len(side)),
        [kept["scale"], place, table, pack, two, partial, made_one[3], kept["two"]] + side,
    )
    one, two = exchange(send)
    own = [kept[name] for name in KEPT_OWN]
    partial, zero, unit_one, known, turned = call(
        again_kernel,
        [rows, rows, rows, shape(1, LANES), shape(LANES, leaves)],
        [vmem] * (7 + len(own)),
        [table, pack, send, image, kept["scale"], made_two[3], kept["fine_back"]] + own,
        flops=2_000_000_000,
        moved=4_000_000,
    )
    partial = call(
        second_one_kernel,
        rows,
        [vmem] * (7 + len(side)),
        [table, one, partial, kept["one"], *made_one[:3]] + side,
        flops=1_000_000_000,
        moved=2_000_000,
    )
    stats = call(
        second_two_kernel,
        shape(1, LANES),
        [vmem] * (10 + len(side)),
        [zero, unit_one, known, table, two, partial, kept["two"], *made_two[:3]] + side,
    )
    gathered = lax.all_to_all(
        jnp.broadcast_to(stats, (count, LANES)), "leaf", 0, 0, tiled=True
    )
    out = call(final_kernel, shape(*flat.shape), [vmem] * 3, (gathered, flat, turned))
    return out.reshape(cotangent.shape)


def solution(mesh):
    placed = (
        P(None, None, "leaf"),
        P(None, "leaf"),
        P(None, "leaf"),
        P(),
        P("leaf"),
        P(None, "leaf"),
        P(None, "leaf"),
    )
    return jax.shard_map(
        on_device, mesh=mesh, in_specs=placed, out_specs=P(None, None, "leaf"), check_vma=False
    )
```

time: 56.9 us -> 55.2 us (0.970)
  Pallas kernels: 19.3 us -> 17 us
  blocking collectives: 27.9 us -> 28.8 us
    pallas_call x8, Pallas kernels: 19.3 us -> 17 us  [call(): pl.pallas_call(kernel, out_shape=outs, in_specs=specs, out_specs=jax.tree...]
    all_to_all x1, blocking collectives: 27.9 us -> 28.8 us  [on_device(): lax.all_to_all(jnp.broadcast_to(stats, (count, LANES)), 'leaf', 0, 0, til...]
  transfers between devices with their start and end apart: 4 -> 4, of which waited for: 0 -> 0; matrix products, arithmetic and copies ran while one was open for 0% -> 0% of each run, Pallas kernels for 21% -> 19%
where the time goes in v5:
time: 55.2 us; the launch traced here: 55 us
  blocking collectives  28.8 us (52%)
  Pallas kernels  17 us (31%)
  starting transfers between devices  8.97 us (16%)
    all_to_all x1, blocking collectives, on_device(): lax.all_to_all(jnp.broadcast_to(stats, (count, LANES)), 'leaf', 0, 0, til...  28.8 us
    pallas_call x8, Pallas kernels, call(): pl.pallas_call(kernel, out_shape=outs, in_specs=specs, out_specs=jax.tree...  17 us
    ppermute x2, starting transfers between devices, exchange(): second = lax.ppermute(values, 'leaf', across_pairs)  5.55 us
    ppermute x2, starting transfers between devices, exchange(): return (lax.ppermute(values, 'leaf', pairs), second)  3.42 us
  transfers between devices with their start and end apart: 4, of which 0 were waited for; matrix products, arithmetic and copies ran while one was open for 0% of the time, Pallas kernels for 19%

profile of v5, /device:TPU:1, one launch (start us, length us, event | category | flops | bytes accessed | tf_op | source)
XLA Modules:
  0.0 55.0 jit_solution(11639802125573730847)
XLA Ops:
  0.0 0.0 copy-start
  0.0 1.2 %shard_map.82.pack_ref.refs_2_ = f32[264,128]{1,0:T(8,128)S(1)} custom-call(f32[128,256]{1,0:T(8,128)} %bitcast.8, s32[1,256]{1,0:T(1,128)} %bitcast.11, s32[6,128]{1,0:T(8,128)} %mortars_hbm.1), custom_call_target="tpu_custom_call" | custom-call | flops 10000000000 | bytes 4000000 | tf_op jit(solution)/shard_map/pallas_call | solution.py:445
  1.2 3.3 %collective-permute-start.1 = (f32[264,128]{1,0:T(8,128)S(1)}, f32[264,128]{1,0:T(8,128)S(1)}, u32[]{:S(2)}, u32[]{:S(2)}) collective-permute-start(f32[264,128]{1,0:T(8,128)S(1)} %shard_map.82.pack_ref.refs_2_), channel_id=1, source_target_pairs={{0,1},{1,0},{2,3},{3,2},{4,5},{5,4},{6,7},{7,6},{8,9},{9,8},{10,11... | collective-permute-start | bytes 405512 | tf_op jit(solution)/shard_map/ppermute | solution.py:463
  4.5 1.9 %collective-permute-start = (f32[264,128]{1,0:T(8,128)S(1)}, f32[264,128]{1,0:T(8,128)S(1)}, u32[]{:S(2)}, u32[]{:S(2)}) collective-permute-start(f32[264,128]{1,0:T(8,128)S(1)} %shard_map.82.pack_ref.refs_2_), channel_id=1, source_target_pairs={{1,2},{3,4},{5,6},{7,8},{9,10},{11,12},{13,14},{15,16},{17,18},{19... | collective-permute-start | bytes 405512 | tf_op jit(solution)/shard_map/ppermute | solution.py:462
  6.4 0.1 pad_add_fusion.place_ref.refs_0_
  6.5 0.0 copy-done
  6.5 4.1 %shard_map.83 = (bf16[2176,256]{1,0:T(8,128)(2,1)S(1)}, bf16[2048,256]{1,0:T(8,128)(2,1)S(1)}, bf16[2048,256]{1,0:T(8,128)(2,1)S(1)}, bf16[256,128]{1,0:T(8,128)...) custom-call(s32[2]{0:T(128)S(1)} %pad_add_fusion.place_ref.refs_0_, ...), custom_call_target="tpu_custom_call" | custom-call | flops 2000000000 | bytes 4000000 | tf_op jit(solution)/shard_map/pallas_call | solution.py:445
  10.7 0.0 collective-permute-done.1.refs_3_
  10.7 2.5 %shard_map.84 = (f32[256,128]{1,0:T(8,128)S(1)}, bf16[128,256]{1,0:T(8,128)(2,1)S(1)}, bf16[256,512]{1,0:T(8,128)(2,1)S(1)}, s32[128,1]{1,0:T(8,128)S(1)}, f32[256,128]{1,0:T(8,128)S(1)}) custom-call(s32[2]{0:T(128)S(1)} %pad_add_fusion.place_ref.refs_0_, bf16[3328,256]{1,0:T(8,128)(2,1)S(1)} %copy-done, f32[264,128]{1,0:T(8,128)S(1)} %shard_map.82.pack_ref.refs_2_, ...), custom_call_target="tpu_custom_call" | custom-call | flops 1000000000 | bytes 2000000 | tf_op jit(solution)/shard_map/pallas_call | solution.py:445
  13.2 0.0 collective-permute-done.refs_3_
  13.2 2.5 %shard_map.85 = (f32[256,128]{1,0:T(8,128)S(1)}, f32[256,128]{1,0:T(8,128)S(1)}, bf16[128,256]{1,0:T(8,128)(2,1)S(1)}, bf16[256,512]{1,0:T(8,128)(2,1)S(1)}, s32...) custom-call(f32[256,128]{1,0:T(8,128)S(1)} %get-tuple-element.34.scale_ref, s32[2]{0:T(128)S(1)} %pad_add_fusion.place_ref.refs_0_, ...), custom_call_target="tpu_custom_call" | custom-call | tf_op jit(solution)/shard_map/pallas_call | solution.py:445
  15.7 0.1 collective-permute-start.3
  15.8 3.6 %collective-permute-start.2 = (f32[256,128]{1,0:T(8,128)S(1)}, f32[256,128]{1,0:T(8,128)S(1)}, u32[]{:S(2)}, u32[]{:S(2)}) collective-permute-start(f32[256,128]{1,0:T(8,128)S(1)} %get-tuple-element.43.send_ref), channel_id=1, source_target_pairs={{1,2},{3,4},{5,6},{7,8},{9,10},{11,12},{13,14},{15,16},{17,18},{19... | collective-permute-start | bytes 393224 | tf_op jit(solution)/shard_map/ppermute | solution.py:462
  19.4 1.9 %shard_map.86 = (f32[256,128]{1,0:T(8,128)S(1)}, f32[256,128]{1,0:T(8,128)S(1)}, f32[256,128]{1,0:T(8,128)S(1)}, f32[1,128]{1,0:T(1,128)S(1)}, f32[128,256]{1,0:T(8,128)S(1)}) custom-call(bf16[3328,256]{1,0:T(8,128)(2,1)S(1)} %copy-done, f32[264,128]{1,0:T(8,128)S(1)} %shard_map.82.pack_ref.refs_2_, f32[256,128]{1,0:T(8,128)S(1)} %get-tuple-element.43.send_ref, ...), custom_call_target="tpu_custom_call" | custom-call | flops 2000000000 | bytes 4000000 | tf_op jit(solution)/shard_map/pallas_call | solution.py:445
  21.3 0.0 collective-permute-done.3.refs_1_
  21.3 1.7 %shard_map.87.refs_2_ = f32[256,128]{1,0:T(8,128)S(1)} custom-call(bf16[3328,256]{1,0:T(8,128)(2,1)S(1)} %copy-done, f32[256,128]{1,0:T(8,128)S(1)} %collective-permute-done.3.refs_1_, f32[256,128]{1,0:T(8,128)S(1)} %get-tuple-element.55.refs_2_, bf16[2048,256]{1,0:T(8,128)(2,1)S(1)} %get-tuple-element.37.refs_6_.refs_3_, ...), custom_call_target="tpu_custom_call" | custom-call | flops 1000000000 | bytes 2000000 | tf_op jit(solution)/shard_map/pallas_call | solution.py:445
  23.0 0.0 collective-permute-done.2.refs_1_
  23.0 0.0 copy-start.1
  23.0 2.0 %shard_map.88 = f32[1,128]{1,0:T(1,128)S(1)} custom-call(f32[256,128]{1,0:T(8,128)S(1)} %get-tuple-element.52.zero_ref, f32[256,128]{1,0:T(8,128)S(1)} %get-tuple-element.53.one_ref, f32[1,128]{1,0:T(1,128)S(1)} %get-tuple-element.54.known_ref, bf16[3328,256]{1,0:T(8,128)(2,1)S(1)} %copy-done, f32[256,128]{1,0:T(8,128)S(1)} %collective-permute-done.2.refs_1_, ...), custom_call_target="tpu_custom_call" | custom-call | tf_op jit(solution)/shard_map/pallas_call | solution.py:445
  25.0 0.1 broadcast_in_dim.2
  25.1 28.8 %all_to_all.8 = f32[256,1,128]{2,1,0:T(1,128)S(1)} all-to-all(f32[256,1,128]{2,1,0:T(1,128)S(1)} %broadcast_in_dim.2), channel_id=1, replica_groups=mesh['leaf'=256] {'leaf'}, dimensions={0} | all-to-all | bytes 262144 | tf_op jit(solution)/shard_map/all_to_all | solution.py:558
  53.9 0.0 copy-done.1
  53.9 1.2 %shard_map.89 = f32[128,256]{1,0:T(8,128)} custom-call(f32[256,128]{1,0:T(8,128)S(1)} %bitcast.7, f32[128,256]{1,0:T(8,128)S(1)} %bitcast.9, f32[128,256]{1,0:T(8,128)S(1)} %get-tuple-element.62.image_ref), custom_call_target="tpu_custom_call" | custom-call | tf_op jit(solution)/shard_map/pallas_call | solution.py:445
Async XLA Ops:
  0.0 6.5 %copy-start = (bf16[3328,256]{1,0:T(8,128)(2,1)S(1)}, bf16[3328,256]{1,0:T(8,128)(2,1)}, u32[]{:S(2)}) copy-start(bf16[3328,256]{1,0:T(8,128)(2,1)} %constant.23.clone.table.refs_1_.refs_0_) | copy-start | bytes 5111812
  1.2 9.5 %collective-permute-start.1 = (f32[264,128]{1,0:T(8,128)S(1)}, f32[264,128]{1,0:T(8,128)S(1)}, u32[]{:S(2)}, u32[]{:S(2)}) collective-permute-start(f32[264,128]{1,0:T(8,128)S(1)} %shard_map.82.pack_ref.refs_2_), channel_id=1, source_target_pairs={{0,1},{1,0},{2,3},{3,2},{4,5},{5,4},{6,7},{7,6},{8,9},{9,8},{10,11... | collective-permute-start | bytes 405512 | tf_op jit(solution)/shard_map/ppermute | solution.py:463
  4.5 8.7 %collective-permute-start = (f32[264,128]{1,0:T(8,128)S(1)}, f32[264,128]{1,0:T(8,128)S(1)}, u32[]{:S(2)}, u32[]{:S(2)}) collective-permute-start(f32[264,128]{1,0:T(8,128)S(1)} %shard_map.82.pack_ref.refs_2_), channel_id=1, source_target_pairs={{1,2},{3,4},{5,6},{7,8},{9,10},{11,12},{13,14},{15,16},{17,18},{19... | collective-permute-start | bytes 405512 | tf_op jit(solution)/shard_map/ppermute | solution.py:462
  15.7 5.6 %collective-permute-start.3 = (f32[256,128]{1,0:T(8,128)S(1)}, f32[256,128]{1,0:T(8,128)S(1)}, u32[]{:S(2)}, u32[]{:S(2)}) collective-permute-start(f32[256,128]{1,0:T(8,128)S(1)} %get-tuple-element.43.send_ref), channel_id=1, source_target_pairs={{0,1},{1,0},{2,3},{3,2},{4,5},{5,4},{6,7},{7,6},{8,9},{9,8},{10,11... | collective-permute-start | bytes 393224 | tf_op jit(solution)/shard_map/ppermute | solution.py:463
  15.8 7.2 %collective-permute-start.2 = (f32[256,128]{1,0:T(8,128)S(1)}, f32[256,128]{1,0:T(8,128)S(1)}, u32[]{:S(2)}, u32[]{:S(2)}) collective-permute-start(f32[256,128]{1,0:T(8,128)S(1)} %get-tuple-element.43.send_ref), channel_id=1, source_target_pairs={{1,2},{3,4},{5,6},{7,8},{9,10},{11,12},{13,14},{15,16},{17,18},{19... | collective-permute-start | bytes 393224 | tf_op jit(solution)/shard_map/ppermute | solution.py:462
  23.0 30.9 %copy-start.1 = (f32[2,64,256]{2,1,0:T(8,128)S(1)}, f32[2,64,256]{2,1,0:T(8,128)}, u32[]{:S(2)}) copy-start(f32[2,64,256]{2,1,0:T(8,128)} %param.8) | copy-start | bytes 393220

commit v6 on v5

v6 whole, which is shorter than its diff:
```python
import jax
import jax.numpy as jnp
import ml_dtypes
import numpy as np
from jax import lax
from jax.experimental import pallas as pl
from jax.experimental.pallas import tpu as pltpu
from jax.sharding import PartitionSpec as P

TAU_WEIGHT = 0.15
EPS_WEIGHT = 0.1
FACES = 6
NODES = 64
LANES = 128
F32 = jnp.float32
BF16 = jnp.bfloat16


def face_tables():
    node_at = np.zeros((6, 16), dtype=np.int64)
    for face_id in range(6):
        for row_pos in range(4):
            for col_pos in range(4):
                coords = [row_pos, col_pos]
                coords.insert(face_id // 2, 3 * (face_id % 2))
                node_at[face_id, 4 * row_pos + col_pos] = (
                    16 * coords[0] + 4 * coords[1] + coords[2]
                )
    points = np.array([-1.0, -1.0 / np.sqrt(5.0), 1.0 / np.sqrt(5.0), 1.0])
    halves = np.zeros((2, 4, 4))
    for half_id in range(2):
        target = (points + 2.0 * half_id - 1.0) / 2.0
        for column in range(4):
            lagrange = np.ones(4)
            for other_id in range(4):
                if other_id != column:
                    lagrange = (
                        lagrange * (target - points[other_id]) / (points[column] - points[other_id])
                    )
            halves[half_id, :, column] = lagrange
    mortar = np.stack([np.kron(halves[quarter // 2], halves[quarter % 2]) for quarter in range(4)])
    return node_at, mortar


def two_parts(table):
    high = table.astype(np.float32).astype(ml_dtypes.bfloat16)
    low = (table - high.astype(np.float64)).astype(np.float32).astype(ml_dtypes.bfloat16)
    return np.concatenate([high, low], axis=-1)


def matrices():
    node_at, mortar = face_tables()
    traces = np.zeros((2 * LANES, 2 * LANES))
    to_fine = np.zeros((4, 2 * LANES, LANES))
    to_coarse = np.zeros((4, 2 * LANES, LANES))
    stay = np.zeros((2 * LANES, LANES))
    square = sum(mortar[quarter].T @ mortar[quarter] for quarter in range(4))
    for face in range(FACES):
        for field in range(2):
            nodes = 64 * field + node_at[face]
            for part in range(2):
                for place in range(16):
                    at = part * LANES + 32 * (face // 2) + 16 * field + place
                    traces[part * LANES + nodes[place], at] = 1.0
                    stay[at, nodes] = -square[:, place]
                    for quarter in range(4):
                        to_fine[quarter, at, nodes] = mortar[quarter][:, place]
                        to_coarse[quarter, at, nodes] = mortar[quarter][place, :]
    return np.concatenate(
        [traces.astype(ml_dtypes.bfloat16)]
        + list(two_parts(to_fine))
        + list(two_parts(to_coarse))
        + [two_parts(stay)],
        axis=0,
    )


TRACES_AT, FINE_AT, COARSE_AT, STAY_AT, TABLE_ROWS = 0, 256, 1280, 2304, 2560


def split(values, axis=1):
    high = values.astype(BF16)
    return jnp.concatenate([high, (values - high.astype(F32)).astype(BF16)], axis=axis)


def dot(left, right):
    return jnp.dot(left, right, preferred_element_type=F32)


def fold(values):
    return values[:, :LANES] + values[:, LANES:]


def pick(index, shape, dim):
    places = lax.broadcasted_iota(jnp.int32, shape, dim).astype(F32).astype(BF16)
    index = jnp.broadcast_to(index.astype(F32), shape).astype(BF16)
    return jnp.where(index == places, jnp.ones(shape, BF16), jnp.zeros(shape, BF16))


def on_axis(face):
    lane = lax.broadcasted_iota(jnp.int32, (1, 2 * LANES), 1)
    axis = jnp.right_shift(face, 1)
    return jnp.where((jnp.right_shift(lane, 5) & 3) == axis, 1.0, 0.0).astype(BF16)


def face_nodes(face):
    lane = lax.broadcasted_iota(jnp.int32, (1, LANES), 1)
    axis = jnp.right_shift(face, 1)
    place = jnp.right_shift(lane, 4 - 2 * axis) & 3
    return jnp.where((place == 3 * (face & 1)) & (face >= 0), 1.0, 0.0)


def opposite(face):
    return jnp.where(face >= 0, face ^ 1, -1)


def level_rows(levels):
    scale = jnp.left_shift(jnp.ones_like(levels), levels).astype(F32)
    return jnp.broadcast_to(scale, (LANES, levels.shape[1])).T


def fetch(pairs, sems):
    copies = [
        pltpu.make_async_copy(source, target, sems.at[at])
        for at, (source, target) in enumerate(pairs)
    ]
    for copy in copies:
        copy.start()
    return copies


def prep_kernel(cot_hbm, levels_hbm, mortars_hbm, pack_ref, cot_ref, levels_ref, mortars_ref, sems):
    for copy in fetch(
        ((cot_hbm, cot_ref), (levels_hbm, levels_ref), (mortars_hbm, mortars_ref)), sems
    ):
        copy.wait()
    leaves = cot_ref.shape[1]
    scale = jnp.left_shift(jnp.ones_like(levels_ref[...]), levels_ref[...]).astype(F32)
    pack_ref[0:leaves, :] = (cot_ref[...] * scale).T
    table = mortars_ref[...].astype(F32) + 1.0
    pack_ref[leaves : leaves + 8, :] = jnp.concatenate(
        [table, jnp.zeros((2, table.shape[1]), F32)], axis=0
    )


CHOSEN = (
    "own", "one", "two", "own_fine", "one_fine", "two_fine", "own_pick", "own_back", "fine_back",
    "face",
)
LOCAL = ("diagonal", "stiff", "mass", "curve", "scale")
KEPT_SIDE = ("own_back", "face")
KEPT_OWN = KEPT_SIDE + ("own", "own_fine", "own_pick", "fine_back", "stiff", "mass", "curve")


def from_rows(parts, chooser, picks, backs, coarse_face, kept, table, own=False):
    own_back, face = kept["own_back"], kept["face"][...]
    slots, leaves = own_back.shape[1], own_back.shape[0]
    faces, fine = chooser
    chosen = dot(jnp.concatenate([fine[...], picks], axis=0), parts).astype(BF16)
    other, coarse_other = opposite(face), opposite(coarse_face)
    nodes = [face_nodes(other)] * 4 + [face_nodes(coarse_face)]
    nodes = jnp.concatenate([mask.astype(BF16) for mask in nodes], axis=0)
    trace = dot(
        chosen * jnp.concatenate([nodes, nodes], axis=1), table[TRACES_AT : TRACES_AT + 256, :]
    ).astype(BF16)
    axis = on_axis(face)
    trace = [trace[slots * q : slots * (q + 1), :] * axis for q in range(4)] + [
        trace[4 * slots :, :] * (axis if own else on_axis(coarse_face))
    ]
    mask = face_nodes(coarse_other)
    sent = [
        split(mask * fold(dot(trace[4], table[FINE_AT + 256 * q : FINE_AT + 256 * (q + 1), :])))
        for q in range(4)
    ]
    last = TABLE_ROWS if own else STAY_AT
    back = dot(jnp.concatenate(trace if own else trace[:4], axis=1), table[COARSE_AT:last, :])
    sent.append(split(face_nodes(face) * fold(back)))
    mortars = dot(
        jnp.concatenate([backs, own_back[...]], axis=1), jnp.concatenate(sent, axis=0)
    )
    result = fold(mortars)
    seen = dot(faces[...], parts)
    for f in range(FACES):
        shift = 3 * 4 ** (2 - f // 2)
        part = fold(seen[leaves * f : leaves * (f + 1), :])
        part = pltpu.roll(part, shift if f % 2 else LANES - shift, 1)
        result = result + face_nodes(jnp.int32(f)) * part
    return result


def placed(lapped):
    first = lax.broadcasted_iota(jnp.int32, lapped.shape, 1) < NODES
    return jnp.where(first, -EPS_WEIGHT, TAU_WEIGHT) * pltpu.roll(lapped, NODES, 1)


def own_part(rows, vector, diagonal, kept, table):
    parts = split(rows)
    lapped = (
        diagonal * rows
        + fold(dot(parts, kept["stiff"][...]))
        - from_rows(
            parts, (kept["own"], kept["own_fine"]), kept["own_pick"][...],
            kept["fine_back"][...], kept["face"][...], kept, table, own=True,
        )
    )
    swapped = pltpu.roll(vector, NODES, 1)
    return kept["mass"][...] * vector + kept["curve"][...] * swapped + placed(lapped)


def fine_count(back, face):
    weights = face_nodes(opposite(face)).astype(BF16)
    return dot(back, jnp.concatenate([weights] * 4, axis=0))


def own_index(index, offset):
    return jnp.where(index < 0, -1, index - offset)


def to_columns(table):
    return table.astype(F32).T.astype(jnp.int32)


def fine_backs(table, offset, leaves):
    index = own_index(table, offset)
    return jnp.concatenate(
        [pick(index[2 + q : 3 + q, :], (leaves, table.shape[1]), 0) for q in range(4)], axis=1
    )


def choose_kernel(place_ref, pack_ref, neighbours_ref, same_ref, *refs):
    made = dict(zip(CHOSEN, refs))
    same_ref[...] = pack_ref[...]
    leaves = pack_ref.shape[0] - 8
    offset, first = place_ref[0:1, 0:1], place_ref[0:1, 1:2]
    mortars = pack_ref[leaves : leaves + 8, :].astype(jnp.int32) - 1
    columns = to_columns(pack_ref[leaves : leaves + 8, :]) - 1
    slots = mortars.shape[1]
    made["face"][...] = columns[:, 1:2]
    made["fine_back"][...] = fine_backs(mortars, offset, leaves)
    made["own_back"][...] = pick(mortars[0:1, :] - offset, (leaves, slots), 0)
    made["own_pick"][...] = pick(columns[:, 0:1] - offset, (slots, leaves), 1)
    neighbours = jnp.concatenate(
        [neighbours_ref[...], jnp.full((2, leaves), -1, jnp.int32)], axis=0
    )
    for name, start in (("own", offset), ("one", offset + first), ("two", offset - first)):
        places = to_columns(own_index(neighbours, start))
        for f in range(FACES):
            made[name][leaves * f : leaves * (f + 1), :] = pick(
                places[:, f : f + 1], (leaves, leaves), 1
            )
        fine = own_index(columns, start)
        for q in range(4):
            made[name + "_fine"][slots * q : slots * (q + 1), :] = pick(
                fine[:, 2 + q : 3 + q], (slots, leaves), 1
            )


def near_kernel(pack_ref, table, mass_ref, curve_ref, stiffness_ref, levels_ref, *refs):
    names = KEPT_OWN[:6]
    kept = dict(zip(names + LOCAL, refs))
    partial_ref = refs[len(names) + len(LOCAL)]
    leaves = pack_ref.shape[0] - 8
    diagonal = fine_count(kept["fine_back"][...], kept["face"][...]) + sum(
        face_nodes(jnp.int32(f)) for f in range(FACES)
    )
    kept["diagonal"][...] = diagonal
    wide = jnp.concatenate([stiffness_ref[...]] * 2, axis=1)
    wide = jnp.concatenate([wide, wide], axis=0)
    same = (lax.broadcasted_iota(jnp.int32, wide.shape, 0) < NODES) == (
        lax.broadcasted_iota(jnp.int32, wide.shape, 1) < NODES
    )
    wide = split(jnp.where(same, wide, 0.0))
    kept["stiff"][...] = jnp.concatenate([wide, wide], axis=0)
    kept["mass"][...] = jnp.concatenate([mass_ref[...]] * 2, axis=0).T
    curve = curve_ref[...]
    kept["curve"][...] = jnp.concatenate([-curve, jnp.zeros_like(curve)], axis=0).T
    scale = level_rows(levels_ref[...])
    kept["scale"][...] = scale
    rows = pack_ref[0:leaves, :]
    partial_ref[...] = own_part(rows, rows / scale, diagonal, kept, table)


def first_side(
    place_ref, table, pack_ref, other_ref, partial_ref, diagonal_ref, faces_ref, fine_ref, kept,
    made, direction,
):
    picks_ref, backs_ref, face_ref, total_ref = made
    leaves = pack_ref.shape[0] - 8
    mortars = other_ref[leaves : leaves + 8, :]
    columns = to_columns(mortars) - 1
    mortars = mortars.astype(jnp.int32) - 1
    slots = mortars.shape[1]
    face = columns[:, 1:2]
    offset = place_ref[0:1, 0:1]
    start = offset + direction * place_ref[0:1, 1:2]
    picks = pick(columns[:, 0:1] - start, (slots, leaves), 1)
    backs = fine_backs(mortars, offset, leaves)
    extra = fine_count(backs, face)
    picks_ref[...] = picks
    backs_ref[...] = backs
    face_ref[...] = face
    total_ref[...] = diagonal_ref[...] + extra
    lapped = extra * pack_ref[0:leaves, :] - from_rows(
        split(other_ref[0:leaves, :]), (faces_ref, fine_ref), picks, backs, face, kept, table
    )
    return partial_ref[...] + placed(lapped)


def first_one_kernel(*refs):
    kept = dict(zip(KEPT_SIDE, refs[8:]))
    refs, rest = refs[:8], refs[8 + len(KEPT_SIDE) :]
    rest[0][...] = first_side(*refs, kept, rest[1:], 1)


def first_two_kernel(scale_ref, *refs):
    kept = dict(zip(KEPT_SIDE, refs[8:]))
    refs, rest = refs[:8], refs[8 + len(KEPT_SIDE) :]
    image = first_side(*refs, kept, rest[2:], -1)
    rest[0][...] = image
    rest[1][...] = image * scale_ref[...]


def total(values):
    return jnp.sum(values, keepdims=True)


def unit(values):
    length = jnp.sqrt(total(values * values))
    return length, values * jnp.where(length > 0.0, 1.0 / jnp.where(length > 0.0, length, 1.0), 0.0)


def in_lanes(shape, values):
    lane = lax.broadcasted_iota(jnp.int32, shape, 1)
    row = jnp.zeros(shape, F32)
    for at, value in enumerate(values):
        row = jnp.where(lane == at, value, row)
    return row


def factor_kernel(pack_ref, send_ref, image_ref, scale_ref, *refs):
    same_ref, zero_ref, one_ref, stats_ref, turned_ref = refs
    same_ref[...] = send_ref[...]
    image = image_ref[...]
    turned_ref[...] = image.T
    r00, zero = unit(pack_ref[0 : image.shape[0], :] / scale_ref[...])
    r01 = total(zero * image)
    image = image - r01 * zero
    again = total(zero * image)
    r11, one = unit(image - again * zero)
    zero_ref[...] = zero
    one_ref[...] = one
    stats_ref[...] = in_lanes(stats_ref.shape, (r00, r01 + again, r11))


def again_kernel(table, send_ref, image_ref, total_ref, *refs):
    kept = dict(zip(KEPT_OWN, refs))
    refs[len(KEPT_OWN)][...] = own_part(
        send_ref[...], image_ref[...], total_ref[...], kept, table
    )


def second_side(
    table, other_ref, partial_ref, faces_ref, fine_ref, picks_ref, backs_ref, face_ref, kept
):
    lapped = from_rows(
        split(other_ref[...]), (faces_ref, fine_ref), picks_ref[...], backs_ref[...],
        face_ref[...], kept, table,
    )
    return partial_ref[...] - placed(lapped)


def second_one_kernel(*refs):
    refs, rest = refs[:8], refs[8:]
    rest[len(KEPT_SIDE)][...] = second_side(*refs, dict(zip(KEPT_SIDE, rest)))


def second_two_kernel(zero_ref, one_ref, known_ref, *refs):
    refs, rest = refs[:8], refs[8:]
    stats_ref = rest[len(KEPT_SIDE)]
    image = second_side(*refs, dict(zip(KEPT_SIDE, rest)))
    zero, one = zero_ref[...], one_ref[...]
    r02 = total(zero * image)
    r12 = total(one * image)
    rest = image - r02 * zero - r12 * one
    r22 = jnp.sqrt(total(rest * rest))
    stats_ref[...] = known_ref[...] + in_lanes(stats_ref.shape, (0.0, 0.0, 0.0, r02, r12, r22))


def final_kernel(stats_ref, cot_ref, image_ref, out_ref):
    table = stats_ref[...].T
    a0, a1, b1, a2, b2, c2 = [table[at : at + 1, :] for at in range(6)]
    r00_sq = total(a0 * a0)
    r00 = jnp.sqrt(r00_sq)
    f01 = total(a0 * a1) / r00_sq
    f02 = total(a0 * a2) / r00_sq
    a1 = a1 - f01 * a0
    a2 = a2 - f02 * a0
    r11_sq = total(a1 * a1) + total(b1 * b1)
    r11 = jnp.sqrt(r11_sq)
    f12 = (total(a1 * a2) + total(b1 * b2)) / r11_sq
    a2 = a2 - f12 * a1
    b2 = b2 - f12 * b1
    r22 = jnp.sqrt(total(a2 * a2) + total(b2 * b2) + total(c2 * c2))
    rhs_norm = r00
    first_diag = f01
    first_below = r11 / r00
    upper_right = (f02 - first_diag * f01) / first_below
    second_diag = f12 - first_diag
    second_below = r22 / r11
    first_len = jnp.sqrt(first_diag * first_diag + first_below * first_below)
    cos_one = first_diag / first_len
    sin_one = first_below / first_len
    rotated_top = cos_one * upper_right + sin_one * second_diag
    rotated_low = cos_one * second_diag - sin_one * upper_right
    second_len = jnp.sqrt(rotated_low * rotated_low + second_below * second_below)
    cos_two = rotated_low / second_len
    y_two = cos_two * (-sin_one * rhs_norm) / second_len
    y_one = (cos_one * rhs_norm - rotated_top * y_two) / first_len
    on_one = y_two / r11
    on_base = y_one / r00 - on_one * f01
    out_ref[...] = on_base * cot_ref[...] + on_one * image_ref[...]


def on_device(cotangent, nodal_mass, curvature, stiffness, levels, neighbours, mortars):
    fields, nodes, leaves = cotangent.shape
    slots = mortars.shape[1]
    count = lax.axis_size("leaf")
    flat = cotangent.reshape(fields * nodes, leaves)
    levels = levels.reshape(1, leaves)
    me = lax.axis_index("leaf").astype(jnp.int32)
    place = jnp.stack([me * leaves, leaves - 2 * leaves * (me & 1)]).reshape(1, 2)
    table = jnp.asarray(matrices())
    vmem = pl.BlockSpec(memory_space=pltpu.VMEM)
    hbm = pl.BlockSpec(memory_space=pltpu.HBM)

    def call(kernel, outs, specs, operands, scratch=(), flops=0, moved=0, mib=40):
        return pl.pallas_call(
            kernel,
            out_shape=outs,
            in_specs=specs,
            out_specs=jax.tree.map(lambda _: vmem, outs),
            scratch_shapes=scratch,
            compiler_params=pltpu.CompilerParams(vmem_limit_bytes=mib * 1024 * 1024),
            cost_estimate=pl.CostEstimate(flops=flops, bytes_accessed=moved, transcendentals=0),
        )(*operands)

    def shape(*dims, dtype=F32):
        return jax.ShapeDtypeStruct(dims, dtype)

    pairs_one = [(i, i ^ 1) for i in range(count) if i ^ 1 < count]
    pairs_two = [(i, i + 1) for i in range(1, count - 1, 2)]
    pairs_two = pairs_two + [(j, i) for i, j in pairs_two]

    wide = 2 * LANES
    rows = shape(leaves, LANES)
    faces = shape(FACES * leaves, leaves, dtype=BF16)
    fine = shape(4 * slots, leaves, dtype=BF16)
    picks = shape(slots, leaves, dtype=BF16)
    backs = shape(leaves, 4 * slots, dtype=BF16)
    face = shape(slots, 1, dtype=jnp.int32)
    shapes = dict(
        own=faces,
        one=faces,
        two=faces,
        own_fine=fine,
        one_fine=fine,
        two_fine=fine,
        own_pick=picks,
        own_back=shape(leaves, slots, dtype=BF16),
        fine_back=backs,
        face=face,
        diagonal=rows,
        stiff=shape(wide, wide, dtype=BF16),
        mass=rows,
        curve=rows,
        scale=rows,
    )

    def stay_out(*arrays):
        return tuple(pltpu.with_memory_space_constraint(array, pltpu.HBM) for array in arrays)

    pack = call(
        prep_kernel,
        shape(leaves + 8, LANES),
        [hbm] * 3,
        stay_out(flat, levels, mortars),
        scratch=[
            pltpu.VMEM(flat.shape, F32),
            pltpu.VMEM(levels.shape, jnp.int32),
            pltpu.VMEM(mortars.shape, jnp.int32),
            pltpu.SemaphoreType.DMA((3,)),
        ],
        flops=10_000_000_000,
        moved=4_000_000,
    )
    two = lax.ppermute(pack, "leaf", pairs_two)
    same, *chosen = call(
        choose_kernel,
        [shape(leaves + 8, LANES)] + [shapes[name] for name in CHOSEN],
        [vmem] * 3,
        (place, pack, neighbours),
        flops=1_000_000_000,
        moved=2_000_000,
    )
    kept = dict(zip(CHOSEN, chosen))
    one = lax.ppermute(same, "leaf", pairs_one)
    own = KEPT_OWN[:6]
    *local, partial = call(
        near_kernel,
        [shapes[name] for name in LOCAL] + [rows],
        [vmem] * (6 + len(own)),
        [pack, table, nodal_mass, curvature, stiffness, levels] + [kept[name] for name in own],
        flops=2_000_000_000,
        moved=4_000_000,
    )
    kept.update(zip(LOCAL, local))
    side = [kept[name] for name in KEPT_SIDE]
    made = [picks, backs, face, rows]
    partial, *made_one = call(
        first_one_kernel,
        [rows] + made,
        [vmem] * (8 + len(side)),
        [place, table, pack, one, partial, kept["diagonal"], kept["one"],
         kept["one_fine"]] + side,
        flops=1_000_000_000,
        moved=2_000_000,
    )
    image, send, *made_two = call(
        first_two_kernel,
        [rows, rows] + made,
        [vmem] * (9 + len(side)),
        [kept["scale"], place, table, pack, two, partial, made_one[3], kept["two"],
         kept["two_fine"]] + side,
    )
    two = lax.ppermute(send, "leaf", pairs_two)
    same, zero, unit_one, known, turned = call(
        factor_kernel,
        [rows, rows, rows, shape(1, LANES), shape(LANES, leaves)],
        [vmem] * 4,
        [pack, send, image, kept["scale"]],
        flops=1_000_000_000,
        moved=2_000_000,
    )
    one = lax.ppermute(same, "leaf", pairs_one)
    partial = call(
        again_kernel,
        rows,
        [vmem] * (4 + len(KEPT_OWN)),
        [table, send, image, made_two[3]] + [kept[name] for name in KEPT_OWN],
        flops=2_000_000_000,
        moved=4_000_000,
    )
    partial = call(
        second_one_kernel,
        rows,
        [vmem] * (8 + len(side)),
        [table, one, partial, kept["one"], kept["one_fine"], *made_one[:3]] + side,
        flops=1_000_000_000,
        moved=2_000_000,
    )
    stats = call(
        second_two_kernel,
        shape(1, LANES),
        [vmem] * (11 + len(side)),
        [zero, unit_one, known, table, two, partial, kept["two"], kept["two_fine"], *made_two[:3]]
        + side,
    )
    gathered = lax.all_to_all(
        jnp.broadcast_to(stats, (count, LANES)), "leaf", 0, 0, tiled=True
    )
    out = call(final_kernel, shape(*flat.shape), [vmem] * 3, (gathered, flat, turned))
    return out.reshape(cotangent.shape)


def solution(mesh):
    placed = (
        P(None, None, "leaf"),
        P(None, "leaf"),
        P(None, "leaf"),
        P(),
        P("leaf"),
        P(None, "leaf"),
        P(None, "leaf"),
    )
    return jax.shard_map(
        on_device, mesh=mesh, in_specs=placed, out_specs=P(None, None, "leaf"), check_vma=False
    )
```

time: 55.2 us -> 53.1 us (0.962)
  Pallas kernels: 17 us -> 13.3 us
  blocking collectives: 28.8 us -> 30.9 us
  starting transfers between devices: 8.97 us -> 8.33 us
    pallas_call x8 -> x10, Pallas kernels: 17 us -> 13.3 us  [call(): pl.pallas_call(kernel, out_shape=outs, in_specs=specs, out_specs=jax.tree...]
    all_to_all x1, blocking collectives: 28.8 us -> 30.9 us  [on_device(): lax.all_to_all(jnp.broadcast_to(stats, (count, LANES)), 'leaf', 0, 0, til...]
    ppermute x4, starting transfers between devices: 8.97 us -> 8.33 us  [the longest x1 4.59 us: on_device(): two = lax.ppermute(pack, 'leaf', pairs_two)]
  transfers between devices with their start and end apart: 4 -> 4, of which waited for: 0 -> 0; matrix products, arithmetic and copies ran while one was open for 0% -> 0% of each run, Pallas kernels for 19% -> 15%
where the time goes in v6:
time: 53.1 us; the launch traced here: 52.9 us
  blocking collectives  30.9 us (58%)
  Pallas kernels  13.3 us (25%)
  starting transfers between devices  8.33 us (16%)
    all_to_all x1, blocking collectives, on_device(): lax.all_to_all(jnp.broadcast_to(stats, (count, LANES)), 'leaf', 0, 0, til...  30.9 us
    pallas_call x10, Pallas kernels, call(): pl.pallas_call(kernel, out_shape=outs, in_specs=specs, out_specs=jax.tree...  13.3 us
    ppermute x1, starting transfers between devices, on_device(): two = lax.ppermute(pack, 'leaf', pairs_two)  4.59 us
    ppermute x1, starting transfers between devices, on_device(): two = lax.ppermute(send, 'leaf', pairs_two)  3.55 us
  transfers between devices with their start and end apart: 4, of which 0 were waited for; matrix products, arithmetic and copies ran while one was open for 0% of the time, Pallas kernels for 15%

profile of v6, /device:TPU:1, one launch (start us, length us, event | category | flops | bytes accessed | tf_op | source)
XLA Modules:
  0.0 52.9 jit_solution(16031969115915792735)
XLA Ops:
  0.0 0.0 copy-start.5
  0.0 1.1 %shard_map.82.pack_ref.refs_2_ = f32[264,128]{1,0:T(8,128)S(1)} custom-call(f32[128,256]{1,0:T(8,128)} %bitcast.10, s32[1,256]{1,0:T(1,128)} %bitcast.13, s32[6,128]{1,0:T(8,128)} %mortars_hbm.1), custom_call_target="tpu_custom_call" | custom-call | flops 10000000000 | bytes 4000000 | tf_op jit(solution)/shard_map/pallas_call | solution.py:437
  1.1 4.6 %collective-permute-start = (f32[264,128]{1,0:T(8,128)S(1)}, f32[264,128]{1,0:T(8,128)S(1)}, u32[]{:S(2)}, u32[]{:S(2)}) collective-permute-start(f32[264,128]{1,0:T(8,128)S(1)} %shard_map.82.pack_ref.refs_2_), channel_id=1, source_target_pairs={{1,2},{3,4},{5,6},{7,8},{9,10},{11,12},{13,14},{15,16},{17,18},{19... | collective-permute-start | bytes 405512 | tf_op jit(solution)/shard_map/ppermute | solution.py:496
  5.7 0.1 add_bitcast_fusion.place_ref.refs_0_
  5.7 0.0 copy-done.5
  5.7 0.0 copy-start
  5.8 0.0 copy-start.2
  5.8 0.0 copy-start.3
  5.8 0.0 copy-start.4
  5.8 0.0 copy-start.6
  5.8 1.3 %shard_map.83 = (f32[264,128]{1,0:T(8,128)S(1)}, bf16[1536,256]{1,0:T(8,128)(2,1)S(1)}, bf16[1536,256]{1,0:T(8,128)(2,1)S(1)}, bf16[1536,256]{1,0:T(8,128)(2,1)S...) custom-call(s32[1,2]{1,0:T(1,128)S(1)} %add_bitcast_fusion.place_ref, ...), custom_call_target="tpu_custom_call" | custom-call | flops 1000000000 | bytes 2000000 | tf_op jit(solution)/shard_map/pallas_call | solution.py:437
  7.1 0.1 collective-permute-start.1
  7.2 0.0 copy-done
  7.2 0.0 copy-done.2
  7.2 0.0 copy-done.3
  7.2 0.0 copy-done.4
  7.2 0.0 copy-done.6
  7.2 1.5 %shard_map.84 = (f32[256,128]{1,0:T(8,128)S(1)}, bf16[256,256]{1,0:T(8,128)(2,1)S(1)}, f32[256,128]{1,0:T(8,128)S(1)}, f32[256,128]{1,0:T(8,128)S(1)}, f32[256,128]{1,0:T(8,128)S(1)}, /*index=5*/f32[256,128]{1,0:T(8,128)S(1)}) custom-call(f32[264,128]{1,0:T(8,128)S(1)} %shard_map.82.pack_ref.refs_2_, bf16[2560,256]{1,0:T(8,128)(2,1)S(1)} %copy-done, ...), custom_call_target="tpu_custom_call" | custom-call | flops 2000000000 | bytes 4000000 | tf_op jit(solution)/shard_map/pallas_call | solution.py:437
  8.7 0.0 collective-permute-done.1.refs_3_
  8.7 1.7 %shard_map.85 = (f32[256,128]{1,0:T(8,128)S(1)}, bf16[128,256]{1,0:T(8,128)(2,1)S(1)}, bf16[256,512]{1,0:T(8,128)(2,1)S(1)}, s32[128,1]{1,0:T(8,128)S(1)}, f32[256,128]{1,0:T(8,128)S(1)}) custom-call(s32[1,2]{1,0:T(1,128)S(1)} %add_bitcast_fusion.place_ref.refs_0_, bf16[2560,256]{1,0:T(8,128)(2,1)S(1)} %copy-done, ...), custom_call_target="tpu_custom_call" | custom-call | flops 1000000000 | bytes 2000000 | tf_op jit(solution)/shard_map/pallas_call | solution.py:437
  10.4 0.0 collective-permute-done.refs_3_
  10.4 1.7 %shard_map.86 = (f32[256,128]{1,0:T(8,128)S(1)}, f32[256,128]{1,0:T(8,128)S(1)}, bf16[128,256]{1,0:T(8,128)(2,1)S(1)}, bf16[256,512]{1,0:T(8,128)(2,1)S(1)}, s32...) custom-call(f32[256,128]{1,0:T(8,128)S(1)} %get-tuple-element.44.scale_ref, s32[1,2]{1,0:T(1,128)S(1)} %add_bitcast_fusion.place_ref.refs_0_, ...), custom_call_target="tpu_custom_call" | custom-call | tf_op jit(solution)/shard_map/pallas_call | solution.py:437
  12.0 3.6 %collective-permute-start.2 = (f32[256,128]{1,0:T(8,128)S(1)}, f32[256,128]{1,0:T(8,128)S(1)}, u32[]{:S(2)}, u32[]{:S(2)}) collective-permute-start(f32[256,128]{1,0:T(8,128)S(1)} %get-tuple-element.54.send_ref), channel_id=1, source_target_pairs={{1,2},{3,4},{5,6},{7,8},{9,10},{11,12},{13,14},{15,16},{17,18},{19... | collective-permute-start | bytes 393224 | tf_op jit(solution)/shard_map/ppermute | solution.py:535
  15.6 0.7 %shard_map.87 = (f32[256,128]{1,0:T(8,128)S(1)}, f32[256,128]{1,0:T(8,128)S(1)}, f32[256,128]{1,0:T(8,128)S(1)}, f32[1,128]{1,0:T(1,128)S(1)}, f32[128,256]{1,0:T(8,128)S(1)}) custom-call(f32[264,128]{1,0:T(8,128)S(1)} %shard_map.82.pack_ref.refs_2_, f32[256,128]{1,0:T(8,128)S(1)} %get-tuple-element.54.send_ref, f32[256,128]{1,0:T(8,128)S(1)} %get-tuple-element.55.image_ref, ...), custom_call_target="tpu_custom_call" | custom-call | flops 1000000000 | bytes 2000000 | tf_op jit(solution)/shard_map/pallas_call | solution.py:437
  16.3 0.1 collective-permute-start.3
  16.4 1.3 %shard_map.88.refs_2_ = f32[256,128]{1,0:T(8,128)S(1)} custom-call(bf16[2560,256]{1,0:T(8,128)(2,1)S(1)} %copy-done, f32[256,128]{1,0:T(8,128)S(1)} %get-tuple-element.54.send_ref, f32[256,128]{1,0:T(8,128)S(1)} %get-tuple-element.55.image_ref, f32[256,128]{1,0:T(8,128)S(1)} %get-tuple-element.60.total_ref, ...), custom_call_target="tpu_custom_call" | custom-call | flops 2000000000 | bytes 4000000 | tf_op jit(solution)/shard_map/pallas_call | solution.py:437
  17.7 0.0 collective-permute-done.3.refs_1_
  17.7 1.4 %shard_map.89.refs_2_ = f32[256,128]{1,0:T(8,128)S(1)} custom-call(bf16[2560,256]{1,0:T(8,128)(2,1)S(1)} %copy-done, f32[256,128]{1,0:T(8,128)S(1)} %collective-permute-done.3.refs_1_, f32[256,128]{1,0:T(8,128)S(1)} %shard_map.88.refs_2_, bf16[1536,256]{1,0:T(8,128)(2,1)S(1)} %get-tuple-element.48.refs_6_.refs_3_, ...), custom_call_target="tpu_custom_call" | custom-call | flops 1000000000 | bytes 2000000 | tf_op jit(solution)/shard_map/pallas_call | solution.py:437
  19.1 0.0 collective-permute-done.2.refs_1_
  19.1 0.0 copy-start.1
  19.1 1.7 %shard_map.90 = f32[1,128]{1,0:T(1,128)S(1)} custom-call(f32[256,128]{1,0:T(8,128)S(1)} %get-tuple-element.56.zero_ref, f32[256,128]{1,0:T(8,128)S(1)} %get-tuple-element.57.one_ref, f32[1,128]{1,0:T(1,128)S(1)} %get-tuple-element.58.known_ref, bf16[2560,256]{1,0:T(8,128)(2,1)S(1)} %copy-done, f32[256,128]{1,0:T(8,128)S(1)} %collective-permute-done.2.refs_1_, ...), custom_call_target="tpu_custom_call" | custom-call | tf_op jit(solution)/shard_map/pallas_call | solution.py:437
  20.8 0.1 broadcast_in_dim.2
  20.8 30.9 %all_to_all.8 = f32[256,1,128]{2,1,0:T(1,128)S(1)} all-to-all(f32[256,1,128]{2,1,0:T(1,128)S(1)} %broadcast_in_dim.2), channel_id=1, replica_groups=mesh['leaf'=256] {'leaf'}, dimensions={0} | all-to-all | bytes 262144 | tf_op jit(solution)/shard_map/all_to_all | solution.py:568
  51.8 0.0 copy-done.1
  51.8 1.2 %shard_map.91 = f32[128,256]{1,0:T(8,128)} custom-call(f32[256,128]{1,0:T(8,128)S(1)} %bitcast.9, f32[128,256]{1,0:T(8,128)S(1)} %bitcast.11, f32[128,256]{1,0:T(8,128)S(1)} %get-tuple-element.70.image_ref), custom_call_target="tpu_custom_call" | custom-call | tf_op jit(solution)/shard_map/pallas_call | solution.py:437
Async XLA Ops:
  0.0 5.7 %copy-start.5 = (s32[6,256]{1,0:T(8,128)S(1)}, s32[6,256]{1,0:T(8,128)}, u32[]{:S(2)}) copy-start(s32[6,256]{1,0:T(8,128)} %neighbours_ref.1) | copy-start | bytes 18436
  1.1 9.3 %collective-permute-start = (f32[264,128]{1,0:T(8,128)S(1)}, f32[264,128]{1,0:T(8,128)S(1)}, u32[]{:S(2)}, u32[]{:S(2)}) collective-permute-start(f32[264,128]{1,0:T(8,128)S(1)} %shard_map.82.pack_ref.refs_2_), channel_id=1, source_target_pairs={{1,2},{3,4},{5,6},{7,8},{9,10},{11,12},{13,14},{15,16},{17,18},{19... | collective-permute-start | bytes 405512 | tf_op jit(solution)/shard_map/ppermute | solution.py:496
  5.7 1.4 %copy-start = (bf16[2560,256]{1,0:T(8,128)(2,1)S(1)}, bf16[2560,256]{1,0:T(8,128)(2,1)}, u32[]{:S(2)}) copy-start(bf16[2560,256]{1,0:T(8,128)(2,1)} %constant.12.clone.table.refs_1_.refs_0_) | copy-start | bytes 3932164
  5.8 1.4 %copy-start.2 = (f32[64,256]{1,0:T(8,128)S(1)}, f32[64,256]{1,0:T(8,128)}, u32[]{:S(2)}) copy-start(f32[64,256]{1,0:T(8,128)} %mass_ref.1) | copy-start | bytes 196612
  5.8 1.4 %copy-start.3 = (f32[64,256]{1,0:T(8,128)S(1)}, f32[64,256]{1,0:T(8,128)}, u32[]{:S(2)}) copy-start(f32[64,256]{1,0:T(8,128)} %curve_ref.1) | copy-start | bytes 196612
  5.8 1.4 %copy-start.4 = (f32[64,64]{1,0:T(8,128)S(1)}, f32[64,64]{1,0:T(8,128)}, u32[]{:S(2)}) copy-start(f32[64,64]{1,0:T(8,128)} %stiffness_ref.1) | copy-start | bytes 49156
  5.8 1.4 %copy-start.6 = (s32[256]{0:T(256)S(1)}, s32[256]{0:T(256)}, u32[]{:S(2)}) copy-start(s32[256]{0:T(256)} %param.12) | copy-start | bytes 3076
  7.1 1.6 %collective-permute-start.1 = (f32[264,128]{1,0:T(8,128)S(1)}, f32[264,128]{1,0:T(8,128)S(1)}, u32[]{:S(2)}, u32[]{:S(2)}) collective-permute-start(f32[264,128]{1,0:T(8,128)S(1)} %get-tuple-element.45), channel_id=1, source_target_pairs={{0,1},{1,0},{2,3},{3,2},{4,5},{5,4},{6,7},{7,6},{8,9},{9,8},{10,11... | collective-permute-start | bytes 405512 | tf_op jit(solution)/shard_map/ppermute | solution.py:506
  12.0 7.0 %collective-permute-start.2 = (f32[256,128]{1,0:T(8,128)S(1)}, f32[256,128]{1,0:T(8,128)S(1)}, u32[]{:S(2)}, u32[]{:S(2)}) collective-permute-start(f32[256,128]{1,0:T(8,128)S(1)} %get-tuple-element.54.send_ref), channel_id=1, source_target_pairs={{1,2},{3,4},{5,6},{7,8},{9,10},{11,12},{13,14},{15,16},{17,18},{19... | collective-permute-start | bytes 393224 | tf_op jit(solution)/shard_map/ppermute | solution.py:535
  16.3 1.4 %collective-permute-start.3 = (f32[256,128]{1,0:T(8,128)S(1)}, f32[256,128]{1,0:T(8,128)S(1)}, u32[]{:S(2)}, u32[]{:S(2)}) collective-permute-start(f32[256,128]{1,0:T(8,128)S(1)} %get-tuple-element.59), channel_id=1, source_target_pairs={{0,1},{1,0},{2,3},{3,2},{4,5},{5,4},{6,7},{7,6},{8,9},{9,8},{10,11... | collective-permute-start | bytes 393224 | tf_op jit(solution)/shard_map/ppermute | solution.py:544
  19.1 32.7 %copy-start.1 = (f32[2,64,256]{2,1,0:T(8,128)S(1)}, f32[2,64,256]{2,1,0:T(8,128)}, u32[]{:S(2)}) copy-start(f32[2,64,256]{2,1,0:T(8,128)} %param.8) | copy-start | bytes 393220

commit v7 on v6

--- a/solution.py
+++ b/solution.py
@@ -138,48 +138,19 @@
     scale = jnp.left_shift(jnp.ones_like(levels_ref[...]), levels_ref[...]).astype(F32)
     pack_ref[0:leaves, :] = (cot_ref[...] * scale).T
     table = mortars_ref[...].astype(F32) + 1.0
-    pack_ref[leaves : leaves + 8, :] = jnp.concatenate(
-        [table, jnp.zeros((2, table.shape[1]), F32)], axis=0
-    )
+    halves = [scale[:, k * table.shape[1] : (k + 1) * table.shape[1]] for k in range(2)]
+    pack_ref[leaves : leaves + 8, :] = jnp.concatenate([table] + halves, axis=0)
 
 
 CHOSEN = (
-    "own", "one", "two", "own_fine", "one_fine", "two_fine", "own_pick", "own_back", "fine_back",
-    "face",
+    "own", "one", "own_fine", "one_fine", "own_pick", "own_back", "fine_back", "face",
 )
-LOCAL = ("diagonal", "stiff", "mass", "curve", "scale")
-KEPT_SIDE = ("own_back", "face")
-KEPT_OWN = KEPT_SIDE + ("own", "own_fine", "own_pick", "fine_back", "stiff", "mass", "curve")
-
-
-def from_rows(parts, chooser, picks, backs, coarse_face, kept, table, own=False):
-    own_back, face = kept["own_back"], kept["face"][...]
-    slots, leaves = own_back.shape[1], own_back.shape[0]
-    faces, fine = chooser
-    chosen = dot(jnp.concatenate([fine[...], picks], axis=0), parts).astype(BF16)
-    other, coarse_other = opposite(face), opposite(coarse_face)
-    nodes = [face_nodes(other)] * 4 + [face_nodes(coarse_face)]
-    nodes = jnp.concatenate([mask.astype(BF16) for mask in nodes], axis=0)
-    trace = dot(
-        chosen * jnp.concatenate([nodes, nodes], axis=1), table[TRACES_AT : TRACES_AT + 256, :]
-    ).astype(BF16)
-    axis = on_axis(face)
-    trace = [trace[slots * q : slots * (q + 1), :] * axis for q in range(4)] + [
-        trace[4 * slots :, :] * (axis if own else on_axis(coarse_face))
-    ]
-    mask = face_nodes(coarse_other)
-    sent = [
-        split(mask * fold(dot(trace[4], table[FINE_AT + 256 * q : FINE_AT + 256 * (q + 1), :])))
-        for q in range(4)
-    ]
-    last = TABLE_ROWS if own else STAY_AT
-    back = dot(jnp.concatenate(trace if own else trace[:4], axis=1), table[COARSE_AT:last, :])
-    sent.append(split(face_nodes(face) * fold(back)))
-    mortars = dot(
-        jnp.concatenate([backs, own_back[...]], axis=1), jnp.concatenate(sent, axis=0)
-    )
-    result = fold(mortars)
-    seen = dot(faces[...], parts)
+MADE = ("diagonal", "stiff", "mass", "curve", "scale", "one_pick", "one_back", "one_face")
+
+
+def across_faces(seen):
+    leaves = seen.shape[0] // FACES
+    result = jnp.zeros((leaves, LANES), F32)
     for f in range(FACES):
         shift = 3 * 4 ** (2 - f // 2)
         part = fold(seen[leaves * f : leaves * (f + 1), :])
@@ -188,28 +159,56 @@
     return result
 
 
+def side_traces(chosen, faces, table):
+    nodes = jnp.concatenate([face_nodes(face).astype(BF16) for face in faces], axis=0)
+    axes = jnp.concatenate([on_axis(face) for face in faces], axis=0)
+    nodes = jnp.concatenate([nodes, nodes], axis=1)
+    trace = dot(chosen.astype(BF16) * nodes, table[TRACES_AT : TRACES_AT + 256, :])
+    return trace.astype(BF16) * axes
+
+
+def lift(trace, faces, table):
+    mask = jnp.concatenate([face_nodes(opposite(face)) for face in faces], axis=0)
+    return [
+        split(mask * fold(dot(trace, table[FINE_AT + 256 * q : FINE_AT + 256 * (q + 1), :])))
+        for q in range(4)
+    ]
+
+
+def lower(traces, face, table, last):
+    back = dot(jnp.concatenate(traces, axis=1), table[COARSE_AT:last, :])
+    return split(face_nodes(face) * fold(back))
+
+
+def from_blocks(parts, faces, fine, picks, backs, coarse_faces, face, own_back, table, own):
+    slots = own_back.shape[1]
+    rows = jnp.concatenate(parts, axis=0)
+    seen = dot(jnp.concatenate(faces, axis=1), rows)
+    chosen = [dot(jnp.concatenate(fine, axis=1), rows)]
+    chosen += [dot(pick_rows, part) for pick_rows, part in zip(picks, parts)]
+    trace = side_traces(
+        jnp.concatenate(chosen, axis=0), [opposite(face)] * 4 + coarse_faces, table
+    )
+    quarters = [trace[slots * q : slots * (q + 1), :] for q in range(4)]
+    sent = lift(trace[4 * slots :, :], coarse_faces, table)
+    ordered = [
+        sent[q][slots * k : slots * (k + 1), :] for k in range(len(parts)) for q in range(4)
+    ]
+    if own:
+        quarters.append(trace[4 * slots : 5 * slots, :])
+    ordered.append(lower(quarters, face, table, TABLE_ROWS if own else STAY_AT))
+    mortars = dot(jnp.concatenate(backs + [own_back], axis=1), jnp.concatenate(ordered, axis=0))
+    return fold(mortars) + across_faces(seen)
+
+
 def placed(lapped):
     first = lax.broadcasted_iota(jnp.int32, lapped.shape, 1) < NODES
     return jnp.where(first, -EPS_WEIGHT, TAU_WEIGHT) * pltpu.roll(lapped, NODES, 1)
 
 
-def own_part(rows, vector, diagonal, kept, table):
-    parts = split(rows)
-    lapped = (
-        diagonal * rows
-        + fold(dot(parts, kept["stiff"][...]))
-        - from_rows(
-            parts, (kept["own"], kept["own_fine"]), kept["own_pick"][...],
-            kept["fine_back"][...], kept["face"][...], kept, table, own=True,
-        )
-    )
-    swapped = pltpu.roll(vector, NODES, 1)
-    return kept["mass"][...] * vector + kept["curve"][...] * swapped + placed(lapped)
-
-
-def fine_count(back, face):
-    weights = face_nodes(opposite(face)).astype(BF16)
-    return dot(back, jnp.concatenate([weights] * 4, axis=0))
+def fine_count(backs, faces):
+    weights = [face_nodes(opposite(face)).astype(BF16) for face in faces for _ in range(4)]
+    return dot(jnp.concatenate(backs, axis=1), jnp.concatenate(weights, axis=0))
 
 
 def own_index(index, offset):
@@ -227,41 +226,72 @@
     )
 
 
-def choose_kernel(place_ref, pack_ref, neighbours_ref, same_ref, *refs):
+def choose(refs, kinds, columns, neighbours, leaves):
+    slots = columns.shape[0]
+    for faces_ref, fine_ref, start in kinds:
+        places = to_columns(own_index(neighbours, start))
+        for f in range(FACES):
+            refs[faces_ref][leaves * f : leaves * (f + 1), :] = pick(
+                places[:, f : f + 1], (leaves, leaves), 1
+            )
+        fine = own_index(columns, start)
+        for q in range(4):
+            refs[fine_ref][slots * q : slots * (q + 1), :] = pick(
+                fine[:, 2 + q : 3 + q], (slots, leaves), 1
+            )
+
+
+def read_tables(pack_ref, leaves):
+    table = pack_ref[leaves : leaves + 8, :]
+    columns = table.T
+    scale = jnp.concatenate([columns[:, 6:7], columns[:, 7:8]], axis=0)
+    return table.astype(jnp.int32) - 1, columns.astype(jnp.int32) - 1, scale
+
+
+def pad_rows(neighbours):
+    return jnp.concatenate(
+        [neighbours, jnp.full((2, neighbours.shape[1]), -1, jnp.int32)], axis=0
+    )
+
+
+def choose_kernel(place_ref, pack_ref, neighbours_ref, *refs):
     made = dict(zip(CHOSEN, refs))
-    same_ref[...] = pack_ref[...]
     leaves = pack_ref.shape[0] - 8
     offset, first = place_ref[0:1, 0:1], place_ref[0:1, 1:2]
-    mortars = pack_ref[leaves : leaves + 8, :].astype(jnp.int32) - 1
-    columns = to_columns(pack_ref[leaves : leaves + 8, :]) - 1
+    mortars, columns, _ = read_tables(pack_ref, leaves)
     slots = mortars.shape[1]
     made["face"][...] = columns[:, 1:2]
     made["fine_back"][...] = fine_backs(mortars, offset, leaves)
     made["own_back"][...] = pick(mortars[0:1, :] - offset, (leaves, slots), 0)
     made["own_pick"][...] = pick(columns[:, 0:1] - offset, (slots, leaves), 1)
-    neighbours = jnp.concatenate(
-        [neighbours_ref[...], jnp.full((2, leaves), -1, jnp.int32)], axis=0
-    )
-    for name, start in (("own", offset), ("one", offset + first), ("two", offset - first)):
-        places = to_columns(own_index(neighbours, start))
-        for f in range(FACES):
-            made[name][leaves * f : leaves * (f + 1), :] = pick(
-                places[:, f : f + 1], (leaves, leaves), 1
-            )
-        fine = own_index(columns, start)
-        for q in range(4):
-            made[name + "_fine"][slots * q : slots * (q + 1), :] = pick(
-                fine[:, 2 + q : 3 + q], (slots, leaves), 1
-            )
-
-
-def near_kernel(pack_ref, table, mass_ref, curve_ref, stiffness_ref, levels_ref, *refs):
-    names = KEPT_OWN[:6]
-    kept = dict(zip(names + LOCAL, refs))
-    partial_ref = refs[len(names) + len(LOCAL)]
+    kinds = (("own", "own_fine", offset), ("one", "one_fine", offset + first))
+    choose(made, kinds, columns, pad_rows(neighbours_ref[...]), leaves)
+
+
+def image_of(vector, lapped, kept):
+    swapped = pltpu.roll(vector, NODES, 1)
+    return kept["mass"][...] * vector + kept["curve"][...] * swapped + placed(lapped)
+
+
+def first_kernel(
+    place_ref, pack_ref, other_ref, table, mass_ref, curve_ref, stiffness_ref, levels_ref, *refs
+):
+    kept = dict(zip(CHOSEN + MADE, refs))
+    image_ref, far_ref = refs[len(CHOSEN) + len(MADE) :]
     leaves = pack_ref.shape[0] - 8
-    diagonal = fine_count(kept["fine_back"][...], kept["face"][...]) + sum(
-        face_nodes(jnp.int32(f)) for f in range(FACES)
+    offset, first = place_ref[0:1, 0:1], place_ref[0:1, 1:2]
+    mortars, columns, _ = read_tables(other_ref, leaves)
+    slots = mortars.shape[1]
+    face, other_face = kept["face"][...], columns[:, 1:2]
+    other_pick = pick(columns[:, 0:1] - (offset + first), (slots, leaves), 1)
+    other_back = fine_backs(mortars, offset, leaves)
+    kept["one_pick"][...] = other_pick
+    kept["one_back"][...] = other_back
+    kept["one_face"][...] = other_face
+    back = kept["fine_back"][...]
+    diagonal = (
+        fine_count([back, other_back], [face, other_face])
+        + sum(face_nodes(jnp.int32(f)) for f in range(FACES))
     )
     kept["diagonal"][...] = diagonal
     wide = jnp.concatenate([stiffness_ref[...]] * 2, axis=1)
@@ -270,54 +300,111 @@
         lax.broadcasted_iota(jnp.int32, wide.shape, 1) < NODES
     )
     wide = split(jnp.where(same, wide, 0.0))
-    kept["stiff"][...] = jnp.concatenate([wide, wide], axis=0)
+    wide = jnp.concatenate([wide, wide], axis=0)
+    kept["stiff"][...] = wide
     kept["mass"][...] = jnp.concatenate([mass_ref[...]] * 2, axis=0).T
     curve = curve_ref[...]
     kept["curve"][...] = jnp.concatenate([-curve, jnp.zeros_like(curve)], axis=0).T
     scale = level_rows(levels_ref[...])
     kept["scale"][...] = scale
     rows = pack_ref[0:leaves, :]
-    partial_ref[...] = own_part(rows, rows / scale, diagonal, kept, table)
-
-
-def first_side(
-    place_ref, table, pack_ref, other_ref, partial_ref, diagonal_ref, faces_ref, fine_ref, kept,
-    made, direction,
+    parts = [split(rows), split(other_ref[0:leaves, :])]
+    lapped = diagonal * rows + fold(dot(parts[0], wide)) - from_blocks(
+        parts,
+        [kept["own"][...], kept["one"][...]],
+        [kept["own_fine"][...], kept["one_fine"][...]],
+        [kept["own_pick"][...], other_pick],
+        [back, other_back],
+        [face, other_face],
+        face,
+        kept["own_back"][...],
+        table,
+        True,
+    )
+    image = image_of(rows / scale, lapped, kept)
+    image_ref[...] = image
+    far_ref[0 : leaves + 8, :] = pack_ref[...]
+    far_ref[leaves + 8 :, :] = image * scale
+
+
+def over_there_kernel(
+    place_ref, pack_ref, neighbours_ref, table, scale_ref, face_ref, own_pick_ref, two_ref,
+    two_fine_ref, given_ref, extra_ref, zero_ref, length_ref
 ):
-    picks_ref, backs_ref, face_ref, total_ref = made
     leaves = pack_ref.shape[0] - 8
-    mortars = other_ref[leaves : leaves + 8, :]
-    columns = to_columns(mortars) - 1
-    mortars = mortars.astype(jnp.int32) - 1
+    offset = place_ref[0:1, 0:1]
+    far = offset - place_ref[0:1, 1:2]
+    mortars, columns, _ = read_tables(pack_ref, leaves)
+    neighbours = pad_rows(neighbours_ref[...])
+    choose((two_ref, two_fine_ref), ((0, 1, far),), columns, neighbours, leaves)
+    face = face_ref[...]
+    rows = pack_ref[0:leaves, :]
+    parts = split(rows)
+    index = own_index(neighbours, far)
+    seen = jnp.concatenate(
+        [dot(pick(index[f ^ 1 : (f ^ 1) + 1, :], (leaves, leaves), 0), parts) for f in range(FACES)],
+        axis=0,
+    )
+    back = fine_backs(mortars, far, leaves)
+    trace = side_traces(dot(own_pick_ref[...], parts), [face], table)
+    sent = jnp.concatenate(lift(trace, [face], table), axis=0)
+    given_ref[...] = -across_faces(seen) - fold(dot(back, sent))
+    extra_ref[...] = fine_count([back], [face])
+    length, zero = unit(rows / scale_ref[...])
+    zero_ref[...] = zero
+    length_ref[...] = length
+
+
+def far_kernel(
+    place_ref, pack_ref, far_ref, table, scale_ref, diagonal_ref, partial_ref, two_ref,
+    two_fine_ref, own_back_ref, face_ref, image_ref, send_ref, pick_ref, back_ref, far_face_ref,
+    total_ref
+):
+    leaves = pack_ref.shape[0] - 8
+    offset = place_ref[0:1, 0:1]
+    mortars, columns, _ = read_tables(far_ref, leaves)
     slots = mortars.shape[1]
     face = columns[:, 1:2]
+    chosen = pick(columns[:, 0:1] - (offset - place_ref[0:1, 1:2]), (slots, leaves), 1)
+    back = fine_backs(mortars, offset, leaves)
+    pick_ref[...] = chosen
+    back_ref[...] = back
+    far_face_ref[...] = face
+    extra = fine_count([back], [face])
+    total_ref[...] = diagonal_ref[...] + extra
+    lapped = extra * pack_ref[0:leaves, :] - from_blocks(
+        [split(far_ref[0:leaves, :])], [two_ref[...]], [two_fine_ref[...]], [chosen], [back],
+        [face], face_ref[...], own_back_ref[...], table, False,
+    )
+    image = partial_ref[...] + placed(lapped)
+    image_ref[...] = image
+    send_ref[...] = image * scale_ref[...]
+
+
+def far_rows_kernel(
+    place_ref, pack_ref, far_ref, table, given_ref, extra_ref, image_ref, rows_ref, turned_ref
+):
+    leaves = pack_ref.shape[0] - 8
     offset = place_ref[0:1, 0:1]
-    start = offset + direction * place_ref[0:1, 1:2]
-    picks = pick(columns[:, 0:1] - start, (slots, leaves), 1)
-    backs = fine_backs(mortars, offset, leaves)
-    extra = fine_count(backs, face)
-    picks_ref[...] = picks
-    backs_ref[...] = backs
-    face_ref[...] = face
-    total_ref[...] = diagonal_ref[...] + extra
-    lapped = extra * pack_ref[0:leaves, :] - from_rows(
-        split(other_ref[0:leaves, :]), (faces_ref, fine_ref), picks, backs, face, kept, table
-    )
-    return partial_ref[...] + placed(lapped)
-
-
-def first_one_kernel(*refs):
-    kept = dict(zip(KEPT_SIDE, refs[8:]))
-    refs, rest = refs[:8], refs[8 + len(KEPT_SIDE) :]
-    rest[0][...] = first_side(*refs, kept, rest[1:], 1)
-
-
-def first_two_kernel(scale_ref, *refs):
-    kept = dict(zip(KEPT_SIDE, refs[8:]))
-    refs, rest = refs[:8], refs[8 + len(KEPT_SIDE) :]
-    image = first_side(*refs, kept, rest[2:], -1)
-    rest[0][...] = image
-    rest[1][...] = image * scale_ref[...]
+    mortars, columns, scale = read_tables(far_ref, leaves)
+    slots = mortars.shape[1]
+    face = columns[:, 1:2]
+    fine = own_index(columns, offset)
+    fine = jnp.concatenate(
+        [pick(fine[:, 2 + q : 3 + q], (slots, leaves), 1) for q in range(4)], axis=0
+    )
+    trace = side_traces(
+        dot(fine, split(pack_ref[0:leaves, :])), [opposite(face)] * 4, table
+    )
+    quarters = [trace[slots * q : slots * (q + 1), :] for q in range(4)]
+    back = pick(mortars[0:1, :] - (offset - place_ref[0:1, 1:2]), (leaves, slots), 0)
+    lapped = (
+        given_ref[...]
+        + extra_ref[...] * far_ref[0:leaves, :]
+        - fold(dot(back, lower(quarters, face, table, STAY_AT)))
+    )
+    rows_ref[...] = far_ref[leaves + 8 :, :] + scale * placed(lapped)
+    turned_ref[...] = image_ref[...].T
 
 
 def total(values):
@@ -337,53 +424,39 @@
     return row
 
 
-def factor_kernel(pack_ref, send_ref, image_ref, scale_ref, *refs):
-    same_ref, zero_ref, one_ref, stats_ref, turned_ref = refs
-    same_ref[...] = send_ref[...]
-    image = image_ref[...]
-    turned_ref[...] = image.T
-    r00, zero = unit(pack_ref[0 : image.shape[0], :] / scale_ref[...])
+def second_kernel(
+    table, send_ref, one_ref, two_ref, image_ref, total_ref, zero_ref, length_ref, faces_two_ref,
+    two_fine_ref, two_pick_ref, two_back_ref, two_face_ref, *refs
+):
+    kept = dict(zip(CHOSEN + MADE[1:], refs))
+    stats_ref = refs[len(CHOSEN) + len(MADE) - 1]
+    image, zero = image_ref[...], zero_ref[...]
     r01 = total(zero * image)
-    image = image - r01 * zero
-    again = total(zero * image)
-    r11, one = unit(image - again * zero)
-    zero_ref[...] = zero
-    one_ref[...] = one
-    stats_ref[...] = in_lanes(stats_ref.shape, (r00, r01 + again, r11))
-
-
-def again_kernel(table, send_ref, image_ref, total_ref, *refs):
-    kept = dict(zip(KEPT_OWN, refs))
-    refs[len(KEPT_OWN)][...] = own_part(
-        send_ref[...], image_ref[...], total_ref[...], kept, table
-    )
-
-
-def second_side(
-    table, other_ref, partial_ref, faces_ref, fine_ref, picks_ref, backs_ref, face_ref, kept
-):
-    lapped = from_rows(
-        split(other_ref[...]), (faces_ref, fine_ref), picks_ref[...], backs_ref[...],
-        face_ref[...], kept, table,
-    )
-    return partial_ref[...] - placed(lapped)
-
-
-def second_one_kernel(*refs):
-    refs, rest = refs[:8], refs[8:]
-    rest[len(KEPT_SIDE)][...] = second_side(*refs, dict(zip(KEPT_SIDE, rest)))
-
-
-def second_two_kernel(zero_ref, one_ref, known_ref, *refs):
-    refs, rest = refs[:8], refs[8:]
-    stats_ref = rest[len(KEPT_SIDE)]
-    image = second_side(*refs, dict(zip(KEPT_SIDE, rest)))
-    zero, one = zero_ref[...], one_ref[...]
+    rest = image - r01 * zero
+    again = total(zero * rest)
+    r11, one = unit(rest - again * zero)
+    rows = send_ref[...]
+    parts = [split(rows), split(one_ref[...]), split(two_ref[...])]
+    face = kept["face"][...]
+    lapped = total_ref[...] * rows + fold(dot(parts[0], kept["stiff"][...])) - from_blocks(
+        parts,
+        [kept["own"][...], kept["one"][...], faces_two_ref[...]],
+        [kept["own_fine"][...], kept["one_fine"][...], two_fine_ref[...]],
+        [kept["own_pick"][...], kept["one_pick"][...], two_pick_ref[...]],
+        [kept["fine_back"][...], kept["one_back"][...], two_back_ref[...]],
+        [face, kept["one_face"][...], two_face_ref[...]],
+        face,
+        kept["own_back"][...],
+        table,
+        True,
+    )
+    image = image_of(image, lapped, kept)
     r02 = total(zero * image)
     r12 = total(one * image)
     rest = image - r02 * zero - r12 * one
     r22 = jnp.sqrt(total(rest * rest))
-    stats_ref[...] = known_ref[...] + in_lanes(stats_ref.shape, (0.0, 0.0, 0.0, r02, r12, r22))
+    values = (length_ref[...], r01 + again, r11, r02, r12, r22)
+    stats_ref[...] = in_lanes(stats_ref.shape, values)
 
 
 def final_kernel(stats_ref, cot_ref, image_ref, out_ref):
@@ -461,10 +534,8 @@
     shapes = dict(
         own=faces,
         one=faces,
-        two=faces,
         own_fine=fine,
         one_fine=fine,
-        two_fine=fine,
         own_pick=picks,
         own_back=shape(leaves, slots, dtype=BF16),
         fine_back=backs,
@@ -474,6 +545,9 @@
         mass=rows,
         curve=rows,
         scale=rows,
+        one_pick=picks,
+        one_back=backs,
+        one_face=face,
     )
 
     def stay_out(*arrays):
@@ -493,77 +567,53 @@
         flops=10_000_000_000,
         moved=4_000_000,
     )
-    two = lax.ppermute(pack, "leaf", pairs_two)
-    same, *chosen = call(
+    one = lax.ppermute(pack, "leaf", pairs_one)
+    chosen = call(
         choose_kernel,
-        [shape(leaves + 8, LANES)] + [shapes[name] for name in CHOSEN],
+        [shapes[name] for name in CHOSEN],
         [vmem] * 3,
         (place, pack, neighbours),
         flops=1_000_000_000,
         moved=2_000_000,
     )
-    kept = dict(zip(CHOSEN, chosen))
-    one = lax.ppermute(same, "leaf", pairs_one)
-    own = KEPT_OWN[:6]
-    *local, partial = call(
-        near_kernel,
-        [shapes[name] for name in LOCAL] + [rows],
-        [vmem] * (6 + len(own)),
-        [pack, table, nodal_mass, curvature, stiffness, levels] + [kept[name] for name in own],
+    *made, partial, far = call(
+        first_kernel,
+        [shapes[name] for name in MADE] + [rows, shape(2 * leaves + 8, LANES)],
+        [vmem] * (8 + len(CHOSEN)),
+        [place, pack, one, table, nodal_mass, curvature, stiffness, levels, *chosen],
+    )
+    kept = dict(zip(CHOSEN + MADE, [*chosen, *made]))
+    far = lax.ppermute(far, "leaf", pairs_two)
+    faces_two, two_fine, given, extra, zero, length = call(
+        over_there_kernel,
+        [faces, fine, rows, rows, rows, shape(1, 1)],
+        [vmem] * 7,
+        [place, pack, neighbours, table, kept["scale"], kept["face"], kept["own_pick"]],
         flops=2_000_000_000,
         moved=4_000_000,
     )
-    kept.update(zip(LOCAL, local))
-    side = [kept[name] for name in KEPT_SIDE]
-    made = [picks, backs, face, rows]
-    partial, *made_one = call(
-        first_one_kernel,
-        [rows] + made,
-        [vmem] * (8 + len(side)),
-        [place, table, pack, one, partial, kept["diagonal"], kept["one"],
-         kept["one_fine"]] + side,
+    image, send, two_pick, two_back, two_face, diagonal = call(
+        far_kernel,
+        [rows, rows, picks, backs, face, rows],
+        [vmem] * 11,
+        [place, pack, far, table, kept["scale"], kept["diagonal"], partial, faces_two, two_fine,
+         kept["own_back"], kept["face"]],
+    )
+    one = lax.ppermute(send, "leaf", pairs_one)
+    two, turned = call(
+        far_rows_kernel,
+        [rows, shape(LANES, leaves)],
+        [vmem] * 7,
+        [place, pack, far, table, given, extra, image],
         flops=1_000_000_000,
         moved=2_000_000,
     )
-    image, send, *made_two = call(
-        first_two_kernel,
-        [rows, rows] + made,
-        [vmem] * (9 + len(side)),
-        [kept["scale"], place, table, pack, two, partial, made_one[3], kept["two"],
-         kept["two_fine"]] + side,
-    )
-    two = lax.ppermute(send, "leaf", pairs_two)
-    same, zero, unit_one, known, turned = call(
-        factor_kernel,
-        [rows, rows, rows, shape(1, LANES), shape(LANES, leaves)],
-        [vmem] * 4,
-        [pack, send, image, kept["scale"]],
-        flops=1_000_000_000,
-        moved=2_000_000,
-    )
-    one = lax.ppermute(same, "leaf", pairs_one)
-    partial = call(
-        again_kernel,
-        rows,
-        [vmem] * (4 + len(KEPT_OWN)),
-        [table, send, image, made_two[3]] + [kept[name] for name in KEPT_OWN],
-        flops=2_000_000_000,
-        moved=4_000_000,
-    )
-    partial = call(
-        second_one_kernel,
-        rows,
-        [vmem] * (8 + len(side)),
-        [table, one, partial, kept["one"], kept["one_fine"], *made_one[:3]] + side,
-        flops=1_000_000_000,
-        moved=2_000_000,
-    )
     stats = call(
-        second_two_kernel,
+        second_kernel,
         shape(1, LANES),
-        [vmem] * (11 + len(side)),
-        [zero, unit_one, known, table, two, partial, kept["two"], kept["two_fine"], *made_two[:3]]
-        + side,
+        [vmem] * (13 + len(CHOSEN) + len(MADE) - 1),
+        [table, send, one, two, image, diagonal, zero, length, faces_two, two_fine, two_pick,
+         two_back, two_face] + [kept[name] for name in CHOSEN + MADE[1:]],
     )
     gathered = lax.all_to_all(
         jnp.broadcast_to(stats, (count, LANES)), "leaf", 0, 0, tiled=True

time: 53.1 us -> 51.2 us (0.964)
  waiting for transfers between devices: 0.02 us -> 4.72 us
  blocking collectives: 30.9 us -> 27.9 us
  starting transfers between devices: 8.33 us -> 5.34 us
  Pallas kernels: 13.3 us -> 12.4 us
    ppermute x4 -> x3, waiting for transfers between devices: 0.02 us -> 4.72 us  [the longest x1 4.26 us: on_device(): far = lax.ppermute(far, 'leaf', pairs_two)]
    ppermute x4 -> x3, starting transfers between devices: 8.33 us -> 5.34 us  [the longest x1 3.33 us: on_device(): one = lax.ppermute(pack, 'leaf', pairs_one)]
    all_to_all x1, blocking collectives: 30.9 us -> 27.9 us  [on_device(): lax.all_to_all(jnp.broadcast_to(stats, (count, LANES)), 'leaf', 0, 0, til...]
    pallas_call x10 -> x8, Pallas kernels: 13.3 us -> 12.4 us  [call(): pl.pallas_call(kernel, out_shape=outs, in_specs=specs, out_specs=jax.tree...]
  transfers between devices with their start and end apart: 4 -> 3, of which waited for: 0 -> 3; matrix products, arithmetic and copies ran while one was open for 0% -> 0% of each run, Pallas kernels for 15% -> 6%
where the time goes in v7:
time: 51.2 us; the launch traced here: 51 us
  blocking collectives  27.9 us (54%)
  Pallas kernels  12.4 us (24%)
  starting transfers between devices  5.34 us (10%)
  waiting for transfers between devices  4.72 us (9%)
    all_to_all x1, blocking collectives, on_device(): lax.all_to_all(jnp.broadcast_to(stats, (count, LANES)), 'leaf', 0, 0, til...  27.9 us
    pallas_call x8, Pallas kernels, call(): pl.pallas_call(kernel, out_shape=outs, in_specs=specs, out_specs=jax.tree...  12.4 us
    ppermute x1, waiting for transfers between devices, on_device(): far = lax.ppermute(far, 'leaf', pairs_two)  4.26 us
    ppermute x1, starting transfers between devices, on_device(): one = lax.ppermute(pack, 'leaf', pairs_one)  3.33 us
    ppermute x1, starting transfers between devices, on_device(): far = lax.ppermute(far, 'leaf', pairs_two)  1.92 us
  transfers between devices with their start and end apart: 3, of which 3 were waited for; matrix products, arithmetic and copies ran while one was open for 0% of the time, Pallas kernels for 6%

profile of v7, /device:TPU:1, one launch (start us, length us, event | category | flops | bytes accessed | tf_op | source)
XLA Modules:
  0.0 51.0 jit_solution(9500327288281691696)
XLA Ops:
  0.0 0.0 copy-start.6
  0.0 1.1 %shard_map.82.pack_ref = f32[264,128]{1,0:T(8,128)S(1)} custom-call(f32[128,256]{1,0:T(8,128)} %bitcast.10, s32[1,256]{1,0:T(1,128)} %bitcast.13, s32[6,128]{1,0:T(8,128)} %mortars_hbm.1), custom_call_target="tpu_custom_call" | custom-call | flops 10000000000 | bytes 4000000 | tf_op jit(solution)/shard_map/pallas_call | solution.py:510
  1.1 3.3 %collective-permute-start = (f32[264,128]{1,0:T(8,128)S(1)}, f32[264,128]{1,0:T(8,128)S(1)}, u32[]{:S(2)}, u32[]{:S(2)}) collective-permute-start(f32[264,128]{1,0:T(8,128)S(1)} %shard_map.82.pack_ref), channel_id=1, source_target_pairs={{0,1},{1,0},{2,3},{3,2},{4,5},{5,4},{6,7},{7,6},{8,9},{9,8},{10,11... | collective-permute-start | bytes 405512 | tf_op jit(solution)/shard_map/ppermute | solution.py:570
  4.4 0.1 add_bitcast_fusion.place_ref
  4.5 0.0 copy-done.6
  4.5 0.0 copy-start
  4.5 0.0 copy-start.2
  4.5 0.0 copy-start.3
  4.5 0.0 copy-start.4
  4.5 0.0 copy-start.5
  4.5 0.8 %shard_map.83 = (bf16[1536,256]{1,0:T(8,128)(2,1)S(1)}, bf16[1536,256]{1,0:T(8,128)(2,1)S(1)}, bf16[512,256]{1,0:T(8,128)(2,1)S(1)}, bf16[512,256]{1,0:T(8,128)(...) custom-call(s32[1,2]{1,0:T(1,128)S(1)} %add_bitcast_fusion.place_ref, ...), custom_call_target="tpu_custom_call" | custom-call | flops 1000000000 | bytes 2000000 | tf_op jit(solution)/shard_map/pallas_call | solution.py:510
  5.3 0.1 collective-permute-done.other_ref
  5.4 0.4 copy-done
  5.8 0.0 copy-done.2
  5.8 0.0 copy-done.3
  5.8 0.0 copy-done.4
  5.8 0.0 copy-done.5
  5.8 2.3 %shard_map.84 = (f32[256,128]{1,0:T(8,128)S(1)}, bf16[256,256]{1,0:T(8,128)(2,1)S(1)}, f32[256,128]{1,0:T(8,128)S(1)}, f32[256,128]{1,0:T(8,128)S(1)}, f32[256,1...) custom-call(s32[1,2]{1,0:T(1,128)S(1)} %add_bitcast_fusion.place_ref, ...), custom_call_target="tpu_custom_call" | custom-call | tf_op jit(solution)/shard_map/pallas_call | solution.py:510
  8.2 1.9 %collective-permute-start.1 = (f32[520,128]{1,0:T(8,128)S(1)}, f32[520,128]{1,0:T(8,128)S(1)}, u32[]{:S(2)}, u32[]{:S(2)}) collective-permute-start(f32[520,128]{1,0:T(8,128)S(1)} %get-tuple-element.45), channel_id=1, source_target_pairs={{1,2},{3,4},{5,6},{7,8},{9,10},{11,12},{13,14},{15,16},{17,18},{19... | collective-permute-start | bytes 798728 | tf_op jit(solution)/shard_map/ppermute | solution.py:586
  10.1 1.5 %shard_map.85 = (bf16[1536,256]{1,0:T(8,128)(2,1)S(1)}, bf16[512,256]{1,0:T(8,128)(2,1)S(1)}, f32[256,128]{1,0:T(8,128)S(1)}, f32[256,128]{1,0:T(8,128)S(1)}, f32[256,128]{1,0:T(8,128)S(1)}, /*index=5*/f32[1,1]{1,0:T(1,128)}) custom-call(s32[1,2]{1,0:T(1,128)S(1)} %add_bitcast_fusion.place_ref, f32[264,128]{1,0:T(8,128)S(1)} %shard_map.82.pack_ref, ...), custom_call_target="tpu_custom_call" | custom-call | flops 2000000000 | bytes 4000000 | tf_op jit(solution)/shard_map/pallas_call | solution.py:510
  11.6 4.3 %collective-permute-done.1.far_ref = f32[520,128]{1,0:T(8,128)S(1)} collective-permute-done((f32[520,128]{1,0:T(8,128)S(1)}, f32[520,128]{1,0:T(8,128)S(1)}, u32[]{:S(2)}, u32[]{:S(2)}) %collective-permute-start.1) | collective-permute-done | bytes 266272 | tf_op jit(solution)/shard_map/ppermute | solution.py:586
  15.9 1.4 %shard_map.86 = (f32[256,128]{1,0:T(8,128)S(1)}, f32[256,128]{1,0:T(8,128)S(1)}, bf16[128,256]{1,0:T(8,128)(2,1)S(1)}, bf16[256,512]{1,0:T(8,128)(2,1)S(1)}, s32...) custom-call(s32[1,2]{1,0:T(1,128)S(1)} %add_bitcast_fusion.place_ref, f32[264,128]{1,0:T(8,128)S(1)} %shard_map.82.pack_ref, ...), custom_call_target="tpu_custom_call" | custom-call | tf_op jit(solution)/shard_map/pallas_call | solution.py:510
  17.2 0.1 collective-permute-start.2
  17.4 1.0 %shard_map.87 = (f32[256,128]{1,0:T(8,128)S(1)}, f32[128,256]{1,0:T(8,128)S(1)}) custom-call(s32[1,2]{1,0:T(1,128)S(1)} %add_bitcast_fusion.place_ref, f32[264,128]{1,0:T(8,128)S(1)} %shard_map.82.pack_ref, f32[520,128]{1,0:T(8,128)S(1)} %collective-permute-done.1.far_ref, bf16[2560,256]{1,0:T(8,128)(2,1)S(1)} %copy-done, ...), custom_call_target="tpu_custom_call" | custom-call | flops 1000000000 | bytes 2000000 | tf_op jit(solution)/shard_map/pallas_call | solution.py:510
  18.3 0.4 collective-permute-done.2.one_ref
  18.7 0.0 copy-start.1
  18.7 3.2 %shard_map.88 = f32[1,128]{1,0:T(1,128)S(1)} custom-call(bf16[2560,256]{1,0:T(8,128)(2,1)S(1)} %copy-done, f32[256,128]{1,0:T(8,128)S(1)} %get-tuple-element.51.send_ref, f32[256,128]{1,0:T(8,128)S(1)} %collective-permute-done.2.one_ref, f32[256,128]{1,0:T(8,128)S(1)} %get-tuple-element.55.two_ref, f32[256,128]{1,0:T(8,128)S(1)} %get-tuple-element.54.image_ref, ...), custom_call_target="tpu_custom_call" | custom-call | tf_op jit(solution)/shard_map/pallas_call | solution.py:510
  21.9 0.1 broadcast_in_dim.2
  21.9 27.9 %all_to_all.8 = f32[256,1,128]{2,1,0:T(1,128)S(1)} all-to-all(f32[256,1,128]{2,1,0:T(1,128)S(1)} %broadcast_in_dim.2), channel_id=1, replica_groups=mesh['leaf'=256] {'leaf'}, dimensions={0} | all-to-all | bytes 262144 | tf_op jit(solution)/shard_map/all_to_all | solution.py:618
  49.9 0.0 copy-done.1
  49.9 1.2 %shard_map.89 = f32[128,256]{1,0:T(8,128)} custom-call(f32[256,128]{1,0:T(8,128)S(1)} %bitcast.9, f32[128,256]{1,0:T(8,128)S(1)} %bitcast.11, f32[128,256]{1,0:T(8,128)S(1)} %get-tuple-element.68.image_ref), custom_call_target="tpu_custom_call" | custom-call | tf_op jit(solution)/shard_map/pallas_call | solution.py:510
Async XLA Ops:
  0.0 4.5 %copy-start.6 = (s32[6,256]{1,0:T(8,128)S(1)}, s32[6,256]{1,0:T(8,128)}, u32[]{:S(2)}) copy-start(s32[6,256]{1,0:T(8,128)} %neighbours_ref.3) | copy-start | bytes 18436
  1.1 4.3 %collective-permute-start = (f32[264,128]{1,0:T(8,128)S(1)}, f32[264,128]{1,0:T(8,128)S(1)}, u32[]{:S(2)}, u32[]{:S(2)}) collective-permute-start(f32[264,128]{1,0:T(8,128)S(1)} %shard_map.82.pack_ref), channel_id=1, source_target_pairs={{0,1},{1,0},{2,3},{3,2},{4,5},{5,4},{6,7},{7,6},{8,9},{9,8},{10,11... | collective-permute-start | bytes 405512 | tf_op jit(solution)/shard_map/ppermute | solution.py:570
  4.5 1.3 %copy-start = (bf16[2560,256]{1,0:T(8,128)(2,1)S(1)}, bf16[2560,256]{1,0:T(8,128)(2,1)}, u32[]{:S(2)}) copy-start(bf16[2560,256]{1,0:T(8,128)(2,1)} %constant.12.clone.table) | copy-start | bytes 3932164
  4.5 1.3 %copy-start.2 = (f32[64,256]{1,0:T(8,128)S(1)}, f32[64,256]{1,0:T(8,128)}, u32[]{:S(2)}) copy-start(f32[64,256]{1,0:T(8,128)} %mass_ref.1) | copy-start | bytes 196612
  4.5 1.3 %copy-start.3 = (f32[64,256]{1,0:T(8,128)S(1)}, f32[64,256]{1,0:T(8,128)}, u32[]{:S(2)}) copy-start(f32[64,256]{1,0:T(8,128)} %curve_ref.1) | copy-start | bytes 196612
  4.5 1.3 %copy-start.4 = (f32[64,64]{1,0:T(8,128)S(1)}, f32[64,64]{1,0:T(8,128)}, u32[]{:S(2)}) copy-start(f32[64,64]{1,0:T(8,128)} %stiffness_ref.1) | copy-start | bytes 49156
  4.5 1.3 %copy-start.5 = (s32[256]{0:T(256)S(1)}, s32[256]{0:T(256)}, u32[]{:S(2)}) copy-start(s32[256]{0:T(256)} %param.12) | copy-start | bytes 3076
  8.2 7.7 %collective-permute-start.1 = (f32[520,128]{1,0:T(8,128)S(1)}, f32[520,128]{1,0:T(8,128)S(1)}, u32[]{:S(2)}, u32[]{:S(2)}) collective-permute-start(f32[520,128]{1,0:T(8,128)S(1)} %get-tuple-element.45), channel_id=1, source_target_pairs={{1,2},{3,4},{5,6},{7,8},{9,10},{11,12},{13,14},{15,16},{17,18},{19... | collective-permute-start | bytes 798728 | tf_op jit(solution)/shard_map/ppermute | solution.py:586
  17.2 1.4 %collective-permute-start.2 = (f32[256,128]{1,0:T(8,128)S(1)}, f32[256,128]{1,0:T(8,128)S(1)}, u32[]{:S(2)}, u32[]{:S(2)}) collective-permute-start(f32[256,128]{1,0:T(8,128)S(1)} %get-tuple-element.51.send_ref), channel_id=1, source_target_pairs={{0,1},{1,0},{2,3},{3,2},{4,5},{5,4},{6,7},{7,6},{8,9},{9,8},{10,11... | collective-permute-start | bytes 393224 | tf_op jit(solution)/shard_map/ppermute | solution.py:602
  18.7 31.2 %copy-start.1 = (f32[2,64,256]{2,1,0:T(8,128)S(1)}, f32[2,64,256]{2,1,0:T(8,128)}, u32[]{:S(2)}) copy-start(f32[2,64,256]{2,1,0:T(8,128)} %param.8) | copy-start | bytes 393220

commit v8 on v7

--- a/solution.py
+++ b/solution.py
@@ -323,8 +323,7 @@
     )
     image = image_of(rows / scale, lapped, kept)
     image_ref[...] = image
-    far_ref[0 : leaves + 8, :] = pack_ref[...]
-    far_ref[leaves + 8 :, :] = image * scale
+    far_ref[...] = image * scale
 
 
 def over_there_kernel(
@@ -403,7 +402,7 @@
         + extra_ref[...] * far_ref[0:leaves, :]
         - fold(dot(back, lower(quarters, face, table, STAY_AT)))
     )
-    rows_ref[...] = far_ref[leaves + 8 :, :] + scale * placed(lapped)
+    rows_ref[...] = scale * placed(lapped)
     turned_ref[...] = image_ref[...].T
 
 
@@ -425,7 +424,7 @@
 
 
 def second_kernel(
-    table, send_ref, one_ref, two_ref, image_ref, total_ref, zero_ref, length_ref, faces_two_ref,
+    table, send_ref, one_ref, two_ref, lacked_ref, image_ref, total_ref, zero_ref, length_ref, faces_two_ref,
     two_fine_ref, two_pick_ref, two_back_ref, two_face_ref, *refs
 ):
     kept = dict(zip(CHOSEN + MADE[1:], refs))
@@ -436,7 +435,7 @@
     again = total(zero * rest)
     r11, one = unit(rest - again * zero)
     rows = send_ref[...]
-    parts = [split(rows), split(one_ref[...]), split(two_ref[...])]
+    parts = [split(rows), split(one_ref[...]), split(two_ref[...] + lacked_ref[...])]
     face = kept["face"][...]
     lapped = total_ref[...] * rows + fold(dot(parts[0], kept["stiff"][...])) - from_blocks(
         parts,
@@ -567,6 +566,7 @@
         flops=10_000_000_000,
         moved=4_000_000,
     )
+    far = lax.ppermute(pack, "leaf", pairs_two)
     one = lax.ppermute(pack, "leaf", pairs_one)
     chosen = call(
         choose_kernel,
@@ -576,14 +576,14 @@
         flops=1_000_000_000,
         moved=2_000_000,
     )
-    *made, partial, far = call(
+    *made, partial, scaled = call(
         first_kernel,
-        [shapes[name] for name in MADE] + [rows, shape(2 * leaves + 8, LANES)],
+        [shapes[name] for name in MADE] + [rows, rows],
         [vmem] * (8 + len(CHOSEN)),
         [place, pack, one, table, nodal_mass, curvature, stiffness, levels, *chosen],
     )
     kept = dict(zip(CHOSEN + MADE, [*chosen, *made]))
-    far = lax.ppermute(far, "leaf", pairs_two)
+    two = lax.ppermute(scaled, "leaf", pairs_two)
     faces_two, two_fine, given, extra, zero, length = call(
         over_there_kernel,
         [faces, fine, rows, rows, rows, shape(1, 1)],
@@ -600,7 +600,7 @@
          kept["own_back"], kept["face"]],
     )
     one = lax.ppermute(send, "leaf", pairs_one)
-    two, turned = call(
+    lacked, turned = call(
         far_rows_kernel,
         [rows, shape(LANES, leaves)],
         [vmem] * 7,
@@ -611,8 +611,8 @@
     stats = call(
         second_kernel,
         shape(1, LANES),
-        [vmem] * (13 + len(CHOSEN) + len(MADE) - 1),
-        [table, send, one, two, image, diagonal, zero, length, faces_two, two_fine, two_pick,
+        [vmem] * (14 + len(CHOSEN) + len(MADE) - 1),
+        [table, send, one, two, lacked, image, diagonal, zero, length, faces_two, two_fine, two_pick,
          two_back, two_face] + [kept[name] for name in CHOSEN + MADE[1:]],
     )
     gathered = lax.all_to_all(

time: 51.2 us -> 50.6 us (0.988)
  waiting for transfers between devices: 4.72 us -> 0.36 us
  starting transfers between devices: 5.34 us -> 8.97 us
    ppermute x1 -> x2, waiting for transfers between devices: 4.26 us -> 0.01 us  [the longest x1 0.01 us: on_device(): far = lax.ppermute(pack, 'leaf', pairs_two)]
    ppermute x1 -> x2, starting transfers between devices: 1.92 us -> 5.55 us  [the longest x1 3.64 us: on_device(): two = lax.ppermute(scaled, 'leaf', pairs_two)]
  transfers between devices with their start and end apart: 3 -> 4, of which waited for: 3 -> 1; matrix products, arithmetic and copies ran while one was open for 0% -> 0% of each run, Pallas kernels for 6% -> 14%
where the time goes in v8:
time: 50.6 us; the launch traced here: 50.4 us
  blocking collectives  28 us (55%)
  Pallas kernels  12.4 us (25%)
  starting transfers between devices  8.97 us (18%)
  local copies, waits for them, and re-layouts  0.59 us (1%)
    all_to_all x1, blocking collectives, on_device(): lax.all_to_all(jnp.broadcast_to(stats, (count, LANES)), 'leaf', 0, 0, til...  28 us
    pallas_call x8, Pallas kernels, call(): pl.pallas_call(kernel, out_shape=outs, in_specs=specs, out_specs=jax.tree...  12.4 us
    ppermute x1, starting transfers between devices, on_device(): two = lax.ppermute(scaled, 'leaf', pairs_two)  3.64 us
    ppermute x1, starting transfers between devices, on_device(): one = lax.ppermute(pack, 'leaf', pairs_one)  3.33 us
    ppermute x1, starting transfers between devices, on_device(): far = lax.ppermute(pack, 'leaf', pairs_two)  1.91 us
  transfers between devices with their start and end apart: 4, of which 1 were waited for; matrix products, arithmetic and copies ran while one was open for 0% of the time, Pallas kernels for 14%

profile of v8, /device:TPU:1, one launch (start us, length us, event | category | flops | bytes accessed | tf_op | source)
XLA Modules:
  0.0 50.4 jit_solution(3366103910349126743)
XLA Ops:
  0.0 0.0 copy-start.6
  0.0 1.1 %shard_map.82.pack_ref = f32[264,128]{1,0:T(8,128)S(1)} custom-call(f32[128,256]{1,0:T(8,128)} %bitcast.10, s32[1,256]{1,0:T(1,128)} %bitcast.13, s32[6,128]{1,0:T(8,128)} %mortars_hbm.1), custom_call_target="tpu_custom_call" | custom-call | flops 10000000000 | bytes 4000000 | tf_op jit(solution)/shard_map/pallas_call | solution.py:509
  1.1 3.3 %collective-permute-start.1 = (f32[264,128]{1,0:T(8,128)S(1)}, f32[264,128]{1,0:T(8,128)S(1)}, u32[]{:S(2)}, u32[]{:S(2)}) collective-permute-start(f32[264,128]{1,0:T(8,128)S(1)} %shard_map.82.pack_ref), channel_id=1, source_target_pairs={{0,1},{1,0},{2,3},{3,2},{4,5},{5,4},{6,7},{7,6},{8,9},{9,8},{10,11... | collective-permute-start | bytes 405512 | tf_op jit(solution)/shard_map/ppermute | solution.py:570
  4.4 1.9 %collective-permute-start = (f32[264,128]{1,0:T(8,128)S(1)}, f32[264,128]{1,0:T(8,128)S(1)}, u32[]{:S(2)}, u32[]{:S(2)}) collective-permute-start(f32[264,128]{1,0:T(8,128)S(1)} %shard_map.82.pack_ref), channel_id=1, source_target_pairs={{1,2},{3,4},{5,6},{7,8},{9,10},{11,12},{13,14},{15,16},{17,18},{19... | collective-permute-start | bytes 405512 | tf_op jit(solution)/shard_map/ppermute | solution.py:569
  6.3 0.1 add_bitcast_fusion.place_ref
  6.4 0.0 copy-done.6
  6.4 0.0 copy-start
  6.4 0.0 copy-start.2
  6.4 0.0 copy-start.3
  6.4 0.0 copy-start.4
  6.4 0.0 copy-start.5
  6.4 0.8 %shard_map.83 = (bf16[1536,256]{1,0:T(8,128)(2,1)S(1)}, bf16[1536,256]{1,0:T(8,128)(2,1)S(1)}, bf16[512,256]{1,0:T(8,128)(2,1)S(1)}, bf16[512,256]{1,0:T(8,128)(...) custom-call(s32[1,2]{1,0:T(1,128)S(1)} %add_bitcast_fusion.place_ref, ...), custom_call_target="tpu_custom_call" | custom-call | flops 1000000000 | bytes 2000000 | tf_op jit(solution)/shard_map/pallas_call | solution.py:509
  7.2 0.0 collective-permute-done.1.other_ref
  7.2 0.5 copy-done
  7.7 0.0 copy-done.2
  7.7 0.0 copy-done.3
  7.7 0.0 copy-done.4
  7.7 0.0 copy-done.5
  7.7 2.3 %shard_map.84 = (f32[256,128]{1,0:T(8,128)S(1)}, bf16[256,256]{1,0:T(8,128)(2,1)S(1)}, f32[256,128]{1,0:T(8,128)S(1)}, f32[256,128]{1,0:T(8,128)S(1)}, f32[256,1...) custom-call(s32[1,2]{1,0:T(1,128)S(1)} %add_bitcast_fusion.place_ref, ...), custom_call_target="tpu_custom_call" | custom-call | tf_op jit(solution)/shard_map/pallas_call | solution.py:509
  10.1 3.6 %collective-permute-start.3 = (f32[256,128]{1,0:T(8,128)S(1)}, f32[256,128]{1,0:T(8,128)S(1)}, u32[]{:S(2)}, u32[]{:S(2)}) collective-permute-start(f32[256,128]{1,0:T(8,128)S(1)} %get-tuple-element.51), channel_id=1, source_target_pairs={{1,2},{3,4},{5,6},{7,8},{9,10},{11,12},{13,14},{15,16},{17,18},{19... | collective-permute-start | bytes 393224 | tf_op jit(solution)/shard_map/ppermute | solution.py:586
  13.7 1.5 %shard_map.85 = (bf16[1536,256]{1,0:T(8,128)(2,1)S(1)}, bf16[512,256]{1,0:T(8,128)(2,1)S(1)}, f32[256,128]{1,0:T(8,128)S(1)}, f32[256,128]{1,0:T(8,128)S(1)}, f32[256,128]{1,0:T(8,128)S(1)}, /*index=5*/f32[1,1]{1,0:T(1,128)}) custom-call(s32[1,2]{1,0:T(1,128)S(1)} %add_bitcast_fusion.place_ref, f32[264,128]{1,0:T(8,128)S(1)} %shard_map.82.pack_ref, ...), custom_call_target="tpu_custom_call" | custom-call | flops 2000000000 | bytes 4000000 | tf_op jit(solution)/shard_map/pallas_call | solution.py:509
  15.3 0.0 collective-permute-done.far_ref
  15.3 1.4 %shard_map.86 = (f32[256,128]{1,0:T(8,128)S(1)}, f32[256,128]{1,0:T(8,128)S(1)}, bf16[128,256]{1,0:T(8,128)(2,1)S(1)}, bf16[256,512]{1,0:T(8,128)(2,1)S(1)}, s32...) custom-call(s32[1,2]{1,0:T(1,128)S(1)} %add_bitcast_fusion.place_ref, f32[264,128]{1,0:T(8,128)S(1)} %shard_map.82.pack_ref, ...), custom_call_target="tpu_custom_call" | custom-call | tf_op jit(solution)/shard_map/pallas_call | solution.py:509
  16.6 0.1 collective-permute-start.2
  16.7 1.0 %shard_map.87 = (f32[256,128]{1,0:T(8,128)S(1)}, f32[128,256]{1,0:T(8,128)S(1)}) custom-call(s32[1,2]{1,0:T(1,128)S(1)} %add_bitcast_fusion.place_ref, f32[264,128]{1,0:T(8,128)S(1)} %shard_map.82.pack_ref, f32[264,128]{1,0:T(8,128)S(1)} %collective-permute-done.far_ref, bf16[2560,256]{1,0:T(8,128)(2,1)S(1)} %copy-done, ...), custom_call_target="tpu_custom_call" | custom-call | flops 1000000000 | bytes 2000000 | tf_op jit(solution)/shard_map/pallas_call | solution.py:509
  17.7 0.0 collective-permute-done.3.two_ref
  17.7 0.3 collective-permute-done.2.one_ref
  18.1 0.0 copy-start.1
  18.1 3.2 %shard_map.88 = f32[1,128]{1,0:T(1,128)S(1)} custom-call(bf16[2560,256]{1,0:T(8,128)(2,1)S(1)} %copy-done, f32[256,128]{1,0:T(8,128)S(1)} %get-tuple-element.50.send_ref, f32[256,128]{1,0:T(8,128)S(1)} %collective-permute-done.2.one_ref, f32[256,128]{1,0:T(8,128)S(1)} %collective-permute-done.3.two_ref, f32[256,128]{1,0:T(8,128)S(1)} %get-tuple-element.55.lacked_ref, ...), custom_call_target="tpu_custom_call" | custom-call | tf_op jit(solution)/shard_map/pallas_call | solution.py:509
  21.3 0.1 broadcast_in_dim.2
  21.3 28.0 %all_to_all.8 = f32[256,1,128]{2,1,0:T(1,128)S(1)} all-to-all(f32[256,1,128]{2,1,0:T(1,128)S(1)} %broadcast_in_dim.2), channel_id=1, replica_groups=mesh['leaf'=256] {'leaf'}, dimensions={0} | all-to-all | bytes 262144 | tf_op jit(solution)/shard_map/all_to_all | solution.py:618
  49.3 0.0 copy-done.1
  49.3 1.2 %shard_map.89 = f32[128,256]{1,0:T(8,128)} custom-call(f32[256,128]{1,0:T(8,128)S(1)} %bitcast.9, f32[128,256]{1,0:T(8,128)S(1)} %bitcast.11, f32[128,256]{1,0:T(8,128)S(1)} %get-tuple-element.68.image_ref), custom_call_target="tpu_custom_call" | custom-call | tf_op jit(solution)/shard_map/pallas_call | solution.py:509
Async XLA Ops:
  0.0 6.4 %copy-start.6 = (s32[6,256]{1,0:T(8,128)S(1)}, s32[6,256]{1,0:T(8,128)}, u32[]{:S(2)}) copy-start(s32[6,256]{1,0:T(8,128)} %neighbours_ref.3) | copy-start | bytes 18436
  1.1 6.2 %collective-permute-start.1 = (f32[264,128]{1,0:T(8,128)S(1)}, f32[264,128]{1,0:T(8,128)S(1)}, u32[]{:S(2)}, u32[]{:S(2)}) collective-permute-start(f32[264,128]{1,0:T(8,128)S(1)} %shard_map.82.pack_ref), channel_id=1, source_target_pairs={{0,1},{1,0},{2,3},{3,2},{4,5},{5,4},{6,7},{7,6},{8,9},{9,8},{10,11... | collective-permute-start | bytes 405512 | tf_op jit(solution)/shard_map/ppermute | solution.py:570
  4.4 10.9 %collective-permute-start = (f32[264,128]{1,0:T(8,128)S(1)}, f32[264,128]{1,0:T(8,128)S(1)}, u32[]{:S(2)}, u32[]{:S(2)}) collective-permute-start(f32[264,128]{1,0:T(8,128)S(1)} %shard_map.82.pack_ref), channel_id=1, source_target_pairs={{1,2},{3,4},{5,6},{7,8},{9,10},{11,12},{13,14},{15,16},{17,18},{19... | collective-permute-start | bytes 405512 | tf_op jit(solution)/shard_map/ppermute | solution.py:569
  6.4 1.3 %copy-start = (bf16[2560,256]{1,0:T(8,128)(2,1)S(1)}, bf16[2560,256]{1,0:T(8,128)(2,1)}, u32[]{:S(2)}) copy-start(bf16[2560,256]{1,0:T(8,128)(2,1)} %constant.12.clone.table) | copy-start | bytes 3932164
  6.4 1.3 %copy-start.2 = (f32[64,256]{1,0:T(8,128)S(1)}, f32[64,256]{1,0:T(8,128)}, u32[]{:S(2)}) copy-start(f32[64,256]{1,0:T(8,128)} %mass_ref.1) | copy-start | bytes 196612
  6.4 1.3 %copy-start.3 = (f32[64,256]{1,0:T(8,128)S(1)}, f32[64,256]{1,0:T(8,128)}, u32[]{:S(2)}) copy-start(f32[64,256]{1,0:T(8,128)} %curve_ref.1) | copy-start | bytes 196612
  6.4 1.3 %copy-start.4 = (f32[64,64]{1,0:T(8,128)S(1)}, f32[64,64]{1,0:T(8,128)}, u32[]{:S(2)}) copy-start(f32[64,64]{1,0:T(8,128)} %stiffness_ref.1) | copy-start | bytes 49156
  6.4 1.3 %copy-start.5 = (s32[256]{0:T(256)S(1)}, s32[256]{0:T(256)}, u32[]{:S(2)}) copy-start(s32[256]{0:T(256)} %param.12) | copy-start | bytes 3076
  10.1 7.6 %collective-permute-start.3 = (f32[256,128]{1,0:T(8,128)S(1)}, f32[256,128]{1,0:T(8,128)S(1)}, u32[]{:S(2)}, u32[]{:S(2)}) collective-permute-start(f32[256,128]{1,0:T(8,128)S(1)} %get-tuple-element.51), channel_id=1, source_target_pairs={{1,2},{3,4},{5,6},{7,8},{9,10},{11,12},{13,14},{15,16},{17,18},{19... | collective-permute-start | bytes 393224 | tf_op jit(solution)/shard_map/ppermute | solution.py:586
  16.6 1.4 %collective-permute-start.2 = (f32[256,128]{1,0:T(8,128)S(1)}, f32[256,128]{1,0:T(8,128)S(1)}, u32[]{:S(2)}, u32[]{:S(2)}) collective-permute-start(f32[256,128]{1,0:T(8,128)S(1)} %get-tuple-element.50.send_ref), channel_id=1, source_target_pairs={{0,1},{1,0},{2,3},{3,2},{4,5},{5,4},{6,7},{7,6},{8,9},{9,8},{10,11... | collective-permute-start | bytes 393224 | tf_op jit(solution)/shard_map/ppermute | solution.py:602
  18.1 31.2 %copy-start.1 = (f32[2,64,256]{2,1,0:T(8,128)S(1)}, f32[2,64,256]{2,1,0:T(8,128)}, u32[]{:S(2)}) copy-start(f32[2,64,256]{2,1,0:T(8,128)} %param.8) | copy-start | bytes 393220

commit v9 on v8

--- a/solution.py
+++ b/solution.py
@@ -351,7 +351,7 @@
     extra_ref[...] = fine_count([back], [face])
     length, zero = unit(rows / scale_ref[...])
     zero_ref[...] = zero
-    length_ref[...] = length
+    length_ref[...] = jnp.broadcast_to(length, length_ref.shape)
 
 
 def far_kernel(
@@ -454,7 +454,7 @@
     r12 = total(one * image)
     rest = image - r02 * zero - r12 * one
     r22 = jnp.sqrt(total(rest * rest))
-    values = (length_ref[...], r01 + again, r11, r02, r12, r22)
+    values = (length_ref[0:1, 0:1], r01 + again, r11, r02, r12, r22)
     stats_ref[...] = in_lanes(stats_ref.shape, values)
 
 
@@ -573,8 +573,6 @@
         [shapes[name] for name in CHOSEN],
         [vmem] * 3,
         (place, pack, neighbours),
-        flops=1_000_000_000,
-        moved=2_000_000,
     )
     *made, partial, scaled = call(
         first_kernel,
@@ -586,7 +584,7 @@
     two = lax.ppermute(scaled, "leaf", pairs_two)
     faces_two, two_fine, given, extra, zero, length = call(
         over_there_kernel,
-        [faces, fine, rows, rows, rows, shape(1, 1)],
+        [faces, fine, rows, rows, rows, shape(1, LANES)],
         [vmem] * 7,
         [place, pack, neighbours, table, kept["scale"], kept["face"], kept["own_pick"]],
         flops=2_000_000_000,

time: 50.6 us -> 49.1 us (0.970)
  Pallas kernels: 12.4 us -> 11.3 us
    pallas_call x8, Pallas kernels: 12.4 us -> 11.3 us  [call(): pl.pallas_call(kernel, out_shape=outs, in_specs=specs, out_specs=jax.tree...]
  transfers between devices with their start and end apart: 4 -> 4, of which waited for: 1 -> 1; matrix products, arithmetic and copies ran while one was open for 0% -> 0% of each run, Pallas kernels for 14% -> 13%
where the time goes in v9:
time: 49.1 us; the launch traced here: 48.9 us
  blocking collectives  28 us (57%)
  Pallas kernels  11.3 us (23%)
  starting transfers between devices  8.96 us (18%)
    all_to_all x1, blocking collectives, on_device(): lax.all_to_all(jnp.broadcast_to(stats, (count, LANES)), 'leaf', 0, 0, til...  28 us
    pallas_call x8, Pallas kernels, call(): pl.pallas_call(kernel, out_shape=outs, in_specs=specs, out_specs=jax.tree...  11.3 us
    ppermute x1, starting transfers between devices, on_device(): two = lax.ppermute(scaled, 'leaf', pairs_two)  3.64 us
    ppermute x1, starting transfers between devices, on_device(): one = lax.ppermute(pack, 'leaf', pairs_one)  3.32 us
    ppermute x1, starting transfers between devices, on_device(): far = lax.ppermute(pack, 'leaf', pairs_two)  1.91 us
  transfers between devices with their start and end apart: 4, of which 1 were waited for; matrix products, arithmetic and copies ran while one was open for 0% of the time, Pallas kernels for 13%

profile of v9, /device:TPU:1, one launch (start us, length us, event | category | flops | bytes accessed | tf_op | source)
XLA Modules:
  0.0 48.9 jit_solution(12620276595402255700)
XLA Ops:
  0.0 0.0 copy-start.5
  0.0 0.0 copy-start
  0.0 0.0 copy-start.2
  0.0 0.0 copy-start.3
  0.0 0.0 copy-start.4
  0.0 0.0 copy-start.6
  0.0 1.1 %shard_map.82.pack_ref = f32[264,128]{1,0:T(8,128)S(1)} custom-call(f32[128,256]{1,0:T(8,128)} %bitcast.10, s32[1,256]{1,0:T(1,128)} %bitcast.13, s32[6,128]{1,0:T(8,128)} %mortars_hbm.1), custom_call_target="tpu_custom_call" | custom-call | flops 10000000000 | bytes 4000000 | tf_op jit(solution)/shard_map/pallas_call | solution.py:509
  1.2 3.3 %collective-permute-start.1 = (f32[264,128]{1,0:T(8,128)S(1)}, f32[264,128]{1,0:T(8,128)S(1)}, u32[]{:S(2)}, u32[]{:S(2)}) collective-permute-start(f32[264,128]{1,0:T(8,128)S(1)} %shard_map.82.pack_ref), channel_id=1, source_target_pairs={{0,1},{1,0},{2,3},{3,2},{4,5},{5,4},{6,7},{7,6},{8,9},{9,8},{10,11... | collective-permute-start | bytes 405512 | tf_op jit(solution)/shard_map/ppermute | solution.py:570
  4.5 1.9 %collective-permute-start = (f32[264,128]{1,0:T(8,128)S(1)}, f32[264,128]{1,0:T(8,128)S(1)}, u32[]{:S(2)}, u32[]{:S(2)}) collective-permute-start(f32[264,128]{1,0:T(8,128)S(1)} %shard_map.82.pack_ref), channel_id=1, source_target_pairs={{1,2},{3,4},{5,6},{7,8},{9,10},{11,12},{13,14},{15,16},{17,18},{19... | collective-permute-start | bytes 405512 | tf_op jit(solution)/shard_map/ppermute | solution.py:569
  6.4 0.1 add_bitcast_fusion.place_ref
  6.5 0.0 copy-done.5
  6.5 0.8 %shard_map.83 = (bf16[1536,256]{1,0:T(8,128)(2,1)S(1)}, bf16[1536,256]{1,0:T(8,128)(2,1)S(1)}, bf16[512,256]{1,0:T(8,128)(2,1)S(1)}, bf16[512,256]{1,0:T(8,128)(...) custom-call(s32[1,2]{1,0:T(1,128)S(1)} %add_bitcast_fusion.place_ref, ...), custom_call_target="tpu_custom_call" | custom-call | tf_op jit(solution)/shard_map/pallas_call | solution.py:509
  7.3 0.0 collective-permute-done.1.other_ref
  7.3 0.0 copy-done
  7.3 0.0 copy-done.2
  7.3 0.0 copy-done.3
  7.3 0.0 copy-done.4
  7.3 0.0 copy-done.6
  7.4 2.3 %shard_map.84 = (f32[256,128]{1,0:T(8,128)S(1)}, bf16[256,256]{1,0:T(8,128)(2,1)S(1)}, f32[256,128]{1,0:T(8,128)S(1)}, f32[256,128]{1,0:T(8,128)S(1)}, f32[256,1...) custom-call(s32[1,2]{1,0:T(1,128)S(1)} %add_bitcast_fusion.place_ref, ...), custom_call_target="tpu_custom_call" | custom-call | tf_op jit(solution)/shard_map/pallas_call | solution.py:509
  9.7 3.6 %collective-permute-start.3 = (f32[256,128]{1,0:T(8,128)S(1)}, f32[256,128]{1,0:T(8,128)S(1)}, u32[]{:S(2)}, u32[]{:S(2)}) collective-permute-start(f32[256,128]{1,0:T(8,128)S(1)} %get-tuple-element.51), channel_id=1, source_target_pairs={{1,2},{3,4},{5,6},{7,8},{9,10},{11,12},{13,14},{15,16},{17,18},{19... | collective-permute-start | bytes 393224 | tf_op jit(solution)/shard_map/ppermute | solution.py:584
  13.3 1.1 %shard_map.85 = (bf16[1536,256]{1,0:T(8,128)(2,1)S(1)}, bf16[512,256]{1,0:T(8,128)(2,1)S(1)}, f32[256,128]{1,0:T(8,128)S(1)}, f32[256,128]{1,0:T(8,128)S(1)}, f3...) custom-call(s32[1,2]{1,0:T(1,128)S(1)} %add_bitcast_fusion.place_ref, f32[264,128]{1,0:T(8,128)S(1)} %shard_map.82.pack_ref, ...), custom_call_target="tpu_custom_call" | custom-call | flops 2000000000 | bytes 4000000 | tf_op jit(solution)/shard_map/pallas_call | solution.py:509
  14.4 0.0 collective-permute-done.far_ref
  14.5 1.3 %shard_map.86 = (f32[256,128]{1,0:T(8,128)S(1)}, f32[256,128]{1,0:T(8,128)S(1)}, bf16[128,256]{1,0:T(8,128)(2,1)S(1)}, bf16[256,512]{1,0:T(8,128)(2,1)S(1)}, s32...) custom-call(s32[1,2]{1,0:T(1,128)S(1)} %add_bitcast_fusion.place_ref, f32[264,128]{1,0:T(8,128)S(1)} %shard_map.82.pack_ref, ...), custom_call_target="tpu_custom_call" | custom-call | tf_op jit(solution)/shard_map/pallas_call | solution.py:509
  15.8 0.1 collective-permute-start.2
  15.9 1.0 %shard_map.87 = (f32[256,128]{1,0:T(8,128)S(1)}, f32[128,256]{1,0:T(8,128)S(1)}) custom-call(s32[1,2]{1,0:T(1,128)S(1)} %add_bitcast_fusion.place_ref, f32[264,128]{1,0:T(8,128)S(1)} %shard_map.82.pack_ref, f32[264,128]{1,0:T(8,128)S(1)} %collective-permute-done.far_ref, bf16[2560,256]{1,0:T(8,128)(2,1)S(1)} %copy-done, ...), custom_call_target="tpu_custom_call" | custom-call | flops 1000000000 | bytes 2000000 | tf_op jit(solution)/shard_map/pallas_call | solution.py:509
  16.9 0.0 collective-permute-done.3.two_ref
  16.9 0.4 collective-permute-done.2.one_ref
  17.2 0.0 copy-start.1
  17.2 2.4 %shard_map.88 = f32[1,128]{1,0:T(1,128)S(1)} custom-call(bf16[2560,256]{1,0:T(8,128)(2,1)S(1)} %copy-done, f32[256,128]{1,0:T(8,128)S(1)} %get-tuple-element.50.send_ref, f32[256,128]{1,0:T(8,128)S(1)} %collective-permute-done.2.one_ref, f32[256,128]{1,0:T(8,128)S(1)} %collective-permute-done.3.two_ref, f32[256,128]{1,0:T(8,128)S(1)} %get-tuple-element.55.lacked_ref, ...), custom_call_target="tpu_custom_call" | custom-call | tf_op jit(solution)/shard_map/pallas_call | solution.py:509
  19.7 0.1 broadcast_in_dim.2
  19.8 28.0 %all_to_all.8 = f32[256,1,128]{2,1,0:T(1,128)S(1)} all-to-all(f32[256,1,128]{2,1,0:T(1,128)S(1)} %broadcast_in_dim.2), channel_id=1, replica_groups=mesh['leaf'=256] {'leaf'}, dimensions={0} | all-to-all | bytes 262144 | tf_op jit(solution)/shard_map/all_to_all | solution.py:616
  47.8 0.0 copy-done.1
  47.8 1.2 %shard_map.89 = f32[128,256]{1,0:T(8,128)} custom-call(f32[256,128]{1,0:T(8,128)S(1)} %bitcast.9, f32[128,256]{1,0:T(8,128)S(1)} %bitcast.11, f32[128,256]{1,0:T(8,128)S(1)} %get-tuple-element.68.image_ref), custom_call_target="tpu_custom_call" | custom-call | tf_op jit(solution)/shard_map/pallas_call | solution.py:509
Async XLA Ops:
  0.0 6.5 %copy-start.5 = (s32[6,256]{1,0:T(8,128)S(1)}, s32[6,256]{1,0:T(8,128)}, u32[]{:S(2)}) copy-start(s32[6,256]{1,0:T(8,128)} %neighbours_ref.3) | copy-start | bytes 18436
  0.0 7.3 %copy-start = (bf16[2560,256]{1,0:T(8,128)(2,1)S(1)}, bf16[2560,256]{1,0:T(8,128)(2,1)}, u32[]{:S(2)}) copy-start(bf16[2560,256]{1,0:T(8,128)(2,1)} %constant.12.clone.table) | copy-start | bytes 3932164
  0.0 7.3 %copy-start.2 = (f32[64,256]{1,0:T(8,128)S(1)}, f32[64,256]{1,0:T(8,128)}, u32[]{:S(2)}) copy-start(f32[64,256]{1,0:T(8,128)} %mass_ref.1) | copy-start | bytes 196612
  0.0 7.3 %copy-start.3 = (f32[64,256]{1,0:T(8,128)S(1)}, f32[64,256]{1,0:T(8,128)}, u32[]{:S(2)}) copy-start(f32[64,256]{1,0:T(8,128)} %curve_ref.1) | copy-start | bytes 196612
  0.0 7.3 %copy-start.4 = (f32[64,64]{1,0:T(8,128)S(1)}, f32[64,64]{1,0:T(8,128)}, u32[]{:S(2)}) copy-start(f32[64,64]{1,0:T(8,128)} %stiffness_ref.1) | copy-start | bytes 49156
  0.0 7.3 %copy-start.6 = (s32[256]{0:T(256)S(1)}, s32[256]{0:T(256)}, u32[]{:S(2)}) copy-start(s32[256]{0:T(256)} %param.12) | copy-start | bytes 3076
  1.2 6.1 %collective-permute-start.1 = (f32[264,128]{1,0:T(8,128)S(1)}, f32[264,128]{1,0:T(8,128)S(1)}, u32[]{:S(2)}, u32[]{:S(2)}) collective-permute-start(f32[264,128]{1,0:T(8,128)S(1)} %shard_map.82.pack_ref), channel_id=1, source_target_pairs={{0,1},{1,0},{2,3},{3,2},{4,5},{5,4},{6,7},{7,6},{8,9},{9,8},{10,11... | collective-permute-start | bytes 405512 | tf_op jit(solution)/shard_map/ppermute | solution.py:570
  4.5 9.9 %collective-permute-start = (f32[264,128]{1,0:T(8,128)S(1)}, f32[264,128]{1,0:T(8,128)S(1)}, u32[]{:S(2)}, u32[]{:S(2)}) collective-permute-start(f32[264,128]{1,0:T(8,128)S(1)} %shard_map.82.pack_ref), channel_id=1, source_target_pairs={{1,2},{3,4},{5,6},{7,8},{9,10},{11,12},{13,14},{15,16},{17,18},{19... | collective-permute-start | bytes 405512 | tf_op jit(solution)/shard_map/ppermute | solution.py:569
  9.7 7.2 %collective-permute-start.3 = (f32[256,128]{1,0:T(8,128)S(1)}, f32[256,128]{1,0:T(8,128)S(1)}, u32[]{:S(2)}, u32[]{:S(2)}) collective-permute-start(f32[256,128]{1,0:T(8,128)S(1)} %get-tuple-element.51), channel_id=1, source_target_pairs={{1,2},{3,4},{5,6},{7,8},{9,10},{11,12},{13,14},{15,16},{17,18},{19... | collective-permute-start | bytes 393224 | tf_op jit(solution)/shard_map/ppermute | solution.py:584
  15.8 1.4 %collective-permute-start.2 = (f32[256,128]{1,0:T(8,128)S(1)}, f32[256,128]{1,0:T(8,128)S(1)}, u32[]{:S(2)}, u32[]{:S(2)}) collective-permute-start(f32[256,128]{1,0:T(8,128)S(1)} %get-tuple-element.50.send_ref), channel_id=1, source_target_pairs={{0,1},{1,0},{2,3},{3,2},{4,5},{5,4},{6,7},{7,6},{8,9},{9,8},{10,11... | collective-permute-start | bytes 393224 | tf_op jit(solution)/shard_map/ppermute | solution.py:600
  17.2 30.5 %copy-start.1 = (f32[2,64,256]{2,1,0:T(8,128)S(1)}, f32[2,64,256]{2,1,0:T(8,128)}, u32[]{:S(2)}) copy-start(f32[2,64,256]{2,1,0:T(8,128)} %param.8) | copy-start | bytes 393220

commit v10 on v9

--- a/solution.py
+++ b/solution.py
@@ -326,45 +326,21 @@
     far_ref[...] = image * scale
 
 
-def over_there_kernel(
-    place_ref, pack_ref, neighbours_ref, table, scale_ref, face_ref, own_pick_ref, two_ref,
-    two_fine_ref, given_ref, extra_ref, zero_ref, length_ref
+def far_kernel(
+    place_ref, pack_ref, neighbours_ref, far_ref, table, scale_ref, diagonal_ref, partial_ref,
+    own_back_ref, face_ref, image_ref, send_ref, two_ref, two_fine_ref, pick_ref, back_ref,
+    far_face_ref, total_ref
 ):
     leaves = pack_ref.shape[0] - 8
     offset = place_ref[0:1, 0:1]
-    far = offset - place_ref[0:1, 1:2]
-    mortars, columns, _ = read_tables(pack_ref, leaves)
+    start = offset - place_ref[0:1, 1:2]
+    _, columns, _ = read_tables(pack_ref, leaves)
     neighbours = pad_rows(neighbours_ref[...])
-    choose((two_ref, two_fine_ref), ((0, 1, far),), columns, neighbours, leaves)
-    face = face_ref[...]
-    rows = pack_ref[0:leaves, :]
-    parts = split(rows)
-    index = own_index(neighbours, far)
-    seen = jnp.concatenate(
-        [dot(pick(index[f ^ 1 : (f ^ 1) + 1, :], (leaves, leaves), 0), parts) for f in range(FACES)],
-        axis=0,
-    )
-    back = fine_backs(mortars, far, leaves)
-    trace = side_traces(dot(own_pick_ref[...], parts), [face], table)
-    sent = jnp.concatenate(lift(trace, [face], table), axis=0)
-    given_ref[...] = -across_faces(seen) - fold(dot(back, sent))
-    extra_ref[...] = fine_count([back], [face])
-    length, zero = unit(rows / scale_ref[...])
-    zero_ref[...] = zero
-    length_ref[...] = jnp.broadcast_to(length, length_ref.shape)
-
-
-def far_kernel(
-    place_ref, pack_ref, far_ref, table, scale_ref, diagonal_ref, partial_ref, two_ref,
-    two_fine_ref, own_back_ref, face_ref, image_ref, send_ref, pick_ref, back_ref, far_face_ref,
-    total_ref
-):
-    leaves = pack_ref.shape[0] - 8
-    offset = place_ref[0:1, 0:1]
+    choose((two_ref, two_fine_ref), ((0, 1, start),), columns, neighbours, leaves)
     mortars, columns, _ = read_tables(far_ref, leaves)
     slots = mortars.shape[1]
     face = columns[:, 1:2]
-    chosen = pick(columns[:, 0:1] - (offset - place_ref[0:1, 1:2]), (slots, leaves), 1)
+    chosen = pick(columns[:, 0:1] - start, (slots, leaves), 1)
     back = fine_backs(mortars, offset, leaves)
     pick_ref[...] = chosen
     back_ref[...] = back
@@ -381,29 +357,41 @@
 
 
 def far_rows_kernel(
-    place_ref, pack_ref, far_ref, table, given_ref, extra_ref, image_ref, rows_ref, turned_ref
+    place_ref, pack_ref, neighbours_ref, far_ref, table, scale_ref, face_ref, own_pick_ref,
+    image_ref, rows_ref, turned_ref, zero_ref, length_ref
 ):
     leaves = pack_ref.shape[0] - 8
     offset = place_ref[0:1, 0:1]
-    mortars, columns, scale = read_tables(far_ref, leaves)
+    far = offset - place_ref[0:1, 1:2]
+    rows = pack_ref[0:leaves, :]
+    parts = split(rows)
+    index = own_index(pad_rows(neighbours_ref[...]), far)
+    seen = jnp.concatenate(
+        [dot(pick(index[f ^ 1 : (f ^ 1) + 1, :], (leaves, leaves), 0), parts) for f in range(FACES)],
+        axis=0,
+    )
+    face = face_ref[...]
+    mortars, _, _ = read_tables(pack_ref, leaves)
+    far_mortars, columns, scale = read_tables(far_ref, leaves)
     slots = mortars.shape[1]
-    face = columns[:, 1:2]
+    far_face = columns[:, 1:2]
     fine = own_index(columns, offset)
-    fine = jnp.concatenate(
-        [pick(fine[:, 2 + q : 3 + q], (slots, leaves), 1) for q in range(4)], axis=0
-    )
-    trace = side_traces(
-        dot(fine, split(pack_ref[0:leaves, :])), [opposite(face)] * 4, table
-    )
+    chosen = [pick(fine[:, 2 + q : 3 + q], (slots, leaves), 1) for q in range(4)]
+    chosen = dot(jnp.concatenate(chosen + [own_pick_ref[...]], axis=0), parts)
+    trace = side_traces(chosen, [opposite(far_face)] * 4 + [face], table)
     quarters = [trace[slots * q : slots * (q + 1), :] for q in range(4)]
-    back = pick(mortars[0:1, :] - (offset - place_ref[0:1, 1:2]), (leaves, slots), 0)
-    lapped = (
-        given_ref[...]
-        + extra_ref[...] * far_ref[0:leaves, :]
-        - fold(dot(back, lower(quarters, face, table, STAY_AT)))
-    )
+    sent = lift(trace[4 * slots :, :], [face], table)
+    sent.append(lower(quarters, far_face, table, STAY_AT))
+    back = fine_backs(mortars, far, leaves)
+    extra = fine_count([back], [face])
+    backs = [back, pick(far_mortars[0:1, :] - far, (leaves, slots), 0)]
+    mortars = dot(jnp.concatenate(backs, axis=1), jnp.concatenate(sent, axis=0))
+    lapped = extra * far_ref[0:leaves, :] - across_faces(seen) - fold(mortars)
     rows_ref[...] = scale * placed(lapped)
     turned_ref[...] = image_ref[...].T
+    length, zero = unit(rows / scale_ref[...])
+    zero_ref[...] = zero
+    length_ref[...] = jnp.broadcast_to(length, length_ref.shape)
 
 
 def total(values):
@@ -582,27 +570,20 @@
     )
     kept = dict(zip(CHOSEN + MADE, [*chosen, *made]))
     two = lax.ppermute(scaled, "leaf", pairs_two)
-    faces_two, two_fine, given, extra, zero, length = call(
-        over_there_kernel,
-        [faces, fine, rows, rows, rows, shape(1, LANES)],
-        [vmem] * 7,
-        [place, pack, neighbours, table, kept["scale"], kept["face"], kept["own_pick"]],
-        flops=2_000_000_000,
-        moved=4_000_000,
-    )
-    image, send, two_pick, two_back, two_face, diagonal = call(
+    image, send, faces_two, two_fine, two_pick, two_back, two_face, diagonal = call(
         far_kernel,
-        [rows, rows, picks, backs, face, rows],
-        [vmem] * 11,
-        [place, pack, far, table, kept["scale"], kept["diagonal"], partial, faces_two, two_fine,
+        [rows, rows, faces, fine, picks, backs, face, rows],
+        [vmem] * 10,
+        [place, pack, neighbours, far, table, kept["scale"], kept["diagonal"], partial,
          kept["own_back"], kept["face"]],
     )
     one = lax.ppermute(send, "leaf", pairs_one)
-    lacked, turned = call(
+    lacked, turned, zero, length = call(
         far_rows_kernel,
-        [rows, shape(LANES, leaves)],
-        [vmem] * 7,
-        [place, pack, far, table, given, extra, image],
+        [rows, shape(LANES, leaves), rows, shape(1, LANES)],
+        [vmem] * 9,
+        [place, pack, neighbours, far, table, kept["scale"], kept["face"], kept["own_pick"],
+         image],
         flops=1_000_000_000,
         moved=2_000_000,
     )

time: 49.1 us -> 48.7 us (level)
    pallas_call x8 -> x7, Pallas kernels: 11.3 us -> 10.9 us  [call(): pl.pallas_call(kernel, out_shape=outs, in_specs=specs, out_specs=jax.tree...]
  transfers between devices with their start and end apart: 4 -> 4, of which waited for: 1 -> 0; matrix products, arithmetic and copies ran while one was open for 0% -> 0% of each run, Pallas kernels for 13% -> 13%
where the time goes in v10:
time: 48.7 us; the launch traced here: 48.5 us
  blocking collectives  28.3 us (58%)
  Pallas kernels  10.9 us (22%)
  starting transfers between devices  8.96 us (18%)
    all_to_all x1, blocking collectives, on_device(): lax.all_to_all(jnp.broadcast_to(stats, (count, LANES)), 'leaf', 0, 0, til...  28.3 us
    pallas_call x7, Pallas kernels, call(): pl.pallas_call(kernel, out_shape=outs, in_specs=specs, out_specs=jax.tree...  10.9 us
    ppermute x1, starting transfers between devices, on_device(): two = lax.ppermute(scaled, 'leaf', pairs_two)  3.64 us
    ppermute x1, starting transfers between devices, on_device(): one = lax.ppermute(pack, 'leaf', pairs_one)  3.32 us
    ppermute x1, starting transfers between devices, on_device(): far = lax.ppermute(pack, 'leaf', pairs_two)  1.91 us
  transfers between devices with their start and end apart: 4, of which 0 were waited for; matrix products, arithmetic and copies ran while one was open for 0% of the time, Pallas kernels for 13%

profile of v10, /device:TPU:1, one launch (start us, length us, event | category | flops | bytes accessed | tf_op | source)
XLA Modules:
  0.0 48.5 jit_solution(10542886215560165031)
XLA Ops:
  0.0 0.0 copy-start.5
  0.0 0.0 copy-start
  0.0 0.0 copy-start.2
  0.0 0.0 copy-start.3
  0.0 0.0 copy-start.4
  0.0 0.0 copy-start.6
  0.0 1.1 %shard_map.82.pack_ref = f32[264,128]{1,0:T(8,128)S(1)} custom-call(f32[128,256]{1,0:T(8,128)} %bitcast.10, s32[1,256]{1,0:T(1,128)} %bitcast.13, s32[6,128]{1,0:T(8,128)} %mortars_hbm.1), custom_call_target="tpu_custom_call" | custom-call | flops 10000000000 | bytes 4000000 | tf_op jit(solution)/shard_map/pallas_call | solution.py:497
  1.2 3.3 %collective-permute-start.1 = (f32[264,128]{1,0:T(8,128)S(1)}, f32[264,128]{1,0:T(8,128)S(1)}, u32[]{:S(2)}, u32[]{:S(2)}) collective-permute-start(f32[264,128]{1,0:T(8,128)S(1)} %shard_map.82.pack_ref), channel_id=1, source_target_pairs={{0,1},{1,0},{2,3},{3,2},{4,5},{5,4},{6,7},{7,6},{8,9},{9,8},{10,11... | collective-permute-start | bytes 405512 | tf_op jit(solution)/shard_map/ppermute | solution.py:558
  4.5 1.9 %collective-permute-start = (f32[264,128]{1,0:T(8,128)S(1)}, f32[264,128]{1,0:T(8,128)S(1)}, u32[]{:S(2)}, u32[]{:S(2)}) collective-permute-start(f32[264,128]{1,0:T(8,128)S(1)} %shard_map.82.pack_ref), channel_id=1, source_target_pairs={{1,2},{3,4},{5,6},{7,8},{9,10},{11,12},{13,14},{15,16},{17,18},{19... | collective-permute-start | bytes 405512 | tf_op jit(solution)/shard_map/ppermute | solution.py:557
  6.4 0.1 add_bitcast_fusion.place_ref
  6.5 0.0 copy-done.5
  6.5 0.8 %shard_map.83 = (bf16[1536,256]{1,0:T(8,128)(2,1)S(1)}, bf16[1536,256]{1,0:T(8,128)(2,1)S(1)}, bf16[512,256]{1,0:T(8,128)(2,1)S(1)}, bf16[512,256]{1,0:T(8,128)(...) custom-call(s32[1,2]{1,0:T(1,128)S(1)} %add_bitcast_fusion.place_ref, ...), custom_call_target="tpu_custom_call" | custom-call | tf_op jit(solution)/shard_map/pallas_call | solution.py:497
  7.3 0.0 collective-permute-done.1.other_ref
  7.3 0.0 copy-done
  7.3 0.0 copy-done.2
  7.3 0.0 copy-done.3
  7.3 0.0 copy-done.4
  7.3 0.0 copy-done.6
  7.4 2.3 %shard_map.84 = (f32[256,128]{1,0:T(8,128)S(1)}, bf16[256,256]{1,0:T(8,128)(2,1)S(1)}, f32[256,128]{1,0:T(8,128)S(1)}, f32[256,128]{1,0:T(8,128)S(1)}, f32[256,1...) custom-call(s32[1,2]{1,0:T(1,128)S(1)} %add_bitcast_fusion.place_ref, ...), custom_call_target="tpu_custom_call" | custom-call | tf_op jit(solution)/shard_map/pallas_call | solution.py:497
  9.7 3.6 %collective-permute-start.3 = (f32[256,128]{1,0:T(8,128)S(1)}, f32[256,128]{1,0:T(8,128)S(1)}, u32[]{:S(2)}, u32[]{:S(2)}) collective-permute-start(f32[256,128]{1,0:T(8,128)S(1)} %get-tuple-element.47), channel_id=1, source_target_pairs={{1,2},{3,4},{5,6},{7,8},{9,10},{11,12},{13,14},{15,16},{17,18},{19... | collective-permute-start | bytes 393224 | tf_op jit(solution)/shard_map/ppermute | solution.py:572
  13.3 0.0 collective-permute-done.far_ref
  13.3 1.6 %shard_map.85 = (f32[256,128]{1,0:T(8,128)S(1)}, f32[256,128]{1,0:T(8,128)S(1)}, bf16[1536,256]{1,0:T(8,128)(2,1)S(1)}, bf16[512,256]{1,0:T(8,128)(2,1)S(1)}, bf...) custom-call(s32[1,2]{1,0:T(1,128)S(1)} %add_bitcast_fusion.place_ref, ...), custom_call_target="tpu_custom_call" | custom-call | tf_op jit(solution)/shard_map/pallas_call | solution.py:497
  14.9 0.1 collective-permute-start.2
  15.0 1.5 %shard_map.86 = (f32[256,128]{1,0:T(8,128)S(1)}, f32[128,256]{1,0:T(8,128)S(1)}, f32[256,128]{1,0:T(8,128)S(1)}, f32[1,128]{1,0:T(1,128)S(1)}) custom-call(s32[1,2]{1,0:T(1,128)S(1)} %add_bitcast_fusion.place_ref, f32[264,128]{1,0:T(8,128)S(1)} %shard_map.82.pack_ref, s32[6,256]{1,0:T(8,128)S(1)} %copy-done.5, f32[264,128]{1,0:T(8,128)S(1)} %collective-permute-done.far_ref, ...), custom_call_target="tpu_custom_call" | custom-call | flops 1000000000 | bytes 2000000 | tf_op jit(solution)/shard_map/pallas_call | solution.py:497
  16.4 0.0 collective-permute-done.3.two_ref
  16.5 0.0 collective-permute-done.2.one_ref
  16.5 0.0 copy-start.1
  16.5 2.5 %shard_map.87 = f32[1,128]{1,0:T(1,128)S(1)} custom-call(bf16[2560,256]{1,0:T(8,128)(2,1)S(1)} %copy-done, f32[256,128]{1,0:T(8,128)S(1)} %get-tuple-element.46.send_ref, f32[256,128]{1,0:T(8,128)S(1)} %collective-permute-done.2.one_ref, f32[256,128]{1,0:T(8,128)S(1)} %collective-permute-done.3.two_ref, f32[256,128]{1,0:T(8,128)S(1)} %get-tuple-element.49.lacked_ref, ...), custom_call_target="tpu_custom_call" | custom-call | tf_op jit(solution)/shard_map/pallas_call | solution.py:497
  19.0 0.1 broadcast_in_dim.2
  19.0 28.3 %all_to_all.8 = f32[256,1,128]{2,1,0:T(1,128)S(1)} all-to-all(f32[256,1,128]{2,1,0:T(1,128)S(1)} %broadcast_in_dim.2), channel_id=1, replica_groups=mesh['leaf'=256] {'leaf'}, dimensions={0} | all-to-all | bytes 262144 | tf_op jit(solution)/shard_map/all_to_all | solution.py:597
  47.3 0.0 copy-done.1
  47.3 1.2 %shard_map.88 = f32[128,256]{1,0:T(8,128)} custom-call(f32[256,128]{1,0:T(8,128)S(1)} %bitcast.9, f32[128,256]{1,0:T(8,128)S(1)} %bitcast.11, f32[128,256]{1,0:T(8,128)S(1)} %get-tuple-element.64.image_ref), custom_call_target="tpu_custom_call" | custom-call | tf_op jit(solution)/shard_map/pallas_call | solution.py:497
Async XLA Ops:
  0.0 6.5 %copy-start.5 = (s32[6,256]{1,0:T(8,128)S(1)}, s32[6,256]{1,0:T(8,128)}, u32[]{:S(2)}) copy-start(s32[6,256]{1,0:T(8,128)} %neighbours_ref.5) | copy-start | bytes 18436
  0.0 7.3 %copy-start = (bf16[2560,256]{1,0:T(8,128)(2,1)S(1)}, bf16[2560,256]{1,0:T(8,128)(2,1)}, u32[]{:S(2)}) copy-start(bf16[2560,256]{1,0:T(8,128)(2,1)} %constant.12.clone.table) | copy-start | bytes 3932164
  0.0 7.3 %copy-start.2 = (f32[64,256]{1,0:T(8,128)S(1)}, f32[64,256]{1,0:T(8,128)}, u32[]{:S(2)}) copy-start(f32[64,256]{1,0:T(8,128)} %mass_ref.1) | copy-start | bytes 196612
  0.0 7.3 %copy-start.3 = (f32[64,256]{1,0:T(8,128)S(1)}, f32[64,256]{1,0:T(8,128)}, u32[]{:S(2)}) copy-start(f32[64,256]{1,0:T(8,128)} %curve_ref.1) | copy-start | bytes 196612
  0.0 7.3 %copy-start.4 = (f32[64,64]{1,0:T(8,128)S(1)}, f32[64,64]{1,0:T(8,128)}, u32[]{:S(2)}) copy-start(f32[64,64]{1,0:T(8,128)} %stiffness_ref.1) | copy-start | bytes 49156
  0.0 7.3 %copy-start.6 = (s32[256]{0:T(256)S(1)}, s32[256]{0:T(256)}, u32[]{:S(2)}) copy-start(s32[256]{0:T(256)} %param.12) | copy-start | bytes 3076
  1.2 6.1 %collective-permute-start.1 = (f32[264,128]{1,0:T(8,128)S(1)}, f32[264,128]{1,0:T(8,128)S(1)}, u32[]{:S(2)}, u32[]{:S(2)}) collective-permute-start(f32[264,128]{1,0:T(8,128)S(1)} %shard_map.82.pack_ref), channel_id=1, source_target_pairs={{0,1},{1,0},{2,3},{3,2},{4,5},{5,4},{6,7},{7,6},{8,9},{9,8},{10,11... | collective-permute-start | bytes 405512 | tf_op jit(solution)/shard_map/ppermute | solution.py:558
  4.5 8.8 %collective-permute-start = (f32[264,128]{1,0:T(8,128)S(1)}, f32[264,128]{1,0:T(8,128)S(1)}, u32[]{:S(2)}, u32[]{:S(2)}) collective-permute-start(f32[264,128]{1,0:T(8,128)S(1)} %shard_map.82.pack_ref), channel_id=1, source_target_pairs={{1,2},{3,4},{5,6},{7,8},{9,10},{11,12},{13,14},{15,16},{17,18},{19... | collective-permute-start | bytes 405512 | tf_op jit(solution)/shard_map/ppermute | solution.py:557
  9.7 6.8 %collective-permute-start.3 = (f32[256,128]{1,0:T(8,128)S(1)}, f32[256,128]{1,0:T(8,128)S(1)}, u32[]{:S(2)}, u32[]{:S(2)}) collective-permute-start(f32[256,128]{1,0:T(8,128)S(1)} %get-tuple-element.47), channel_id=1, source_target_pairs={{1,2},{3,4},{5,6},{7,8},{9,10},{11,12},{13,14},{15,16},{17,18},{19... | collective-permute-start | bytes 393224 | tf_op jit(solution)/shard_map/ppermute | solution.py:572
  14.9 1.6 %collective-permute-start.2 = (f32[256,128]{1,0:T(8,128)S(1)}, f32[256,128]{1,0:T(8,128)S(1)}, u32[]{:S(2)}, u32[]{:S(2)}) collective-permute-start(f32[256,128]{1,0:T(8,128)S(1)} %get-tuple-element.46.send_ref), channel_id=1, source_target_pairs={{0,1},{1,0},{2,3},{3,2},{4,5},{5,4},{6,7},{7,6},{8,9},{9,8},{10,11... | collective-permute-start | bytes 393224 | tf_op jit(solution)/shard_map/ppermute | solution.py:580
  16.5 30.9 %copy-start.1 = (f32[2,64,256]{2,1,0:T(8,128)S(1)}, f32[2,64,256]{2,1,0:T(8,128)}, u32[]{:S(2)}) copy-start(f32[2,64,256]{2,1,0:T(8,128)} %param.8) | copy-start | bytes 393220

commit v11 on v10

--- a/solution.py
+++ b/solution.py
@@ -114,11 +114,6 @@
     return jnp.where(face >= 0, face ^ 1, -1)
 
 
-def level_rows(levels):
-    scale = jnp.left_shift(jnp.ones_like(levels), levels).astype(F32)
-    return jnp.broadcast_to(scale, (LANES, levels.shape[1])).T
-
-
 def fetch(pairs, sems):
     copies = [
         pltpu.make_async_copy(source, target, sems.at[at])
@@ -228,11 +223,14 @@
 
 def choose(refs, kinds, columns, neighbours, leaves):
     slots = columns.shape[0]
-    for faces_ref, fine_ref, start in kinds:
-        places = to_columns(own_index(neighbours, start))
+    for faces_ref, fine_ref, start, own in kinds:
+        index = own_index(neighbours, start)
+        across = index if own else to_columns(index)
         for f in range(FACES):
-            refs[faces_ref][leaves * f : leaves * (f + 1), :] = pick(
-                places[:, f : f + 1], (leaves, leaves), 1
+            refs[faces_ref][leaves * f : leaves * (f + 1), :] = (
+                pick(across[f ^ 1 : (f ^ 1) + 1, :], (leaves, leaves), 0)
+                if own
+                else pick(across[:, f : f + 1], (leaves, leaves), 1)
             )
         fine = own_index(columns, start)
         for q in range(4):
@@ -264,7 +262,7 @@
     made["fine_back"][...] = fine_backs(mortars, offset, leaves)
     made["own_back"][...] = pick(mortars[0:1, :] - offset, (leaves, slots), 0)
     made["own_pick"][...] = pick(columns[:, 0:1] - offset, (slots, leaves), 1)
-    kinds = (("own", "own_fine", offset), ("one", "one_fine", offset + first))
+    kinds = (("own", "own_fine", offset, True), ("one", "one_fine", offset + first, False))
     choose(made, kinds, columns, pad_rows(neighbours_ref[...]), leaves)
 
 
@@ -274,7 +272,7 @@
 
 
 def first_kernel(
-    place_ref, pack_ref, other_ref, table, mass_ref, curve_ref, stiffness_ref, levels_ref, *refs
+    place_ref, pack_ref, other_ref, table, mass_ref, curve_ref, stiffness_ref, *refs
 ):
     kept = dict(zip(CHOSEN + MADE, refs))
     image_ref, far_ref = refs[len(CHOSEN) + len(MADE) :]
@@ -302,10 +300,12 @@
     wide = split(jnp.where(same, wide, 0.0))
     wide = jnp.concatenate([wide, wide], axis=0)
     kept["stiff"][...] = wide
-    kept["mass"][...] = jnp.concatenate([mass_ref[...]] * 2, axis=0).T
-    curve = curve_ref[...]
-    kept["curve"][...] = jnp.concatenate([-curve, jnp.zeros_like(curve)], axis=0).T
-    scale = level_rows(levels_ref[...])
+    both = jnp.concatenate([mass_ref[...], curve_ref[...]], axis=0).T
+    turned = pltpu.roll(both, NODES, 1)
+    low = lax.broadcasted_iota(jnp.int32, (1, LANES), 1) < NODES
+    kept["mass"][...] = jnp.where(low, both, turned)
+    kept["curve"][...] = jnp.where(low, -turned, 0.0)
+    scale = jnp.broadcast_to(read_tables(pack_ref, leaves)[2], both.shape)
     kept["scale"][...] = scale
     rows = pack_ref[0:leaves, :]
     parts = [split(rows), split(other_ref[0:leaves, :])]
@@ -336,7 +336,7 @@
     start = offset - place_ref[0:1, 1:2]
     _, columns, _ = read_tables(pack_ref, leaves)
     neighbours = pad_rows(neighbours_ref[...])
-    choose((two_ref, two_fine_ref), ((0, 1, start),), columns, neighbours, leaves)
+    choose((two_ref, two_fine_ref), ((0, 1, start, False),), columns, neighbours, leaves)
     mortars, columns, _ = read_tables(far_ref, leaves)
     slots = mortars.shape[1]
     face = columns[:, 1:2]
@@ -565,8 +565,8 @@
     *made, partial, scaled = call(
         first_kernel,
         [shapes[name] for name in MADE] + [rows, rows],
-        [vmem] * (8 + len(CHOSEN)),
-        [place, pack, one, table, nodal_mass, curvature, stiffness, levels, *chosen],
+        [vmem] * (7 + len(CHOSEN)),
+        [place, pack, one, table, nodal_mass, curvature, stiffness, *chosen],
     )
     kept = dict(zip(CHOSEN + MADE, [*chosen, *made]))
     two = lax.ppermute(scaled, "leaf", pairs_two)

time: 48.7 us -> 48.4 us (level)
  transfers between devices with their start and end apart: 4 -> 4, of which waited for: 0 -> 0; matrix products, arithmetic and copies ran while one was open for 0% -> 0% of each run, Pallas kernels for 13% -> 12%
where the time goes in v11:
time: 48.4 us; the launch traced here: 48.3 us
  blocking collectives  28.3 us (58%)
  Pallas kernels  10.7 us (22%)
  starting transfers between devices  8.96 us (19%)
    all_to_all x1, blocking collectives, on_device(): lax.all_to_all(jnp.broadcast_to(stats, (count, LANES)), 'leaf', 0, 0, til...  28.3 us
    pallas_call x7, Pallas kernels, call(): pl.pallas_call(kernel, out_shape=outs, in_specs=specs, out_specs=jax.tree...  10.7 us
    ppermute x1, starting transfers between devices, on_device(): two = lax.ppermute(scaled, 'leaf', pairs_two)  3.64 us
    ppermute x1, starting transfers between devices, on_device(): one = lax.ppermute(pack, 'leaf', pairs_one)  3.32 us
    ppermute x1, starting transfers between devices, on_device(): far = lax.ppermute(pack, 'leaf', pairs_two)  1.91 us
  transfers between devices with their start and end apart: 4, of which 0 were waited for; matrix products, arithmetic and copies ran while one was open for 0% of the time, Pallas kernels for 12%

profile of v11, /device:TPU:1, one launch (start us, length us, event | category | flops | bytes accessed | tf_op | source)
XLA Modules:
  0.0 48.3 jit_solution(14004083002407906111)
XLA Ops:
  0.0 0.0 copy-start.5
  0.0 0.0 copy-start
  0.0 0.0 copy-start.2
  0.0 0.0 copy-start.3
  0.0 0.0 copy-start.4
  0.0 1.1 %shard_map.82.pack_ref = f32[264,128]{1,0:T(8,128)S(1)} custom-call(f32[128,256]{1,0:T(8,128)} %bitcast.10, s32[1,256]{1,0:T(1,128)} %bitcast.13, s32[6,128]{1,0:T(8,128)} %mortars_hbm.1), custom_call_target="tpu_custom_call" | custom-call | flops 10000000000 | bytes 4000000 | tf_op jit(solution)/shard_map/pallas_call | solution.py:497
  1.2 3.3 %collective-permute-start.1 = (f32[264,128]{1,0:T(8,128)S(1)}, f32[264,128]{1,0:T(8,128)S(1)}, u32[]{:S(2)}, u32[]{:S(2)}) collective-permute-start(f32[264,128]{1,0:T(8,128)S(1)} %shard_map.82.pack_ref), channel_id=1, source_target_pairs={{0,1},{1,0},{2,3},{3,2},{4,5},{5,4},{6,7},{7,6},{8,9},{9,8},{10,11... | collective-permute-start | bytes 405512 | tf_op jit(solution)/shard_map/ppermute | solution.py:558
  4.5 1.9 %collective-permute-start = (f32[264,128]{1,0:T(8,128)S(1)}, f32[264,128]{1,0:T(8,128)S(1)}, u32[]{:S(2)}, u32[]{:S(2)}) collective-permute-start(f32[264,128]{1,0:T(8,128)S(1)} %shard_map.82.pack_ref), channel_id=1, source_target_pairs={{1,2},{3,4},{5,6},{7,8},{9,10},{11,12},{13,14},{15,16},{17,18},{19... | collective-permute-start | bytes 405512 | tf_op jit(solution)/shard_map/ppermute | solution.py:557
  6.4 0.1 add_bitcast_fusion.place_ref
  6.5 0.0 copy-done.5
  6.5 0.6 %shard_map.83 = (bf16[1536,256]{1,0:T(8,128)(2,1)S(1)}, bf16[1536,256]{1,0:T(8,128)(2,1)S(1)}, bf16[512,256]{1,0:T(8,128)(2,1)S(1)}, bf16[512,256]{1,0:T(8,128)(...) custom-call(s32[1,2]{1,0:T(1,128)S(1)} %add_bitcast_fusion.place_ref, ...), custom_call_target="tpu_custom_call" | custom-call | tf_op jit(solution)/shard_map/pallas_call | solution.py:497
  7.1 0.0 collective-permute-done.1.other_ref
  7.1 0.0 copy-done
  7.1 0.0 copy-done.2
  7.1 0.0 copy-done.3
  7.1 0.0 copy-done.4
  7.1 2.3 %shard_map.84 = (f32[256,128]{1,0:T(8,128)S(1)}, bf16[256,256]{1,0:T(8,128)(2,1)S(1)}, f32[256,128]{1,0:T(8,128)S(1)}, f32[256,128]{1,0:T(8,128)S(1)}, f32[256,1...) custom-call(s32[1,2]{1,0:T(1,128)S(1)} %add_bitcast_fusion.place_ref, ...), custom_call_target="tpu_custom_call" | custom-call | tf_op jit(solution)/shard_map/pallas_call | solution.py:497
  9.5 3.6 %collective-permute-start.3 = (f32[256,128]{1,0:T(8,128)S(1)}, f32[256,128]{1,0:T(8,128)S(1)}, u32[]{:S(2)}, u32[]{:S(2)}) collective-permute-start(f32[256,128]{1,0:T(8,128)S(1)} %get-tuple-element.47), channel_id=1, source_target_pairs={{1,2},{3,4},{5,6},{7,8},{9,10},{11,12},{13,14},{15,16},{17,18},{19... | collective-permute-start | bytes 393224 | tf_op jit(solution)/shard_map/ppermute | solution.py:572
  13.1 0.0 collective-permute-done.far_ref
  13.1 1.6 %shard_map.85 = (f32[256,128]{1,0:T(8,128)S(1)}, f32[256,128]{1,0:T(8,128)S(1)}, bf16[1536,256]{1,0:T(8,128)(2,1)S(1)}, bf16[512,256]{1,0:T(8,128)(2,1)S(1)}, bf...) custom-call(s32[1,2]{1,0:T(1,128)S(1)} %add_bitcast_fusion.place_ref, ...), custom_call_target="tpu_custom_call" | custom-call | tf_op jit(solution)/shard_map/pallas_call | solution.py:497
  14.7 0.1 collective-permute-start.2
  14.8 1.5 %shard_map.86 = (f32[256,128]{1,0:T(8,128)S(1)}, f32[128,256]{1,0:T(8,128)S(1)}, f32[256,128]{1,0:T(8,128)S(1)}, f32[1,128]{1,0:T(1,128)S(1)}) custom-call(s32[1,2]{1,0:T(1,128)S(1)} %add_bitcast_fusion.place_ref, f32[264,128]{1,0:T(8,128)S(1)} %shard_map.82.pack_ref, s32[6,256]{1,0:T(8,128)S(1)} %copy-done.5, f32[264,128]{1,0:T(8,128)S(1)} %collective-permute-done.far_ref, ...), custom_call_target="tpu_custom_call" | custom-call | flops 1000000000 | bytes 2000000 | tf_op jit(solution)/shard_map/pallas_call | solution.py:497
  16.2 0.0 collective-permute-done.3.two_ref
  16.3 0.0 collective-permute-done.2.one_ref
  16.3 0.0 copy-start.1
  16.3 2.5 %shard_map.87 = f32[1,128]{1,0:T(1,128)S(1)} custom-call(bf16[2560,256]{1,0:T(8,128)(2,1)S(1)} %copy-done, f32[256,128]{1,0:T(8,128)S(1)} %get-tuple-element.46.send_ref, f32[256,128]{1,0:T(8,128)S(1)} %collective-permute-done.2.one_ref, f32[256,128]{1,0:T(8,128)S(1)} %collective-permute-done.3.two_ref, f32[256,128]{1,0:T(8,128)S(1)} %get-tuple-element.49.lacked_ref, ...), custom_call_target="tpu_custom_call" | custom-call | tf_op jit(solution)/shard_map/pallas_call | solution.py:497
  18.8 0.1 broadcast_in_dim.2
  18.8 28.3 %all_to_all.8 = f32[256,1,128]{2,1,0:T(1,128)S(1)} all-to-all(f32[256,1,128]{2,1,0:T(1,128)S(1)} %broadcast_in_dim.2), channel_id=1, replica_groups=mesh['leaf'=256] {'leaf'}, dimensions={0} | all-to-all | bytes 262144 | tf_op jit(solution)/shard_map/all_to_all | solution.py:597
  47.1 0.0 copy-done.1
  47.1 1.2 %shard_map.88 = f32[128,256]{1,0:T(8,128)} custom-call(f32[256,128]{1,0:T(8,128)S(1)} %bitcast.9, f32[128,256]{1,0:T(8,128)S(1)} %bitcast.11, f32[128,256]{1,0:T(8,128)S(1)} %get-tuple-element.64.image_ref), custom_call_target="tpu_custom_call" | custom-call | tf_op jit(solution)/shard_map/pallas_call | solution.py:497
Async XLA Ops:
  0.0 6.5 %copy-start.5 = (s32[6,256]{1,0:T(8,128)S(1)}, s32[6,256]{1,0:T(8,128)}, u32[]{:S(2)}) copy-start(s32[6,256]{1,0:T(8,128)} %neighbours_ref.5) | copy-start | bytes 18436
  0.0 7.1 %copy-start = (bf16[2560,256]{1,0:T(8,128)(2,1)S(1)}, bf16[2560,256]{1,0:T(8,128)(2,1)}, u32[]{:S(2)}) copy-start(bf16[2560,256]{1,0:T(8,128)(2,1)} %constant.12.clone.table) | copy-start | bytes 3932164
  0.0 7.1 %copy-start.2 = (f32[64,256]{1,0:T(8,128)S(1)}, f32[64,256]{1,0:T(8,128)}, u32[]{:S(2)}) copy-start(f32[64,256]{1,0:T(8,128)} %mass_ref.1) | copy-start | bytes 196612
  0.0 7.1 %copy-start.3 = (f32[64,256]{1,0:T(8,128)S(1)}, f32[64,256]{1,0:T(8,128)}, u32[]{:S(2)}) copy-start(f32[64,256]{1,0:T(8,128)} %curve_ref.1) | copy-start | bytes 196612
  0.0 7.1 %copy-start.4 = (f32[64,64]{1,0:T(8,128)S(1)}, f32[64,64]{1,0:T(8,128)}, u32[]{:S(2)}) copy-start(f32[64,64]{1,0:T(8,128)} %stiffness_ref.1) | copy-start | bytes 49156
  1.2 5.9 %collective-permute-start.1 = (f32[264,128]{1,0:T(8,128)S(1)}, f32[264,128]{1,0:T(8,128)S(1)}, u32[]{:S(2)}, u32[]{:S(2)}) collective-permute-start(f32[264,128]{1,0:T(8,128)S(1)} %shard_map.82.pack_ref), channel_id=1, source_target_pairs={{0,1},{1,0},{2,3},{3,2},{4,5},{5,4},{6,7},{7,6},{8,9},{9,8},{10,11... | collective-permute-start | bytes 405512 | tf_op jit(solution)/shard_map/ppermute | solution.py:558
  4.5 8.6 %collective-permute-start = (f32[264,128]{1,0:T(8,128)S(1)}, f32[264,128]{1,0:T(8,128)S(1)}, u32[]{:S(2)}, u32[]{:S(2)}) collective-permute-start(f32[264,128]{1,0:T(8,128)S(1)} %shard_map.82.pack_ref), channel_id=1, source_target_pairs={{1,2},{3,4},{5,6},{7,8},{9,10},{11,12},{13,14},{15,16},{17,18},{19... | collective-permute-start | bytes 405512 | tf_op jit(solution)/shard_map/ppermute | solution.py:557
  9.5 6.8 %collective-permute-start.3 = (f32[256,128]{1,0:T(8,128)S(1)}, f32[256,128]{1,0:T(8,128)S(1)}, u32[]{:S(2)}, u32[]{:S(2)}) collective-permute-start(f32[256,128]{1,0:T(8,128)S(1)} %get-tuple-element.47), channel_id=1, source_target_pairs={{1,2},{3,4},{5,6},{7,8},{9,10},{11,12},{13,14},{15,16},{17,18},{19... | collective-permute-start | bytes 393224 | tf_op jit(solution)/shard_map/ppermute | solution.py:572
  14.7 1.6 %collective-permute-start.2 = (f32[256,128]{1,0:T(8,128)S(1)}, f32[256,128]{1,0:T(8,128)S(1)}, u32[]{:S(2)}, u32[]{:S(2)}) collective-permute-start(f32[256,128]{1,0:T(8,128)S(1)} %get-tuple-element.46.send_ref), channel_id=1, source_target_pairs={{0,1},{1,0},{2,3},{3,2},{4,5},{5,4},{6,7},{7,6},{8,9},{9,8},{10,11... | collective-permute-start | bytes 393224 | tf_op jit(solution)/shard_map/ppermute | solution.py:580
  16.3 30.9 %copy-start.1 = (f32[2,64,256]{2,1,0:T(8,128)S(1)}, f32[2,64,256]{2,1,0:T(8,128)}, u32[]{:S(2)}) copy-start(f32[2,64,256]{2,1,0:T(8,128)} %param.8) | copy-start | bytes 393220

commit v12 on v11

--- a/solution.py
+++ b/solution.py
@@ -403,8 +403,8 @@
     return length, values * jnp.where(length > 0.0, 1.0 / jnp.where(length > 0.0, length, 1.0), 0.0)
 
 
-def in_lanes(shape, values):
-    lane = lax.broadcasted_iota(jnp.int32, shape, 1)
+def in_lanes(shape, values, first):
+    lane = lax.broadcasted_iota(jnp.int32, shape, 1) - first
     row = jnp.zeros(shape, F32)
     for at, value in enumerate(values):
         row = jnp.where(lane == at, value, row)
@@ -443,12 +443,16 @@
     rest = image - r02 * zero - r12 * one
     r22 = jnp.sqrt(total(rest * rest))
     values = (length_ref[0:1, 0:1], r01 + again, r11, r02, r12, r22)
-    stats_ref[...] = in_lanes(stats_ref.shape, values)
+    first = len(values) * (lax.axis_index("leaf") % 2)
+    stats_ref[...] = in_lanes(stats_ref.shape, values, first)
 
 
 def final_kernel(stats_ref, cot_ref, image_ref, out_ref):
     table = stats_ref[...].T
-    a0, a1, b1, a2, b2, c2 = [table[at : at + 1, :] for at in range(6)]
+    a0, a1, b1, a2, b2, c2 = [
+        jnp.concatenate([table[at : at + 1, :], table[at + 6 : at + 7, :]], axis=1)
+        for at in range(6)
+    ]
     r00_sq = total(a0 * a0)
     r00 = jnp.sqrt(r00_sq)
     f01 = total(a0 * a1) / r00_sq
@@ -594,8 +598,14 @@
         [table, send, one, two, lacked, image, diagonal, zero, length, faces_two, two_fine, two_pick,
          two_back, two_face] + [kept[name] for name in CHOSEN + MADE[1:]],
     )
+    stats = stats + lax.ppermute(stats, "leaf", pairs_one)
     gathered = lax.all_to_all(
-        jnp.broadcast_to(stats, (count, LANES)), "leaf", 0, 0, tiled=True
+        jnp.broadcast_to(stats, (count // 2, LANES)),
+        "leaf",
+        0,
+        0,
+        axis_index_groups=[list(range(0, count, 2)), list(range(1, count, 2))],
+        tiled=True,
     )
     out = call(final_kernel, shape(*flat.shape), [vmem] * 3, (gathered, flat, turned))
     return out.reshape(cotangent.shape)

time: 48.4 us -> 48.4 us (level)
  blocking collectives: 28.3 us -> 26.9 us
  waiting for transfers between devices: 0.01 us -> 0.83 us
  starting transfers between devices: 8.96 us -> 9.54 us
    all_to_all x1, blocking collectives: 28.3 us -> 26.9 us  [on_device(): lax.all_to_all(jnp.broadcast_to(stats, (count // 2, LANES)), 'leaf', 0, 0...]
    ppermute x0 -> x1, waiting for transfers between devices: none -> 0.82 us  [on_device(): stats = stats + lax.ppermute(stats, 'leaf', pairs_one)]
    ppermute x0 -> x1, starting transfers between devices: none -> 0.58 us  [on_device(): stats = stats + lax.ppermute(stats, 'leaf', pairs_one)]
  transfers between devices with their start and end apart: 4 -> 5, of which waited for: 0 -> 1; matrix products, arithmetic and copies ran while one was open for 0% -> 0% of each run, Pallas kernels for 12% -> 12%
where the time goes in v12:
time: 48.4 us; the launch traced here: 48.2 us
  blocking collectives  26.9 us (56%)
  Pallas kernels  10.7 us (22%)
  starting transfers between devices  9.54 us (20%)
  waiting for transfers between devices  0.83 us (2%)
    all_to_all x1, blocking collectives, on_device(): lax.all_to_all(jnp.broadcast_to(stats, (count // 2, LANES)), 'leaf', 0, 0...  26.9 us
    pallas_call x7, Pallas kernels, call(): pl.pallas_call(kernel, out_shape=outs, in_specs=specs, out_specs=jax.tree...  10.7 us
    ppermute x1, starting transfers between devices, on_device(): two = lax.ppermute(scaled, 'leaf', pairs_two)  3.64 us
    ppermute x1, starting transfers between devices, on_device(): one = lax.ppermute(pack, 'leaf', pairs_one)  3.32 us
    ppermute x1, starting transfers between devices, on_device(): far = lax.ppermute(pack, 'leaf', pairs_two)  1.91 us
  transfers between devices with their start and end apart: 5, of which 1 were waited for; matrix products, arithmetic and copies ran while one was open for 0% of the time, Pallas kernels for 12%

profile of v12, /device:TPU:1, one launch (start us, length us, event | category | flops | bytes accessed | tf_op | source)
XLA Modules:
  0.0 48.2 jit_solution(6372273819524258891)
XLA Ops:
  0.0 0.0 copy-start.5
  0.0 0.0 copy-start
  0.0 0.0 copy-start.2
  0.0 0.0 copy-start.3
  0.0 0.0 copy-start.4
  0.0 1.1 %shard_map.82.pack_ref = f32[264,128]{1,0:T(8,128)S(1)} custom-call(f32[128,256]{1,0:T(8,128)} %bitcast.11, s32[1,256]{1,0:T(1,128)} %bitcast.13, s32[6,128]{1,0:T(8,128)} %mortars_hbm.1), custom_call_target="tpu_custom_call" | custom-call | flops 10000000000 | bytes 4000000 | tf_op jit(solution)/shard_map/pallas_call | solution.py:501
  1.2 3.3 %collective-permute-start.1 = (f32[264,128]{1,0:T(8,128)S(1)}, f32[264,128]{1,0:T(8,128)S(1)}, u32[]{:S(2)}, u32[]{:S(2)}) collective-permute-start(f32[264,128]{1,0:T(8,128)S(1)} %shard_map.82.pack_ref), channel_id=1, source_target_pairs={{0,1},{1,0},{2,3},{3,2},{4,5},{5,4},{6,7},{7,6},{8,9},{9,8},{10,11... | collective-permute-start | bytes 405512 | tf_op jit(solution)/shard_map/ppermute | solution.py:562
  4.5 1.9 %collective-permute-start = (f32[264,128]{1,0:T(8,128)S(1)}, f32[264,128]{1,0:T(8,128)S(1)}, u32[]{:S(2)}, u32[]{:S(2)}) collective-permute-start(f32[264,128]{1,0:T(8,128)S(1)} %shard_map.82.pack_ref), channel_id=1, source_target_pairs={{1,2},{3,4},{5,6},{7,8},{9,10},{11,12},{13,14},{15,16},{17,18},{19... | collective-permute-start | bytes 405512 | tf_op jit(solution)/shard_map/ppermute | solution.py:561
  6.4 0.1 add_bitcast_fusion.place_ref
  6.5 0.0 copy-done.5
  6.5 0.6 %shard_map.83 = (bf16[1536,256]{1,0:T(8,128)(2,1)S(1)}, bf16[1536,256]{1,0:T(8,128)(2,1)S(1)}, bf16[512,256]{1,0:T(8,128)(2,1)S(1)}, bf16[512,256]{1,0:T(8,128)(...) custom-call(s32[1,2]{1,0:T(1,128)S(1)} %add_bitcast_fusion.place_ref, ...), custom_call_target="tpu_custom_call" | custom-call | tf_op jit(solution)/shard_map/pallas_call | solution.py:501
  7.1 0.0 collective-permute-done.1.other_ref
  7.1 0.0 copy-done
  7.1 0.0 copy-done.2
  7.1 0.0 copy-done.3
  7.1 0.0 copy-done.4
  7.1 2.3 %shard_map.84 = (f32[256,128]{1,0:T(8,128)S(1)}, bf16[256,256]{1,0:T(8,128)(2,1)S(1)}, f32[256,128]{1,0:T(8,128)S(1)}, f32[256,128]{1,0:T(8,128)S(1)}, f32[256,1...) custom-call(s32[1,2]{1,0:T(1,128)S(1)} %add_bitcast_fusion.place_ref, ...), custom_call_target="tpu_custom_call" | custom-call | tf_op jit(solution)/shard_map/pallas_call | solution.py:501
  9.5 3.6 %collective-permute-start.3 = (f32[256,128]{1,0:T(8,128)S(1)}, f32[256,128]{1,0:T(8,128)S(1)}, u32[]{:S(2)}, u32[]{:S(2)}) collective-permute-start(f32[256,128]{1,0:T(8,128)S(1)} %get-tuple-element.47), channel_id=1, source_target_pairs={{1,2},{3,4},{5,6},{7,8},{9,10},{11,12},{13,14},{15,16},{17,18},{19... | collective-permute-start | bytes 393224 | tf_op jit(solution)/shard_map/ppermute | solution.py:576
  13.1 0.0 collective-permute-done.far_ref
  13.1 1.6 %shard_map.85 = (f32[256,128]{1,0:T(8,128)S(1)}, f32[256,128]{1,0:T(8,128)S(1)}, bf16[1536,256]{1,0:T(8,128)(2,1)S(1)}, bf16[512,256]{1,0:T(8,128)(2,1)S(1)}, bf...) custom-call(s32[1,2]{1,0:T(1,128)S(1)} %add_bitcast_fusion.place_ref, ...), custom_call_target="tpu_custom_call" | custom-call | tf_op jit(solution)/shard_map/pallas_call | solution.py:501
  14.7 0.1 collective-permute-start.2
  14.8 1.5 %shard_map.86 = (f32[256,128]{1,0:T(8,128)S(1)}, f32[128,256]{1,0:T(8,128)S(1)}, f32[256,128]{1,0:T(8,128)S(1)}, f32[1,128]{1,0:T(1,128)S(1)}) custom-call(s32[1,2]{1,0:T(1,128)S(1)} %add_bitcast_fusion.place_ref, f32[264,128]{1,0:T(8,128)S(1)} %shard_map.82.pack_ref, s32[6,256]{1,0:T(8,128)S(1)} %copy-done.5, f32[264,128]{1,0:T(8,128)S(1)} %collective-permute-done.far_ref, ...), custom_call_target="tpu_custom_call" | custom-call | flops 1000000000 | bytes 2000000 | tf_op jit(solution)/shard_map/pallas_call | solution.py:501
  16.2 0.0 collective-permute-done.3.two_ref
  16.3 0.0 collective-permute-done.2.one_ref
  16.3 0.0 copy-start.1
  16.3 2.5 %shard_map.87 = f32[1,128]{1,0:T(1,128)S(1)} custom-call(bf16[2560,256]{1,0:T(8,128)(2,1)S(1)} %copy-done, f32[256,128]{1,0:T(8,128)S(1)} %get-tuple-element.46.send_ref, f32[256,128]{1,0:T(8,128)S(1)} %collective-permute-done.2.one_ref, f32[256,128]{1,0:T(8,128)S(1)} %collective-permute-done.3.two_ref, f32[256,128]{1,0:T(8,128)S(1)} %get-tuple-element.49.lacked_ref, ...), custom_call_target="tpu_custom_call" | custom-call | tf_op jit(solution)/shard_map/pallas_call | solution.py:501
  18.8 0.6 %collective-permute-start.4 = (f32[1,128]{1,0:T(1,128)S(1)}, f32[1,128]{1,0:T(1,128)S(1)}, u32[]{:S(2)}, u32[]{:S(2)}) collective-permute-start(f32[1,128]{1,0:T(1,128)S(1)} %shard_map.87), channel_id=1, source_target_pairs={{0,1},{1,0},{2,3},{3,2},{4,5},{5,4},{6,7},{7,6},{8,9},{9,8},{10,11... | collective-permute-start | bytes 1544 | tf_op jit(solution)/shard_map/ppermute | solution.py:601
  19.3 0.8 %collective-permute-done.4 = f32[1,128]{1,0:T(1,128)S(1)} collective-permute-done((f32[1,128]{1,0:T(1,128)S(1)}, f32[1,128]{1,0:T(1,128)S(1)}, u32[]{:S(2)}, u32[]{:S(2)}) %collective-permute-start.4) | collective-permute-done | bytes 544 | tf_op jit(solution)/shard_map/ppermute | solution.py:601
  20.2 26.9 %all_to_all.8 = f32[128,1,128]{2,1,0:T(1,128)S(1)} all-to-all(f32[128,1,128]{2,1,0:T(1,128)S(1)} %broadcast_in_dim.2), channel_id=1, replica_groups={{0,2,4,6,8,10,12,14,16,18,20,22,24,26,28,30,32,34,36,38,40,42,44,46,48,..., dimensions={0} | all-to-all | bytes 131072 | tf_op jit(solution)/shard_map/all_to_all | solution.py:602
  47.1 0.0 copy-done.1
  47.1 1.2 %shard_map.88 = f32[128,256]{1,0:T(8,128)} custom-call(f32[128,128]{1,0:T(8,128)S(1)} %bitcast.10, f32[128,256]{1,0:T(8,128)S(1)} %bitcast.12, f32[128,256]{1,0:T(8,128)S(1)} %get-tuple-element.64.image_ref), custom_call_target="tpu_custom_call" | custom-call | tf_op jit(solution)/shard_map/pallas_call | solution.py:501
  (2 shorter events, 0.0 us)
Async XLA Ops:
  0.0 6.5 %copy-start.5 = (s32[6,256]{1,0:T(8,128)S(1)}, s32[6,256]{1,0:T(8,128)}, u32[]{:S(2)}) copy-start(s32[6,256]{1,0:T(8,128)} %neighbours_ref.5) | copy-start | bytes 18436
  0.0 7.1 %copy-start = (bf16[2560,256]{1,0:T(8,128)(2,1)S(1)}, bf16[2560,256]{1,0:T(8,128)(2,1)}, u32[]{:S(2)}) copy-start(bf16[2560,256]{1,0:T(8,128)(2,1)} %constant.12.clone.table) | copy-start | bytes 3932164
  0.0 7.1 %copy-start.2 = (f32[64,256]{1,0:T(8,128)S(1)}, f32[64,256]{1,0:T(8,128)}, u32[]{:S(2)}) copy-start(f32[64,256]{1,0:T(8,128)} %mass_ref.1) | copy-start | bytes 196612
  0.0 7.1 %copy-start.3 = (f32[64,256]{1,0:T(8,128)S(1)}, f32[64,256]{1,0:T(8,128)}, u32[]{:S(2)}) copy-start(f32[64,256]{1,0:T(8,128)} %curve_ref.1) | copy-start | bytes 196612
  0.0 7.1 %copy-start.4 = (f32[64,64]{1,0:T(8,128)S(1)}, f32[64,64]{1,0:T(8,128)}, u32[]{:S(2)}) copy-start(f32[64,64]{1,0:T(8,128)} %stiffness_ref.1) | copy-start | bytes 49156
  1.2 5.9 %collective-permute-start.1 = (f32[264,128]{1,0:T(8,128)S(1)}, f32[264,128]{1,0:T(8,128)S(1)}, u32[]{:S(2)}, u32[]{:S(2)}) collective-permute-start(f32[264,128]{1,0:T(8,128)S(1)} %shard_map.82.pack_ref), channel_id=1, source_target_pairs={{0,1},{1,0},{2,3},{3,2},{4,5},{5,4},{6,7},{7,6},{8,9},{9,8},{10,11... | collective-permute-start | bytes 405512 | tf_op jit(solution)/shard_map/ppermute | solution.py:562
  4.5 8.6 %collective-permute-start = (f32[264,128]{1,0:T(8,128)S(1)}, f32[264,128]{1,0:T(8,128)S(1)}, u32[]{:S(2)}, u32[]{:S(2)}) collective-permute-start(f32[264,128]{1,0:T(8,128)S(1)} %shard_map.82.pack_ref), channel_id=1, source_target_pairs={{1,2},{3,4},{5,6},{7,8},{9,10},{11,12},{13,14},{15,16},{17,18},{19... | collective-permute-start | bytes 405512 | tf_op jit(solution)/shard_map/ppermute | solution.py:561
  9.5 6.8 %collective-permute-start.3 = (f32[256,128]{1,0:T(8,128)S(1)}, f32[256,128]{1,0:T(8,128)S(1)}, u32[]{:S(2)}, u32[]{:S(2)}) collective-permute-start(f32[256,128]{1,0:T(8,128)S(1)} %get-tuple-element.47), channel_id=1, source_target_pairs={{1,2},{3,4},{5,6},{7,8},{9,10},{11,12},{13,14},{15,16},{17,18},{19... | collective-permute-start | bytes 393224 | tf_op jit(solution)/shard_map/ppermute | solution.py:576
  14.7 1.6 %collective-permute-start.2 = (f32[256,128]{1,0:T(8,128)S(1)}, f32[256,128]{1,0:T(8,128)S(1)}, u32[]{:S(2)}, u32[]{:S(2)}) collective-permute-start(f32[256,128]{1,0:T(8,128)S(1)} %get-tuple-element.46.send_ref), channel_id=1, source_target_pairs={{0,1},{1,0},{2,3},{3,2},{4,5},{5,4},{6,7},{7,6},{8,9},{9,8},{10,11... | collective-permute-start | bytes 393224 | tf_op jit(solution)/shard_map/ppermute | solution.py:584
  16.3 30.8 %copy-start.1 = (f32[2,64,256]{2,1,0:T(8,128)S(1)}, f32[2,64,256]{2,1,0:T(8,128)}, u32[]{:S(2)}) copy-start(f32[2,64,256]{2,1,0:T(8,128)} %param.8) | copy-start | bytes 393220
  18.8 1.4 %collective-permute-start.4 = (f32[1,128]{1,0:T(1,128)S(1)}, f32[1,128]{1,0:T(1,128)S(1)}, u32[]{:S(2)}, u32[]{:S(2)}) collective-permute-start(f32[1,128]{1,0:T(1,128)S(1)} %shard_map.87), channel_id=1, source_target_pairs={{0,1},{1,0},{2,3},{3,2},{4,5},{5,4},{6,7},{7,6},{8,9},{9,8},{10,11... | collective-permute-start | bytes 1544 | tf_op jit(solution)/shard_map/ppermute | solution.py:601

commit v13 on v11

--- a/solution.py
+++ b/solution.py
@@ -125,8 +125,10 @@
 
 
 def prep_kernel(cot_hbm, levels_hbm, mortars_hbm, pack_ref, cot_ref, levels_ref, mortars_ref, sems):
+    quarters = [pl.ds(32 * at, 32) for at in range(4)]
+    pairs = [(cot_hbm.at[rows, :], cot_ref.at[rows, :]) for rows in quarters]
     for copy in fetch(
-        ((cot_hbm, cot_ref), (levels_hbm, levels_ref), (mortars_hbm, mortars_ref)), sems
+        pairs + [(levels_hbm, levels_ref), (mortars_hbm, mortars_ref)], sems
     ):
         copy.wait()
     leaves = cot_ref.shape[1]
@@ -178,22 +180,26 @@
 def from_blocks(parts, faces, fine, picks, backs, coarse_faces, face, own_back, table, own):
     slots = own_back.shape[1]
     rows = jnp.concatenate(parts, axis=0)
-    seen = dot(jnp.concatenate(faces, axis=1), rows)
     chosen = [dot(jnp.concatenate(fine, axis=1), rows)]
     chosen += [dot(pick_rows, part) for pick_rows, part in zip(picks, parts)]
     trace = side_traces(
         jnp.concatenate(chosen, axis=0), [opposite(face)] * 4 + coarse_faces, table
     )
     quarters = [trace[slots * q : slots * (q + 1), :] for q in range(4)]
+    if own:
+        quarters.append(trace[4 * slots : 5 * slots, :])
+    back = lower(quarters, face, table, TABLE_ROWS if own else STAY_AT)
+    seen = dot(jnp.concatenate(faces, axis=1), rows)
     sent = lift(trace[4 * slots :, :], coarse_faces, table)
     ordered = [
         sent[q][slots * k : slots * (k + 1), :] for k in range(len(parts)) for q in range(4)
     ]
-    if own:
-        quarters.append(trace[4 * slots : 5 * slots, :])
-    ordered.append(lower(quarters, face, table, TABLE_ROWS if own else STAY_AT))
-    mortars = dot(jnp.concatenate(backs + [own_back], axis=1), jnp.concatenate(ordered, axis=0))
-    return fold(mortars) + across_faces(seen)
+    mortars = dot(
+        jnp.concatenate(backs + [own_back], axis=1), jnp.concatenate(ordered + [back], axis=0)
+    )
+    mortars = fold(mortars)
+    seen = across_faces(seen)
+    return mortars + seen
 
 
 def placed(lapped):
@@ -366,10 +372,6 @@
     rows = pack_ref[0:leaves, :]
     parts = split(rows)
     index = own_index(pad_rows(neighbours_ref[...]), far)
-    seen = jnp.concatenate(
-        [dot(pick(index[f ^ 1 : (f ^ 1) + 1, :], (leaves, leaves), 0), parts) for f in range(FACES)],
-        axis=0,
-    )
     face = face_ref[...]
     mortars, _, _ = read_tables(pack_ref, leaves)
     far_mortars, columns, scale = read_tables(far_ref, leaves)
@@ -380,8 +382,12 @@
     chosen = dot(jnp.concatenate(chosen + [own_pick_ref[...]], axis=0), parts)
     trace = side_traces(chosen, [opposite(far_face)] * 4 + [face], table)
     quarters = [trace[slots * q : slots * (q + 1), :] for q in range(4)]
-    sent = lift(trace[4 * slots :, :], [face], table)
-    sent.append(lower(quarters, far_face, table, STAY_AT))
+    lowered = lower(quarters, far_face, table, STAY_AT)
+    seen = jnp.concatenate(
+        [dot(pick(index[f ^ 1 : (f ^ 1) + 1, :], (leaves, leaves), 0), parts) for f in range(FACES)],
+        axis=0,
+    )
+    sent = lift(trace[4 * slots :, :], [face], table) + [lowered]
     back = fine_backs(mortars, far, leaves)
     extra = fine_count([back], [face])
     backs = [back, pick(far_mortars[0:1, :] - far, (leaves, slots), 0)]
@@ -549,7 +555,7 @@
             pltpu.VMEM(flat.shape, F32),
             pltpu.VMEM(levels.shape, jnp.int32),
             pltpu.VMEM(mortars.shape, jnp.int32),
-            pltpu.SemaphoreType.DMA((3,)),
+            pltpu.SemaphoreType.DMA((6,)),
         ],
         flops=10_000_000_000,
         moved=4_000_000,

time: 48.4 us -> 47.8 us (0.988)
  Pallas kernels: 10.7 us -> 10 us
    pallas_call x7, Pallas kernels: 10.7 us -> 10 us  [call(): pl.pallas_call(kernel, out_shape=outs, in_specs=specs, out_specs=jax.tree...]
where the time goes in v13:
time: 47.8 us; the launch traced here: 47.6 us
  blocking collectives  28.3 us (59%)
  Pallas kernels  10 us (21%)
  starting transfers between devices  8.95 us (19%)
    all_to_all x1, blocking collectives, on_device(): lax.all_to_all(jnp.broadcast_to(stats, (count, LANES)), 'leaf', 0, 0, til...  28.3 us
    pallas_call x7, Pallas kernels, call(): pl.pallas_call(kernel, out_shape=outs, in_specs=specs, out_specs=jax.tree...  10 us
    ppermute x1, starting transfers between devices, on_device(): two = lax.ppermute(scaled, 'leaf', pairs_two)  3.64 us
    ppermute x1, starting transfers between devices, on_device(): one = lax.ppermute(pack, 'leaf', pairs_one)  3.31 us
    ppermute x1, starting transfers between devices, on_device(): far = lax.ppermute(pack, 'leaf', pairs_two)  1.91 us
  transfers between devices with their start and end apart: 4, of which 0 were waited for; matrix products, arithmetic and copies ran while one was open for 0% of the time, Pallas kernels for 12%

profile of v13, /device:TPU:1, one launch (start us, length us, event | category | flops | bytes accessed | tf_op | source)
XLA Modules:
  0.0 47.6 jit_solution(6331661228786470029)
XLA Ops:
  0.0 0.0 copy-start.5
  0.0 0.0 copy-start
  0.0 0.0 copy-start.2
  0.0 0.0 copy-start.3
  0.0 0.0 copy-start.4
  0.0 1.1 %shard_map.82.pack_ref = f32[264,128]{1,0:T(8,128)S(1)} custom-call(f32[128,256]{1,0:T(8,128)} %bitcast.10, s32[1,256]{1,0:T(1,128)} %bitcast.13, s32[6,128]{1,0:T(8,128)} %mortars_hbm.1), custom_call_target="tpu_custom_call" | custom-call | flops 10000000000 | bytes 4000000 | tf_op jit(solution)/shard_map/pallas_call | solution.py:503
  1.1 3.3 %collective-permute-start.1 = (f32[264,128]{1,0:T(8,128)S(1)}, f32[264,128]{1,0:T(8,128)S(1)}, u32[]{:S(2)}, u32[]{:S(2)}) collective-permute-start(f32[264,128]{1,0:T(8,128)S(1)} %shard_map.82.pack_ref), channel_id=1, source_target_pairs={{0,1},{1,0},{2,3},{3,2},{4,5},{5,4},{6,7},{7,6},{8,9},{9,8},{10,11... | collective-permute-start | bytes 405512 | tf_op jit(solution)/shard_map/ppermute | solution.py:564
  4.4 1.9 %collective-permute-start = (f32[264,128]{1,0:T(8,128)S(1)}, f32[264,128]{1,0:T(8,128)S(1)}, u32[]{:S(2)}, u32[]{:S(2)}) collective-permute-start(f32[264,128]{1,0:T(8,128)S(1)} %shard_map.82.pack_ref), channel_id=1, source_target_pairs={{1,2},{3,4},{5,6},{7,8},{9,10},{11,12},{13,14},{15,16},{17,18},{19... | collective-permute-start | bytes 405512 | tf_op jit(solution)/shard_map/ppermute | solution.py:563
  6.4 0.1 add_bitcast_fusion.place_ref
  6.4 0.0 copy-done.5
  6.4 0.6 %shard_map.83 = (bf16[1536,256]{1,0:T(8,128)(2,1)S(1)}, bf16[1536,256]{1,0:T(8,128)(2,1)S(1)}, bf16[512,256]{1,0:T(8,128)(2,1)S(1)}, bf16[512,256]{1,0:T(8,128)(...) custom-call(s32[1,2]{1,0:T(1,128)S(1)} %add_bitcast_fusion.place_ref, ...), custom_call_target="tpu_custom_call" | custom-call | tf_op jit(solution)/shard_map/pallas_call | solution.py:503
  7.0 0.0 collective-permute-done.1.other_ref
  7.0 0.0 copy-done
  7.0 0.0 copy-done.2
  7.1 0.0 copy-done.3
  7.1 0.0 copy-done.4
  7.1 2.0 %shard_map.84 = (f32[256,128]{1,0:T(8,128)S(1)}, bf16[256,256]{1,0:T(8,128)(2,1)S(1)}, f32[256,128]{1,0:T(8,128)S(1)}, f32[256,128]{1,0:T(8,128)S(1)}, f32[256,1...) custom-call(s32[1,2]{1,0:T(1,128)S(1)} %add_bitcast_fusion.place_ref, ...), custom_call_target="tpu_custom_call" | custom-call | tf_op jit(solution)/shard_map/pallas_call | solution.py:503
  9.1 3.6 %collective-permute-start.3 = (f32[256,128]{1,0:T(8,128)S(1)}, f32[256,128]{1,0:T(8,128)S(1)}, u32[]{:S(2)}, u32[]{:S(2)}) collective-permute-start(f32[256,128]{1,0:T(8,128)S(1)} %get-tuple-element.47), channel_id=1, source_target_pairs={{1,2},{3,4},{5,6},{7,8},{9,10},{11,12},{13,14},{15,16},{17,18},{19... | collective-permute-start | bytes 393224 | tf_op jit(solution)/shard_map/ppermute | solution.py:578
  12.8 0.0 collective-permute-done.far_ref
  12.8 1.5 %shard_map.85 = (f32[256,128]{1,0:T(8,128)S(1)}, f32[256,128]{1,0:T(8,128)S(1)}, bf16[1536,256]{1,0:T(8,128)(2,1)S(1)}, bf16[512,256]{1,0:T(8,128)(2,1)S(1)}, bf...) custom-call(s32[1,2]{1,0:T(1,128)S(1)} %add_bitcast_fusion.place_ref, ...), custom_call_target="tpu_custom_call" | custom-call | tf_op jit(solution)/shard_map/pallas_call | solution.py:503
  14.3 0.1 collective-permute-start.2
  14.4 1.4 %shard_map.86 = (f32[256,128]{1,0:T(8,128)S(1)}, f32[128,256]{1,0:T(8,128)S(1)}, f32[256,128]{1,0:T(8,128)S(1)}, f32[1,128]{1,0:T(1,128)S(1)}) custom-call(s32[1,2]{1,0:T(1,128)S(1)} %add_bitcast_fusion.place_ref, f32[264,128]{1,0:T(8,128)S(1)} %shard_map.82.pack_ref, s32[6,256]{1,0:T(8,128)S(1)} %copy-done.5, f32[264,128]{1,0:T(8,128)S(1)} %collective-permute-done.far_ref, ...), custom_call_target="tpu_custom_call" | custom-call | flops 1000000000 | bytes 2000000 | tf_op jit(solution)/shard_map/pallas_call | solution.py:503
  15.8 0.0 collective-permute-done.3.two_ref
  15.8 0.0 collective-permute-done.2.one_ref
  15.8 0.0 copy-start.1
  15.8 2.3 %shard_map.87 = f32[1,128]{1,0:T(1,128)S(1)} custom-call(bf16[2560,256]{1,0:T(8,128)(2,1)S(1)} %copy-done, f32[256,128]{1,0:T(8,128)S(1)} %get-tuple-element.46.send_ref, f32[256,128]{1,0:T(8,128)S(1)} %collective-permute-done.2.one_ref, f32[256,128]{1,0:T(8,128)S(1)} %collective-permute-done.3.two_ref, f32[256,128]{1,0:T(8,128)S(1)} %get-tuple-element.49.lacked_ref, ...), custom_call_target="tpu_custom_call" | custom-call | tf_op jit(solution)/shard_map/pallas_call | solution.py:503
  18.1 0.1 broadcast_in_dim.2
  18.2 28.3 %all_to_all.8 = f32[256,1,128]{2,1,0:T(1,128)S(1)} all-to-all(f32[256,1,128]{2,1,0:T(1,128)S(1)} %broadcast_in_dim.2), channel_id=1, replica_groups=mesh['leaf'=256] {'leaf'}, dimensions={0} | all-to-all | bytes 262144 | tf_op jit(solution)/shard_map/all_to_all | solution.py:603
  46.5 0.0 copy-done.1
  46.5 1.2 %shard_map.88 = f32[128,256]{1,0:T(8,128)} custom-call(f32[256,128]{1,0:T(8,128)S(1)} %bitcast.9, f32[128,256]{1,0:T(8,128)S(1)} %bitcast.11, f32[128,256]{1,0:T(8,128)S(1)} %get-tuple-element.64.image_ref), custom_call_target="tpu_custom_call" | custom-call | tf_op jit(solution)/shard_map/pallas_call | solution.py:503
Async XLA Ops:
  0.0 6.4 %copy-start.5 = (s32[6,256]{1,0:T(8,128)S(1)}, s32[6,256]{1,0:T(8,128)}, u32[]{:S(2)}) copy-start(s32[6,256]{1,0:T(8,128)} %neighbours_ref.5) | copy-start | bytes 18436
  0.0 7.0 %copy-start = (bf16[2560,256]{1,0:T(8,128)(2,1)S(1)}, bf16[2560,256]{1,0:T(8,128)(2,1)}, u32[]{:S(2)}) copy-start(bf16[2560,256]{1,0:T(8,128)(2,1)} %constant.12.clone.table) | copy-start | bytes 3932164
  0.0 7.0 %copy-start.2 = (f32[64,256]{1,0:T(8,128)S(1)}, f32[64,256]{1,0:T(8,128)}, u32[]{:S(2)}) copy-start(f32[64,256]{1,0:T(8,128)} %mass_ref.1) | copy-start | bytes 196612
  0.0 7.0 %copy-start.3 = (f32[64,256]{1,0:T(8,128)S(1)}, f32[64,256]{1,0:T(8,128)}, u32[]{:S(2)}) copy-start(f32[64,256]{1,0:T(8,128)} %curve_ref.1) | copy-start | bytes 196612
  0.0 7.0 %copy-start.4 = (f32[64,64]{1,0:T(8,128)S(1)}, f32[64,64]{1,0:T(8,128)}, u32[]{:S(2)}) copy-start(f32[64,64]{1,0:T(8,128)} %stiffness_ref.1) | copy-start | bytes 49156
  1.1 5.9 %collective-permute-start.1 = (f32[264,128]{1,0:T(8,128)S(1)}, f32[264,128]{1,0:T(8,128)S(1)}, u32[]{:S(2)}, u32[]{:S(2)}) collective-permute-start(f32[264,128]{1,0:T(8,128)S(1)} %shard_map.82.pack_ref), channel_id=1, source_target_pairs={{0,1},{1,0},{2,3},{3,2},{4,5},{5,4},{6,7},{7,6},{8,9},{9,8},{10,11... | collective-permute-start | bytes 405512 | tf_op jit(solution)/shard_map/ppermute | solution.py:564
  4.4 8.3 %collective-permute-start = (f32[264,128]{1,0:T(8,128)S(1)}, f32[264,128]{1,0:T(8,128)S(1)}, u32[]{:S(2)}, u32[]{:S(2)}) collective-permute-start(f32[264,128]{1,0:T(8,128)S(1)} %shard_map.82.pack_ref), channel_id=1, source_target_pairs={{1,2},{3,4},{5,6},{7,8},{9,10},{11,12},{13,14},{15,16},{17,18},{19... | collective-permute-start | bytes 405512 | tf_op jit(solution)/shard_map/ppermute | solution.py:563
  9.1 6.6 %collective-permute-start.3 = (f32[256,128]{1,0:T(8,128)S(1)}, f32[256,128]{1,0:T(8,128)S(1)}, u32[]{:S(2)}, u32[]{:S(2)}) collective-permute-start(f32[256,128]{1,0:T(8,128)S(1)} %get-tuple-element.47), channel_id=1, source_target_pairs={{1,2},{3,4},{5,6},{7,8},{9,10},{11,12},{13,14},{15,16},{17,18},{19... | collective-permute-start | bytes 393224 | tf_op jit(solution)/shard_map/ppermute | solution.py:578
  14.3 1.5 %collective-permute-start.2 = (f32[256,128]{1,0:T(8,128)S(1)}, f32[256,128]{1,0:T(8,128)S(1)}, u32[]{:S(2)}, u32[]{:S(2)}) collective-permute-start(f32[256,128]{1,0:T(8,128)S(1)} %get-tuple-element.46.send_ref), channel_id=1, source_target_pairs={{0,1},{1,0},{2,3},{3,2},{4,5},{5,4},{6,7},{7,6},{8,9},{9,8},{10,11... | collective-permute-start | bytes 393224 | tf_op jit(solution)/shard_map/ppermute | solution.py:586
  15.8 30.7 %copy-start.1 = (f32[2,64,256]{2,1,0:T(8,128)S(1)}, f32[2,64,256]{2,1,0:T(8,128)}, u32[]{:S(2)}) copy-start(f32[2,64,256]{2,1,0:T(8,128)} %param.8) | copy-start | bytes 393220

commit v14 on v13

--- a/solution.py
+++ b/solution.py
@@ -124,7 +124,9 @@
     return copies
 
 
-def prep_kernel(cot_hbm, levels_hbm, mortars_hbm, pack_ref, cot_ref, levels_ref, mortars_ref, sems):
+def prep_kernel(
+    cot_hbm, levels_hbm, mortars_hbm, pack_ref, wide_ref, cot_ref, levels_ref, mortars_ref, sems
+):
     quarters = [pl.ds(32 * at, 32) for at in range(4)]
     pairs = [(cot_hbm.at[rows, :], cot_ref.at[rows, :]) for rows in quarters]
     for copy in fetch(
@@ -137,6 +139,8 @@
     table = mortars_ref[...].astype(F32) + 1.0
     halves = [scale[:, k * table.shape[1] : (k + 1) * table.shape[1]] for k in range(2)]
     pack_ref[leaves : leaves + 8, :] = jnp.concatenate([table] + halves, axis=0)
+    wide_ref[0 : leaves + 8, :] = pack_ref[...]
+    wide_ref[leaves + 8 :, :] = jnp.zeros((8, LANES), F32)
 
 
 CHOSEN = (
@@ -546,9 +550,9 @@
     def stay_out(*arrays):
         return tuple(pltpu.with_memory_space_constraint(array, pltpu.HBM) for array in arrays)
 
-    pack = call(
+    pack, wide = call(
         prep_kernel,
-        shape(leaves + 8, LANES),
+        [shape(leaves + 8, LANES), shape(leaves + 16, LANES)],
         [hbm] * 3,
         stay_out(flat, levels, mortars),
         scratch=[
@@ -560,7 +564,7 @@
         flops=10_000_000_000,
         moved=4_000_000,
     )
-    far = lax.ppermute(pack, "leaf", pairs_two)
+    far = lax.ppermute(wide, "leaf", pairs_two)
     one = lax.ppermute(pack, "leaf", pairs_one)
     chosen = call(
         choose_kernel,

time: 47.8 us -> 48 us (level)
  starting transfers between devices: 8.95 us -> 8 us
  waiting for transfers between devices: 0.01 us -> 0.73 us
    ppermute x1, starting transfers between devices: 3.31 us -> 0.09 us  [on_device(): one = lax.ppermute(pack, 'leaf', pairs_one)]
    ppermute x1, starting transfers between devices: 1.91 us -> 4.59 us  [on_device(): far = lax.ppermute(wide, 'leaf', pairs_two)]
    ppermute x1, waiting for transfers between devices: 0.01 us -> 0.67 us  [on_device(): one = lax.ppermute(pack, 'leaf', pairs_one)]
  transfers between devices with their start and end apart: 4 -> 4, of which waited for: 0 -> 2; matrix products, arithmetic and copies ran while one was open for 0% -> 0% of each run, Pallas kernels for 12% -> 12%
where the time goes in v14:
time: 48 us; the launch traced here: 47.8 us
  blocking collectives  28.7 us (60%)
  Pallas kernels  10 us (21%)
  starting transfers between devices  8 us (17%)
  waiting for transfers between devices  0.73 us (2%)
    all_to_all x1, blocking collectives, on_device(): lax.all_to_all(jnp.broadcast_to(stats, (count, LANES)), 'leaf', 0, 0, til...  28.7 us
    pallas_call x7, Pallas kernels, call(): pl.pallas_call(kernel, out_shape=outs, in_specs=specs, out_specs=jax.tree...  10 us
    ppermute x1, starting transfers between devices, on_device(): far = lax.ppermute(wide, 'leaf', pairs_two)  4.59 us
    ppermute x1, starting transfers between devices, on_device(): two = lax.ppermute(scaled, 'leaf', pairs_two)  3.22 us
  transfers between devices with their start and end apart: 4, of which 2 were waited for; matrix products, arithmetic and copies ran while one was open for 0% of the time, Pallas kernels for 12%

profile of v14, /device:TPU:1, one launch (start us, length us, event | category | flops | bytes accessed | tf_op | source)
XLA Modules:
  0.0 47.8 jit_solution(5132496098930248312)
XLA Ops:
  0.0 0.0 copy-start.5
  0.0 0.0 copy-start
  0.0 0.0 copy-start.2
  0.0 0.0 copy-start.3
  0.0 0.0 copy-start.4
  0.0 1.1 %shard_map.82 = (f32[264,128]{1,0:T(8,128)S(1)}, f32[272,128]{1,0:T(8,128)S(1)}) custom-call(f32[128,256]{1,0:T(8,128)} %bitcast.10, s32[1,256]{1,0:T(1,128)} %bitcast.13, s32[6,128]{1,0:T(8,128)} %mortars_hbm.1), custom_call_target="tpu_custom_call" | custom-call | flops 10000000000 | bytes 4000000 | tf_op jit(solution)/shard_map/pallas_call | solution.py:507
  1.1 4.6 %collective-permute-start = (f32[272,128]{1,0:T(8,128)S(1)}, f32[272,128]{1,0:T(8,128)S(1)}, u32[]{:S(2)}, u32[]{:S(2)}) collective-permute-start(f32[272,128]{1,0:T(8,128)S(1)} %get-tuple-element.38), channel_id=1, source_target_pairs={{1,2},{3,4},{5,6},{7,8},{9,10},{11,12},{13,14},{15,16},{17,18},{19... | collective-permute-start | bytes 417800 | tf_op jit(solution)/shard_map/ppermute | solution.py:567
  5.7 0.1 collective-permute-start.1
  5.8 0.1 add_bitcast_fusion.place_ref
  5.9 0.0 copy-done.5
  5.9 0.6 %shard_map.83 = (bf16[1536,256]{1,0:T(8,128)(2,1)S(1)}, bf16[1536,256]{1,0:T(8,128)(2,1)S(1)}, bf16[512,256]{1,0:T(8,128)(2,1)S(1)}, bf16[512,256]{1,0:T(8,128)(...) custom-call(s32[1,2]{1,0:T(1,128)S(1)} %add_bitcast_fusion.place_ref, ...), custom_call_target="tpu_custom_call" | custom-call | tf_op jit(solution)/shard_map/pallas_call | solution.py:507
  6.5 0.7 %collective-permute-done.1.other_ref = f32[264,128]{1,0:T(8,128)S(1)} collective-permute-done((f32[264,128]{1,0:T(8,128)S(1)}, f32[264,128]{1,0:T(8,128)S(1)}, u32[]{:S(2)}, u32[]{:S(2)}) %collective-permute-start.1) | collective-permute-done | bytes 135200 | tf_op jit(solution)/shard_map/ppermute | solution.py:568
  7.2 0.0 copy-done
  7.2 0.0 copy-done.2
  7.2 0.0 copy-done.3
  7.2 0.0 copy-done.4
  7.2 2.0 %shard_map.84 = (f32[256,128]{1,0:T(8,128)S(1)}, bf16[256,256]{1,0:T(8,128)(2,1)S(1)}, f32[256,128]{1,0:T(8,128)S(1)}, f32[256,128]{1,0:T(8,128)S(1)}, f32[256,1...) custom-call(s32[1,2]{1,0:T(1,128)S(1)} %add_bitcast_fusion.place_ref, ...), custom_call_target="tpu_custom_call" | custom-call | tf_op jit(solution)/shard_map/pallas_call | solution.py:507
  9.2 3.2 %collective-permute-start.3 = (f32[256,128]{1,0:T(8,128)S(1)}, f32[256,128]{1,0:T(8,128)S(1)}, u32[]{:S(2)}, u32[]{:S(2)}) collective-permute-start(f32[256,128]{1,0:T(8,128)S(1)} %get-tuple-element.51), channel_id=1, source_target_pairs={{1,2},{3,4},{5,6},{7,8},{9,10},{11,12},{13,14},{15,16},{17,18},{19... | collective-permute-start | bytes 393224 | tf_op jit(solution)/shard_map/ppermute | solution.py:582
  12.5 0.0 collective-permute-done.far_ref
  12.5 1.5 %shard_map.85 = (f32[256,128]{1,0:T(8,128)S(1)}, f32[256,128]{1,0:T(8,128)S(1)}, bf16[1536,256]{1,0:T(8,128)(2,1)S(1)}, bf16[512,256]{1,0:T(8,128)(2,1)S(1)}, bf...) custom-call(s32[1,2]{1,0:T(1,128)S(1)} %add_bitcast_fusion.place_ref, ...), custom_call_target="tpu_custom_call" | custom-call | tf_op jit(solution)/shard_map/pallas_call | solution.py:507
  14.0 0.1 collective-permute-start.2
  14.1 1.4 %shard_map.86 = (f32[256,128]{1,0:T(8,128)S(1)}, f32[128,256]{1,0:T(8,128)S(1)}, f32[256,128]{1,0:T(8,128)S(1)}, f32[1,128]{1,0:T(1,128)S(1)}) custom-call(s32[1,2]{1,0:T(1,128)S(1)} %add_bitcast_fusion.place_ref, f32[264,128]{1,0:T(8,128)S(1)} %get-tuple-element.37.pack_ref, s32[6,256]{1,0:T(8,128)S(1)} %copy-done.5, ...), custom_call_target="tpu_custom_call" | custom-call | flops 1000000000 | bytes 2000000 | tf_op jit(solution)/shard_map/pallas_call | solution.py:507
  15.4 0.1 collective-permute-done.3.two_ref
  15.5 0.0 collective-permute-done.2.one_ref
  15.5 0.0 copy-start.1
  15.5 2.3 %shard_map.87 = f32[1,128]{1,0:T(1,128)S(1)} custom-call(bf16[2560,256]{1,0:T(8,128)(2,1)S(1)} %copy-done, f32[256,128]{1,0:T(8,128)S(1)} %get-tuple-element.50.send_ref, f32[256,128]{1,0:T(8,128)S(1)} %collective-permute-done.2.one_ref, f32[256,128]{1,0:T(8,128)S(1)} %collective-permute-done.3.two_ref, f32[256,128]{1,0:T(8,128)S(1)} %get-tuple-element.53.lacked_ref, ...), custom_call_target="tpu_custom_call" | custom-call | tf_op jit(solution)/shard_map/pallas_call | solution.py:507
  17.8 0.1 broadcast_in_dim.2
  17.9 28.7 %all_to_all.8 = f32[256,1,128]{2,1,0:T(1,128)S(1)} all-to-all(f32[256,1,128]{2,1,0:T(1,128)S(1)} %broadcast_in_dim.2), channel_id=1, replica_groups=mesh['leaf'=256] {'leaf'}, dimensions={0} | all-to-all | bytes 262144 | tf_op jit(solution)/shard_map/all_to_all | solution.py:607
  46.6 0.0 copy-done.1
  46.6 1.2 %shard_map.88 = f32[128,256]{1,0:T(8,128)} custom-call(f32[256,128]{1,0:T(8,128)S(1)} %bitcast.9, f32[128,256]{1,0:T(8,128)S(1)} %bitcast.11, f32[128,256]{1,0:T(8,128)S(1)} %get-tuple-element.68.image_ref), custom_call_target="tpu_custom_call" | custom-call | tf_op jit(solution)/shard_map/pallas_call | solution.py:507
Async XLA Ops:
  0.0 5.9 %copy-start.5 = (s32[6,256]{1,0:T(8,128)S(1)}, s32[6,256]{1,0:T(8,128)}, u32[]{:S(2)}) copy-start(s32[6,256]{1,0:T(8,128)} %neighbours_ref.5) | copy-start | bytes 18436
  0.0 7.2 %copy-start = (bf16[2560,256]{1,0:T(8,128)(2,1)S(1)}, bf16[2560,256]{1,0:T(8,128)(2,1)}, u32[]{:S(2)}) copy-start(bf16[2560,256]{1,0:T(8,128)(2,1)} %constant.12.clone.table) | copy-start | bytes 3932164
  0.0 7.2 %copy-start.2 = (f32[64,256]{1,0:T(8,128)S(1)}, f32[64,256]{1,0:T(8,128)}, u32[]{:S(2)}) copy-start(f32[64,256]{1,0:T(8,128)} %mass_ref.1) | copy-start | bytes 196612
  0.0 7.2 %copy-start.3 = (f32[64,256]{1,0:T(8,128)S(1)}, f32[64,256]{1,0:T(8,128)}, u32[]{:S(2)}) copy-start(f32[64,256]{1,0:T(8,128)} %curve_ref.1) | copy-start | bytes 196612
  0.0 7.2 %copy-start.4 = (f32[64,64]{1,0:T(8,128)S(1)}, f32[64,64]{1,0:T(8,128)}, u32[]{:S(2)}) copy-start(f32[64,64]{1,0:T(8,128)} %stiffness_ref.1) | copy-start | bytes 49156
  1.1 11.3 %collective-permute-start = (f32[272,128]{1,0:T(8,128)S(1)}, f32[272,128]{1,0:T(8,128)S(1)}, u32[]{:S(2)}, u32[]{:S(2)}) collective-permute-start(f32[272,128]{1,0:T(8,128)S(1)} %get-tuple-element.38), channel_id=1, source_target_pairs={{1,2},{3,4},{5,6},{7,8},{9,10},{11,12},{13,14},{15,16},{17,18},{19... | collective-permute-start | bytes 417800 | tf_op jit(solution)/shard_map/ppermute | solution.py:567
  5.7 1.4 %collective-permute-start.1 = (f32[264,128]{1,0:T(8,128)S(1)}, f32[264,128]{1,0:T(8,128)S(1)}, u32[]{:S(2)}, u32[]{:S(2)}) collective-permute-start(f32[264,128]{1,0:T(8,128)S(1)} %get-tuple-element.37.pack_ref), channel_id=1, source_target_pairs={{0,1},{1,0},{2,3},{3,2},{4,5},{5,4},{6,7},{7,6},{8,9},{9,8},{10,11... | collective-permute-start | bytes 405512 | tf_op jit(solution)/shard_map/ppermute | solution.py:568
  9.2 6.3 %collective-permute-start.3 = (f32[256,128]{1,0:T(8,128)S(1)}, f32[256,128]{1,0:T(8,128)S(1)}, u32[]{:S(2)}, u32[]{:S(2)}) collective-permute-start(f32[256,128]{1,0:T(8,128)S(1)} %get-tuple-element.51), channel_id=1, source_target_pairs={{1,2},{3,4},{5,6},{7,8},{9,10},{11,12},{13,14},{15,16},{17,18},{19... | collective-permute-start | bytes 393224 | tf_op jit(solution)/shard_map/ppermute | solution.py:582
  14.0 1.5 %collective-permute-start.2 = (f32[256,128]{1,0:T(8,128)S(1)}, f32[256,128]{1,0:T(8,128)S(1)}, u32[]{:S(2)}, u32[]{:S(2)}) collective-permute-start(f32[256,128]{1,0:T(8,128)S(1)} %get-tuple-element.50.send_ref), channel_id=1, source_target_pairs={{0,1},{1,0},{2,3},{3,2},{4,5},{5,4},{6,7},{7,6},{8,9},{9,8},{10,11... | collective-permute-start | bytes 393224 | tf_op jit(solution)/shard_map/ppermute | solution.py:590
  15.5 31.1 %copy-start.1 = (f32[2,64,256]{2,1,0:T(8,128)S(1)}, f32[2,64,256]{2,1,0:T(8,128)}, u32[]{:S(2)}) copy-start(f32[2,64,256]{2,1,0:T(8,128)} %param.8) | copy-start | bytes 393220

commit v15 on v14

--- a/solution.py
+++ b/solution.py
@@ -145,8 +145,10 @@
 
 CHOSEN = (
     "own", "one", "own_fine", "one_fine", "own_pick", "own_back", "fine_back", "face",
+    "stiff", "mass", "curve", "scale",
 )
-MADE = ("diagonal", "stiff", "mass", "curve", "scale", "one_pick", "one_back", "one_face")
+AHEAD = ("two", "two_fine", "count")
+MADE = ("diagonal", "one_pick", "one_back", "one_face")
 
 
 def across_faces(seen):
@@ -262,8 +264,10 @@
     )
 
 
-def choose_kernel(place_ref, pack_ref, neighbours_ref, *refs):
-    made = dict(zip(CHOSEN, refs))
+def choose_kernel(
+    place_ref, pack_ref, neighbours_ref, mass_ref, curve_ref, stiffness_ref, *refs
+):
+    made = dict(zip(CHOSEN + AHEAD, refs))
     leaves = pack_ref.shape[0] - 8
     offset, first = place_ref[0:1, 0:1], place_ref[0:1, 1:2]
     mortars, columns, _ = read_tables(pack_ref, leaves)
@@ -272,8 +276,30 @@
     made["fine_back"][...] = fine_backs(mortars, offset, leaves)
     made["own_back"][...] = pick(mortars[0:1, :] - offset, (leaves, slots), 0)
     made["own_pick"][...] = pick(columns[:, 0:1] - offset, (slots, leaves), 1)
-    kinds = (("own", "own_fine", offset, True), ("one", "one_fine", offset + first, False))
+    kinds = (
+        ("own", "own_fine", offset, True),
+        ("one", "one_fine", offset + first, False),
+        ("two", "two_fine", offset - first, False),
+    )
     choose(made, kinds, columns, pad_rows(neighbours_ref[...]), leaves)
+    made["count"][...] = fine_count([made["fine_back"][...]], [columns[:, 1:2]]) + sum(
+        face_nodes(jnp.int32(f)) for f in range(FACES)
+    )
+    wide = jnp.concatenate([stiffness_ref[...]] * 2, axis=1)
+    wide = jnp.concatenate([wide, wide], axis=0)
+    same = (lax.broadcasted_iota(jnp.int32, wide.shape, 0) < NODES) == (
+        lax.broadcasted_iota(jnp.int32, wide.shape, 1) < NODES
+    )
+    wide = split(jnp.where(same, wide, 0.0))
+    wide = jnp.concatenate([wide, wide], axis=0)
+    made["stiff"][...] = wide
+    both = jnp.concatenate([mass_ref[...], curve_ref[...]], axis=0).T
+    turned = pltpu.roll(both, NODES, 1)
+    low = lax.broadcasted_iota(jnp.int32, (1, LANES), 1) < NODES
+    made["mass"][...] = jnp.where(low, both, turned)
+    made["curve"][...] = jnp.where(low, -turned, 0.0)
+    scale = jnp.broadcast_to(read_tables(pack_ref, leaves)[2], both.shape)
+    made["scale"][...] = scale
 
 
 def image_of(vector, lapped, kept):
@@ -282,7 +308,7 @@
 
 
 def first_kernel(
-    place_ref, pack_ref, other_ref, table, mass_ref, curve_ref, stiffness_ref, *refs
+    place_ref, pack_ref, other_ref, table, count_ref, *refs
 ):
     kept = dict(zip(CHOSEN + MADE, refs))
     image_ref, far_ref = refs[len(CHOSEN) + len(MADE) :]
@@ -297,29 +323,12 @@
     kept["one_back"][...] = other_back
     kept["one_face"][...] = other_face
     back = kept["fine_back"][...]
-    diagonal = (
-        fine_count([back, other_back], [face, other_face])
-        + sum(face_nodes(jnp.int32(f)) for f in range(FACES))
-    )
+    diagonal = count_ref[...] + fine_count([other_back], [other_face])
     kept["diagonal"][...] = diagonal
-    wide = jnp.concatenate([stiffness_ref[...]] * 2, axis=1)
-    wide = jnp.concatenate([wide, wide], axis=0)
-    same = (lax.broadcasted_iota(jnp.int32, wide.shape, 0) < NODES) == (
-        lax.broadcasted_iota(jnp.int32, wide.shape, 1) < NODES
-    )
-    wide = split(jnp.where(same, wide, 0.0))
-    wide = jnp.concatenate([wide, wide], axis=0)
-    kept["stiff"][...] = wide
-    both = jnp.concatenate([mass_ref[...], curve_ref[...]], axis=0).T
-    turned = pltpu.roll(both, NODES, 1)
-    low = lax.broadcasted_iota(jnp.int32, (1, LANES), 1) < NODES
-    kept["mass"][...] = jnp.where(low, both, turned)
-    kept["curve"][...] = jnp.where(low, -turned, 0.0)
-    scale = jnp.broadcast_to(read_tables(pack_ref, leaves)[2], both.shape)
-    kept["scale"][...] = scale
+    scale = kept["scale"][...]
     rows = pack_ref[0:leaves, :]
     parts = [split(rows), split(other_ref[0:leaves, :])]
-    lapped = diagonal * rows + fold(dot(parts[0], wide)) - from_blocks(
+    lapped = diagonal * rows + fold(dot(parts[0], kept["stiff"][...])) - from_blocks(
         parts,
         [kept["own"][...], kept["one"][...]],
         [kept["own_fine"][...], kept["one_fine"][...]],
@@ -337,16 +346,13 @@
 
 
 def far_kernel(
-    place_ref, pack_ref, neighbours_ref, far_ref, table, scale_ref, diagonal_ref, partial_ref,
-    own_back_ref, face_ref, image_ref, send_ref, two_ref, two_fine_ref, pick_ref, back_ref,
-    far_face_ref, total_ref
+    place_ref, pack_ref, far_ref, table, scale_ref, diagonal_ref, partial_ref, own_back_ref,
+    face_ref, two_ref, two_fine_ref, image_ref, send_ref, pick_ref, back_ref, far_face_ref,
+    total_ref
 ):
     leaves = pack_ref.shape[0] - 8
     offset = place_ref[0:1, 0:1]
     start = offset - place_ref[0:1, 1:2]
-    _, columns, _ = read_tables(pack_ref, leaves)
-    neighbours = pad_rows(neighbours_ref[...])
-    choose((two_ref, two_fine_ref), ((0, 1, start, False),), columns, neighbours, leaves)
     mortars, columns, _ = read_tables(far_ref, leaves)
     slots = mortars.shape[1]
     face = columns[:, 1:2]
@@ -566,26 +572,26 @@
     )
     far = lax.ppermute(wide, "leaf", pairs_two)
     one = lax.ppermute(pack, "leaf", pairs_one)
-    chosen = call(
+    *chosen, faces_two, two_fine, count_own = call(
         choose_kernel,
-        [shapes[name] for name in CHOSEN],
-        [vmem] * 3,
-        (place, pack, neighbours),
+        [shapes[name] for name in CHOSEN] + [faces, fine, rows],
+        [vmem] * 6,
+        (place, pack, neighbours, nodal_mass, curvature, stiffness),
     )
     *made, partial, scaled = call(
         first_kernel,
         [shapes[name] for name in MADE] + [rows, rows],
-        [vmem] * (7 + len(CHOSEN)),
-        [place, pack, one, table, nodal_mass, curvature, stiffness, *chosen],
+        [vmem] * (5 + len(CHOSEN)),
+        [place, pack, one, table, count_own, *chosen],
     )
     kept = dict(zip(CHOSEN + MADE, [*chosen, *made]))
     two = lax.ppermute(scaled, "leaf", pairs_two)
-    image, send, faces_two, two_fine, two_pick, two_back, two_face, diagonal = call(
+    image, send, two_pick, two_back, two_face, diagonal = call(
         far_kernel,
-        [rows, rows, faces, fine, picks, backs, face, rows],
-        [vmem] * 10,
-        [place, pack, neighbours, far, table, kept["scale"], kept["diagonal"], partial,
-         kept["own_back"], kept["face"]],
+        [rows, rows, picks, backs, face, rows],
+        [vmem] * 11,
+        [place, pack, far, table, kept["scale"], kept["diagonal"], partial, kept["own_back"],
+         kept["face"], faces_two, two_fine],
     )
     one = lax.ppermute(send, "leaf", pairs_one)
     lacked, turned, zero, length = call(

time: 48 us -> 47.9 us (level)
  waiting for transfers between devices: 0.73 us -> 0.01 us
    ppermute x1, waiting for transfers between devices: 0.67 us -> 0.01 us  [on_device(): one = lax.ppermute(pack, 'leaf', pairs_one)]
  transfers between devices with their start and end apart: 4 -> 4, of which waited for: 2 -> 0; matrix products, arithmetic and copies ran while one was open for 0% -> 0% of each run, Pallas kernels for 12% -> 12%
where the time goes in v15:
time: 47.9 us; the launch traced here: 47.7 us
  blocking collectives  28.6 us (60%)
  Pallas kernels  10.4 us (22%)
  starting transfers between devices  8.36 us (17%)
    all_to_all x1, blocking collectives, on_device(): lax.all_to_all(jnp.broadcast_to(stats, (count, LANES)), 'leaf', 0, 0, til...  28.6 us
    pallas_call x7, Pallas kernels, call(): pl.pallas_call(kernel, out_shape=outs, in_specs=specs, out_specs=jax.tree...  10.4 us
    ppermute x1, starting transfers between devices, on_device(): far = lax.ppermute(wide, 'leaf', pairs_two)  4.59 us
    ppermute x1, starting transfers between devices, on_device(): two = lax.ppermute(scaled, 'leaf', pairs_two)  3.58 us
  transfers between devices with their start and end apart: 4, of which 0 were waited for; matrix products, arithmetic and copies ran while one was open for 0% of the time, Pallas kernels for 12%

profile of v15, /device:TPU:1, one launch (start us, length us, event | category | flops | bytes accessed | tf_op | source)
XLA Modules:
  0.0 47.7 jit_solution(3122453222353666972)
XLA Ops:
  0.0 0.0 copy-start.2
  0.0 0.0 copy-start.3
  0.0 0.0 copy-start.4
  0.0 0.0 copy-start.5
  0.0 0.0 copy-start
  0.0 1.1 %shard_map.82 = (f32[264,128]{1,0:T(8,128)S(1)}, f32[272,128]{1,0:T(8,128)S(1)}) custom-call(f32[128,256]{1,0:T(8,128)} %bitcast.10, s32[1,256]{1,0:T(1,128)} %bitcast.13, s32[6,128]{1,0:T(8,128)} %mortars_hbm.1), custom_call_target="tpu_custom_call" | custom-call | flops 10000000000 | bytes 4000000 | tf_op jit(solution)/shard_map/pallas_call | solution.py:513
  1.1 4.6 %collective-permute-start = (f32[272,128]{1,0:T(8,128)S(1)}, f32[272,128]{1,0:T(8,128)S(1)}, u32[]{:S(2)}, u32[]{:S(2)}) collective-permute-start(f32[272,128]{1,0:T(8,128)S(1)} %get-tuple-element.39), channel_id=1, source_target_pairs={{1,2},{3,4},{5,6},{7,8},{9,10},{11,12},{13,14},{15,16},{17,18},{19... | collective-permute-start | bytes 417800 | tf_op jit(solution)/shard_map/ppermute | solution.py:573
  5.7 0.1 collective-permute-start.1
  5.8 0.1 add_bitcast_fusion.place_ref
  5.9 0.0 copy-done.2
  5.9 0.0 copy-done.3
  5.9 0.0 copy-done.4
  5.9 0.0 copy-done.5
  5.9 1.3 %shard_map.83 = (bf16[1536,256]{1,0:T(8,128)(2,1)S(1)}, bf16[1536,256]{1,0:T(8,128)(2,1)S(1)}, bf16[512,256]{1,0:T(8,128)(2,1)S(1)}, bf16[512,256]{1,0:T(8,128)(...) custom-call(s32[1,2]{1,0:T(1,128)S(1)} %add_bitcast_fusion.place_ref, ...), custom_call_target="tpu_custom_call" | custom-call | tf_op jit(solution)/shard_map/pallas_call | solution.py:513
  7.3 0.0 collective-permute-done.1.other_ref
  7.3 0.0 copy-done
  7.3 1.9 %shard_map.84 = (f32[256,128]{1,0:T(8,128)S(1)}, bf16[128,256]{1,0:T(8,128)(2,1)S(1)}, bf16[256,512]{1,0:T(8,128)(2,1)S(1)}, s32[128,1]{1,0:T(8,128)S(1)}, f32[2...) custom-call(s32[1,2]{1,0:T(1,128)S(1)} %add_bitcast_fusion.place_ref, f32[264,128]{1,0:T(8,128)S(1)} %get-tuple-element.38.pack_ref, ...), custom_call_target="tpu_custom_call" | custom-call | tf_op jit(solution)/shard_map/pallas_call | solution.py:513
  9.1 3.6 %collective-permute-start.3 = (f32[256,128]{1,0:T(8,128)S(1)}, f32[256,128]{1,0:T(8,128)S(1)}, u32[]{:S(2)}, u32[]{:S(2)}) collective-permute-start(f32[256,128]{1,0:T(8,128)S(1)} %get-tuple-element.58), channel_id=1, source_target_pairs={{1,2},{3,4},{5,6},{7,8},{9,10},{11,12},{13,14},{15,16},{17,18},{19... | collective-permute-start | bytes 393224 | tf_op jit(solution)/shard_map/ppermute | solution.py:588
  12.7 0.0 collective-permute-done.far_ref
  12.7 1.3 %shard_map.85 = (f32[256,128]{1,0:T(8,128)S(1)}, f32[256,128]{1,0:T(8,128)S(1)}, bf16[128,256]{1,0:T(8,128)(2,1)S(1)}, bf16[256,512]{1,0:T(8,128)(2,1)S(1)}, s32...) custom-call(s32[1,2]{1,0:T(1,128)S(1)} %add_bitcast_fusion.place_ref, f32[264,128]{1,0:T(8,128)S(1)} %get-tuple-element.38.pack_ref, ...), custom_call_target="tpu_custom_call" | custom-call | tf_op jit(solution)/shard_map/pallas_call | solution.py:513
  14.0 0.1 collective-permute-start.2
  14.1 1.4 %shard_map.86 = (f32[256,128]{1,0:T(8,128)S(1)}, f32[128,256]{1,0:T(8,128)S(1)}, f32[256,128]{1,0:T(8,128)S(1)}, f32[1,128]{1,0:T(1,128)S(1)}) custom-call(s32[1,2]{1,0:T(1,128)S(1)} %add_bitcast_fusion.place_ref, f32[264,128]{1,0:T(8,128)S(1)} %get-tuple-element.38.pack_ref, s32[6,256]{1,0:T(8,128)S(1)} %copy-done.5, ...), custom_call_target="tpu_custom_call" | custom-call | flops 1000000000 | bytes 2000000 | tf_op jit(solution)/shard_map/pallas_call | solution.py:513
  15.5 0.0 collective-permute-done.3.two_ref
  15.5 0.0 collective-permute-done.2.one_ref
  15.5 0.0 copy-start.1
  15.5 2.3 %shard_map.87 = f32[1,128]{1,0:T(1,128)S(1)} custom-call(bf16[2560,256]{1,0:T(8,128)(2,1)S(1)} %copy-done, f32[256,128]{1,0:T(8,128)S(1)} %get-tuple-element.57.send_ref, f32[256,128]{1,0:T(8,128)S(1)} %collective-permute-done.2.one_ref, f32[256,128]{1,0:T(8,128)S(1)} %collective-permute-done.3.two_ref, f32[256,128]{1,0:T(8,128)S(1)} %get-tuple-element.60.lacked_ref, ...), custom_call_target="tpu_custom_call" | custom-call | tf_op jit(solution)/shard_map/pallas_call | solution.py:513
  17.9 0.1 broadcast_in_dim.2
  17.9 28.6 %all_to_all.8 = f32[256,1,128]{2,1,0:T(1,128)S(1)} all-to-all(f32[256,1,128]{2,1,0:T(1,128)S(1)} %broadcast_in_dim.2), channel_id=1, replica_groups=mesh['leaf'=256] {'leaf'}, dimensions={0} | all-to-all | bytes 262144 | tf_op jit(solution)/shard_map/all_to_all | solution.py:613
  46.5 0.0 copy-done.1
  46.5 1.2 %shard_map.88 = f32[128,256]{1,0:T(8,128)} custom-call(f32[256,128]{1,0:T(8,128)S(1)} %bitcast.9, f32[128,256]{1,0:T(8,128)S(1)} %bitcast.11, f32[128,256]{1,0:T(8,128)S(1)} %get-tuple-element.70.image_ref), custom_call_target="tpu_custom_call" | custom-call | tf_op jit(solution)/shard_map/pallas_call | solution.py:513
Async XLA Ops:
  0.0 5.9 %copy-start.2 = (f32[64,256]{1,0:T(8,128)S(1)}, f32[64,256]{1,0:T(8,128)}, u32[]{:S(2)}) copy-start(f32[64,256]{1,0:T(8,128)} %mass_ref.1) | copy-start | bytes 196612
  0.0 5.9 %copy-start.3 = (f32[64,256]{1,0:T(8,128)S(1)}, f32[64,256]{1,0:T(8,128)}, u32[]{:S(2)}) copy-start(f32[64,256]{1,0:T(8,128)} %curve_ref.1) | copy-start | bytes 196612
  0.0 5.9 %copy-start.4 = (f32[64,64]{1,0:T(8,128)S(1)}, f32[64,64]{1,0:T(8,128)}, u32[]{:S(2)}) copy-start(f32[64,64]{1,0:T(8,128)} %stiffness_ref.1) | copy-start | bytes 49156
  0.0 5.9 %copy-start.5 = (s32[6,256]{1,0:T(8,128)S(1)}, s32[6,256]{1,0:T(8,128)}, u32[]{:S(2)}) copy-start(s32[6,256]{1,0:T(8,128)} %neighbours_ref.3) | copy-start | bytes 18436
  0.0 7.2 %copy-start = (bf16[2560,256]{1,0:T(8,128)(2,1)S(1)}, bf16[2560,256]{1,0:T(8,128)(2,1)}, u32[]{:S(2)}) copy-start(bf16[2560,256]{1,0:T(8,128)(2,1)} %constant.12.clone.table) | copy-start | bytes 3932164
  1.1 11.6 %collective-permute-start = (f32[272,128]{1,0:T(8,128)S(1)}, f32[272,128]{1,0:T(8,128)S(1)}, u32[]{:S(2)}, u32[]{:S(2)}) collective-permute-start(f32[272,128]{1,0:T(8,128)S(1)} %get-tuple-element.39), channel_id=1, source_target_pairs={{1,2},{3,4},{5,6},{7,8},{9,10},{11,12},{13,14},{15,16},{17,18},{19... | collective-permute-start | bytes 417800 | tf_op jit(solution)/shard_map/ppermute | solution.py:573
  5.7 1.5 %collective-permute-start.1 = (f32[264,128]{1,0:T(8,128)S(1)}, f32[264,128]{1,0:T(8,128)S(1)}, u32[]{:S(2)}, u32[]{:S(2)}) collective-permute-start(f32[264,128]{1,0:T(8,128)S(1)} %get-tuple-element.38.pack_ref), channel_id=1, source_target_pairs={{0,1},{1,0},{2,3},{3,2},{4,5},{5,4},{6,7},{7,6},{8,9},{9,8},{10,11... | collective-permute-start | bytes 405512 | tf_op jit(solution)/shard_map/ppermute | solution.py:574
  9.1 6.4 %collective-permute-start.3 = (f32[256,128]{1,0:T(8,128)S(1)}, f32[256,128]{1,0:T(8,128)S(1)}, u32[]{:S(2)}, u32[]{:S(2)}) collective-permute-start(f32[256,128]{1,0:T(8,128)S(1)} %get-tuple-element.58), channel_id=1, source_target_pairs={{1,2},{3,4},{5,6},{7,8},{9,10},{11,12},{13,14},{15,16},{17,18},{19... | collective-permute-start | bytes 393224 | tf_op jit(solution)/shard_map/ppermute | solution.py:588
  14.0 1.5 %collective-permute-start.2 = (f32[256,128]{1,0:T(8,128)S(1)}, f32[256,128]{1,0:T(8,128)S(1)}, u32[]{:S(2)}, u32[]{:S(2)}) collective-permute-start(f32[256,128]{1,0:T(8,128)S(1)} %get-tuple-element.57.send_ref), channel_id=1, source_target_pairs={{0,1},{1,0},{2,3},{3,2},{4,5},{5,4},{6,7},{7,6},{8,9},{9,8},{10,11... | collective-permute-start | bytes 393224 | tf_op jit(solution)/shard_map/ppermute | solution.py:596
  15.5 31.0 %copy-start.1 = (f32[2,64,256]{2,1,0:T(8,128)S(1)}, f32[2,64,256]{2,1,0:T(8,128)}, u32[]{:S(2)}) copy-start(f32[2,64,256]{2,1,0:T(8,128)} %param.8) | copy-start | bytes 393220
